TPU v7x, 128 devices: a whole 4x4x4 slice. The times are simulated.
128 devices in a mesh: section: 4 (over y_hi, core), dp: 32 (over z, y_lo, x).
Axes of the slice: x: 4, y: 4 (y_hi: 2, y_lo: 2; y = y_hi * 2 + y_lo), z: 4, core: 2. Of those that a mesh axis runs over, the one named last changes fastest.
Arguments:
- frames_in: bfloat16 [4096, 4, 1024], P('dp', 'section'), may hold values from -6 to 6
- in_weights: bfloat16 [1024, 4, 2, 9728], P('dp', 'section'), may hold values from -0.1875 to 0.1875
- down_weights: bfloat16 [2816, 4, 2, 1024], P('dp', 'section'), may hold values from -0.109375 to 0.109375
- gains: bfloat16 [1024, 4, 2, 2], P(None, 'section'), may hold values from 0.099609375 to 1.8984375
- cotangent: bfloat16 [4096, 4, 1024], P('dp', 'section'), may hold values from -6 to 6
- segment_ids: int32 [4096], P('dp'), may hold values from 0 to 15, as said below
- valid: int32 [4096], P('dp'), may hold values 0 or 1
Outputs:
- output: bfloat16 [4096, 4, 1024], P('dp', 'section')
- input_grad: bfloat16 [4096, 4, 1024], P('dp', 'section')
- in_weights_grad: float32 [1024, 4, 2, 9728], P('dp', 'section')
- down_weights_grad: float32 [2816, 4, 2, 1024], P('dp', 'section')
- gains_grad: float32 [1024, 4, 2, 2], P('dp', 'section')
Inputs may be any that keep to these rules, and one draw needn't show every extreme that they name: `segment_ids`: dialogue numbers never fall along the frames, and each of 0 to 15 occurs.
All inputs are finite; a program needn't handle non-finite values. No bound on the sum of `valid` on one device may be relied on, other than what follows from the above.
Results may differ from a plain program's by a relative error of at most 0.02.
Values may be sent and summed in bfloat16 or wider, within the bound.
No kernel may reach another device: no remote copies, remote signals or barrier semaphores. Data moves between devices by JAX's collectives and lax.ppermute only.
A program may use at most 320 MiB of HBM per device.

v0:
```python
import math

import jax
import jax.numpy as jnp
from jax import lax
from jax.sharding import PartitionSpec as P

HEADS = 16
HEAD = 64
FF = 2816
LAYERS = 2
MICRO = 2
NSEG = 16


EPS = 1e-05
NEG = -1e30
HIGH = lax.Precision.HIGHEST
COUNT_BOOST = 4.0


def normalize(state):
    return state * lax.rsqrt(jnp.mean(state * state, axis=-1, keepdims=True) + EPS)


def norm_backward(grad_out, state, gain_row):
    scale = lax.rsqrt(jnp.mean(state * state, axis=-1, keepdims=True) + EPS)
    normed = state * scale
    grad_norm = grad_out * gain_row[None]
    grad_state = scale * (grad_norm - normed * jnp.mean(grad_norm * normed, axis=-1, keepdims=True))
    grad_gain = jnp.sum(grad_out * normed, axis=0)
    return (grad_state, grad_gain)


def row_adder(left_rows, shard_piece):
    return jnp.einsum("fpr,rpe->fpe", left_rows, shard_piece, preferred_element_type=jnp.float32)


def row_mapper(right_side, shard_piece):
    return jnp.einsum("fpe,rpe->fpr", right_side, shard_piece, preferred_element_type=jnp.float32)


def reduce_pair(left_rows, right_side):
    dp_size = lax.axis_size("dp")
    frame_rows, pos_here, row_total = left_rows.shape
    col_total = right_side.shape[2]
    col_block = math.gcd(col_total, 512)
    block_count = col_total // col_block
    right_blocks = right_side.reshape(frame_rows, pos_here, block_count, col_block).transpose(
        2, 0, 1, 3
    )

    def one_block(carry, right_block):
        term = jnp.einsum(
            "fpr,fpc->rpc", left_rows, right_block, preferred_element_type=jnp.float32
        )
        term = term.reshape(dp_size, row_total // dp_size, pos_here, col_block)
        received = lax.all_to_all(
            term.astype(jnp.bfloat16), "dp", split_axis=0, concat_axis=0, tiled=True
        ).astype(term.dtype)
        return (carry, jnp.sum(received, axis=0))

    unused, summed = lax.scan(one_block, jnp.zeros((), jnp.float32), right_blocks)
    return summed.transpose(1, 2, 0, 3).reshape(row_total // dp_size, pos_here, col_total)


def split_heads(matrix):
    return matrix.reshape(matrix.shape[0], matrix.shape[1], HEADS, HEAD)


def attend(queries, keys_values, query_pos):
    width = queries.shape[2]
    total_pos = keys_values.shape[1]
    scores = jnp.einsum(
        "fphe,fjhe->fhpj",
        split_heads(queries),
        split_heads(keys_values[:, :, :width]),
        preferred_element_type=jnp.float32,
    ) / math.sqrt(HEAD)
    allowed = jnp.arange(total_pos)[None, :] <= query_pos[:, None]
    scores = jnp.where(allowed[None, None], scores, NEG)
    peak = jnp.max(scores, axis=-1, keepdims=True)
    exponent_terms = jnp.exp(scores - peak)
    probs = exponent_terms / jnp.sum(exponent_terms, axis=-1, keepdims=True)
    mixed = jnp.einsum(
        "fhpj,fjhe->fphe",
        probs.astype(jnp.bfloat16),
        split_heads(keys_values[:, :, width:]),
        preferred_element_type=jnp.float32,
    )
    return (probs, mixed.reshape(queries.shape))


def attend_backward(grad_mixed16, queries, keys_values, probs):
    frame_rows, local_pos, width = queries.shape
    total_pos = keys_values.shape[1]
    query_heads = split_heads(queries)
    key_heads = split_heads(keys_values[:, :, :width])
    value_heads = split_heads(keys_values[:, :, width:])
    grad_heads = split_heads(grad_mixed16)
    grad_probs = jnp.einsum(
        "fphe,fjhe->fhpj", grad_heads, value_heads, preferred_element_type=jnp.float32
    )
    grad_scores = (
        probs * (grad_probs - jnp.sum(probs * grad_probs, axis=-1, keepdims=True)) / math.sqrt(HEAD)
    )
    grad_queries = jnp.einsum(
        "fhpj,fjhe->fphe", grad_scores, key_heads.astype(jnp.float32), precision=HIGH
    )
    grad_keys = jnp.einsum(
        "fhpj,fphe->fjhe", grad_scores, query_heads.astype(jnp.float32), precision=HIGH
    )
    grad_values = jnp.einsum(
        "fhpj,fphe->fjhe",
        probs.astype(jnp.bfloat16),
        grad_heads,
        preferred_element_type=jnp.float32,
    )
    grad_kv = jnp.concatenate(
        [
            grad_keys.reshape(frame_rows, total_pos, width),
            grad_values.reshape(frame_rows, total_pos, width),
        ],
        axis=2,
    )
    return (grad_queries.reshape(frame_rows, local_pos, width), grad_kv)


def body(frames_in, in_weights, down_weights, gains, cotangent, segment_ids, valid):
    frame_count, local_pos, width = frames_in.shape
    section_index = lax.axis_index("section")
    query_pos = section_index * local_pos + jnp.arange(local_pos)
    gain_all = gains.astype(jnp.float32)
    micro_rows = frame_count // MICRO
    onehot = (segment_ids[:, None] == jnp.arange(NSEG, dtype=jnp.int32)[None, :]).astype(
        jnp.float32
    )
    valid_f = valid.astype(jnp.float32)
    counts = lax.psum(jnp.sum(onehot * valid_f[:, None], axis=0), "dp")
    own_count = jnp.sum(onehot * counts[None, :], axis=1)
    weight = valid_f * (1.0 + COUNT_BOOST / jnp.maximum(own_count, 1.0))

    def layer_forward(state, layer):
        attn_gain = gain_all[:, :, layer, 0].T
        ffn_gain = gain_all[:, :, layer, 1].T
        normed16 = (normalize(state) * attn_gain[None]).astype(jnp.bfloat16)
        qkv = row_adder(
            normed16, lax.all_gather(in_weights[:, :, layer, : 3 * width], "dp", axis=0, tiled=True)
        )
        qkv16 = qkv.astype(jnp.bfloat16)
        queries = qkv16[:, :, :width]
        kv_local = qkv16[:, :, width:]
        gathered = []
        prob_list = []
        mixed_list = []
        for micro in range(MICRO):
            lower_row = micro * micro_rows
            kv_all = lax.all_gather(
                kv_local[lower_row : lower_row + micro_rows], "section", axis=1, tiled=True
            )
            probs, mixed = attend(queries[lower_row : lower_row + micro_rows], kv_all, query_pos)
            gathered.append(kv_all)
            prob_list.append(probs)
            mixed_list.append(mixed)
        mixed16 = jnp.concatenate(mixed_list, axis=0).astype(jnp.bfloat16)
        attn = row_adder(
            mixed16,
            lax.all_gather(
                in_weights[:, :, layer, 3 * width : 4 * width], "dp", axis=0, tiled=True
            ),
        )
        middle = state + attn
        branch16 = (normalize(middle) * ffn_gain[None]).astype(jnp.bfloat16)
        gate_up = row_adder(
            branch16, lax.all_gather(in_weights[:, :, layer, 4 * width :], "dp", axis=0, tiled=True)
        )
        gate = gate_up[:, :, :FF]
        up_part = gate_up[:, :, FF:]
        activated16 = (jax.nn.silu(gate) * up_part).astype(jnp.bfloat16)
        ffn = row_adder(
            activated16, lax.all_gather(down_weights[:, :, layer, :], "dp", axis=0, tiled=True)
        )
        saved = (
            state,
            normed16,
            queries,
            gathered,
            prob_list,
            mixed16,
            middle,
            branch16,
            gate,
            up_part,
            activated16,
        )
        return (middle + ffn, saved)

    state = frames_in.astype(jnp.float32)
    layer_inputs = []
    for layer in range(LAYERS):
        layer_inputs.append(state)
        state, saved = layer_forward(state, layer)
    output = state.astype(jnp.bfloat16)
    grad_state = cotangent.astype(jnp.float32) * weight[:, None, None]
    in_list = [None] * LAYERS
    down_list = [None] * LAYERS
    gain_list = [None] * LAYERS
    for layer in reversed(range(LAYERS)):
        recomputed, saved = layer_forward(layer_inputs[layer], layer)
        grad_out = grad_state
        (
            layer_state,
            layer_normed16,
            layer_queries,
            layer_gathered,
            layer_prob_list,
            layer_mixed16,
            layer_middle,
            layer_branch16,
            layer_gate,
            layer_up_part,
            layer_activated16,
        ) = saved
        layer_attn_gain = gain_all[:, :, layer, 0].T
        layer_ffn_gain = gain_all[:, :, layer, 1].T
        ffn_grad16 = grad_out.astype(jnp.bfloat16)
        grad_act = row_mapper(
            ffn_grad16, lax.all_gather(down_weights[:, :, layer, :], "dp", axis=0, tiled=True)
        )
        sigma = jax.nn.sigmoid(layer_gate)
        grad_gate = grad_act * layer_up_part * sigma * (1.0 + layer_gate * (1.0 - sigma))
        grad_up = grad_act * layer_gate * sigma
        gate_up_grad16 = jnp.concatenate([grad_gate, grad_up], axis=2).astype(jnp.bfloat16)
        grad_branch = row_mapper(
            gate_up_grad16,
            lax.all_gather(in_weights[:, :, layer, 4 * width :], "dp", axis=0, tiled=True),
        )
        grad_norm_two, gain_grad_two = norm_backward(grad_branch, layer_middle, layer_ffn_gain)
        grad_middle = grad_out + grad_norm_two
        attn_grad16 = grad_middle.astype(jnp.bfloat16)
        grad_mixed = row_mapper(
            attn_grad16,
            lax.all_gather(
                in_weights[:, :, layer, 3 * width : 4 * width], "dp", axis=0, tiled=True
            ),
        )
        grad_mixed16 = grad_mixed.astype(jnp.bfloat16)
        query_grads = []
        kv_grads = []
        for layer_micro in range(MICRO):
            layer_lower_row = layer_micro * micro_rows
            grad_query, grad_kv = attend_backward(
                grad_mixed16[layer_lower_row : layer_lower_row + micro_rows],
                layer_queries[layer_lower_row : layer_lower_row + micro_rows],
                layer_gathered[layer_micro],
                layer_prob_list[layer_micro],
            )
            query_grads.append(grad_query)
            kv_grads.append(
                lax.psum_scatter(
                    grad_kv.astype(jnp.bfloat16), "section", scatter_dimension=1, tiled=True
                ).astype(jnp.float32)
            )
        qkv_grad16 = jnp.concatenate(
            [jnp.concatenate(query_grads, axis=0), jnp.concatenate(kv_grads, axis=0)], axis=2
        ).astype(jnp.bfloat16)
        grad_normed = row_mapper(
            qkv_grad16,
            lax.all_gather(in_weights[:, :, layer, : 3 * width], "dp", axis=0, tiled=True),
        )
        grad_norm_one, gain_grad_one = norm_backward(grad_normed, layer_state, layer_attn_gain)
        layer_grad_state = grad_middle + grad_norm_one
        in_pairs = (
            (layer_normed16, qkv_grad16),
            (layer_mixed16, attn_grad16),
            (layer_branch16, gate_up_grad16),
        )
        down_pairs = ((layer_activated16, ffn_grad16),)
        gain_grad = jnp.stack([gain_grad_one, gain_grad_two], axis=-1).transpose(1, 0, 2)
        grad_state, in_pairs, down_pairs, gain_grad = (
            layer_grad_state,
            in_pairs,
            down_pairs,
            gain_grad,
        )
        in_list[layer] = jnp.concatenate(
            [reduce_pair(left_rows, right_side) for left_rows, right_side in in_pairs], axis=2
        )
        down_list[layer] = reduce_pair(down_pairs[0][0], down_pairs[0][1])
        gain_list[layer] = gain_grad
    in_grads = jnp.stack(in_list, axis=2)
    down_grads = jnp.stack(down_list, axis=2)
    gains_grad = lax.psum_scatter(
        jnp.stack(gain_list, axis=2), "dp", scatter_dimension=0, tiled=True
    )
    return (output, grad_state.astype(jnp.bfloat16), in_grads, down_grads, gains_grad)


def solution(mesh):
    placed = (
        P("dp", "section", None),
        P("dp", "section", None, None),
        P("dp", "section", None, None),
        P(None, "section", None, None),
        P("dp", "section", None),
        P("dp"),
        P("dp"),
    )
    return jax.shard_map(
        body,
        mesh=mesh,
        in_specs=placed,
        out_specs=(
            P("dp", "section", None),
            P("dp", "section", None),
            P("dp", "section", None, None),
            P("dp", "section", None, None),
            P("dp", "section", None, None),
        ),
        check_vma=False,
    )
```

profile of v0, /device:TPU:1, one launch (start us, length us, event | category | flops | bytes accessed | tf_op | source)
XLA Modules:
  0.0 2629.9 jit_solution(14668528609625980734)
XLA Ops:
  11.6 146.4 %all-gather.29.cloned.1.call-done = bf16[1024,1,1,3072]{3,0,2,1:T(8,128)(2,1)} async-done(((bf16[32,1,1,3072]{3,0,2,1:T(8,128)(2,1)}), bf16[1024,1,1,3072]{3,0,2,1:T(8,128)(2,1)}) %all-gather.29.cloned.1.call-update) | async-done | bytes 6291472 | tf_op jit(solution)/shard_map/all_gather | solution.py:148
  173.0 30.3 %all-gather.21.cloned.1.call-done = bf16[64,4,2048]{2,0,1:T(8,128)(2,1)} async-done(((bf16[64,1,2048]{2,0,1:T(8,128)(2,1)}), bf16[64,4,2048]{2,0,1:T(8,128)(2,1)}) %all-gather.21.cloned.1.call-update) | async-done | bytes 1048592 | tf_op jit(solution)/shard_map/all_gather | solution.py:158
  209.3 16.4 all-gather.23.cloned.1.call-done
  243.5 115.3 %all-gather.31.cloned.1.call-done = bf16[1024,1,1,1024]{3,0,2,1:T(8,128)(2,1)} async-done(((bf16[32,1,1,1024]{3,0,2,1:T(8,128)(2,1)}), bf16[1024,1,1,1024]{3,0,2,1:T(8,128)(2,1)}) %all-gather.31.cloned.1.call-update) | async-done | bytes 2097168 | tf_op jit(solution)/shard_map/all_gather | solution.py:168
  361.1 177.1 %all-gather.33.cloned.1.call-done = bf16[1024,1,1,5632]{3,0,2,1:T(8,128)(2,1)} async-done(((bf16[32,1,1,5632]{3,0,2,1:T(8,128)(2,1)}), bf16[1024,1,1,5632]{3,0,2,1:T(8,128)(2,1)}) %all-gather.33.cloned.1.call-update) | async-done | bytes 11534352 | tf_op jit(solution)/shard_map/all_gather | solution.py:175
  546.1 151.4 %all-gather.35.cloned.1.call-done = bf16[2816,1,1,1024]{3,0,2,1:T(8,128)(2,1)} async-done(((bf16[88,1,1,1024]{3,0,2,1:T(8,128)(2,1)}), bf16[2816,1,1,1024]{3,0,2,1:T(8,128)(2,1)}) %all-gather.35.cloned.1.call-update) | async-done | bytes 5767184 | tf_op jit(solution)/shard_map/all_gather | solution.py:181
  701.9 160.5 %all-gather.37.cloned.1.call-done = bf16[1024,1,1,3072]{3,0,2,1:T(8,128)(2,1)} async-done(((bf16[32,1,1,3072]{3,0,2,1:T(8,128)(2,1)}), bf16[1024,1,1,3072]{3,0,2,1:T(8,128)(2,1)}) %all-gather.37.cloned.1.call-update) | async-done | bytes 6291472 | tf_op jit(solution)/shard_map/all_gather | solution.py:148
  871.4 68.1 %psum.7 = f32[16]{0:T(128)S(1)} all-reduce(f32[16]{0:T(128)S(1)} %select_reduce_fusion.1), channel_id=1, replica_groups=mesh['section'=4,'dp'=32] {'dp'}, use_global_device_ids=true, to_apply=%region_13.14 | all-reduce | flops 16 | bytes 128 | tf_op jit(solution)/shard_map/psum | solution.py:139
  972.4 90.9 %all-gather.39.cloned.1.call-done = bf16[1024,1,1,1024]{3,0,2,1:T(8,128)(2,1)} async-done(((bf16[32,1,1,1024]{3,0,2,1:T(8,128)(2,1)}), bf16[1024,1,1,1024]{3,0,2,1:T(8,128)(2,1)}) %all-gather.39.cloned.1.call-update) | async-done | bytes 2097168 | tf_op jit(solution)/shard_map/all_gather | solution.py:168
  1065.6 177.5 %all-gather.41.cloned.1.call-done = bf16[1024,1,1,5632]{3,0,2,1:T(8,128)(2,1)} async-done(((bf16[32,1,1,5632]{3,0,2,1:T(8,128)(2,1)}), bf16[1024,1,1,5632]{3,0,2,1:T(8,128)(2,1)}) %all-gather.41.cloned.1.call-update) | async-done | bytes 11534352 | tf_op jit(solution)/shard_map/all_gather | solution.py:175
  1250.7 151.7 %all-gather.43.cloned.1.call-done = bf16[2816,1,1,1024]{3,0,2,1:T(8,128)(2,1)} async-done(((bf16[88,1,1,1024]{3,0,2,1:T(8,128)(2,1)}), bf16[2816,1,1,1024]{3,0,2,1:T(8,128)(2,1)}) %all-gather.43.cloned.1.call-update) | async-done | bytes 5767184 | tf_op jit(solution)/shard_map/all_gather | solution.py:181
  1454.2 74.7 %while.87 = (s32[]{:T(128)}, f32[2,88,1,512]{3,2,1,0:T(1,128)}, bf16[2,128,1,512]{3,1,2,0:T(8,128)(2,1)S(1)}, bf16[128,1,2816]{2,0,1:T(8,128)(2,1)}, s32[]{:T(128)}) while((s32[]{:T(128)}, f32[2,88,1,512]{3,2,1,0:T(1,128)}, bf16[2,128,1,512]{3,1,2,0:T(8,128)(2,1)S(1)}, bf16[128,1,2816]{2,0,1:T(8,128)(2,1)}, s32[]{:T(128)}) %tuple.243), condition=%wide.region_50.51_spmd, body=%wide.region_48.50_spmd.sunk | while | flops 373379072 | bytes 24461476 | solution.py:63
  1464.8 21.9 all-to-all-done.7
  1499.1 27.9 %all-to-all-done.7 = bf16[32,88,1,512]{3,1,2,0:T(8,128)(2,1)S(1)} async-done(((bf16[32,88,1,512]{3,1,2,0:T(8,128)(2,1)}), bf16[32,88,1,512]{3,1,2,0:T(8,128)(2,1)S(1)}, u32[]{:S(2)}, u32[]{:S(2)}) %all-to-all-start.7) | async-done | bytes 2883616 | tf_op jit(solution)/shard_map/while/body/eval_jaxpr/all_to_all | solution.py:58
  1533.3 49.6 %while.84 = (s32[]{:T(128)}, f32[2,32,1,512]{3,2,1,0:T(1,128)S(1)}, bf16[2,128,1,512]{3,1,2,0:T(8,128)(2,1)S(1)}, bf16[128,1,1024]{2,0,1:T(8,128)(2,1)S(1)}, s32[]{:T(128)}) while((s32[]{:T(128)}, f32[2,32,1,512]{3,2,1,0:T(1,128)S(1)}, bf16[2,128,1,512]{3,1,2,0:T(8,128)(2,1)S(1)}, bf16[128,1,1024]{2,0,1:T(8,128)(2,1)S(1)}, ...), condition=%wide.region_41.42_spmd, body=%wide.region_39.41_spmd.sunk | while | flops 135774208 | bytes 7929965 | solution.py:63
  1542.2 16.9 all-to-all-done.4
  1589.6 239.9 %while.85 = (s32[]{:T(128)}, f32[11,32,1,512]{3,2,1,0:T(1,128)}, bf16[11,128,1,512]{1,3,0,2:T(8,128)(2,1)S(1)}, bf16[128,1,1024]{2,0,1:T(8,128)(2,1)S(1)}, s32[]{:T(128)}) while((s32[]{:T(128)}, f32[11,32,1,512]{3,2,1,0:T(1,128)}, bf16[11,128,1,512]{1,3,0,2:T(8,128)(2,1)S(1)}, bf16[128,1,1024]{2,0,1:T(8,128)(2,1)S(1)}, s32[]{:T(128)}) %tuple.247), condition=%wide.region_44.45_spmd, body=%wide.region_42.44_spmd.sunk | while | flops 135774208 | bytes 7929965 | solution.py:63
  1673.0 16.1 all-to-all-done.5
  1696.4 16.2 all-to-all-done.5
  1720.1 14.6 all-to-all-done.5
  1743.6 14.4 all-to-all-done.5
  1767.1 14.3 all-to-all-done.5
  1790.7 14.3 all-to-all-done.5
  1814.3 14.4 all-to-all-done.5
  1894.7 76.8 %while.86 = (s32[]{:T(128)}, f32[2,88,1,512]{3,2,1,0:T(1,128)}, bf16[2,128,1,512]{3,1,2,0:T(8,128)(2,1)}, bf16[128,1,2816]{2,0,1:T(8,128)(2,1)}, s32[]{:T(128)}) while((s32[]{:T(128)}, f32[2,88,1,512]{3,2,1,0:T(1,128)}, bf16[2,128,1,512]{3,1,2,0:T(8,128)(2,1)}, bf16[128,1,2816]{2,0,1:T(8,128)(2,1)}, s32[]{:T(128)}) %tuple.244), condition=%wide.region_47.48_spmd, body=%wide.region_45.47_spmd.sunk | while | flops 373379072 | bytes 24461476 | solution.py:63
  1906.3 21.9 all-to-all-done.6
  1940.7 29.0 %all-to-all-done.6 = bf16[32,88,1,512]{3,1,2,0:T(8,128)(2,1)S(1)} async-done(((bf16[32,88,1,512]{3,1,2,0:T(8,128)(2,1)}), bf16[32,88,1,512]{3,1,2,0:T(8,128)(2,1)S(1)}, u32[]{:S(2)}, u32[]{:S(2)}) %all-to-all-start.6) | async-done | bytes 2883616 | tf_op jit(solution)/shard_map/while/body/eval_jaxpr/all_to_all | solution.py:58
  1977.8 263.8 %while.82 = (s32[]{:T(128)}, f32[11,32,1,512]{3,2,1,0:T(1,128)S(1)}, bf16[11,128,1,512]{1,3,0,2:T(8,128)(2,1)}, bf16[128,1,1024]{2,0,1:T(8,128)(2,1)S(1)}, s32[]{:T(128)}) while((s32[]{:T(128)}, f32[11,32,1,512]{3,2,1,0:T(1,128)S(1)}, bf16[11,128,1,512]{1,3,0,2:T(8,128)(2,1)}, bf16[128,1,1024]{2,0,1:T(8,128)(2,1)S(1)}, s32[]{:T(128)}) %tuple.248), condition=%wide.region_35.36_spmd, body=%wide.region_33.35_spmd.sunk | while | flops 135774208 | bytes 7929965 | solution.py:63
  1980.4 18.1 all-to-all-start.2
  1998.5 17.0 all-to-all-done.2
  2107.2 16.6 all-to-all-done.2
  2131.6 15.6 all-to-all-done.2
  2155.2 14.2 all-to-all-done.2
  2179.2 14.3 all-to-all-done.2
  2203.1 14.4 all-to-all-done.2
  2227.0 14.3 all-to-all-done.2
  2243.2 45.4 %while.81 = (s32[]{:T(128)}, f32[2,32,1,512]{3,2,1,0:T(1,128)S(1)}, bf16[2,128,1,512]{3,1,2,0:T(8,128)(2,1)S(1)}, bf16[128,1,1024]{2,0,1:T(8,128)(2,1)S(1)}, s32[]{:T(128)}) while((s32[]{:T(128)}, f32[2,32,1,512]{3,2,1,0:T(1,128)S(1)}, bf16[2,128,1,512]{3,1,2,0:T(8,128)(2,1)S(1)}, bf16[128,1,1024]{2,0,1:T(8,128)(2,1)S(1)}, ...), condition=%wide.region_32.33_spmd, body=%wide.region_30.32_spmd.sunk | while | flops 135774208 | bytes 7929965 | solution.py:63
  2251.7 15.4 all-to-all-done.1
  2274.6 13.8 all-to-all-done.1
  2292.5 133.8 %while.83 = (s32[]{:T(128)}, f32[6,32,1,512]{3,2,1,0:T(1,128)S(1)}, bf16[6,128,1,512]{1,3,0,2:T(8,128)(2,1)S(1)}, bf16[128,1,1024]{2,0,1:T(8,128)(2,1)S(1)}, s32[]{:T(128)}) while((s32[]{:T(128)}, f32[6,32,1,512]{3,2,1,0:T(1,128)S(1)}, bf16[6,128,1,512]{1,3,0,2:T(8,128)(2,1)S(1)}, bf16[128,1,1024]{2,0,1:T(8,128)(2,1)S(1)}, ...), condition=%wide.region_38.39_spmd, body=%wide.region_36.38_spmd.sunk | while | flops 135774208 | bytes 7929965 | solution.py:63
  2301.4 16.6 all-to-all-done.3
  2324.7 15.1 all-to-all-done.3
  2438.8 132.5 %while.80 = (s32[]{:T(128)}, f32[6,32,1,512]{3,2,1,0:T(1,128)S(1)}, bf16[6,128,1,512]{1,3,0,2:T(8,128)(2,1)}, bf16[128,1,1024]{2,0,1:T(8,128)(2,1)S(1)}, s32[]{:T(128)}) while((s32[]{:T(128)}, f32[6,32,1,512]{3,2,1,0:T(1,128)S(1)}, bf16[6,128,1,512]{1,3,0,2:T(8,128)(2,1)}, bf16[128,1,1024]{2,0,1:T(8,128)(2,1)S(1)}, s32[]{:T(128)}) %tuple.250), condition=%wide.region_29.30_spmd, body=%wide.region_27.29_spmd.sunk | while | flops 135774208 | bytes 7929965 | solution.py:63
  2486.2 14.0 all-to-all-done
  2509.7 14.2 all-to-all-done
  2533.9 14.6 all-to-all-done
  2557.1 14.0 all-to-all-done
  2578.1 43.5 %reduce-scatter.16.cloned.1.call-done = f32[32,4]{1,0:T(8,128)} async-done(((f32[1024,4]{1,0:T(8,128)}), f32[32,4]{1,0:T(8,128)}) %reduce-scatter.16.cloned.1.call-update) | async-done | bytes 528
  (694 shorter events, 818.5 us)
Async XLA Ops:
  7.2 150.8 %all-gather.29.cloned.1.call-start = ((), (), s32[]{:S(2)}) async-start(), calls=%async_computation.21 | async-start | bytes 6488064 | tf_op jit(solution)/shard_map/all_gather | solution.py:148
  10.6 192.7 %all-gather.21.cloned.1.call-start = ((), (), s32[]{:S(2)}) async-start(), calls=%async_computation.13 | async-start | bytes 1310720 | tf_op jit(solution)/shard_map/all_gather | solution.py:158
  162.6 63.1 %all-gather.23.cloned.1.call-start = ((), (), s32[]{:S(2)}) async-start(), calls=%async_computation.14 | async-start | bytes 1310720 | tf_op jit(solution)/shard_map/all_gather | solution.py:158
  163.4 195.5 %all-gather.31.cloned.1.call-start = ((), (), s32[]{:S(2)}) async-start(), calls=%async_computation.22 | async-start | bytes 2162688 | tf_op jit(solution)/shard_map/all_gather | solution.py:168
  164.9 373.3 %all-gather.33.cloned.1.call-start = ((), (), s32[]{:S(2)}) async-start(), calls=%async_computation.23 | async-start | bytes 11894784 | tf_op jit(solution)/shard_map/all_gather | solution.py:175
  166.8 530.7 %all-gather.35.cloned.1.call-start = ((), (), s32[]{:S(2)}) async-start(), calls=%async_computation.24 | async-start | bytes 5947392 | tf_op jit(solution)/shard_map/all_gather | solution.py:181
  170.0 692.4 %all-gather.37.cloned.1.call-start = ((), (), s32[]{:S(2)}) async-start(), calls=%async_computation.25 | async-start | bytes 6488064 | tf_op jit(solution)/shard_map/all_gather | solution.py:148
  170.9 776.4 %all-gather.27.cloned.1.call-start = ((), (), s32[]{:S(2)}) async-start(), calls=%async_computation.16 | async-start | bytes 1310720 | tf_op jit(solution)/shard_map/all_gather | solution.py:158
  867.1 87.1 %all-gather.25.cloned.1.call-start = ((), (), s32[]{:S(2)}) async-start(), calls=%async_computation.15 | async-start | bytes 1310720 | tf_op jit(solution)/shard_map/all_gather | solution.py:158
  867.9 195.4 %all-gather.39.cloned.1.call-start = ((), (), s32[]{:S(2)}) async-start(), calls=%async_computation.26 | async-start | bytes 2162688 | tf_op jit(solution)/shard_map/all_gather | solution.py:168
  868.6 374.5 %all-gather.41.cloned.1.call-start = ((), (), s32[]{:S(2)}) async-start(), calls=%async_computation.27 | async-start | bytes 11894784 | tf_op jit(solution)/shard_map/all_gather | solution.py:175
  869.5 533.0 %all-gather.43.cloned.1.call-start = ((), (), s32[]{:S(2)}) async-start(), calls=%async_computation.28 | async-start | bytes 5947392 | tf_op jit(solution)/shard_map/all_gather | solution.py:181
  871.2 966.0 %reduce-scatter.8.cloned.1.call-start = ((), (), s32[]{:S(2)}) async-start(), calls=%async_computation.17 | async-start | bytes 1310720 | tf_op jit(solution)/shard_map/reduce_scatter | solution.py:260
  1453.2 385.1 %reduce-scatter.10.cloned.1.call-start = ((), (), s32[]{:S(2)}) async-start(), calls=%async_computation.18 | async-start | bytes 1310720 | tf_op jit(solution)/shard_map/reduce_scatter | solution.py:260
  1459.1 27.6 %all-to-all-start.7 = ((bf16[32,88,1,512]{3,1,2,0:T(8,128)(2,1)}), bf16[32,88,1,512]{3,1,2,0:T(8,128)(2,1)S(1)}, u32[]{:S(2)}, u32[]{:S(2)}) async-start(bf16[32,88,1,512]{3,1,2,0:T(8,128)(2,1)} %bitcast.736), calls=%async_computation.7 | async-start | bytes 5767168 | tf_op jit(solution)/shard_map/while/body/eval_jaxpr/all_to_all | solution.py:58
  1493.4 33.6 %all-to-all-start.7 = ((bf16[32,88,1,512]{3,1,2,0:T(8,128)(2,1)}), bf16[32,88,1,512]{3,1,2,0:T(8,128)(2,1)S(1)}, u32[]{:S(2)}, u32[]{:S(2)}) async-start(bf16[32,88,1,512]{3,1,2,0:T(8,128)(2,1)} %bitcast.736), calls=%async_computation.7 | async-start | bytes 5767168 | tf_op jit(solution)/shard_map/while/body/eval_jaxpr/all_to_all | solution.py:58
  1535.1 24.0 all-to-all-start.4
  1561.2 21.5 all-to-all-start.4
  1588.1 840.2 %reduce-scatter.12.cloned.1.call-start = ((), (), s32[]{:S(2)}) async-start(), calls=%async_computation.19 | async-start | bytes 1310720 | tf_op jit(solution)/shard_map/reduce_scatter | solution.py:260
  1668.3 20.8 all-to-all-start.5
  1691.6 21.0 all-to-all-start.5
  1715.2 19.5 all-to-all-start.5
  1737.3 20.7 all-to-all-start.5
  1760.6 20.9 all-to-all-start.5
  1784.1 21.0 all-to-all-start.5
  1807.7 21.0 all-to-all-start.5
  1893.0 536.4 %reduce-scatter.14.cloned.1.call-start = ((), (), s32[]{:S(2)}) async-start(), calls=%async_computation.20 | async-start | bytes 1310720 | tf_op jit(solution)/shard_map/reduce_scatter | solution.py:260
  1899.7 28.5 %all-to-all-start.6 = ((bf16[32,88,1,512]{3,1,2,0:T(8,128)(2,1)}), bf16[32,88,1,512]{3,1,2,0:T(8,128)(2,1)S(1)}, u32[]{:S(2)}, u32[]{:S(2)}) async-start(bf16[32,88,1,512]{3,1,2,0:T(8,128)(2,1)} %bitcast.737), calls=%async_computation.6 | async-start | bytes 5767168 | tf_op jit(solution)/shard_map/while/body/eval_jaxpr/all_to_all | solution.py:58
  1935.0 34.6 %all-to-all-start.6 = ((bf16[32,88,1,512]{3,1,2,0:T(8,128)(2,1)}), bf16[32,88,1,512]{3,1,2,0:T(8,128)(2,1)S(1)}, u32[]{:S(2)}, u32[]{:S(2)}) async-start(bf16[32,88,1,512]{3,1,2,0:T(8,128)(2,1)} %bitcast.737), calls=%async_computation.6 | async-start | bytes 5767168 | tf_op jit(solution)/shard_map/while/body/eval_jaxpr/all_to_all | solution.py:58
  1980.4 35.1 %all-to-all-start.2 = ((bf16[32,32,1,512]{3,1,2,0:T(8,128)(2,1)}), bf16[32,32,1,512]{3,1,2,0:T(8,128)(2,1)S(1)}, u32[]{:S(2)}, u32[]{:S(2)}) async-start(bf16[32,32,1,512]{3,1,2,0:T(8,128)(2,1)} %bitcast.715), calls=%async_computation.2 | async-start | bytes 2097152 | tf_op jit(solution)/shard_map/while/body/eval_jaxpr/all_to_all | solution.py:58
  2018.5 21.3 all-to-all-start.2
  2102.3 21.4 all-to-all-start.2
  2126.6 20.6 all-to-all-start.2
  2150.1 19.3 all-to-all-start.2
  2172.3 21.2 all-to-all-start.2
  2196.5 21.0 all-to-all-start.2
  2220.4 21.0 all-to-all-start.2
  2245.0 22.1 all-to-all-start.1
  2269.1 19.3 all-to-all-start.1
  2292.2 329.4 %reduce-scatter.16.cloned.1.call-start = ((), (), s32[]{:S(2)}) async-start(), calls=%async_computation.29 | async-start | bytes 540672
  2294.5 23.5 all-to-all-start.3
  2320.0 19.8 all-to-all-start.3
  2379.4 24.5 all-to-all-start.3
  2405.9 20.1 all-to-all-start.3
  2441.5 18.5 all-to-all-start
  2503.1 20.8 all-to-all-start
  2526.8 21.7 all-to-all-start
  2551.3 19.8 all-to-all-start
  (106 other events, 3677.9 us)
Sparse Core Ops, SparseCore 0:
  10.7 147.2 all-gather.28
  162.7 40.4 all-gather.20
  205.5 20.1 all-gather.22
  227.2 131.5 all-gather.30
  360.3 177.8 all-gather.32
  539.7 157.7 all-gather.34
  699.1 163.2 all-gather.36
  867.2 40.6 all-gather.26
  910.2 20.0 all-gather.24
  931.7 131.5 all-gather.38
  1064.9 178.1 all-gather.40
  1244.6 157.7 all-gather.42
  1453.3 70.1 reduce-scatter.7
  1588.3 63.4 reduce-scatter.9
  1893.1 87.6 reduce-scatter.11
  2292.3 92.1 reduce-scatter.13
  2437.4 184.0 reduce-scatter.15
where the time goes:
time: 2660 us; the launch traced here: 2630 us
  waiting for transfers between devices  1890 us (71%)
  starting transfers between devices  265 us (10%)
  local copies, waits for them, and re-layouts  191 us (7%)
  matrix products  159 us (6%)
  blocking collectives  68.1 us (3%)
  other arithmetic  39.7 us (1%)
    all_to_all x42, waiting for transfers between devices, one_block(): lax.all_to_all(term.astype(jnp.bfloat16), 'dp', split_axis=0, concat_axis...  627 us
    all_gather x2, waiting for transfers between devices, layer_forward(): lax.all_gather(in_weights[:, :, layer, 4 * width:], 'dp', axis=0, tiled=T...  355 us
    all_gather x2, waiting for transfers between devices, layer_forward(): lax.all_gather(in_weights[:, :, layer, :3 * width], 'dp', axis=0, tiled=T...  307 us
    all_gather x2, waiting for transfers between devices, layer_forward(): lax.all_gather(down_weights[:, :, layer, :], 'dp', axis=0, tiled=True)  303 us
    all_to_all x42, starting transfers between devices, one_block(): lax.all_to_all(term.astype(jnp.bfloat16), 'dp', split_axis=0, concat_axis...  263 us
    all_gather x2, waiting for transfers between devices, layer_forward(): lax.all_gather(in_weights[:, :, layer, 3 * width:4 * width], 'dp', axis=0...  206 us
    psum x1, blocking collectives, body(): counts = lax.psum(jnp.sum(onehot * valid_f[:, None], axis=0), 'dp')  68.1 us
    convert_element_type x42, local copies, waits for them, and re-layouts, one_block(): term.astype(jnp.bfloat16)  62.4 us
  transfers between devices with their start and end apart: 59, of which 53 were waited for; matrix products, arithmetic and copies ran while one was open for 10% of the time, Pallas kernels for 0%

commit v1 on v0

v1 whole, which is shorter than its diff:
```python
import math

import jax
import jax.numpy as jnp
from jax import lax
from jax.experimental import pallas as pl
from jax.experimental.pallas import tpu as pltpu
from jax.sharding import Mesh, PartitionSpec as P

D = 1024
HEAD = 64
FF = 2816
LAYERS = 2
POS = 4
NSEG = 16
EPS = 1e-05
NEG = -1e30
COUNT_BOOST = 4.0

HALF = D // 2
FFH = FF // 2
HEADS_HERE = HALF // HEAD
FRAMES_HERE = 256
LANES = 128

BF = jnp.bfloat16
F32 = jnp.float32

PLANE = ("c", "z", "x")
COLUMN = ("yh", "yl")
FIRST = ("x", "z")
SECOND = ("z", "x")
OFFSETS = (0, -1, 1, 2)


def ring_pairs(axis_of_core, step):
    pairs = []
    for c in range(2):
        for z in range(4):
            for x in range(4):
                if axis_of_core[c] == "x":
                    target = (c * 4 + z) * 4 + (x + step) % 4
                else:
                    target = (c * 4 + (z + step) % 4) * 4 + x
                pairs.append(((c * 4 + z) * 4 + x, target))
    return pairs


def shift(value, axis_of_core, step):
    return lax.ppermute(value, PLANE, ring_pairs(axis_of_core, step))


def gather_ring(piece, axis_of_core):
    half = piece.shape[1] // 2
    left = shift(piece, axis_of_core, 1)
    right = shift(piece, axis_of_core, -1)
    far_a = shift(left[:, :half], axis_of_core, 1)
    far_b = shift(right[:, half:], axis_of_core, -1)
    return jnp.concatenate([piece, left, right, jnp.concatenate([far_a, far_b], axis=1)], axis=0)


def gather_plane(piece):
    return gather_ring(gather_ring(piece, FIRST), SECOND)


def plus(one, two):
    return one.astype(F32) + two.astype(F32)


def scatter_ring(terms, axis_of_core, dtype):
    rows = terms.shape[0] // 4
    half = terms.shape[1] // 2
    own, left, right, far = [terms[k * rows : (k + 1) * rows] for k in range(4)]
    far_a = shift(far[:, :half], axis_of_core, 1)
    far_b = shift(far[:, half:], axis_of_core, -1)
    right = jnp.concatenate([plus(right[:, :half], far_a).astype(BF), right[:, half:]], axis=1)
    left = jnp.concatenate([left[:, :half], plus(left[:, half:], far_b).astype(BF)], axis=1)
    from_left = shift(right, axis_of_core, 1)
    from_right = shift(left, axis_of_core, -1)
    return (plus(own, from_left) + from_right.astype(F32)).astype(dtype)


def scatter_plane(terms):
    return scatter_ring(scatter_ring(terms, SECOND, BF), FIRST, BF)


def to_chip(value, place):
    pairs = [(c * 2 + yl, (yl ^ place) * 2 + c) for c in range(2) for yl in range(2)]
    return lax.ppermute(value, ("c", "yl"), pairs)


def to_owner(value, place):
    pairs = [(c * 2 + yl, yl * 2 + (c ^ place)) for c in range(2) for yl in range(2)]
    return lax.ppermute(value, ("c", "yl"), pairs)


def other_core(value):
    return lax.ppermute(value, "c", [(0, 1), (1, 0)])


def xor_order(blocks, y):
    swapped = jnp.where((y & 1) == 1, blocks[jnp.array([1, 0, 3, 2])], blocks)
    return jnp.where((y & 2) == 2, swapped[jnp.array([2, 3, 0, 1])], swapped)


def pick(flag, one, two):
    return jnp.where(flag, one, two), jnp.where(flag, two, one)


def exchange_column(blocks):
    got = [blocks[0]]
    for k in range(1, POS):
        got.append(lax.ppermute(blocks[k], COLUMN, [(y, y ^ k) for y in range(POS)]))
    return jnp.stack(got)


def matmul(one, two):
    return jnp.dot(one, two, preferred_element_type=F32)


def matmul_nt(one, two):
    return lax.dot_general(one, two, (((1,), (1,)), ((), ())), preferred_element_type=F32)


def matmul_tn(one, two):
    return lax.dot_general(one, two, (((0,), (0,)), ((), ())), preferred_element_type=F32)


def mover(source):
    size = source.shape[0]
    return (lax.broadcasted_iota(jnp.int32, (size, size), 0) == source[None, :]).astype(BF)


def normalize(state):
    return state * lax.rsqrt(jnp.mean(state * state, axis=-1, keepdims=True) + EPS)


def norm_backward(grad_out, state, gain_row):
    scale = lax.rsqrt(jnp.mean(state * state, axis=-1, keepdims=True) + EPS)
    normed = state * scale
    grad_norm = grad_out * gain_row[None]
    grad_state = scale * (grad_norm - normed * jnp.mean(grad_norm * normed, axis=-1, keepdims=True))
    return grad_state, jnp.sum(grad_out * normed, axis=0)


PAIRS = [(p, r) for p in range(POS) for r in range(p + 1)]


def head_matrix(shape, feature_dim):
    feature = lax.broadcasted_iota(jnp.int32, shape, feature_dim) // HEAD
    head = lax.broadcasted_iota(jnp.int32, shape, 1 - feature_dim)
    return (feature == head).astype(F32).astype(BF)


def head_sums(products):
    ones = head_matrix((HALF, LANES), 0)
    high = products.astype(BF)
    low = (products - high.astype(F32)).astype(BF)
    return matmul(high, ones) + matmul(low, ones)


def head_spread(values16):
    return matmul(values16, head_matrix((LANES, HALF), 1))


def pair_probs(queries, keys):
    rows = queries[0].shape[0]
    products = jnp.concatenate([queries[p] * keys[r] for p, r in PAIRS], axis=0)
    scores = head_sums(products) * (1.0 / math.sqrt(HEAD))
    probs = {}
    for p in range(POS):
        own = [scores[i * rows : (i + 1) * rows] for i, pair in enumerate(PAIRS) if pair[0] == p]
        peak = own[0]
        for term in own[1:]:
            peak = jnp.maximum(peak, term)
        terms = [jnp.exp(term - peak) for term in own]
        total = terms[0]
        for term in terms[1:]:
            total = total + term
        for r in range(p + 1):
            probs[p, r] = terms[r] / total
    return probs


def attend_kernel(y_ref, qkv_ref, out_ref):
    y = y_ref[0]
    rows = qkv_ref.shape[1]
    parts = [
        [qkv_ref[p ^ y, :, t * HALF : (t + 1) * HALF].astype(F32) for p in range(POS)]
        for t in range(3)
    ]
    queries, keys, values = parts
    probs = pair_probs(queries, keys)
    spread = head_spread(jnp.concatenate([probs[pair].astype(BF) for pair in PAIRS], axis=0))
    for p in range(POS):
        total = None
        for i, (pp, r) in enumerate(PAIRS):
            if pp == p:
                term = spread[i * rows : (i + 1) * rows] * values[r]
                total = term if total is None else total + term
        out_ref[p ^ y] = total.astype(BF)


def attend_backward_kernel(y_ref, qkv_ref, grad_ref, out_ref):
    y = y_ref[0]
    rows = qkv_ref.shape[1]
    parts = [
        [qkv_ref[p ^ y, :, t * HALF : (t + 1) * HALF].astype(F32) for p in range(POS)]
        for t in range(3)
    ]
    queries, keys, values = parts
    grads = [grad_ref[p ^ y].astype(F32) for p in range(POS)]
    probs = pair_probs(queries, keys)
    products = jnp.concatenate([grads[p] * values[r] for p, r in PAIRS], axis=0)
    grad_probs = head_sums(products)
    grad_probs = {pair: grad_probs[i * rows : (i + 1) * rows] for i, pair in enumerate(PAIRS)}
    grad_scores = []
    for p, r in PAIRS:
        mean = probs[p, 0] * grad_probs[p, 0]
        for other in range(1, p + 1):
            mean = mean + probs[p, other] * grad_probs[p, other]
        grad_scores.append(probs[p, r] * (grad_probs[p, r] - mean) * (1.0 / math.sqrt(HEAD)))
    stacked = jnp.concatenate(grad_scores, axis=0)
    high = stacked.astype(BF)
    low = (stacked - high.astype(F32)).astype(BF)
    spread_scores = head_spread(high) + head_spread(low)
    spread_probs = head_spread(jnp.concatenate([probs[pair].astype(BF) for pair in PAIRS], axis=0))
    grad_q = [None] * POS
    grad_k = [None] * POS
    grad_v = [None] * POS

    def put(totals, place, term):
        totals[place] = term if totals[place] is None else totals[place] + term

    for i, (p, r) in enumerate(PAIRS):
        score = spread_scores[i * rows : (i + 1) * rows]
        put(grad_q, p, score * keys[r])
        put(grad_k, r, score * queries[p])
        put(grad_v, r, spread_probs[i * rows : (i + 1) * rows] * grads[p])
    for p in range(POS):
        for t, totals in enumerate((grad_q, grad_k, grad_v)):
            out_ref[p ^ y, :, t * HALF : (t + 1) * HALF] = totals[p].astype(BF)


VMEM_LIMIT = 48 * 1024 * 1024


def call_kernel(kernel, y, operands, width, flops):
    rows = FRAMES_HERE // POS
    return pl.pallas_call(
        kernel,
        out_shape=jax.ShapeDtypeStruct((POS, rows, width), BF),
        in_specs=[pl.BlockSpec(memory_space=pltpu.SMEM)]
        + [pl.BlockSpec(memory_space=pltpu.VMEM)] * len(operands),
        out_specs=pl.BlockSpec(memory_space=pltpu.VMEM),
        compiler_params=pltpu.CompilerParams(vmem_limit_bytes=VMEM_LIMIT),
        cost_estimate=pl.CostEstimate(flops=flops, bytes_accessed=4 * 2**20, transcendentals=0),
    )(y.reshape(1), *operands)


def body(frames_in, in_weights, down_weights, gains, cotangent, segment_ids, valid):
    core = lax.axis_index("c")
    yl = lax.axis_index("yl")
    y = 2 * lax.axis_index("yh") + yl
    zi = lax.axis_index("z")
    xi = lax.axis_index("x")
    is_first = core == 0
    is_low = yl == 0

    def row_source(block, groups):
        index = jnp.arange(16 * block, dtype=jnp.int32)
        offsets = jnp.array(OFFSETS, dtype=jnp.int32)
        inner = offsets[(index // block) % 4]
        outer = offsets[index // (4 * block)]
        z_step = jnp.where(is_first, outer, inner)
        x_step = jnp.where(is_first, inner, outer)
        return (zi + z_step + 4) % 4, (xi + x_step + 4) % 4, index % block

    z_of, x_of, rest = row_source(64, 2)
    move_model = mover(32 * (8 * z_of + 4 * (core ^ (rest // 32)) + x_of) + rest % 32)
    z_of, x_of, rest = row_source(32, 1)
    move_heads = mover(128 * z_of + 32 * x_of + rest)
    z_of, x_of, rest = row_source(88, 1)
    move_units = mover(352 * z_of + 88 * x_of + rest)

    def frames_to_chip(value):
        one, two = pick(is_first, to_chip(value, 0), to_chip(value, 1))
        return jnp.concatenate([one, two], axis=0)

    def columns_to_chip(value):
        one, two = pick(is_low, value[:, :, 0], value[:, :, 1])
        rows = value.shape[0]
        return jnp.concatenate(
            [to_chip(one.reshape(rows, -1), 0), to_chip(two.reshape(rows, -1), 1)], axis=0
        )

    def columns_to_owner(value, groups, width):
        one = to_owner(value[:32], 0).reshape(32, groups, width)
        two = to_owner(value[32:], 1).reshape(32, groups, width)
        one, two = pick(is_low, one, two)
        return jnp.stack([one, two], axis=2).reshape(32, 2 * groups * width).astype(F32)

    gain_all = to_chip(gains[:, 0].reshape(32, LANES), 0).astype(F32).reshape(D, LAYERS, 2)

    weights = []
    for layer in range(LAYERS):
        shard = in_weights[:, 0, layer]
        qkv_part = columns_to_chip(shard[:, : 3 * D].reshape(32, 12, 2, 128))
        gate_up_part = columns_to_chip(shard[:, 4 * D :].reshape(32, 8, 2, 352))
        out_part = to_chip(shard[:, 3 * D : 4 * D], 0)
        down_part = to_chip(down_weights[:, 0, layer], 0)
        weights.append(
            (
                gather_plane(qkv_part),
                gather_plane(out_part),
                gather_plane(gate_up_part),
                gather_plane(down_part),
            )
        )

    state = frames_to_chip(frames_in[:, 0]).astype(F32)

    onehot = (segment_ids[:, None] == jnp.arange(NSEG, dtype=jnp.int32)[None, :]).astype(F32)
    valid_f = valid.astype(F32)
    counts = jnp.sum(onehot * valid_f[:, None], axis=0)[None]
    for axis, pairs in (
        ("yl", [(0, 1), (1, 0)]),
        ("x", [(0, 1), (1, 0), (2, 3), (3, 2)]),
        ("x", [(0, 3), (3, 0), (1, 2), (2, 1)]),
        ("z", [(0, 1), (1, 0), (2, 3), (3, 2)]),
        ("z", [(0, 3), (3, 0), (1, 2), (2, 1)]),
    ):
        counts = counts + lax.ppermute(counts, axis, pairs)
    own_count = jnp.sum(onehot * counts, axis=1)
    weight = valid_f * (1.0 + COUNT_BOOST / jnp.maximum(own_count, 1.0))
    weight = frames_to_chip(weight[:, None])

    def both_cores(partial):
        mine = partial.astype(BF)
        return plus(mine, other_core(mine))

    saved = []
    for layer in range(LAYERS):
        w_qkv, w_out, w_gate_up, w_down = weights[layer]
        normed = (normalize(state) * gain_all[None, :, layer, 0]).astype(BF)
        normed = matmul(normed, move_model).astype(BF)
        qkv = matmul(normed, w_qkv).astype(BF)
        qkv = exchange_column(xor_order(qkv.reshape(POS, 64, 3 * HALF), y))
        mixed = call_kernel(attend_kernel, y, (qkv,), HALF, 2 * 640 * 512 * 128 * 3)
        mixed = xor_order(exchange_column(mixed), y).reshape(FRAMES_HERE, HALF)
        mixed = matmul(mixed, move_heads).astype(BF)
        middle = state + both_cores(matmul(mixed, w_out))
        branch = (normalize(middle) * gain_all[None, :, layer, 1]).astype(BF)
        branch = matmul(branch, move_model).astype(BF)
        gate_up = matmul(branch, w_gate_up)
        gate = gate_up[:, :FFH]
        up_part = gate_up[:, FFH:]
        activated = (jax.nn.silu(gate) * up_part).astype(BF)
        activated = matmul(activated, move_units).astype(BF)
        saved.append((state, normed, qkv, mixed, middle, branch, gate, up_part, activated))
        state = middle + both_cores(matmul(activated, w_down))

    def frames_to_owner(value):
        value = value.astype(BF)
        return to_owner(jnp.where(is_first, value[:128], value[128:]), 0)[:, None]

    output = frames_to_owner(state)
    grad = frames_to_chip(cotangent[:, 0]).astype(F32) * weight

    in_list = [None] * LAYERS
    down_list = [None] * LAYERS
    gain_list = [None] * LAYERS
    for layer in reversed(range(LAYERS)):
        w_qkv, w_out, w_gate_up, w_down = weights[layer]
        state, normed, qkv, mixed, middle, branch, gate, up_part, activated = saved[layer]
        grad16 = grad.astype(BF)
        grad_down = scatter_plane(matmul_tn(activated, grad16).astype(BF))
        grad_act = matmul_nt(matmul_nt(grad16, w_down).astype(BF), move_units)
        sigma = jax.nn.sigmoid(gate)
        grad_gate = grad_act * up_part * sigma * (1.0 + gate * (1.0 - sigma))
        grad_up = grad_act * gate * sigma
        gate_up16 = jnp.concatenate([grad_gate, grad_up], axis=1).astype(BF)
        grad_gate_up = scatter_plane(matmul_tn(branch, gate_up16).astype(BF))
        grad_branch = both_cores(matmul_nt(matmul_nt(gate_up16, w_gate_up).astype(BF), move_model))
        grad_norm, gain_two = norm_backward(grad_branch, middle, gain_all[:, layer, 1])
        grad_middle = grad + grad_norm
        attn16 = grad_middle.astype(BF)
        grad_out = scatter_plane(matmul_tn(mixed, attn16).astype(BF))
        grad_mixed = matmul_nt(matmul_nt(attn16, w_out).astype(BF), move_heads).astype(BF)
        grad_mixed = exchange_column(xor_order(grad_mixed.reshape(POS, 64, HALF), y))
        grad_qkv = call_kernel(
            attend_backward_kernel, y, (qkv, grad_mixed), 3 * HALF, 2 * 640 * 512 * 128 * 7
        )
        grad_qkv = xor_order(exchange_column(grad_qkv), y).reshape(FRAMES_HERE, 3 * HALF)
        grad_in = scatter_plane(matmul_tn(normed, grad_qkv).astype(BF))
        grad_normed = both_cores(matmul_nt(matmul_nt(grad_qkv, w_qkv).astype(BF), move_model))
        grad_norm, gain_one = norm_backward(grad_normed, state, gain_all[:, layer, 0])
        grad = grad_middle + grad_norm
        in_list[layer] = jnp.concatenate(
            [
                columns_to_owner(grad_in, 12, 128),
                to_owner(grad_out, 0).astype(F32),
                columns_to_owner(grad_gate_up, 8, 352),
            ],
            axis=1,
        )
        down_list[layer] = to_owner(grad_down, 0).astype(F32)
        gain_list[layer] = jnp.stack([gain_one, gain_two], axis=-1)
    in_grads = jnp.stack(in_list, axis=1)[:, None]
    down_grads = jnp.stack(down_list, axis=1)[:, None]
    gain_grads = jnp.stack(gain_list, axis=1).reshape(32, LANES)
    for axis, pairs in (
        ("x", [(0, 1), (1, 0), (2, 3), (3, 2)]),
        ("x", [(0, 3), (3, 0), (1, 2), (2, 1)]),
        ("z", [(0, 1), (1, 0), (2, 3), (3, 2)]),
        ("z", [(0, 3), (3, 0), (1, 2), (2, 1)]),
    ):
        gain_grads = gain_grads + lax.ppermute(gain_grads, axis, pairs)
    gain_grads = gain_grads.reshape(4, 2, 4, LANES)
    gain_grads = lax.dynamic_index_in_dim(gain_grads, zi, 0, keepdims=False)
    gain_grads = lax.dynamic_index_in_dim(gain_grads, core, 0, keepdims=False)
    gain_grads = lax.dynamic_slice_in_dim(gain_grads, xi, 1, 0)
    gains_grad = to_owner(gain_grads, 0).reshape(32, 1, LAYERS, 2)
    return (output, frames_to_owner(grad), in_grads, down_grads, gains_grad)


def solution(mesh):
    parts = Mesh(mesh.devices.reshape(2, 2, 4, 2, 4), ("yh", "c", "z", "yl", "x"))
    dp = ("z", "yl", "x")
    section = ("yh", "c")
    return jax.shard_map(
        body,
        mesh=parts,
        in_specs=(
            P(dp, section, None),
            P(dp, section, None, None),
            P(dp, section, None, None),
            P(None, section, None, None),
            P(dp, section, None),
            P(dp),
            P(dp),
        ),
        out_specs=(
            P(dp, section, None),
            P(dp, section, None),
            P(dp, section, None, None),
            P(dp, section, None, None),
            P(dp, section, None, None),
        ),
        check_vma=False,
    )
```

time: 2660 us -> 900 us (0.34)
  waiting for transfers between devices: 1890 us -> 232 us
  matrix products: 159 us -> 84.3 us
  blocking collectives: 68.1 us -> 0 us
  other arithmetic: 39.7 us -> 104 us
  starting transfers between devices: 265 us -> 312 us
  local copies, waits for them, and re-layouts: 191 us -> 146 us
    all_gather x12 -> x0, waiting for transfers between devices: 1220 us -> none  [the longest x2 355 us: layer_forward(): lax.all_gather(in_weights[:, :, layer, 4 * width:], 'dp', axis=0, tiled=T...]
    all_to_all x42 -> x0, waiting for transfers between devices: 627 us -> none  [one_block(): lax.all_to_all(term.astype(jnp.bfloat16), 'dp', split_axis=0, concat_axis...]
    ppermute x0 -> x203, starting transfers between devices: none -> 312 us  [the longest x128 131 us: shift(): return lax.ppermute(value, PLANE, ring_pairs(axis_of_core, step))]
    all_to_all x42 -> x0, starting transfers between devices: 263 us -> none  [one_block(): lax.all_to_all(term.astype(jnp.bfloat16), 'dp', split_axis=0, concat_axis...]
    ppermute x0 -> x203, waiting for transfers between devices: none -> 232 us  [the longest x128 195 us: shift(): return lax.ppermute(value, PLANE, ring_pairs(axis_of_core, step))]
    dot_general x74 -> x32, matrix products: 159 us -> 84.3 us  [the longest x8 39.7 us: matmul_nt(): lax.dot_general(one, two, (((1,), (1,)), ((), ())), preferred_element_typ...]
    psum x1 -> x0, blocking collectives: 68.1 us -> none  [body(): counts = lax.psum(jnp.sum(onehot * valid_f[:, None], axis=0), 'dp')]
    convert_element_type x46 -> x4, local copies, waits for them, and re-layouts: 65.5 us -> 3.41 us  [columns_to_owner(): jnp.stack([one, two], axis=2).reshape(32, 2 * groups * width).astype(F32)]
  transfers between devices with their start and end apart: 59 -> 203, of which waited for: 53 -> 71; matrix products, arithmetic and copies ran while one was open for 10% -> 33% of each run, Pallas kernels for 0% -> 1%
where the time goes in v1:
time: 900 us; the launch traced here: 888 us
  starting transfers between devices  312 us (35%)
  waiting for transfers between devices  232 us (26%)
  local copies, waits for them, and re-layouts  146 us (16%)
  other arithmetic  104 us (12%)
  matrix products  84.3 us (9%)
    ppermute x128, waiting for transfers between devices, shift(): return lax.ppermute(value, PLANE, ring_pairs(axis_of_core, step))  195 us
    ppermute x128, starting transfers between devices, shift(): return lax.ppermute(value, PLANE, ring_pairs(axis_of_core, step))  131 us
    unnamed x280, local copies, waits for them, and re-layouts  52.5 us
    ppermute x15, starting transfers between devices, to_owner(): return lax.ppermute(value, ('c', 'yl'), pairs)  51.8 us
    ppermute x19, starting transfers between devices, to_chip(): return lax.ppermute(value, ('c', 'yl'), pairs)  51.4 us
    dot_general x8, matrix products, matmul_nt(): lax.dot_general(one, two, (((1,), (1,)), ((), ())), preferred_element_typ...  39.7 us
    ppermute x24, starting transfers between devices, exchange_column(): lax.ppermute(blocks[k], COLUMN, [(y, y ^ k) for y in range(POS)])  34.5 us
    ppermute x8, starting transfers between devices, other_core(): return lax.ppermute(value, 'c', [(0, 1), (1, 0)])  32.9 us
  transfers between devices with their start and end apart: 203, of which 71 were waited for; matrix products, arithmetic and copies ran while one was open for 33% of the time, Pallas kernels for 1%

profile of v1, /device:TPU:1, one launch (start us, length us, event | category | flops | bytes accessed | tf_op | source)
XLA Modules:
  0.0 888.1 jit_solution(16869058497984499143)
XLA Ops:
  8.9 3.9 fusion.149
  32.7 7.9 collective-permute-start.103
  43.3 4.1 collective-permute-start.65
  51.4 26.0 %slice_reduce_fusion = (f32[1024]{0:T(1024)S(1)}, f32[1024]{0:T(1024)S(1)}, f32[1024]{0:T(1024)S(1)}, f32[1024]{0:T(1024)S(1)}) fusion(f32[1024,2,2]{2,1,0:T(2,128)S(1)} %reshape.865), kind=kLoop, calls=%fused_computation.190 | loop fusion | bytes 32768 | tf_op jit(solution)/shard_map/slice | solution.py:353
  77.5 3.6 collective-permute-start.49
  99.1 4.3 collective-permute-done.20
  106.1 7.4 collective-permute-start.39
  113.7 4.5 collective-permute-done.22
  121.0 3.8 collective-permute-start.75
  127.8 3.6 collective-permute-start.29
  137.0 4.2 collective-permute-start.85
  144.4 3.6 collective-permute-start.96
  173.2 4.3 collective-permute-done.53
  195.9 4.6 collective-permute-done.43
  202.3 7.3 collective-permute-done.88
  223.0 5.3 collective-permute-done.27
  234.3 4.1 collective-permute-done.79
  239.5 5.5 collective-permute-done.80
  245.7 7.1 collective-permute-done.33
  253.5 5.9 collective-permute-done.34
  272.1 7.4 collective-permute-done.9
  279.8 12.5 %collective-permute-done.11 = bf16[256,768]{1,0:T(8,128)(2,1)S(1)} collective-permute-done((bf16[256,768]{1,0:T(8,128)(2,1)S(1)}, bf16[256,768]{1,0:T(8,128)(2,1)S(1)}, u32[]{:S(2)}, u32[]{:S(2)}) %collective-permute-start.11) | collective-permute-done | bytes 393248 | tf_op jit(solution)/shard_map/ppermute | solution.py:50
  310.3 12.8 %collective-permute-done.47 = bf16[352,512]{1,0:T(8,128)(2,1)S(1)} collective-permute-done((bf16[352,512]{1,0:T(8,128)(2,1)S(1)}, bf16[352,512]{1,0:T(8,128)(2,1)S(1)}, u32[]{:S(2)}, u32[]{:S(2)}) %collective-permute-start.47) | collective-permute-done | bytes 360480 | tf_op jit(solution)/shard_map/ppermute | solution.py:50
  334.2 16.0 %collective-permute-start.28 = (bf16[256,1024]{1,0:T(8,128)(2,1)S(1)}, bf16[256,1024]{1,0:T(8,128)(2,1)S(1)}, u32[]{:S(2)}, u32[]{:S(2)}) collective-permute-start(bf16[256,1024]{1,0:T(8,128)(2,1)S(1)} %convolution_convert_fusion.13), channel_id=1, source_target_pairs={{0,32},{32,0},{1,33},{33,1},{2,34},{34,2},{3,35},{35,3},{4,36},{36... | collective-permute-start | bytes 1572872 | tf_op jit(solution)/shard_map/ppermute | solution.py:98
  362.6 9.5 %collective-permute-done.37 = bf16[256,1408]{1,0:T(8,128)(2,1)S(1)} collective-permute-done((bf16[256,1408]{1,0:T(8,128)(2,1)S(1)}, bf16[256,1408]{1,0:T(8,128)(2,1)S(1)}, u32[]{:S(2)}, u32[]{:S(2)}) %collective-permute-start.37) | collective-permute-done | bytes 720928 | tf_op jit(solution)/shard_map/ppermute | solution.py:50
  373.3 4.3 fusion.179
  450.0 6.8 multiply_convert_fusion.3
  456.8 3.7 convolution_convert_fusion.2
  460.4 6.3 fusion.34
  466.7 3.8 convolution_convert_fusion
  505.5 5.8 collective-permute-done.163
  521.7 6.7 collective-permute-start.95
  541.6 3.9 fusion.35
  571.0 7.9 collective-permute-done.153
  582.9 7.2 multiply_convert_fusion.1
  590.1 3.7 convolution_convert_fusion.3
  593.8 5.5 fusion.36
  638.5 7.8 collective-permute-done.132
  655.8 17.7 %collective-permute-done.141 = bf16[256,1408]{1,0:T(8,128)(2,1)S(1)} collective-permute-done((bf16[256,1408]{1,0:T(8,128)(2,1)S(1)}, bf16[256,1408]{1,0:T(8,128)(2,1)S(1)}, u32[]{:S(2)}, u32[]{:S(2)}) %collective-permute-start.141) | collective-permute-done | bytes 720928 | tf_op jit(solution)/shard_map/ppermute | solution.py:50
  697.0 4.7 fusion.37
  713.6 6.4 collective-permute-start.120
  729.1 8.3 collective-permute-start.159
  779.9 9.1 %collective-permute-start.197 = (bf16[88,1024]{1,0:T(8,128)(2,1)}, bf16[88,1024]{1,0:T(8,128)(2,1)S(1)}, u32[]{:S(2)}, u32[]{:S(2)}) collective-permute-start(bf16[88,1024]{1,0:T(8,128)(2,1)} %add_convert_fusion.25), channel_id=1, source_target_pairs={{0,0},{4,32},{32,4},{36,36},{1,1},{5,33},{33,5},{37,37},{2,2},{6,3... | collective-permute-start | bytes 540680 | tf_op jit(solution)/shard_map/ppermute | solution.py:94
  792.9 3.6 collective-permute-start.202
  801.4 3.6 collective-permute-start.169
  819.1 15.6 %collective-permute-done.125 = bf16[256,1536]{1,0:T(8,128)(2,1)} collective-permute-done((bf16[256,1536]{1,0:T(8,128)(2,1)}, bf16[256,1536]{1,0:T(8,128)(2,1)}, u32[]{:S(2)}, u32[]{:S(2)}) %collective-permute-start.125) | collective-permute-done | bytes 786464 | tf_op jit(solution)/shard_map/ppermute | solution.py:50
  861.7 4.5 collective-permute-start.130
  869.6 5.3 collective-permute-start.149
  (963 shorter events, 552.1 us)
Async XLA Ops:
  0.6 151.8 %collective-permute-start.1 = (bf16[128,1024]{1,0:T(8,128)(2,1)}, bf16[128,1024]{1,0:T(8,128)(2,1)S(1)}, u32[]{:S(2)}, u32[]{:S(2)}) collective-permute-start(bf16[128,1024]{1,0:T(8,128)(2,1)} %bitcast.308), channel_id=1, source_target_pairs={{0,32},{4,0},{32,36},{36,4},{1,33},{5,1},{33,37},{37,5},{2,34},{6,... | collective-permute-start | bytes 786440 | tf_op jit(solution)/shard_map/ppermute | solution.py:89
  2.8 149.6 %collective-permute-start = (bf16[128,1024]{1,0:T(8,128)(2,1)}, bf16[128,1024]{1,0:T(8,128)(2,1)}, u32[]{:S(2)}, u32[]{:S(2)}) collective-permute-start(bf16[128,1024]{1,0:T(8,128)(2,1)} %bitcast.309), channel_id=1, source_target_pairs={{0,0},{4,32},{32,4},{36,36},{1,1},{5,33},{33,5},{37,37},{2,2},{6,3... | collective-permute-start | bytes 786440 | tf_op jit(solution)/shard_map/ppermute | solution.py:89
  8.6 147.8 %collective-permute-start.97 = (bf16[128,1024]{1,0:T(8,128)(2,1)}, bf16[128,1024]{1,0:T(8,128)(2,1)}, u32[]{:S(2)}, u32[]{:S(2)}) collective-permute-start(bf16[128,1024]{1,0:T(8,128)(2,1)} %bitcast.310), channel_id=1, source_target_pairs={{0,32},{4,0},{32,36},{36,4},{1,33},{5,1},{33,37},{37,5},{2,34},{6,... | collective-permute-start | bytes 786440 | tf_op jit(solution)/shard_map/ppermute | solution.py:89
  43.3 34.2 %collective-permute-start.65 = (bf16[32,1024]{1,0:T(8,128)(2,1)S(1)}, bf16[32,1024]{1,0:T(8,128)(2,1)S(1)}, u32[]{:S(2)}, u32[]{:S(2)}) collective-permute-start(bf16[32,1024]{1,0:T(8,128)(2,1)S(1)} %slice.1117), channel_id=1, source_target_pairs={{0,0},{4,32},{32,4},{36,36},{1,1},{5,33},{33,5},{37,37},{2,2},{6,3... | collective-permute-start | bytes 196616 | tf_op jit(solution)/shard_map/ppermute | solution.py:89
  48.0 29.4 %collective-permute-start.19 = (bf16[32,1024]{1,0:T(8,128)(2,1)S(1)}, bf16[32,1024]{1,0:T(8,128)(2,1)S(1)}, u32[]{:S(2)}, u32[]{:S(2)}) collective-permute-start(bf16[32,1024]{1,0:T(8,128)(2,1)S(1)} %slice.1082), channel_id=1, source_target_pairs={{0,0},{4,32},{32,4},{36,36},{1,1},{5,33},{33,5},{37,37},{2,2},{6,3... | collective-permute-start | bytes 196616 | tf_op jit(solution)/shard_map/ppermute | solution.py:89
  106.1 35.9 %collective-permute-start.39 = (bf16[88,1024]{1,0:T(8,128)(2,1)S(1)}, bf16[88,1024]{1,0:T(8,128)(2,1)S(1)}, u32[]{:S(2)}, u32[]{:S(2)}) collective-permute-start(bf16[88,1024]{1,0:T(8,128)(2,1)S(1)} %bitcast.283), channel_id=1, source_target_pairs={{0,0},{4,32},{32,4},{36,36},{1,1},{5,33},{33,5},{37,37},{2,2},{6,3... | collective-permute-start | bytes 540680 | tf_op jit(solution)/shard_map/ppermute | solution.py:89
  156.5 34.7 %collective-permute-start.71 = (bf16[128,1024]{1,0:T(8,128)(2,1)S(1)}, bf16[128,1024]{1,0:T(8,128)(2,1)S(1)}, u32[]{:S(2)}, u32[]{:S(2)}) collective-permute-start(bf16[128,1024]{1,0:T(8,128)(2,1)S(1)} %maximum_maximum_fusion.3), channel_id=1, source_target_pairs={{0,24},{1,25},{2,26},{3,27},{8,0},{9,1},{10,2},{11,3},{16,8},{17,9... | collective-permute-start | bytes 786440 | tf_op jit(solution)/shard_map/ppermute | solution.py:50
  189.1 28.2 %collective-permute-start.78 = (bf16[64,2816]{1,0:T(8,128)(2,1)S(1)}, bf16[64,2816]{1,0:T(8,128)(2,1)S(1)}, u32[]{:S(2)}, u32[]{:S(2)}) collective-permute-start(bf16[64,2816]{1,0:T(8,128)(2,1)S(1)} %get-tuple-element.235), channel_id=1, source_target_pairs={{0,3},{1,0},{2,1},{3,2},{8,11},{9,8},{10,9},{11,10},{16,19},{17,16... | collective-permute-start | bytes 1081352 | tf_op jit(solution)/shard_map/ppermute | solution.py:50
  191.4 30.4 %collective-permute-start.32 = (bf16[64,2816]{1,0:T(8,128)(2,1)S(1)}, bf16[64,2816]{1,0:T(8,128)(2,1)S(1)}, u32[]{:S(2)}, u32[]{:S(2)}) collective-permute-start(bf16[64,2816]{1,0:T(8,128)(2,1)S(1)} %get-tuple-element.241), channel_id=1, source_target_pairs={{0,3},{1,0},{2,1},{3,2},{8,11},{9,8},{10,9},{11,10},{16,19},{17,16... | collective-permute-start | bytes 1081352 | tf_op jit(solution)/shard_map/ppermute | solution.py:50
  213.3 58.7 %collective-permute-start.10 = (bf16[256,1536]{1,0:T(8,128)(2,1)S(1)}, bf16[256,1536]{1,0:T(8,128)(2,1)S(1)}, u32[]{:S(2)}, u32[]{:S(2)}) collective-permute-start(bf16[256,1536]{1,0:T(8,128)(2,1)S(1)} %maximum_dynamic-update-slice_fusion.10), channel_id=1, source_target_pairs={{0,24},{1,25},{2,26},{3,27},{8,0},{9,1},{10,2},{11,3},{16,8},{17,9... | collective-permute-start | bytes 2359304 | tf_op jit(solution)/shard_map/ppermute | solution.py:50
  228.3 31.8 %collective-permute-start.45 = (bf16[352,1024]{1,0:T(8,128)(2,1)S(1)}, bf16[352,1024]{1,0:T(8,128)(2,1)S(1)}, u32[]{:S(2)}, u32[]{:S(2)}) collective-permute-start(bf16[352,1024]{1,0:T(8,128)(2,1)S(1)} %maximum_maximum_fusion), channel_id=1, source_target_pairs={{0,24},{1,25},{2,26},{3,27},{8,0},{9,1},{10,2},{11,3},{16,8},{17,9... | collective-permute-start | bytes 2162696 | tf_op jit(solution)/shard_map/ppermute | solution.py:50
  231.5 31.1 %collective-permute-start.44 = (bf16[352,1024]{1,0:T(8,128)(2,1)S(1)}, bf16[352,1024]{1,0:T(8,128)(2,1)S(1)}, u32[]{:S(2)}, u32[]{:S(2)}) collective-permute-start(bf16[352,1024]{1,0:T(8,128)(2,1)S(1)} %maximum_maximum_fusion), channel_id=1, source_target_pairs={{0,8},{1,9},{2,10},{3,11},{8,16},{9,17},{10,18},{11,19},{16,24},{1... | collective-permute-start | bytes 2162696 | tf_op jit(solution)/shard_map/ppermute | solution.py:50
  231.6 34.4 %collective-permute-start.91 = (bf16[352,1024]{1,0:T(8,128)(2,1)S(1)}, bf16[352,1024]{1,0:T(8,128)(2,1)S(1)}, u32[]{:S(2)}, u32[]{:S(2)}) collective-permute-start(bf16[352,1024]{1,0:T(8,128)(2,1)S(1)} %maximum_maximum_fusion.1), channel_id=1, source_target_pairs={{0,24},{1,25},{2,26},{3,27},{8,0},{9,1},{10,2},{11,3},{16,8},{17,9... | collective-permute-start | bytes 2162696 | tf_op jit(solution)/shard_map/ppermute | solution.py:50
  262.6 38.1 %collective-permute-start.56 = (bf16[256,1536]{1,0:T(8,128)(2,1)}, bf16[256,1536]{1,0:T(8,128)(2,1)}, u32[]{:S(2)}, u32[]{:S(2)}) collective-permute-start(bf16[256,1536]{1,0:T(8,128)(2,1)} %maximum_dynamic-update-slice_fusion.11), channel_id=1, source_target_pairs={{0,24},{1,25},{2,26},{3,27},{8,0},{9,1},{10,2},{11,3},{16,8},{17,9... | collective-permute-start | bytes 2359304 | tf_op jit(solution)/shard_map/ppermute | solution.py:50
  266.0 36.4 %collective-permute-start.55 = (bf16[256,1536]{1,0:T(8,128)(2,1)}, bf16[256,1536]{1,0:T(8,128)(2,1)}, u32[]{:S(2)}, u32[]{:S(2)}) collective-permute-start(bf16[256,1536]{1,0:T(8,128)(2,1)} %maximum_dynamic-update-slice_fusion.11), channel_id=1, source_target_pairs={{0,8},{1,9},{2,10},{3,11},{8,16},{9,17},{10,18},{11,19},{16,24},{1... | collective-permute-start | bytes 2359304 | tf_op jit(solution)/shard_map/ppermute | solution.py:50
  300.7 33.5 %collective-permute-start.36 = (bf16[256,2816]{1,0:T(8,128)(2,1)}, bf16[256,2816]{1,0:T(8,128)(2,1)}, u32[]{:S(2)}, u32[]{:S(2)}) collective-permute-start(bf16[256,2816]{1,0:T(8,128)(2,1)} %maximum_dynamic-update-slice_fusion.6), channel_id=1, source_target_pairs={{0,24},{1,25},{2,26},{3,27},{8,0},{9,1},{10,2},{11,3},{16,8},{17,9... | collective-permute-start | bytes 4325384 | tf_op jit(solution)/shard_map/ppermute | solution.py:50
  302.5 48.8 %collective-permute-start.35 = (bf16[256,2816]{1,0:T(8,128)(2,1)}, bf16[256,2816]{1,0:T(8,128)(2,1)}, u32[]{:S(2)}, u32[]{:S(2)}) collective-permute-start(bf16[256,2816]{1,0:T(8,128)(2,1)} %maximum_dynamic-update-slice_fusion.6), channel_id=1, source_target_pairs={{0,8},{1,9},{2,10},{3,11},{8,16},{9,17},{10,18},{11,19},{16,24},{1... | collective-permute-start | bytes 4325384 | tf_op jit(solution)/shard_map/ppermute | solution.py:50
  327.9 78.7 %collective-permute-start.82 = (bf16[256,2816]{1,0:T(8,128)(2,1)}, bf16[256,2816]{1,0:T(8,128)(2,1)}, u32[]{:S(2)}, u32[]{:S(2)}) collective-permute-start(bf16[256,2816]{1,0:T(8,128)(2,1)} %maximum_dynamic-update-slice_fusion.7), channel_id=1, source_target_pairs={{0,24},{1,25},{2,26},{3,27},{8,0},{9,1},{10,2},{11,3},{16,8},{17,9... | collective-permute-start | bytes 4325384 | tf_op jit(solution)/shard_map/ppermute | solution.py:50
  327.9 83.3 %collective-permute-start.81 = (bf16[256,2816]{1,0:T(8,128)(2,1)}, bf16[256,2816]{1,0:T(8,128)(2,1)}, u32[]{:S(2)}, u32[]{:S(2)}) collective-permute-start(bf16[256,2816]{1,0:T(8,128)(2,1)} %maximum_dynamic-update-slice_fusion.7), channel_id=1, source_target_pairs={{0,8},{1,9},{2,10},{3,11},{8,16},{9,17},{10,18},{11,19},{16,24},{1... | collective-permute-start | bytes 4325384 | tf_op jit(solution)/shard_map/ppermute | solution.py:50
  329.5 57.1 %collective-permute-start.58 = (bf16[256,768]{1,0:T(8,128)(2,1)}, bf16[256,768]{1,0:T(8,128)(2,1)}, u32[]{:S(2)}, u32[]{:S(2)}) collective-permute-start(bf16[256,768]{1,0:T(8,128)(2,1)} %slice.1108), channel_id=1, source_target_pairs={{0,24},{1,25},{2,26},{3,27},{8,0},{9,1},{10,2},{11,3},{16,8},{17,9... | collective-permute-start | bytes 1179656 | tf_op jit(solution)/shard_map/ppermute | solution.py:50
  334.2 26.6 %collective-permute-start.28 = (bf16[256,1024]{1,0:T(8,128)(2,1)S(1)}, bf16[256,1024]{1,0:T(8,128)(2,1)S(1)}, u32[]{:S(2)}, u32[]{:S(2)}) collective-permute-start(bf16[256,1024]{1,0:T(8,128)(2,1)S(1)} %convolution_convert_fusion.13), channel_id=1, source_target_pairs={{0,32},{32,0},{1,33},{33,1},{2,34},{34,2},{3,35},{35,3},{4,36},{36... | collective-permute-start | bytes 1572872 | tf_op jit(solution)/shard_map/ppermute | solution.py:98
  362.6 27.1 %collective-permute-start.57 = (bf16[256,768]{1,0:T(8,128)(2,1)S(1)}, bf16[256,768]{1,0:T(8,128)(2,1)S(1)}, u32[]{:S(2)}, u32[]{:S(2)}) collective-permute-start(bf16[256,768]{1,0:T(8,128)(2,1)S(1)} %copy-done.64), channel_id=1, source_target_pairs={{0,8},{1,9},{2,10},{3,11},{8,16},{9,17},{10,18},{11,19},{16,24},{1... | collective-permute-start | bytes 1179656 | tf_op jit(solution)/shard_map/ppermute | solution.py:50
  408.6 29.3 %collective-permute-start.84 = (bf16[256,1408]{1,0:T(8,128)(2,1)}, bf16[256,1408]{1,0:T(8,128)(2,1)}, u32[]{:S(2)}, u32[]{:S(2)}) collective-permute-start(bf16[256,1408]{1,0:T(8,128)(2,1)} %slice.1129), channel_id=1, source_target_pairs={{0,24},{1,25},{2,26},{3,27},{8,0},{9,1},{10,2},{11,3},{16,8},{17,9... | collective-permute-start | bytes 2162696 | tf_op jit(solution)/shard_map/ppermute | solution.py:50
  476.0 40.4 %collective-permute-start.170 = (bf16[256,1408]{1,0:T(8,128)(2,1)}, bf16[256,1408]{1,0:T(8,128)(2,1)}, u32[]{:S(2)}, u32[]{:S(2)}) collective-permute-start(bf16[256,1408]{1,0:T(8,128)(2,1)} %get-tuple-element.51), channel_id=1, source_target_pairs={{0,8},{1,9},{2,10},{3,11},{8,16},{9,17},{10,18},{11,19},{16,24},{1... | collective-permute-start | bytes 2162696 | tf_op jit(solution)/shard_map/ppermute | solution.py:50
  479.4 37.5 %collective-permute-start.172 = (bf16[256,1408]{1,0:T(8,128)(2,1)}, bf16[256,1408]{1,0:T(8,128)(2,1)}, u32[]{:S(2)}, u32[]{:S(2)}) collective-permute-start(bf16[256,1408]{1,0:T(8,128)(2,1)} %get-tuple-element.52), channel_id=1, source_target_pairs={{0,24},{1,25},{2,26},{3,27},{8,0},{9,1},{10,2},{11,3},{16,8},{17,9... | collective-permute-start | bytes 2162696 | tf_op jit(solution)/shard_map/ppermute | solution.py:50
  499.2 56.8 %collective-permute-start.192 = (bf16[352,1024]{1,0:T(8,128)(2,1)}, bf16[352,1024]{1,0:T(8,128)(2,1)}, u32[]{:S(2)}, u32[]{:S(2)}) collective-permute-start(bf16[352,1024]{1,0:T(8,128)(2,1)} %pad_maximum_fusion.25), channel_id=1, source_target_pairs={{0,24},{1,25},{2,26},{3,27},{8,0},{9,1},{10,2},{11,3},{16,8},{17,9... | collective-permute-start | bytes 2162696 | tf_op jit(solution)/shard_map/ppermute | solution.py:50
  505.5 52.0 %collective-permute-start.190 = (bf16[352,1024]{1,0:T(8,128)(2,1)}, bf16[352,1024]{1,0:T(8,128)(2,1)}, u32[]{:S(2)}, u32[]{:S(2)}) collective-permute-start(bf16[352,1024]{1,0:T(8,128)(2,1)} %pad_maximum_fusion.24), channel_id=1, source_target_pairs={{0,8},{1,9},{2,10},{3,11},{8,16},{9,17},{10,18},{11,19},{16,24},{1... | collective-permute-start | bytes 2162696 | tf_op jit(solution)/shard_map/ppermute | solution.py:50
  521.7 30.8 %collective-permute-start.95 = (bf16[128,1024]{1,0:T(8,128)(2,1)}, bf16[128,1024]{1,0:T(8,128)(2,1)}, u32[]{:S(2)}, u32[]{:S(2)}) collective-permute-start(bf16[128,1024]{1,0:T(8,128)(2,1)} %slice_select_fusion.1), channel_id=1, source_target_pairs={{0,0},{4,32},{32,4},{36,36},{1,1},{5,33},{33,5},{37,37},{2,2},{6,3... | collective-permute-start | bytes 786440 | tf_op jit(solution)/shard_map/ppermute | solution.py:94
  552.5 149.2 %collective-permute-start.173 = (bf16[256,2816]{1,0:T(8,128)(2,1)}, bf16[256,2816]{1,0:T(8,128)(2,1)}, u32[]{:S(2)}, u32[]{:S(2)}) collective-permute-start(bf16[256,2816]{1,0:T(8,128)(2,1)} %pad_maximum_fusion.5), channel_id=1, source_target_pairs={{0,24},{1,25},{2,26},{3,27},{8,0},{9,1},{10,2},{11,3},{16,8},{17,9... | collective-permute-start | bytes 4325384 | tf_op jit(solution)/shard_map/ppermute | solution.py:50
  554.8 26.2 %collective-permute-start.112 = (bf16[256,1024]{1,0:T(8,128)(2,1)S(1)}, bf16[256,1024]{1,0:T(8,128)(2,1)S(1)}, u32[]{:S(2)}, u32[]{:S(2)}) collective-permute-start(bf16[256,1024]{1,0:T(8,128)(2,1)S(1)} %fusion.35), channel_id=1, source_target_pairs={{0,32},{32,0},{1,33},{33,1},{2,34},{34,2},{3,35},{35,3},{4,36},{36... | collective-permute-start | bytes 1572872 | tf_op jit(solution)/shard_map/ppermute | solution.py:98
  568.5 39.2 %collective-permute-start.196 = (bf16[88,1024]{1,0:T(8,128)(2,1)}, bf16[88,1024]{1,0:T(8,128)(2,1)}, u32[]{:S(2)}, u32[]{:S(2)}) collective-permute-start(bf16[88,1024]{1,0:T(8,128)(2,1)} %pad_maximum_fusion.51), channel_id=1, source_target_pairs={{0,3},{1,0},{2,1},{3,2},{8,11},{9,8},{10,9},{11,10},{16,19},{17,16... | collective-permute-start | bytes 540680 | tf_op jit(solution)/shard_map/ppermute | solution.py:50
  570.8 38.4 %collective-permute-start.194 = (bf16[88,1024]{1,0:T(8,128)(2,1)}, bf16[88,1024]{1,0:T(8,128)(2,1)}, u32[]{:S(2)}, u32[]{:S(2)}) collective-permute-start(bf16[88,1024]{1,0:T(8,128)(2,1)} %pad_maximum_fusion.50), channel_id=1, source_target_pairs={{0,1},{1,2},{2,3},{3,0},{8,9},{9,10},{10,11},{11,8},{16,17},{17,18... | collective-permute-start | bytes 540680 | tf_op jit(solution)/shard_map/ppermute | solution.py:50
  607.6 40.3 %collective-permute-start.154 = (bf16[256,1536]{1,0:T(8,128)(2,1)}, bf16[256,1536]{1,0:T(8,128)(2,1)}, u32[]{:S(2)}, u32[]{:S(2)}) collective-permute-start(bf16[256,1536]{1,0:T(8,128)(2,1)} %pad_maximum_fusion.21), channel_id=1, source_target_pairs={{0,24},{1,25},{2,26},{3,27},{8,0},{9,1},{10,2},{11,3},{16,8},{17,9... | collective-permute-start | bytes 2359304 | tf_op jit(solution)/shard_map/ppermute | solution.py:50
  646.3 56.4 %collective-permute-start.171 = (bf16[256,2816]{1,0:T(8,128)(2,1)}, bf16[256,2816]{1,0:T(8,128)(2,1)}, u32[]{:S(2)}, u32[]{:S(2)}) collective-permute-start(bf16[256,2816]{1,0:T(8,128)(2,1)} %pad_maximum_fusion.4), channel_id=1, source_target_pairs={{0,8},{1,9},{2,10},{3,11},{8,16},{9,17},{10,18},{11,19},{16,24},{1... | collective-permute-start | bytes 4325384 | tf_op jit(solution)/shard_map/ppermute | solution.py:50
  646.3 27.3 %collective-permute-start.141 = (bf16[256,1408]{1,0:T(8,128)(2,1)S(1)}, bf16[256,1408]{1,0:T(8,128)(2,1)S(1)}, u32[]{:S(2)}, u32[]{:S(2)}) collective-permute-start(bf16[256,1408]{1,0:T(8,128)(2,1)S(1)} %copy-done.59), channel_id=1, source_target_pairs={{0,8},{1,9},{2,10},{3,11},{8,16},{9,17},{10,18},{11,19},{16,24},{1... | collective-permute-start | bytes 2162696 | tf_op jit(solution)/shard_map/ppermute | solution.py:50
  650.6 35.4 %collective-permute-start.119 = (bf16[64,1536]{1,0:T(8,128)(2,1)S(1)}, bf16[64,1536]{1,0:T(8,128)(2,1)S(1)}, u32[]{:S(2)}, u32[]{:S(2)}) collective-permute-start(bf16[64,1536]{1,0:T(8,128)(2,1)S(1)} %get-tuple-element.124), channel_id=1, source_target_pairs={{0,68},{4,64},{64,4},{68,0},{1,69},{5,65},{65,5},{69,1},{2,70},{6,... | collective-permute-start | bytes 589832 | tf_op jit(solution)/shard_map/ppermute | solution.py:113
  686.0 60.0 %collective-permute-start.183 = (bf16[352,1024]{1,0:T(8,128)(2,1)}, bf16[352,1024]{1,0:T(8,128)(2,1)}, u32[]{:S(2)}, u32[]{:S(2)}) collective-permute-start(bf16[352,1024]{1,0:T(8,128)(2,1)} %pad_maximum_fusion.23), channel_id=1, source_target_pairs={{0,24},{1,25},{2,26},{3,27},{8,0},{9,1},{10,2},{11,3},{16,8},{17,9... | collective-permute-start | bytes 2162696 | tf_op jit(solution)/shard_map/ppermute | solution.py:50
  686.4 59.5 %collective-permute-start.181 = (bf16[352,1024]{1,0:T(8,128)(2,1)}, bf16[352,1024]{1,0:T(8,128)(2,1)}, u32[]{:S(2)}, u32[]{:S(2)}) collective-permute-start(bf16[352,1024]{1,0:T(8,128)(2,1)} %pad_maximum_fusion.22), channel_id=1, source_target_pairs={{0,8},{1,9},{2,10},{3,11},{8,16},{9,17},{10,18},{11,19},{16,24},{1... | collective-permute-start | bytes 2162696 | tf_op jit(solution)/shard_map/ppermute | solution.py:50
  713.6 51.6 %collective-permute-start.120 = (bf16[256,1024]{1,0:T(8,128)(2,1)}, bf16[256,1024]{1,0:T(8,128)(2,1)}, u32[]{:S(2)}, u32[]{:S(2)}) collective-permute-start(bf16[256,1024]{1,0:T(8,128)(2,1)} %fusion.37), channel_id=1, source_target_pairs={{0,32},{32,0},{1,33},{33,1},{2,34},{34,2},{3,35},{35,3},{4,36},{36... | collective-permute-start | bytes 1572872 | tf_op jit(solution)/shard_map/ppermute | solution.py:98
  754.9 41.7 %collective-permute-start.177 = (bf16[64,2816]{1,0:T(8,128)(2,1)}, bf16[64,2816]{1,0:T(8,128)(2,1)}, u32[]{:S(2)}, u32[]{:S(2)}) collective-permute-start(bf16[64,2816]{1,0:T(8,128)(2,1)} %pad_maximum_fusion.33), channel_id=1, source_target_pairs={{0,3},{1,0},{2,1},{3,2},{8,11},{9,8},{10,9},{11,10},{16,19},{17,16... | collective-permute-start | bytes 1081352 | tf_op jit(solution)/shard_map/ppermute | solution.py:50
  754.9 41.6 %collective-permute-start.175 = (bf16[64,2816]{1,0:T(8,128)(2,1)}, bf16[64,2816]{1,0:T(8,128)(2,1)}, u32[]{:S(2)}, u32[]{:S(2)}) collective-permute-start(bf16[64,2816]{1,0:T(8,128)(2,1)} %pad_maximum_fusion.32), channel_id=1, source_target_pairs={{0,1},{1,2},{2,3},{3,0},{8,9},{9,10},{10,11},{11,8},{16,17},{17,18... | collective-permute-start | bytes 1081352 | tf_op jit(solution)/shard_map/ppermute | solution.py:50
  760.6 28.3 %collective-permute-start.187 = (bf16[88,1024]{1,0:T(8,128)(2,1)}, bf16[88,1024]{1,0:T(8,128)(2,1)}, u32[]{:S(2)}, u32[]{:S(2)}) collective-permute-start(bf16[88,1024]{1,0:T(8,128)(2,1)} %pad_maximum_fusion.49), channel_id=1, source_target_pairs={{0,3},{1,0},{2,1},{3,2},{8,11},{9,8},{10,9},{11,10},{16,19},{17,16... | collective-permute-start | bytes 540680 | tf_op jit(solution)/shard_map/ppermute | solution.py:50
  762.1 27.0 %collective-permute-start.185 = (bf16[88,1024]{1,0:T(8,128)(2,1)}, bf16[88,1024]{1,0:T(8,128)(2,1)}, u32[]{:S(2)}, u32[]{:S(2)}) collective-permute-start(bf16[88,1024]{1,0:T(8,128)(2,1)} %pad_maximum_fusion.48), channel_id=1, source_target_pairs={{0,1},{1,2},{2,3},{3,0},{8,9},{9,10},{10,11},{11,8},{16,17},{17,18... | collective-permute-start | bytes 540680 | tf_op jit(solution)/shard_map/ppermute | solution.py:50
  779.9 27.2 %collective-permute-start.197 = (bf16[88,1024]{1,0:T(8,128)(2,1)}, bf16[88,1024]{1,0:T(8,128)(2,1)S(1)}, u32[]{:S(2)}, u32[]{:S(2)}) collective-permute-start(bf16[88,1024]{1,0:T(8,128)(2,1)} %add_convert_fusion.25), channel_id=1, source_target_pairs={{0,0},{4,32},{32,4},{36,36},{1,1},{5,33},{33,5},{37,37},{2,2},{6,3... | collective-permute-start | bytes 540680 | tf_op jit(solution)/shard_map/ppermute | solution.py:94
  801.4 38.5 %collective-permute-start.169 = (bf16[32,1024]{1,0:T(8,128)(2,1)}, bf16[32,1024]{1,0:T(8,128)(2,1)}, u32[]{:S(2)}, u32[]{:S(2)}) collective-permute-start(bf16[32,1024]{1,0:T(8,128)(2,1)} %add_convert_fusion.43), channel_id=1, source_target_pairs={{0,0},{4,32},{32,4},{36,36},{1,1},{5,33},{33,5},{37,37},{2,2},{6,3... | collective-permute-start | bytes 196616 | tf_op jit(solution)/shard_map/ppermute | solution.py:94
  807.0 42.6 %collective-permute-start.144 = (bf16[256,2816]{1,0:T(8,128)(2,1)}, bf16[256,2816]{1,0:T(8,128)(2,1)}, u32[]{:S(2)}, u32[]{:S(2)}) collective-permute-start(bf16[256,2816]{1,0:T(8,128)(2,1)} %pad_maximum_fusion.3), channel_id=1, source_target_pairs={{0,24},{1,25},{2,26},{3,27},{8,0},{9,1},{10,2},{11,3},{16,8},{17,9... | collective-permute-start | bytes 4325384 | tf_op jit(solution)/shard_map/ppermute | solution.py:50
  810.0 39.7 %collective-permute-start.142 = (bf16[256,2816]{1,0:T(8,128)(2,1)}, bf16[256,2816]{1,0:T(8,128)(2,1)}, u32[]{:S(2)}, u32[]{:S(2)}) collective-permute-start(bf16[256,2816]{1,0:T(8,128)(2,1)} %pad_maximum_fusion.2), channel_id=1, source_target_pairs={{0,8},{1,9},{2,10},{3,11},{8,16},{9,17},{10,18},{11,19},{16,24},{1... | collective-permute-start | bytes 4325384 | tf_op jit(solution)/shard_map/ppermute | solution.py:50
  843.6 38.1 %collective-permute-start.140 = (bf16[32,1024]{1,0:T(8,128)(2,1)S(1)}, bf16[32,1024]{1,0:T(8,128)(2,1)S(1)}, u32[]{:S(2)}, u32[]{:S(2)}) collective-permute-start(bf16[32,1024]{1,0:T(8,128)(2,1)S(1)} %copy-done.69), channel_id=1, source_target_pairs={{0,0},{4,32},{32,4},{36,36},{1,1},{5,33},{33,5},{37,37},{2,2},{6,3... | collective-permute-start | bytes 196616 | tf_op jit(solution)/shard_map/ppermute | solution.py:94
  (258 other events, 4485.3 us)

commit v2 on v1

v2 whole, which is shorter than its diff:
```python
import math

import jax
import jax.numpy as jnp
import numpy as np
from jax import lax
from jax.experimental import pallas as pl
from jax.experimental.pallas import tpu as pltpu
from jax.sharding import Mesh, PartitionSpec as P

D = 1024
HEAD = 64
LAYERS = 2
POS = 4
NSEG = 16
EPS = 1e-05
COUNT_BOOST = 4.0

HALF = D // 2
UNITS = 1536
TOKENS = 256
ROWS = TOKENS // POS
LANES = 128
TILE = 256

BF = jnp.bfloat16
F32 = jnp.float32

PLANE = ("c", "z", "x")
COLUMN = ("yh", "yl")
FIRST = ("x", "z")
SECOND = ("z", "x")

QKV = 3 * HALF
ATTN = QKV + HALF
GATE_UP = 2 * UNITS
FFN = GATE_UP + D + HALF
ATTN_GAINS = ATTN + LANES
PAIR = 1408


def unit_picks():
    unit = np.arange(768)
    rest = unit - HALF
    source = np.where(
        unit < HALF,
        704 * (unit // 256) + 88 * (unit % 256 // 64) + unit % 64,
        704 * (rest // 128) + 88 * (rest % 128 // 32) + 64 + rest % 32,
    )
    source = np.where((unit >= HALF) & (rest % 32 >= 24), -PAIR, source)
    row = np.arange(PAIR)[:, None]
    return [jnp.asarray(row == (source + 352 * half)[None, :], BF) for half in range(2)]


def ring_pairs(axis_of_core, step):
    pairs = []
    for c in range(2):
        for z in range(4):
            for x in range(4):
                if axis_of_core[c] == "x":
                    target = (c * 4 + z) * 4 + (x + step) % 4
                else:
                    target = (c * 4 + (z + step) % 4) * 4 + x
                pairs.append(((c * 4 + z) * 4 + x, target))
    return pairs


def shift(value, axis_of_core, step):
    return lax.ppermute(value, PLANE, ring_pairs(axis_of_core, step))


def after(value, *others):
    return lax.optimization_barrier((value, others))[0]


class Gather:
    def __init__(self, piece):
        self.piece = piece

    def near(self, axis_of_core, *deps):
        self.piece = after(self.piece, *deps)
        self.left = shift(self.piece, axis_of_core, 1)
        self.right = shift(self.piece, axis_of_core, -1)
        return self.left, self.right

    def far(self, axis_of_core, *deps):
        half = self.piece.shape[1] // 2
        far_a = shift(after(self.left[:, :half], *deps), axis_of_core, 1)
        far_b = shift(after(self.right[:, half:], *deps), axis_of_core, -1)
        self.blocks = [(self.piece,), (self.left,), (self.right,), (far_a, far_b)]
        return far_a, far_b

    def one(self, *deps):
        return self.near(FIRST, *deps)

    def two(self, *deps):
        done = self.far(FIRST, *deps)
        rows, width = self.piece.shape
        half = width // 2
        whole, part = ((0, rows), (0, width)), ((0, rows), (0, half))
        blocks = [(self.piece, whole, 0, 0), (self.left, whole, rows, 0)]
        blocks += [(self.right, whole, 2 * rows, 0)]
        blocks += [(done[0], part, 3 * rows, 0), (done[1], part, 3 * rows, half)]
        self.piece = place_blocks(blocks, (4 * rows, width))
        return done

    def three(self, *deps):
        return self.near(SECOND, *deps)

    def four(self, *deps):
        return self.far(SECOND, *deps)


def plus(one, two):
    return one.astype(F32) + two.astype(F32)


class Scatter:
    def __init__(self, own, left, right, far_a, far_b):
        self.parts = own, left, right, far_a, far_b
        self.parts_half = far_a.shape[1]

    def far(self, axis_of_core, *deps):
        own, left, right, far_a, far_b = self.parts
        half = far_a.shape[1]
        far_a = shift(after(far_a, *deps), axis_of_core, 1)
        far_b = shift(after(far_b, *deps), axis_of_core, -1)
        right = jnp.concatenate([plus(right[:, :half], far_a).astype(BF), right[:, half:]], axis=1)
        left = jnp.concatenate([left[:, :half], plus(left[:, half:], far_b).astype(BF)], axis=1)
        self.parts = own, left, right
        return far_a, far_b

    def near(self, axis_of_core, *deps):
        own, left, right = self.parts
        from_left = shift(after(right, *deps), axis_of_core, 1)
        from_right = shift(after(left, *deps), axis_of_core, -1)
        self.block = (plus(own, from_left) + from_right.astype(F32)).astype(BF)
        return (self.block,)

    def one(self, *deps):
        return self.far(SECOND, *deps)

    def two(self, *deps):
        done = self.near(SECOND, *deps)
        own, left, right, far = [self.block[k * 64 : (k + 1) * 64] for k in range(4)]
        half = self.parts_half
        self.parts = own, left, right, far[:, :half], far[:, half:]
        return done

    def three(self, *deps):
        return self.far(FIRST, *deps)

    def four(self, *deps):
        return self.near(FIRST, *deps)


def to_chip(value, place):
    pairs = [(c * 2 + yl, (yl ^ place) * 2 + c) for c in range(2) for yl in range(2)]
    return lax.ppermute(value, ("c", "yl"), pairs)


def to_owner(value, place):
    pairs = [(c * 2 + yl, yl * 2 + (c ^ place)) for c in range(2) for yl in range(2)]
    return lax.ppermute(value, ("c", "yl"), pairs)


def other_core(value):
    return lax.ppermute(value, "c", [(0, 1), (1, 0)])


def pick(flag, one, two):
    return jnp.where(flag, one, two), jnp.where(flag, two, one)


def exchange_column(blocks):
    got = [blocks[0]]
    for k in range(1, POS):
        got.append(lax.ppermute(blocks[k], COLUMN, [(y, y ^ k) for y in range(POS)]))
    return got


def dot(one, two):
    return jnp.dot(one, two, preferred_element_type=F32)


def dot_nt(one, two):
    return lax.dot_general(one, two, (((1,), (1,)), ((), ())), preferred_element_type=F32)


Y, YL = 16, 17


def identity(size):
    row = lax.broadcasted_iota(jnp.int32, (size, size), 0)
    return (row == lax.broadcasted_iota(jnp.int32, (size, size), 1)).astype(F32).astype(BF)


def row_block(step):
    return pl.ds(pl.multiple_of(step * 32, 32), 32)


def lane_tile(step):
    return pl.ds(pl.multiple_of(step * TILE, TILE), TILE)


def chip_rows(meta, k):
    return pl.ds(pl.multiple_of((meta[Y] ^ k) * ROWS, ROWS), ROWS)


def rsqrt_mean(state):
    return lax.rsqrt(jnp.mean(state * state, axis=-1, keepdims=True) + EPS)


def norm_rows(step, state, gain_ref, out_ref):
    out_ref[row_block(step), :] = (state * rsqrt_mean(state) * gain_ref[...]).astype(BF)


def move_rows(a_s, mv_ref, mvt_ref, moved_s, moved_t_ref):
    for j in range(D // TILE):
        cols = slice(j * TILE, (j + 1) * TILE)
        moved_s[:, cols] = dot(a_s[...], mv_ref[:, cols]).astype(BF)
        moved_t_ref[cols, :] = dot_nt(mvt_ref[cols, :], a_s[...]).astype(BF)


def dot_pieces(left_s, pieces, cols):
    total = None
    for k, piece in enumerate(pieces):
        term = dot(left_s[:, k * TILE : (k + 1) * TILE], piece[:, cols])
        total = term if total is None else total + term
    return total


def qkv_kernel(first, meta, ready, *refs):
    if first:
        x_ref, gain_ref, mv_ref, mvt_ref, *refs = refs
    else:
        x_ref, own_ref, other_ref, gain_ref, mv_ref, mvt_ref, *refs = refs
    pieces, refs = refs[:4], refs[4:]
    h_ref, art_ref, *refs = refs
    outs, (a_s, ar_s, qkv_s) = refs[:4], refs[4:]

    @pl.loop(0, TOKENS // 32)
    def _(step):
        state = x_ref[row_block(step), :].astype(F32)
        if not first:
            state = state + own_ref[row_block(step), :].astype(F32)
            state = state + other_ref[row_block(step), :].astype(F32)
        h_ref[row_block(step), :] = state
        norm_rows(step, state, gain_ref, a_s)

    move_rows(a_s, mv_ref, mvt_ref, ar_s, art_ref)
    ready()

    @pl.loop(0, QKV // TILE)
    def _(step):
        qkv_s[:, lane_tile(step)] = dot_pieces(ar_s, pieces, lane_tile(step)).astype(BF)

    for k in range(POS):
        outs[k][...] = qkv_s[chip_rows(meta, k), :]


PAIRS = [(p, r) for p in range(POS) for r in range(p + 1)]


def head_matrix(shape, feature_dim):
    feature = lax.broadcasted_iota(jnp.int32, shape, feature_dim) // HEAD
    head = lax.broadcasted_iota(jnp.int32, shape, 1 - feature_dim)
    return (feature == head).astype(F32).astype(BF)


def head_sums(products):
    ones = head_matrix((HALF, LANES), 0)
    high = products.astype(BF)
    low = (products - high.astype(F32)).astype(BF)
    return dot(high, ones) + dot(low, ones)


def head_spread(values16):
    return dot(values16, head_matrix((LANES, HALF), 1))


def pair_probs(queries, keys):
    products = jnp.concatenate([queries[p] * keys[r] for p, r in PAIRS], axis=0)
    scores = head_sums(products) * (1.0 / math.sqrt(HEAD))
    probs = {}
    for p in range(POS):
        own = [scores[i * ROWS : (i + 1) * ROWS] for i, pair in enumerate(PAIRS) if pair[0] == p]
        peak = own[0]
        for term in own[1:]:
            peak = jnp.maximum(peak, term)
        terms = [jnp.exp(term - peak) for term in own]
        total = terms[0]
        for term in terms[1:]:
            total = total + term
        for r in range(p + 1):
            probs[p, r] = terms[r] / total
    return probs


def split_qkv(meta, blocks, qkv_s):
    for k in range(POS):
        qkv_s[k] = blocks[k][...]
    return [
        [qkv_s[p ^ meta[Y], :, t * HALF : (t + 1) * HALF].astype(F32) for p in range(POS)]
        for t in range(3)
    ]


def attend_kernel(meta, ready, *refs):
    blocks, outs, (qkv_s, out_s) = refs[:4], refs[4:8], refs[8:]
    queries, keys, values = split_qkv(meta, blocks, qkv_s)
    probs = pair_probs(queries, keys)
    spread = head_spread(jnp.concatenate([probs[pair].astype(BF) for pair in PAIRS], axis=0))
    for p in range(POS):
        total = None
        for i, (pp, r) in enumerate(PAIRS):
            if pp == p:
                term = spread[i * ROWS : (i + 1) * ROWS] * values[r]
                total = term if total is None else total + term
        out_s[p ^ meta[Y]] = total.astype(BF)
    for k in range(POS):
        outs[k][...] = out_s[k]


def attend_backward_kernel(meta, ready, *refs):
    blocks, grad_blocks, outs, (qkv_s, grad_s, out_s) = refs[:4], refs[4:8], refs[8:12], refs[12:]
    queries, keys, values = split_qkv(meta, blocks, qkv_s)
    for k in range(POS):
        grad_s[k] = grad_blocks[k][...]
    grads = [grad_s[p ^ meta[Y]].astype(F32) for p in range(POS)]
    probs = pair_probs(queries, keys)
    products = jnp.concatenate([grads[p] * values[r] for p, r in PAIRS], axis=0)
    grad_probs = head_sums(products)
    grad_probs = {pair: grad_probs[i * ROWS : (i + 1) * ROWS] for i, pair in enumerate(PAIRS)}
    grad_scores = []
    for p, r in PAIRS:
        mean = probs[p, 0] * grad_probs[p, 0]
        for other in range(1, p + 1):
            mean = mean + probs[p, other] * grad_probs[p, other]
        grad_scores.append(probs[p, r] * (grad_probs[p, r] - mean) * (1.0 / math.sqrt(HEAD)))
    stacked = jnp.concatenate(grad_scores, axis=0)
    high = stacked.astype(BF)
    low = (stacked - high.astype(F32)).astype(BF)
    spread_scores = head_spread(high) + head_spread(low)
    spread_probs = head_spread(jnp.concatenate([probs[pair].astype(BF) for pair in PAIRS], axis=0))
    grad_q = [None] * POS
    grad_k = [None] * POS
    grad_v = [None] * POS

    def put(totals, place, term):
        totals[place] = term if totals[place] is None else totals[place] + term

    for i, (p, r) in enumerate(PAIRS):
        score = spread_scores[i * ROWS : (i + 1) * ROWS]
        put(grad_q, p, score * keys[r])
        put(grad_k, r, score * queries[p])
        put(grad_v, r, spread_probs[i * ROWS : (i + 1) * ROWS] * grads[p])
    for p in range(POS):
        for t, totals in enumerate((grad_q, grad_k, grad_v)):
            out_s[p ^ meta[Y], :, t * HALF : (t + 1) * HALF] = totals[p].astype(BF)
    for k in range(POS):
        outs[k][...] = out_s[k]


def unpack_rows(meta, pieces, out_ref, start):
    for k in range(16):
        rows = pl.ds(pl.multiple_of(start + meta[k] * 32, 32), 32)
        piece, row = pieces[k // 4], (k % 4) * 64
        out_ref[rows, :HALF] = piece[row : row + 32, :]
        out_ref[rows, HALF:] = piece[row + 32 : row + 64, :]


def transpose_into(source_s, out_s):
    eye = identity(TILE)
    for j in range(source_s.shape[1] // TILE):
        cols = slice(j * TILE, (j + 1) * TILE)
        out_s[cols, :] = dot_nt(eye, source_s[:, cols]).astype(BF)


def out_kernel(meta, ready, *refs):
    blocks, pieces, refs = refs[:4], refs[4:8], refs[8:]
    ort_ref, wo_ref, partial_ref, o_s, ot_s = refs
    for k in range(POS):
        o_s[chip_rows(meta, k), :] = blocks[k][...]
    transpose_into(o_s, ot_s)
    ready()
    unpack_rows(meta, pieces, wo_ref, 0)
    for k in range(16):
        ort_ref[k * 32 : (k + 1) * 32, :] = ot_s[pl.ds(pl.multiple_of(meta[k] * 32, 32), 32), :]
    for j in range(D // TILE):
        cols = slice(j * TILE, (j + 1) * TILE)
        partial_ref[:, cols] = dot(o_s[...], wo_ref[:, cols]).astype(BF)


def ffn_kernel(counting, meta, ready, *refs):
    h_ref, own_ref, other_ref, gain_ref, mv_ref, mvt_ref, *refs = refs
    pieces, refs = refs[:4], refs[4:]
    m_ref, brt_ref, gate_ref, up_ref, actrt_ref, wd_ref, partial_ref, *refs = refs
    if counting:
        total_ref, *refs = refs
    b_s, br_s, act_s, actt_s = refs

    @pl.loop(0, TOKENS // 32)
    def _(step):
        state = h_ref[row_block(step), :] + own_ref[row_block(step), :].astype(F32)
        state = state + other_ref[row_block(step), :].astype(F32)
        m_ref[row_block(step), :] = state
        norm_rows(step, state, gain_ref, b_s)

    move_rows(b_s, mv_ref, mvt_ref, br_s, brt_ref)
    ready()

    @pl.loop(0, UNITS // TILE)
    def _(step):
        cols = lane_tile(step)
        gate = dot_pieces(br_s, pieces, cols)
        gate_ref[:, cols] = gate
        up = dot_pieces(br_s, pieces, lane_tile(step + UNITS // TILE))
        up_ref[:, cols] = up
        act_s[:, cols] = (gate * jax.nn.sigmoid(gate) * up).astype(BF)

    for k in range(16):
        rows = pl.ds(pl.multiple_of(meta[k] * 64, 64), 64)
        wd_ref[rows, :] = pieces[k // 4][
            (k % 4) * 64 : (k % 4 + 1) * 64, GATE_UP : GATE_UP + D
        ]
    unpack_rows(meta, [piece.at[:, pl.ds(GATE_UP + D, HALF)] for piece in pieces], wd_ref, D)
    if counting:
        total = jnp.zeros((1, LANES), F32)
        for k in range(16):
            rows = slice(D + k * 32, D + (k + 1) * 32)
            total = total + wd_ref[rows, :LANES].astype(F32)[24:25]
        total_ref[...] = total
    transpose_into(act_s, actt_s)
    for k in range(16):
        rows = pl.ds(pl.multiple_of(meta[k] * 64, 64), 64)
        actrt_ref[k * 64 : (k + 1) * 64, :] = actt_s[rows, :]
        rows = pl.ds(pl.multiple_of(D + meta[k] * 32, 32), 32)
        actrt_ref[D + k * 32 : D + (k + 1) * 32, :] = actt_s[rows, :]

    @pl.loop(0, D // TILE)
    def _(step):
        cols = lane_tile(step)
        partial_ref[:, cols] = dot(act_s[...], wd_ref[:, cols]).astype(BF)


def norm_backward(base_ref, own_ref, other_ref, state_ref, gain_ref, put):
    def one_block(step, total):
        rows = row_block(step)
        own = own_ref[rows, :].astype(F32)
        grad = own + other_ref[rows, :].astype(F32)
        state = state_ref[rows, :].astype(F32)
        scale = rsqrt_mean(state)
        normed = state * scale
        grad_norm = grad * gain_ref[...]
        mean = jnp.mean(grad_norm * normed, axis=-1, keepdims=True)
        put(rows, base_ref[rows, :] + scale * (grad_norm - normed * mean))
        return total + jnp.sum((own * normed).reshape(4, 8, D), axis=0)

    total = lax.fori_loop(0, TOKENS // 32, one_block, jnp.zeros((8, D), F32))
    return jnp.sum(total, axis=0, keepdims=True)


def put_piece(refs, k, rows, start, value):
    width = value.shape[1]
    if len(refs) == 1:
        refs[0][slice(k * TILE + rows.start, k * TILE + rows.stop), start : start + width] = value
    elif k < 3:
        refs[k][rows, start : start + width] = value
    else:
        half = refs[3].shape[1]
        if start < half:
            refs[3][rows, start : start + width] = value
        else:
            refs[4][rows, start - half : start - half + width] = value


def put_packed(refs, k, start, step, value):
    for i in range(4):
        row = i * 64 + (step // 2) * 32
        put_piece(
            refs, k, slice(row, row + 32), start + (step % 2) * TILE, value[i * 32 : (i + 1) * 32]
        )


def ffn_backward_kernel(last, meta, ready, *refs):
    if last:
        cot_ref, marks_ref, totals_ref, other_totals_ref, *refs = refs
    else:
        base_ref, own_ref, other_ref, state_ref, gain_ref, *refs = refs
    actrt_ref, brt_ref, gate_ref, up_ref, wd_ref, mv_ref, *refs = refs
    held = 4 if last else 8
    pieces, refs = refs[:held], refs[held:]
    g_ref, *refs = refs
    if not last:
        dgain_ref, *refs = refs
    partial_ref, *refs = refs
    outs, (gf_s, dgu_s, dbr_s) = refs[:-3], refs[-3:]
    pieces, above = pieces[:4], pieces[4:]

    def put(rows, value):
        g_ref[rows, :] = value
        gf_s[rows, :] = value.astype(BF)

    if last:

        @pl.loop(0, TOKENS // 32)
        def _(step):
            rows = row_block(step)
            marks = marks_ref[rows, :].astype(F32)
            totals = totals_ref[...] + other_totals_ref[...]
            place = lax.broadcasted_iota(jnp.int32, (32, LANES), 1).astype(F32)
            count = jnp.sum(jnp.where(place == marks[:, :1], totals, 0.0), axis=1, keepdims=True)
            weight = marks[:, 1:2] * (1.0 + COUNT_BOOST / jnp.maximum(count, 1.0))
            put(rows, cot_ref[rows, :].astype(F32) * weight)

    else:
        dgain_ref[...] = norm_backward(base_ref, own_ref, other_ref, state_ref, gain_ref, put)

    @pl.loop(0, UNITS // TILE)
    def _(step):
        cols = lane_tile(step)
        grad_act = dot_nt(gf_s[...], wd_ref[cols, :])
        gate = gate_ref[:, cols]
        sigma = jax.nn.sigmoid(gate)
        grad_up = grad_act * gate * sigma
        grad_gate = grad_act * up_ref[:, cols] * sigma * (1.0 + gate * (1.0 - sigma))
        dgu_s[:, cols] = grad_gate.astype(BF)
        dgu_s[:, lane_tile(step + UNITS // TILE)] = grad_up.astype(BF)

    everything = slice(0, TILE)
    for k in (3, 1, 2, 0):
        rows = slice(k * TILE, (k + 1) * TILE)
        for j in range(GATE_UP // TILE):
            value = dot(brt_ref[rows, :], dgu_s[:, j * TILE : (j + 1) * TILE]).astype(BF)
            put_piece(outs, k, everything, j * TILE, value)
        for j in range(D // TILE):
            value = dot(actrt_ref[rows, :], gf_s[:, j * TILE : (j + 1) * TILE]).astype(BF)
            put_piece(outs, k, everything, GATE_UP + j * TILE, value)
        tail = slice(D + k * 128, D + (k + 1) * 128)
        for j in range(D // TILE):
            value = dot(actrt_ref[tail, :], gf_s[:, j * TILE : (j + 1) * TILE]).astype(BF)
            put_packed(outs, k, GATE_UP + D, j, value)
    ready()
    for k, sums in enumerate(above):
        for j in range(ATTN // TILE):
            put_piece(outs, k, everything, FFN + j * TILE, sums[:, j * TILE : (j + 1) * TILE])
    for k in range(4):
        dbr_s[:, k * TILE : (k + 1) * TILE] = dot_nt(dgu_s[...], pieces[k][...]).astype(BF)
    for j in range(D // TILE):
        cols = slice(j * TILE, (j + 1) * TILE)
        partial_ref[:, cols] = dot_nt(dbr_s[...], mv_ref[cols, :]).astype(BF)


def out_backward_kernel(meta, ready, *refs):
    base_ref, own_ref, other_ref, state_ref, gain_ref, ort_ref, wo_ref, *refs = refs
    gm_ref, dgain_ref, dwo_ref, *refs = refs
    outs, (ga_s, do_s) = refs[:4], refs[4:]

    def put(rows, value):
        gm_ref[rows, :] = value
        ga_s[rows, :] = value.astype(BF)

    dgain_ref[...] = norm_backward(base_ref, own_ref, other_ref, state_ref, gain_ref, put)
    for j in range(HALF // TILE):
        cols = slice(j * TILE, (j + 1) * TILE)
        do_s[:, cols] = dot_nt(ga_s[...], wo_ref[cols, :]).astype(BF)
    for k in range(POS):
        outs[k][...] = do_s[chip_rows(meta, k), :]
    for k in range(4):
        for j in range(D // TILE):
            cols = slice(j * TILE, (j + 1) * TILE)
            value = dot(ort_ref[k * 128 : (k + 1) * 128, :], ga_s[:, cols]).astype(BF)
            for i in range(4):
                row = k * TILE + i * 64 + (j // 2) * 32
                part = slice((j % 2) * TILE, (j % 2 + 1) * TILE)
                dwo_ref[row : row + 32, part] = value[i * 32 : (i + 1) * 32]


def qkv_backward_kernel(first, meta, ready, *refs):
    blocks, refs = refs[:4], refs[4:]
    art_ref, dwo_ref, mv_ref, *refs = refs
    if first:
        mvt_ref, state_ref, *gain_refs = refs[:5]
        refs = refs[5:]
    pieces, refs = refs[:4], refs[4:]
    partial_ref, *refs = refs
    outs, (dqkv_s, dar_s) = refs[:-2], refs[-2:]
    for k in range(POS):
        dqkv_s[chip_rows(meta, k), :] = blocks[k][...]
    ready()
    for k in range(4):
        dar_s[:, k * TILE : (k + 1) * TILE] = dot_nt(dqkv_s[...], pieces[k][...]).astype(BF)
    for j in range(D // TILE):
        cols = slice(j * TILE, (j + 1) * TILE)
        partial_ref[:, cols] = dot_nt(dar_s[...], mv_ref[cols, :]).astype(BF)
    everything = slice(0, TILE)
    if first:
        def one_block(step, total):
            state = state_ref[row_block(step), :]
            term = partial_ref[row_block(step), :].astype(F32) * state * rsqrt_mean(state)
            return total + jnp.sum(term.reshape(4, 8, D), axis=0)

        total = lax.fori_loop(0, TOKENS // 32, one_block, jnp.zeros((8, D), F32))
        grads = [jnp.sum(total, axis=0, keepdims=True)] + [ref[...] for ref in gain_refs]
        grads = jnp.concatenate(grads + [jnp.zeros((LANES - 4, D), F32)], axis=0).astype(BF)
        for k in range(4):
            value = dot_nt(mvt_ref[k * TILE : (k + 1) * TILE, :], grads).astype(BF)
            put_piece(outs, k, everything, ATTN, value)
    for k in (3, 1, 2, 0):
        rows = slice(k * TILE, (k + 1) * TILE)
        for j in range(QKV // TILE):
            value = dot(art_ref[rows, :], dqkv_s[:, j * TILE : (j + 1) * TILE]).astype(BF)
            put_piece(outs, k, everything, j * TILE, value)
        put_piece(outs, k, everything, QKV, dwo_ref[rows, :])


def last_kernel(meta, ready, *refs):
    base_ref, own_ref, other_ref, state_ref, gain_ref, out_ref = refs

    def put(rows, value):
        out_ref[rows, :] = value.astype(BF)

    norm_backward(base_ref, own_ref, other_ref, state_ref, gain_ref, put)


def pack_attn_kernel(meta, ready, *refs):
    shard, one_ref, two_ref = refs
    low = meta[YL] == 0
    for k in range(QKV // LANES):
        first = shard[:, 2 * k * LANES : (2 * k + 1) * LANES]
        second = shard[:, (2 * k + 1) * LANES : (2 * k + 2) * LANES]
        cols = slice(k * LANES, (k + 1) * LANES)
        one_ref[:, cols] = jnp.where(low, first, second)
        two_ref[:, cols] = jnp.where(low, second, first)
    one_ref[:, QKV:] = shard[:, 3 * D :]


def pack_ffn_kernel(meta, ready, *refs):
    shard, down_ref, *picks = refs[:4]
    one_ref, two_ref = refs[4:]
    low = meta[YL] == 0
    parts = jnp.concatenate([shard[:, k * PAIR : (k + 1) * PAIR] for k in range(4)], axis=0)
    first, second = [dot(parts, pick_ref[...]).astype(BF) for pick_ref in picks]
    for ref, value in (
        (one_ref, jnp.where(low, first, second)),
        (two_ref, jnp.where(low, second, first)),
    ):
        for k in range(4):
            rows = slice(k * 32, (k + 1) * 32)
            start = (k // 2) * UNITS + (k % 2) * HALF
            ref[:, start : start + HALF] = value[rows, :HALF]
            start = (k // 2) * UNITS + D + (k % 2) * TILE
            ref[:, start : start + TILE] = value[rows, HALF:]
    for k in range(3):
        one_ref[:, GATE_UP + k * D : GATE_UP + (k + 1) * D] = down_ref[k * 32 : (k + 1) * 32, :]


def unpack_attn_kernel(meta, ready, *refs):
    one_ref, two_ref, out_ref = refs
    low = meta[YL] == 0
    for k in range(QKV // LANES):
        cols = slice(k * LANES, (k + 1) * LANES)
        first, second = one_ref[:, cols].astype(F32), two_ref[:, cols].astype(F32)
        out_ref[:, 2 * k * LANES : (2 * k + 1) * LANES] = jnp.where(low, first, second)
        out_ref[:, (2 * k + 1) * LANES : (2 * k + 2) * LANES] = jnp.where(low, second, first)
    out_ref[:, 3 * D :] = one_ref[:, QKV : QKV + D].astype(F32)


def unpack_ffn_kernel(meta, ready, *refs):
    one_ref, two_ref, *picks = refs[:4]
    out_ref, down_ref = refs[4:]
    low = meta[YL] == 0
    halves = []
    for ref in (one_ref, two_ref):
        parts = []
        for k in range(4):
            start = (k // 2) * UNITS + (k % 2) * HALF
            main = ref[:, start : start + HALF]
            start = (k // 2) * UNITS + D + (k % 2) * TILE
            parts.append(jnp.concatenate([main, ref[:, start : start + TILE]], axis=1))
        halves.append(jnp.concatenate(parts, axis=0))
    first = jnp.where(low, halves[0], halves[1])
    second = jnp.where(low, halves[1], halves[0])
    total = dot_nt(first, picks[0][...]) + dot_nt(second, picks[1][...])
    for k in range(4):
        out_ref[:, k * PAIR : (k + 1) * PAIR] = total[k * 32 : (k + 1) * 32]
    for k in range(3):
        part = one_ref[:, GATE_UP + k * D : GATE_UP + (k + 1) * D].astype(F32)
        down_ref[k * 32 : (k + 1) * 32, :] = part


RATE = 3.4e6
VMEM_LIMIT = 56 * 1024 * 1024


def run(kernel, meta, operands, outs, scratch, micros, early=()):
    arrays, specs, places, windows = [], [], [], []
    for operand in operands:
        places.append(len(arrays))
        if not isinstance(operand, tuple):
            arrays.append(operand)
            specs.append(pl.BlockSpec(memory_space=pltpu.VMEM))
            continue
        parts, first, (start, end) = operand
        moves, at = [], 0
        for part in parts:
            low, high = max(start, at), min(end, at + part.shape[1])
            if low < high:
                moves.append((len(arrays), low - at, low - start, high - low))
                arrays.append(part)
                specs.append(pl.BlockSpec(memory_space=pl.ANY))
            at += part.shape[1]
        windows.append((len(places) - 1, first, end - start, moves))
    n_in, n_out, n_early = len(arrays), len(outs), len(early)
    n_windows, n_copies = len(windows), sum(len(window[3]) for window in windows)
    arrays += early
    specs += [pl.BlockSpec(memory_space=pl.ANY)] * n_early
    held = [pltpu.VMEM((TILE, width), BF) for _, _, width, _ in windows]

    def whole(meta_ref, *refs):
        ins, rest = refs[:n_in], refs[n_in + n_early :]
        given = [ins[place] if place < n_in else None for place in places]
        if not windows:
            kernel(meta_ref, lambda: None, *given, *rest)
            return
        sems = rest[-1]
        slots = rest[-1 - n_windows : -1]
        copies = []
        for slot, (place, first, _, moves) in zip(slots, windows):
            for index, source, target, width in moves:
                source = ins[index].at[pl.ds(first, TILE), pl.ds(source, width)]
                target = slot.at[:, pl.ds(target, width)]
                copies.append(pltpu.make_async_copy(source, target, sems.at[len(copies)]))
                copies[-1].start()
            given[place] = slot

        def ready():
            for copy in copies:
                copy.wait()

        kernel(meta_ref, ready, *given, *rest[: -1 - n_windows])

    extra = held + [pltpu.SemaphoreType.DMA((n_copies,))] if windows else []
    return pl.pallas_call(
        whole,
        out_shape=[jax.ShapeDtypeStruct(shape, dtype) for shape, dtype in outs],
        in_specs=[pl.BlockSpec(memory_space=pltpu.SMEM)] + specs,
        out_specs=[pl.BlockSpec(memory_space=pltpu.VMEM)] * n_out,
        scratch_shapes=[pltpu.VMEM(shape, BF) for shape in scratch] + extra,
        compiler_params=pltpu.CompilerParams(vmem_limit_bytes=VMEM_LIMIT),
        cost_estimate=pl.CostEstimate(
            flops=int(micros * 2e9), bytes_accessed=int(micros * RATE), transcendentals=0
        ),
    )(meta, *arrays)


def place_blocks(blocks, shape):
    count = len(blocks)

    def kernel(*refs):
        out_ref, sems = refs[count], refs[count + 1]
        copies = []
        for i, (_, (rows, columns), row, column) in enumerate(blocks):
            source = refs[i].at[pl.ds(rows[0], rows[1]), pl.ds(columns[0], columns[1])]
            target = out_ref.at[pl.ds(row, rows[1]), pl.ds(column, columns[1])]
            copies.append(pltpu.make_async_copy(source, target, sems.at[i]))
            copies[-1].start()
        for copy in copies:
            copy.wait()

    return pl.pallas_call(
        kernel,
        out_shape=jax.ShapeDtypeStruct(shape, BF),
        in_specs=[pl.BlockSpec(memory_space=pl.ANY)] * count,
        out_specs=pl.BlockSpec(memory_space=pltpu.VMEM),
        scratch_shapes=[pltpu.SemaphoreType.DMA((count,))],
        compiler_params=pltpu.CompilerParams(vmem_limit_bytes=VMEM_LIMIT),
        cost_estimate=pl.CostEstimate(
            flops=0, bytes_accessed=4 * math.prod(shape), transcendentals=0
        ),
    )(*[block[0] for block in blocks])


def body(frames_in, in_weights, down_weights, gains, cotangent, segment_ids, valid):
    core = lax.axis_index("c")
    yl = lax.axis_index("yl")
    y = 2 * lax.axis_index("yh") + yl
    zi = lax.axis_index("z")
    xi = lax.axis_index("x")
    is_first = core == 0
    is_low = yl == 0

    block = jnp.arange(16, dtype=jnp.int32)

    def offset(k):
        return jnp.where(k == 1, 3, k - k // 2)

    inner, outer = offset(block % 4), offset(block // 4)
    z_of = (zi + jnp.where(is_first, outer, inner)) % 4
    x_of = (xi + jnp.where(is_first, inner, outer)) % 4
    arrived = 4 * z_of + x_of
    chip = jnp.stack([y, yl])

    meta = jnp.concatenate([arrived, chip]).astype(jnp.int32)
    source = 32 * (8 * z_of[:, None] + x_of[:, None])
    source = source + 128 * jnp.stack([core, 1 - core])[None, :]
    source = (source[:, :, None] + jnp.arange(32, dtype=jnp.int32)).reshape(D)
    move = (lax.broadcasted_iota(jnp.int32, (D, D), 0) == source[None, :]).astype(BF)
    move_t = (lax.broadcasted_iota(jnp.int32, (D, D), 1) == source[:, None]).astype(BF)
    picks = unit_picks()

    def frames_to_chip(value):
        one, two = pick(is_first, to_chip(value, 0), to_chip(value, 1))
        return jnp.concatenate([one, two], axis=0)

    def pack_attn(shard):
        return run(
            pack_attn_kernel,
            meta,
            [shard],
            [((32, QKV + D), BF), ((32, QKV), BF)],
            [],
            1.7,
        )

    def attn_blocks(one, two, column):
        one, two = to_chip(one, 0), to_chip(two, 1)
        rows = (0, 32)
        return [
            (one, (rows, (0, ATTN)), 0, column),
            (two, (rows, (0, QKV)), 32, column),
            (one, (rows, (ATTN, HALF)), 32, column + QKV),
        ]

    def pack_ffn(shard, down, marks):
        padding = jnp.zeros((8, D), BF)
        if marks is not None:
            padding = lax.dynamic_update_slice(padding, marks[None], (0, 0))
        down = jnp.concatenate([down, padding], axis=0)
        return run(
            pack_ffn_kernel,
            meta,
            [shard, down, *picks],
            [((32, GATE_UP + 3 * D), BF), ((32, GATE_UP), BF)],
            [],
            4.5,
        )

    def ffn_blocks(one, two):
        one, two = to_chip(one, 0), to_chip(two, 1)
        rows, down, tail = (0, 32), GATE_UP + D, GATE_UP + 2 * D
        return [
            (one, (rows, (0, down)), 0, 0),
            (one, (rows, (tail, HALF)), 0, down),
            (two, (rows, (0, GATE_UP)), 32, 0),
            (one, (rows, (down, D)), 32, GATE_UP),
            (one, (rows, (tail + HALF, HALF)), 32, down),
        ]

    def attn_to_owner(block, column, extra):
        low, high = (0, 32), (32, 32)
        one = [(block, (low, (column, ATTN)), 0, 0), (block, (high, (column + QKV, HALF)), 0, ATTN)]
        two = [(block, (high, (column, QKV)), 0, 0)]
        if extra:
            columns = (column + ATTN, extra)
            one.append((block, (low, columns), 0, ATTN + HALF))
            two.append((block, (high, columns), 0, QKV))
        one = to_owner(place_blocks(one, (32, ATTN + HALF + extra)), 0)
        two = to_owner(place_blocks(two, (32, QKV + extra)), 1)
        sums = plus(one[:, ATTN + HALF :], two[:, QKV:])[:, :4] if extra else None
        return run(unpack_attn_kernel, meta, [one, two], [((32, 4 * D), F32)], [], 1.8)[0], sums

    def ffn_to_owner(block):
        low, high, down = (0, 32), (32, 32), GATE_UP + D
        one = [
            (block, (low, (0, down)), 0, 0),
            (block, (high, (GATE_UP, D)), 0, down),
            (block, (low, (down, HALF)), 0, down + D),
            (block, (high, (down, HALF)), 0, down + D + HALF),
        ]
        one = to_owner(place_blocks(one, (32, GATE_UP + 3 * D)), 0)
        two = to_owner(place_blocks([(block, (high, (0, GATE_UP)), 0, 0)], (32, GATE_UP)), 1)
        units, down = run(
            unpack_ffn_kernel,
            meta,
            [one, two, *picks],
            [((32, 4 * PAIR), F32), ((96, D), F32)],
            [],
            4.5,
        )
        return units, down[:88]

    gain_rows = gains[:, 0].transpose(1, 2, 0).reshape(4, D)

    def gain_row(layer, which):
        place = 2 * layer + which
        return gain_all[place : place + 1]

    onehot = segment_ids[:, None] == jnp.arange(LANES, dtype=jnp.int32)[None, :]
    counts = jnp.sum(jnp.where(onehot, valid.astype(F32)[:, None], 0.0), axis=0).astype(BF)
    marks = jnp.stack([segment_ids, valid], axis=1).astype(BF)
    marked = jnp.concatenate([frames_in[:, 0], jnp.pad(marks, ((0, 0), (0, LANES - 2)))], axis=1)

    attn0 = pack_attn(in_weights[:, 0, 0, : 4 * D])
    attn0 = Gather(place_blocks(attn_blocks(*attn0, 0), (64, ATTN)))
    attn0.one()
    later = after(in_weights, attn0.piece)
    ffn0_parts = pack_ffn(later[:, 0, 0, 4 * D :], down_weights[:, 0, 0], None)
    attn0.two(*ffn0_parts)
    attn1_parts = pack_attn(after(later, *ffn0_parts)[:, 0, 1, : 4 * D])
    attn0_three = attn0.three()
    blocks = ffn_blocks(*ffn0_parts)
    blocks += attn_blocks(*after(tuple(attn1_parts), blocks[0][0]), FFN)
    middle0 = Gather(place_blocks(blocks, (64, FFN + ATTN)))
    later = after(in_weights, *attn1_parts)
    ffn1_parts = pack_ffn(later[:, 0, 1, 4 * D :], down_weights[:, 0, 1], counts)
    blocks = ffn_blocks(*after(tuple(ffn1_parts), blocks[-1][0]))
    ffn1 = Gather(place_blocks(blocks, (64, FFN)))
    marked = frames_to_chip(after(marked, blocks[0][0]))
    state = marked[:, :D]
    marks = marked[:, D:]
    gain_all = to_chip(after(gain_rows, blocks[0][0]), 0).astype(F32)
    attn0_four = attn0.four()
    middle0.one()
    middle0.two()
    ffn1.one()
    ffn1_two = ffn1.two()
    ffn1_joined = ffn1.piece
    middle0_three = middle0.three(attn0_four, ffn1_two)
    ffn1.three(middle0_three)
    ffn1.four()

    def windows(gathered, start, end):
        if isinstance(gathered, list):
            return [(parts, 0, (start, end)) for parts in gathered]
        return [((gathered,), k * TILE, (start, end)) for k in range(4)]

    near = [(0, 1), (1, 0), (2, 3), (3, 2)]
    across = [(0, 3), (3, 0), (1, 2), (2, 1)]

    wide = ((TOKENS, D), F32)
    wide16 = ((TOKENS, D), BF)
    turned = ((D, TOKENS), BF)
    row = ((1, D), F32)
    saved = []
    base = None
    for layer in range(LAYERS):
        first = layer == 0
        attn, at = (attn0.blocks, 0) if first else (middle0.blocks, FFN)
        carried = [state] if first else list(base)
        state, turned_a, *blocks = run(
            lambda *refs, first=first: qkv_kernel(first, *refs),
            meta,
            [*carried, gain_row(layer, 0), move, move_t] + windows(attn, at, at + QKV),
            [wide, turned] + [((ROWS, QKV), BF)] * 4,
            [(TOKENS, D), (TOKENS, D), (TOKENS, QKV)],
            7.7,
        )
        blocks = exchange_column(blocks)
        if not first:
            cot = frames_to_chip(after(cotangent[:, 0], blocks[1]))
        mixed = run(
            attend_kernel,
            meta,
            blocks,
            [((ROWS, HALF), BF)] * 4,
            [(POS, ROWS, QKV), (POS, ROWS, HALF)],
            3.0,
        )
        if first:
            middle0.four()
        mixed = exchange_column(mixed)
        turned_o, w_out, partial = run(
            out_kernel,
            meta,
            mixed + windows(attn, at + QKV, at + ATTN),
            [((HALF, TOKENS), BF), ((HALF, D), BF), wide16],
            [(TOKENS, HALF), (HALF, TOKENS)],
            3.6,
        )
        ffn = (middle0 if first else ffn1).blocks
        middle, turned_b, gate, up_part, turned_act, w_down, down_partial, *totals = run(
            lambda *refs, first=first: ffn_kernel(not first, *refs),
            meta,
            [state, partial, other_core(partial), gain_row(layer, 1), move, move_t]
            + windows(ffn, 0, FFN),
            [wide, turned, ((TOKENS, UNITS), F32), ((TOKENS, UNITS), F32)]
            + [((UNITS, TOKENS), BF), ((UNITS, D), BF), wide16]
            + ([] if first else [((1, LANES), F32)]),
            [(TOKENS, D), (TOKENS, D), (TOKENS, UNITS), (UNITS, TOKENS)],
            15.0,
            (ffn1_joined,) if first else (),
        )
        saved.append(
            (state, turned_a, blocks, turned_o, w_out, middle, turned_b, gate, up_part)
            + (turned_act, w_down, attn, at, ffn)
        )
        base = (middle, down_partial, other_core(down_partial))
    totals = totals[0]
    other_totals = other_core(totals)

    def frames_to_owner(value):
        return to_owner(jnp.where(is_first, value[:128], value[128:]), 0)[:, None]

    output = frames_to_owner((base[0] + plus(base[1], base[2])).astype(BF))

    gain_list = [[None, None] for _ in range(LAYERS)]

    down_list = [None] * LAYERS

    def gradient_blocks(width):
        half = width // TILE // 2 * TILE
        return [((TILE, width), BF)] * 3 + [((TILE, half), BF), ((TILE, width - half), BF)]

    for layer in reversed(range(LAYERS)):
        (state, turned_a, blocks, turned_o, w_out, middle, turned_b, gate, up_part) = saved[layer][:9]
        turned_act, w_down, attn, at, ffn = saved[layer][9:]
        last = layer == LAYERS - 1
        carried = [cot, marks, totals, other_totals] if last else list(base)
        results = run(
            lambda *refs, last=last: ffn_backward_kernel(last, *refs),
            meta,
            [*carried, turned_act, turned_b, gate, up_part, w_down, move]
            + windows(ffn, 0, GATE_UP)
            + ([] if last else windows(attn_above, 0, ATTN)),
            [wide]
            + ([] if last else [row])
            + [wide16]
            + gradient_blocks(FFN if last else FFN + ATTN),
            [(TOKENS, D), (TOKENS, GATE_UP), (TOKENS, D)],
            18.0,
            () if last else above_three,
        )
        grad, *results = results
        if not last:
            gain_list[layer + 1][0], *results = results
        partial, *pieces = results
        if last:
            ffn_above = Scatter(*pieces)
            above_one = ffn_above.one()
            above_two = ffn_above.two()
            above_three = ffn_above.three()
            above_four = ffn_above.four()
        else:
            ffn_sum = Scatter(*pieces)
            ffn_one = ffn_sum.one()
        other = other_core(partial)
        grad, gain_list[layer][1], out_terms, *mixed = run(
            out_backward_kernel,
            meta,
            [grad, partial, other, middle, gain_row(layer, 1), turned_o, w_out],
            [wide, row, ((D, HALF), BF)] + [((ROWS, HALF), BF)] * 4,
            [(TOKENS, D), (TOKENS, HALF)],
            5.8,
            () if last else above_four,
        )
        mixed = exchange_column(mixed)
        if not last:
            ffn_two = ffn_sum.two()
        grads = run(
            attend_backward_kernel,
            meta,
            [*blocks, *mixed],
            [((ROWS, QKV), BF)] * 4,
            [(POS, ROWS, QKV), (POS, ROWS, HALF), (POS, ROWS, QKV)],
            3.8,
            above_one if last else ffn_one,
        )
        own = grads[0]
        grads = exchange_column(grads)
        if last:
            grads[0] = after(own, output)
        partial, *pieces = run(
            lambda *refs, first=not last: qkv_backward_kernel(first, *refs),
            meta,
            [*grads, turned_a, out_terms, move]
            + ([] if last else [move_t, state, gain_list[0][1], *gain_list[1]])
            + windows(attn, at, at + QKV),
            [wide16] + ([((D, ATTN), BF)] if last else gradient_blocks(ATTN_GAINS)),
            [(TOKENS, QKV), (TOKENS, D)],
            10.0,
        )
        if last:
            attn_above = pieces[0]
        else:
            attn_sum = Scatter(*pieces)
            attn_sum.one()
        base = (grad, partial, other_core(partial), state, gain_row(layer, 0))
    input_grad = run(last_kernel, meta, list(base), [wide16], [], 4.3, ffn_two)[0]
    ffn_sum.three()
    attn_sum.two(ffn_two)
    ffn_sum.four()
    last_sums = attn_sum.three()
    units_above, down_list[1] = ffn_to_owner(ffn_above.block)
    attn_sum.four()
    both = after(ffn_sum.block, last_sums)
    attn_part, _ = attn_to_owner(both, FFN, 0)
    in_parts = [None, [attn_part, units_above]]
    units, down_list[0] = ffn_to_owner(both)
    attn_part, gain_sums = attn_to_owner(attn_sum.block, 0, LANES)
    in_parts[0] = [attn_part, units]
    in_list = [jnp.concatenate(parts, axis=1) for parts in in_parts]
    in_grads = jnp.stack(in_list, axis=1)[:, None]
    down_grads = jnp.stack(down_list, axis=1)[:, None]

    gains_grad = gain_sums.reshape(32, 1, LAYERS, 2)
    return (output, frames_to_owner(input_grad), in_grads, down_grads, gains_grad)


def solution(mesh):
    parts = Mesh(mesh.devices.reshape(2, 2, 4, 2, 4), ("yh", "c", "z", "yl", "x"))
    dp = ("z", "yl", "x")
    section = ("yh", "c")
    return jax.shard_map(
        body,
        mesh=parts,
        in_specs=(
            P(dp, section, None),
            P(dp, section, None, None),
            P(dp, section, None, None),
            P(None, section, None, None),
            P(dp, section, None),
            P(dp),
            P(dp),
        ),
        out_specs=(
            P(dp, section, None),
            P(dp, section, None),
            P(dp, section, None, None),
            P(dp, section, None, None),
            P(dp, section, None, None),
        ),
        check_vma=False,
    )
```

time: 900 us -> 559 us (0.62)
  Pallas kernels: 5.2 us -> 189 us
  starting transfers between devices: 312 us -> 158 us
  waiting for transfers between devices: 232 us -> 116 us
  local copies, waits for them, and re-layouts: 146 us -> 51.4 us
  matrix products: 84.3 us -> 0 us
  other arithmetic: 104 us -> 32.6 us
    pallas_call x4 -> x39, Pallas kernels: 5.2 us -> 189 us  [the longest x25 161 us: run(): pl.pallas_call(whole, out_shape=[jax.ShapeDtypeStruct(shape, dtype) for s...]
    ppermute x128 -> x48, waiting for transfers between devices: 195 us -> 82.6 us  [shift(): return lax.ppermute(value, PLANE, ring_pairs(axis_of_core, step))]
    dot_general x32 -> x0, matrix products: 84.3 us -> none  [the longest x8 39.7 us: matmul_nt(): lax.dot_general(one, two, (((1,), (1,)), ((), ())), preferred_element_typ...]
    ppermute x128 -> x48, starting transfers between devices: 131 us -> 57.4 us  [shift(): return lax.ppermute(value, PLANE, ring_pairs(axis_of_core, step))]
    slice x73 -> x29, local copies, waits for them, and re-layouts: 53.6 us -> 15.7 us  [the longest x6 4.89 us: far(): far_a = shift(after(self.left[:, :half], *deps), axis_of_core, 1)]
    concatenate x48 -> x15, other arithmetic: 34.6 us -> 6.16 us  [the longest x6 3.28 us: far(): jnp.concatenate([plus(right[:, :half], far_a).astype(BF), right[:, half:]...]
    ppermute x19 -> x13, starting transfers between devices: 51.4 us -> 24.8 us  [to_chip(): return lax.ppermute(value, ('c', 'yl'), pairs)]
    ppermute x15 -> x10, starting transfers between devices: 51.8 us -> 29.1 us  [to_owner(): return lax.ppermute(value, ('c', 'yl'), pairs)]
  transfers between devices with their start and end apart: 203 -> 104, of which waited for: 71 -> 29; matrix products, arithmetic and copies ran while one was open for 33% -> 9% of each run, Pallas kernels for 1% -> 25%
where the time goes in v2:
time: 559 us; the launch traced here: 549 us
  Pallas kernels  189 us (34%)
  starting transfers between devices  158 us (28%)
  waiting for transfers between devices  116 us (21%)
  local copies, waits for them, and re-layouts  51.4 us (9%)
  other arithmetic  32.6 us (6%)
    pallas_call x25, Pallas kernels, run(): pl.pallas_call(whole, out_shape=[jax.ShapeDtypeStruct(shape, dtype) for s...  161 us
    ppermute x48, waiting for transfers between devices, shift(): return lax.ppermute(value, PLANE, ring_pairs(axis_of_core, step))  82.6 us
    ppermute x48, starting transfers between devices, shift(): return lax.ppermute(value, PLANE, ring_pairs(axis_of_core, step))  57.4 us
    ppermute x24, starting transfers between devices, exchange_column(): lax.ppermute(blocks[k], COLUMN, [(y, y ^ k) for y in range(POS)])  32.9 us
    unnamed x205, local copies, waits for them, and re-layouts  29.9 us
    ppermute x10, starting transfers between devices, to_owner(): return lax.ppermute(value, ('c', 'yl'), pairs)  29.1 us
    pallas_call x14, Pallas kernels, place_blocks(): pl.pallas_call(kernel, out_shape=jax.ShapeDtypeStruct(shape, BF), in_spec...  27.7 us
    ppermute x13, starting transfers between devices, to_chip(): return lax.ppermute(value, ('c', 'yl'), pairs)  24.8 us
  transfers between devices with their start and end apart: 104, of which 29 were waited for; matrix products, arithmetic and copies ran while one was open for 9% of the time, Pallas kernels for 25%

profile of v2, /device:TPU:1, one launch (start us, length us, event | category | flops | bytes accessed | tf_op | source)
XLA Modules:
  0.0 549.0 jit_solution(15112852434714548708)
XLA Ops:
  16.8 3.8 collective-permute-start.9
  21.6 4.1 shard_map.130
  47.7 3.8 collective-permute-start.26
  51.6 4.1 shard_map.132
  58.8 6.6 %collective-permute-done.4.refs_0_.refs_1_.refs_3_.refs_4_ = bf16[32,6144]{1,0:T(8,128)(2,1)S(1)} collective-permute-done((bf16[32,6144]{1,0:T(8,128)(2,1)}, bf16[32,6144]{1,0:T(8,128)(2,1)S(1)}, u32[]{:S(2)}, u32[]{:S(2)}) %collective-permute-start.4) | collective-permute-done | bytes 393248 | tf_op jit(solution)/shard_map/ppermute | solution.py:159
  79.1 6.5 %collective-permute-done.30.refs_1_ = bf16[64,4608]{1,0:T(8,128)(2,1)} collective-permute-done((bf16[64,4608]{1,0:T(8,128)(2,1)}, bf16[64,4608]{1,0:T(8,128)(2,1)}, u32[]{:S(2)}, u32[]{:S(2)}) %collective-permute-start.30) | collective-permute-done | bytes 589856 | tf_op jit(solution)/shard_map/ppermute | solution.py:69
  88.7 6.0 %collective-permute-done.27.refs_3_ = bf16[64,3328]{1,0:T(8,128)(2,1)S(1)} collective-permute-done((bf16[64,3328]{1,0:T(8,128)(2,1)S(1)}, bf16[64,3328]{1,0:T(8,128)(2,1)S(1)}, u32[]{:S(2)}, u32[]{:S(2)}) %collective-permute-start.27) | collective-permute-done | bytes 426016 | tf_op jit(solution)/shard_map/ppermute | solution.py:69
  95.5 3.7 shard_map.138.refs_6_.refs_4_.refs_7_.refs_11_
  102.8 3.4 collective-permute-start.6
  116.8 7.7 %shard_map.134 = (f32[256,1024]{1,0:T(8,128)}, bf16[1024,256]{1,0:T(8,128)(2,1)}, bf16[64,1536]{1,0:T(8,128)(2,1)}, bf16[64,1536]{1,0:T(8,128)(2,1)}, bf16[64,15...) custom-call(s32[18]{0:T(128)} %pad_add_fusion.meta_ref, bf16[256,1024]{1,0:T(8,128)(2,1)} %fusion.3.refs_0_, ...), custom_call_target="tpu_custom_call" | custom-call | flops 15399999488 | bytes 26180000 | tf_op jit(solution)/shard_map/pallas_call | solution.py:745
  128.5 11.0 %collective-permute-done.35.refs_8_.refs_6_.refs_9_.refs_13_ = bf16[256,6656]{1,0:T(8,128)(2,1)S(1)} collective-permute-done((bf16[256,6656]{1,0:T(8,128)(2,1)}, bf16[256,6656]{1,0:T(8,128)(2,1)S(1)}, u32[]{:S(2)}, u32[]{:S(2)}) %collective-permute-start.35) | collective-permute-done | bytes 3407904 | tf_op jit(solution)/shard_map/ppermute | solution.py:69
  152.9 4.0 collective-permute-done.20.refs_2_
  158.6 3.5 shard_map.136
  163.2 3.0 shard_map.140.refs_11_.refs_6_.refs_10_
  167.1 14.7 %shard_map.141 = (f32[256,1024]{1,0:T(8,128)}, bf16[1024,256]{1,0:T(8,128)(2,1)}, f32[256,1536]{1,0:T(8,128)}, f32[256,1536]{1,0:T(8,128)}, bf16[1536,256]{1,0:T...) custom-call(s32[18]{0:T(128)} %pad_add_fusion.meta_ref, ...), custom_call_target="tpu_custom_call" | custom-call | flops 30000001024 | bytes 51000000 | tf_op jit(solution)/shard_map/pallas_call | solution.py:745
  186.6 8.2 %shard_map.142 = (f32[256,1024]{1,0:T(8,128)}, bf16[1024,256]{1,0:T(8,128)(2,1)}, bf16[64,1536]{1,0:T(8,128)(2,1)}, bf16[64,1536]{1,0:T(8,128)(2,1)}, bf16[64,15...) custom-call(s32[18]{0:T(128)} %pad_add_fusion.meta_ref, f32[256,1024]{1,0:T(8,128)} %get-tuple-element.151.refs_0_.refs_3_, ...), custom_call_target="tpu_custom_call" | custom-call | flops 15399999488 | bytes 26180000 | tf_op jit(solution)/shard_map/pallas_call | solution.py:745
  201.3 5.9 %collective-permute-done.40.refs_2_ = bf16[64,1536]{1,0:T(8,128)(2,1)S(1)} collective-permute-done((bf16[64,1536]{1,0:T(8,128)(2,1)}, bf16[64,1536]{1,0:T(8,128)(2,1)S(1)}, u32[]{:S(2)}, u32[]{:S(2)}) %collective-permute-start.40) | collective-permute-done | bytes 196640 | tf_op jit(solution)/shard_map/ppermute | solution.py:178
  221.0 3.6 shard_map.144
  227.1 3.6 collective-permute-start.52
  231.4 4.7 collective-permute-done.52
  237.4 14.7 %shard_map.145 = (f32[256,1024]{1,0:T(8,128)}, bf16[1024,256]{1,0:T(8,128)(2,1)}, f32[256,1536]{1,0:T(8,128)}, f32[256,1536]{1,0:T(8,128)}, bf16[1536,256]{1,0:T...) custom-call(s32[18]{0:T(128)} %pad_add_fusion.meta_ref, ...), custom_call_target="tpu_custom_call" | custom-call | flops 30000001024 | bytes 51000000 | tf_op jit(solution)/shard_map/pallas_call | solution.py:745
  255.5 15.0 %shard_map.146 = (f32[256,1024]{1,0:T(8,128)}, bf16[256,1024]{1,0:T(8,128)(2,1)}, bf16[256,4608]{1,0:T(8,128)(2,1)}, bf16[256,4608]{1,0:T(8,128)(2,1)}, bf16[256...) custom-call(s32[18]{0:T(128)} %pad_add_fusion.meta_ref, ...), custom_call_target="tpu_custom_call" | custom-call | flops 35999997952 | bytes 61200000 | tf_op jit(solution)/shard_map/pallas_call | solution.py:745
  275.5 11.9 %collective-permute-done.59.refs_8_ = bf16[256,2304]{1,0:T(8,128)(2,1)S(1)} collective-permute-done((bf16[256,2304]{1,0:T(8,128)(2,1)}, bf16[256,2304]{1,0:T(8,128)(2,1)S(1)}, u32[]{:S(2)}, u32[]{:S(2)}) %collective-permute-start.59) | collective-permute-done | bytes 1179680 | tf_op jit(solution)/shard_map/ppermute | solution.py:69
  290.4 3.1 collective-permute-start.66
  293.8 5.8 %shard_map.147 = (f32[256,1024]{1,0:T(8,128)}, f32[1,1024]{1,0:T(1,128)}, bf16[1024,512]{1,0:T(8,128)(2,1)}, bf16[64,512]{1,0:T(8,128)(2,1)}, bf16[64,512]{1,0:T...) custom-call(s32[18]{0:T(128)} %pad_add_fusion.meta_ref, f32[256,1024]{1,0:T(8,128)} %get-tuple-element.173.refs_0_, ...), custom_call_target="tpu_custom_call" | custom-call | flops 11600000000 | bytes 19720000 | tf_op jit(solution)/shard_map/pallas_call | solution.py:745
  303.5 4.7 collective-permute-start.51
  308.9 3.9 shard_map.148
  319.3 3.5 collective-permute-done.65
  322.8 3.2 add_convert_fusion.1
  328.5 8.6 %shard_map.149 = (bf16[256,1024]{1,0:T(8,128)(2,1)}, bf16[1024,2048]{1,0:T(8,128)(2,1)}) custom-call(s32[18]{0:T(128)} %pad_add_fusion.meta_ref, bf16[64,1536]{1,0:T(8,128)(2,1)} %get-tuple-element.185.refs_0_, bf16[64,1536]{1,0:T(8,128)(2,1)} %copy-done.78, bf16[64,1536]{1,0:T(8,128)(2,1)} %copy-done.79, bf16[64,1536]{1,0:T(8,128)(2,1)} %copy-done.80, ...), custom_call_target="tpu_custom_call" | custom-call | flops 20000000000 | bytes 34000000 | tf_op jit(solution)/shard_map/pallas_call | solution.py:745
  337.1 3.5 collective-permute-start.64
  343.2 19.0 %shard_map.150 = (f32[256,1024]{1,0:T(8,128)}, f32[1,1024]{1,0:T(1,128)}, bf16[256,1024]{1,0:T(8,128)(2,1)}, bf16[256,6656]{1,0:T(8,128)(2,1)}, bf16[256,6656]{1...) custom-call(s32[18]{0:T(128)} %pad_add_fusion.meta_ref, ...), custom_call_target="tpu_custom_call" | custom-call | flops 35999997952 | bytes 61200000 | tf_op jit(solution)/shard_map/pallas_call | solution.py:745
  363.1 3.1 collective-permute-start.76
  368.1 5.8 %shard_map.151 = (f32[256,1024]{1,0:T(8,128)}, f32[1,1024]{1,0:T(1,128)}, bf16[1024,512]{1,0:T(8,128)(2,1)}, bf16[64,512]{1,0:T(8,128)(2,1)}, bf16[64,512]{1,0:T...) custom-call(s32[18]{0:T(128)} %pad_add_fusion.meta_ref, f32[256,1024]{1,0:T(8,128)} %get-tuple-element.201.refs_0_, ...), custom_call_target="tpu_custom_call" | custom-call | flops 11600000000 | bytes 19720000 | tf_op jit(solution)/shard_map/pallas_call | solution.py:745
  386.8 3.7 shard_map.152
  400.8 3.0 collective-permute-start.82
  405.3 11.3 %shard_map.153 = (bf16[256,1024]{1,0:T(8,128)(2,1)}, bf16[256,2176]{1,0:T(8,128)(2,1)}, bf16[256,2176]{1,0:T(8,128)(2,1)}, bf16[256,2176]{1,0:T(8,128)(2,1)}, bf...) custom-call(s32[18]{0:T(128)} %pad_add_fusion.meta_ref, bf16[64,1536]{1,0:T(8,128)(2,1)} %get-tuple-element.212.refs_0_, ...), custom_call_target="tpu_custom_call" | custom-call | flops 20000000000 | bytes 34000000 | tf_op jit(solution)/shard_map/pallas_call | solution.py:745
  418.9 4.8 shard_map.166
  426.9 3.2 collective-permute-start.86
  430.0 20.1 %collective-permute-done.84 = bf16[256,1024]{1,0:T(8,128)(2,1)S(1)} collective-permute-done((bf16[256,1024]{1,0:T(8,128)(2,1)}, bf16[256,1024]{1,0:T(8,128)(2,1)S(1)}, u32[]{:S(2)}, u32[]{:S(2)}) %collective-permute-start.84) | collective-permute-done | bytes 524320 | tf_op jit(solution)/shard_map/ppermute | solution.py:69
  452.7 3.2 add_convert_fusion.refs_5_
  459.3 4.2 shard_map.154
  464.6 4.9 collective-permute-start.83
  477.3 12.5 %collective-permute-done.85 = bf16[256,2176]{1,0:T(8,128)(2,1)S(1)} collective-permute-done((bf16[256,2176]{1,0:T(8,128)(2,1)S(1)}, bf16[256,2176]{1,0:T(8,128)(2,1)S(1)}, u32[]{:S(2)}, u32[]{:S(2)}) %collective-permute-start.85) | collective-permute-done | bytes 1114144 | tf_op jit(solution)/shard_map/ppermute | solution.py:69
  506.5 5.0 collective-permute-start.100
  527.2 3.8 collective-permute-start.92
  532.5 4.8 shard_map.160
  543.8 3.4 copy.43
  (499 shorter events, 240.2 us)
Async XLA Ops:
  25.6 18.6 %collective-permute-start.23 = (bf16[32,3072]{1,0:T(8,128)(2,1)}, bf16[32,3072]{1,0:T(8,128)(2,1)S(1)}, u32[]{:S(2)}, u32[]{:S(2)}) collective-permute-start(bf16[32,3072]{1,0:T(8,128)(2,1)} %get-tuple-element.125), channel_id=1, source_target_pairs={{0,32},{4,0},{32,36},{36,4},{1,33},{5,1},{33,37},{37,5},{2,34},{6,... | collective-permute-start | bytes 589832 | tf_op jit(solution)/shard_map/ppermute | solution.py:159
  41.8 29.5 %collective-permute-start.13 = (bf16[256,2048]{1,0:T(8,128)(2,1)}, bf16[256,2048]{1,0:T(8,128)(2,1)S(1)}, u32[]{:S(2)}, u32[]{:S(2)}) collective-permute-start(bf16[256,2048]{1,0:T(8,128)(2,1)} %shard_map.133.refs_4_.refs_12_), channel_id=1, source_target_pairs={{0,24},{1,25},{2,26},{3,27},{8,0},{9,1},{10,2},{11,3},{16,8},{17,9... | collective-permute-start | bytes 3145736 | tf_op jit(solution)/shard_map/ppermute | solution.py:69
  47.7 22.7 %collective-permute-start.26 = (bf16[64,6656]{1,0:T(8,128)(2,1)}, bf16[64,6656]{1,0:T(8,128)(2,1)S(1)}, u32[]{:S(2)}, u32[]{:S(2)}) collective-permute-start(bf16[64,6656]{1,0:T(8,128)(2,1)} %shard_map.137.refs_0_), channel_id=1, source_target_pairs={{0,3},{1,0},{2,1},{3,2},{8,11},{9,8},{10,9},{11,10},{16,19},{17,16... | collective-permute-start | bytes 2555912 | tf_op jit(solution)/shard_map/ppermute | solution.py:69
  55.7 20.5 %collective-permute-start.12 = (bf16[256,2048]{1,0:T(8,128)(2,1)S(1)}, bf16[256,2048]{1,0:T(8,128)(2,1)S(1)}, u32[]{:S(2)}, u32[]{:S(2)}) collective-permute-start(bf16[256,2048]{1,0:T(8,128)(2,1)S(1)} %copy-done.21), channel_id=1, source_target_pairs={{0,8},{1,9},{2,10},{3,11},{8,16},{9,17},{10,18},{11,19},{16,24},{1... | collective-permute-start | bytes 3145736 | tf_op jit(solution)/shard_map/ppermute | solution.py:69
  58.7 20.2 %collective-permute-start.25 = (bf16[64,6656]{1,0:T(8,128)(2,1)S(1)}, bf16[64,6656]{1,0:T(8,128)(2,1)S(1)}, u32[]{:S(2)}, u32[]{:S(2)}) collective-permute-start(bf16[64,6656]{1,0:T(8,128)(2,1)S(1)} %copy-done.5), channel_id=1, source_target_pairs={{0,1},{1,2},{2,3},{3,0},{8,9},{9,10},{10,11},{11,8},{16,17},{17,18... | collective-permute-start | bytes 2555912 | tf_op jit(solution)/shard_map/ppermute | solution.py:69
  70.4 15.2 %collective-permute-start.30 = (bf16[64,4608]{1,0:T(8,128)(2,1)}, bf16[64,4608]{1,0:T(8,128)(2,1)}, u32[]{:S(2)}, u32[]{:S(2)}) collective-permute-start(bf16[64,4608]{1,0:T(8,128)(2,1)} %shard_map.139.refs_0_), channel_id=1, source_target_pairs={{0,1},{1,2},{2,3},{3,0},{8,9},{9,10},{10,11},{11,8},{16,17},{17,18... | collective-permute-start | bytes 1769480 | tf_op jit(solution)/shard_map/ppermute | solution.py:69
  71.3 15.7 %collective-permute-start.28 = (bf16[64,3328]{1,0:T(8,128)(2,1)}, bf16[64,3328]{1,0:T(8,128)(2,1)}, u32[]{:S(2)}, u32[]{:S(2)}) collective-permute-start(bf16[64,3328]{1,0:T(8,128)(2,1)} %slice.307), channel_id=1, source_target_pairs={{0,3},{1,0},{2,1},{3,2},{8,11},{9,8},{10,9},{11,10},{16,19},{17,16... | collective-permute-start | bytes 1277960 | tf_op jit(solution)/shard_map/ppermute | solution.py:69
  76.2 23.0 %collective-permute-start.15 = (bf16[256,1024]{1,0:T(8,128)(2,1)}, bf16[256,1024]{1,0:T(8,128)(2,1)}, u32[]{:S(2)}, u32[]{:S(2)}) collective-permute-start(bf16[256,1024]{1,0:T(8,128)(2,1)} %slice.304), channel_id=1, source_target_pairs={{0,24},{1,25},{2,26},{3,27},{8,0},{9,1},{10,2},{11,3},{16,8},{17,9... | collective-permute-start | bytes 1572872 | tf_op jit(solution)/shard_map/ppermute | solution.py:69
  78.9 21.0 %collective-permute-start.14 = (bf16[256,1024]{1,0:T(8,128)(2,1)}, bf16[256,1024]{1,0:T(8,128)(2,1)}, u32[]{:S(2)}, u32[]{:S(2)}) collective-permute-start(bf16[256,1024]{1,0:T(8,128)(2,1)} %slice.303), channel_id=1, source_target_pairs={{0,8},{1,9},{2,10},{3,11},{8,16},{9,17},{10,18},{11,19},{16,24},{1... | collective-permute-start | bytes 1572872 | tf_op jit(solution)/shard_map/ppermute | solution.py:69
  79.0 15.7 %collective-permute-start.27 = (bf16[64,3328]{1,0:T(8,128)(2,1)S(1)}, bf16[64,3328]{1,0:T(8,128)(2,1)S(1)}, u32[]{:S(2)}, u32[]{:S(2)}) collective-permute-start(bf16[64,3328]{1,0:T(8,128)(2,1)S(1)} %slice.306), channel_id=1, source_target_pairs={{0,1},{1,2},{2,3},{3,0},{8,9},{9,10},{10,11},{11,8},{16,17},{17,18... | collective-permute-start | bytes 1277960 | tf_op jit(solution)/shard_map/ppermute | solution.py:69
  100.0 39.5 %collective-permute-start.35 = (bf16[256,6656]{1,0:T(8,128)(2,1)}, bf16[256,6656]{1,0:T(8,128)(2,1)S(1)}, u32[]{:S(2)}, u32[]{:S(2)}) collective-permute-start(bf16[256,6656]{1,0:T(8,128)(2,1)} %shard_map.138.refs_6_.refs_4_.refs_7_.refs_11_), channel_id=1, source_target_pairs={{0,24},{1,25},{2,26},{3,27},{8,0},{9,1},{10,2},{11,3},{16,8},{17,9... | collective-permute-start | bytes 10223624 | tf_op jit(solution)/shard_map/ppermute | solution.py:69
  101.3 40.9 %collective-permute-start.34 = (bf16[256,6656]{1,0:T(8,128)(2,1)}, bf16[256,6656]{1,0:T(8,128)(2,1)}, u32[]{:S(2)}, u32[]{:S(2)}) collective-permute-start(bf16[256,6656]{1,0:T(8,128)(2,1)} %shard_map.138.refs_6_.refs_4_.refs_7_.refs_11_), channel_id=1, source_target_pairs={{0,8},{1,9},{2,10},{3,11},{8,16},{9,17},{10,18},{11,19},{16,24},{1... | collective-permute-start | bytes 10223624 | tf_op jit(solution)/shard_map/ppermute | solution.py:69
  124.5 19.3 %collective-permute-start.16 = (bf16[64,1536]{1,0:T(8,128)(2,1)}, bf16[64,1536]{1,0:T(8,128)(2,1)S(1)}, u32[]{:S(2)}, u32[]{:S(2)}) collective-permute-start(bf16[64,1536]{1,0:T(8,128)(2,1)} %get-tuple-element.140), channel_id=1, source_target_pairs={{0,4},{4,0},{64,68},{68,64},{1,5},{5,1},{65,69},{69,65},{2,6},{6,2... | collective-permute-start | bytes 589832 | tf_op jit(solution)/shard_map/ppermute | solution.py:178
  124.6 19.3 %collective-permute-start.17 = (bf16[64,1536]{1,0:T(8,128)(2,1)}, bf16[64,1536]{1,0:T(8,128)(2,1)S(1)}, u32[]{:S(2)}, u32[]{:S(2)}) collective-permute-start(bf16[64,1536]{1,0:T(8,128)(2,1)} %get-tuple-element.141), channel_id=1, source_target_pairs={{0,64},{4,68},{64,0},{68,4},{1,65},{5,69},{65,1},{69,5},{2,66},{6,... | collective-permute-start | bytes 589832 | tf_op jit(solution)/shard_map/ppermute | solution.py:178
  127.6 16.3 %collective-permute-start.18 = (bf16[64,1536]{1,0:T(8,128)(2,1)}, bf16[64,1536]{1,0:T(8,128)(2,1)S(1)}, u32[]{:S(2)}, u32[]{:S(2)}) collective-permute-start(bf16[64,1536]{1,0:T(8,128)(2,1)} %get-tuple-element.142), channel_id=1, source_target_pairs={{0,68},{4,64},{64,4},{68,0},{1,69},{5,65},{65,5},{69,1},{2,70},{6,... | collective-permute-start | bytes 589832 | tf_op jit(solution)/shard_map/ppermute | solution.py:178
  139.6 26.7 %collective-permute-start.37 = (bf16[256,3328]{1,0:T(8,128)(2,1)S(1)}, bf16[256,3328]{1,0:T(8,128)(2,1)}, u32[]{:S(2)}, u32[]{:S(2)}) collective-permute-start(bf16[256,3328]{1,0:T(8,128)(2,1)S(1)} %slice.311), channel_id=1, source_target_pairs={{0,24},{1,25},{2,26},{3,27},{8,0},{9,1},{10,2},{11,3},{16,8},{17,9... | collective-permute-start | bytes 5111816 | tf_op jit(solution)/shard_map/ppermute | solution.py:69
  143.8 22.5 %collective-permute-start.36 = (bf16[256,3328]{1,0:T(8,128)(2,1)S(1)}, bf16[256,3328]{1,0:T(8,128)(2,1)}, u32[]{:S(2)}, u32[]{:S(2)}) collective-permute-start(bf16[256,3328]{1,0:T(8,128)(2,1)S(1)} %slice.310), channel_id=1, source_target_pairs={{0,8},{1,9},{2,10},{3,11},{8,16},{9,17},{10,18},{11,19},{16,24},{1... | collective-permute-start | bytes 5111816 | tf_op jit(solution)/shard_map/ppermute | solution.py:69
  184.1 32.9 %collective-permute-start.47 = (bf16[256,4608]{1,0:T(8,128)(2,1)S(1)}, bf16[256,4608]{1,0:T(8,128)(2,1)S(1)}, u32[]{:S(2)}, u32[]{:S(2)}) collective-permute-start(bf16[256,4608]{1,0:T(8,128)(2,1)S(1)} %copy-done.9), channel_id=1, source_target_pairs={{0,24},{1,25},{2,26},{3,27},{8,0},{9,1},{10,2},{11,3},{16,8},{17,9... | collective-permute-start | bytes 7077896 | tf_op jit(solution)/shard_map/ppermute | solution.py:69
  184.1 34.4 %collective-permute-start.46 = (bf16[256,4608]{1,0:T(8,128)(2,1)S(1)}, bf16[256,4608]{1,0:T(8,128)(2,1)}, u32[]{:S(2)}, u32[]{:S(2)}) collective-permute-start(bf16[256,4608]{1,0:T(8,128)(2,1)S(1)} %copy-done.9), channel_id=1, source_target_pairs={{0,8},{1,9},{2,10},{3,11},{8,16},{9,17},{10,18},{11,19},{16,24},{1... | collective-permute-start | bytes 7077896 | tf_op jit(solution)/shard_map/ppermute | solution.py:69
  217.1 19.1 %collective-permute-start.49 = (bf16[256,2304]{1,0:T(8,128)(2,1)S(1)}, bf16[256,2304]{1,0:T(8,128)(2,1)S(1)}, u32[]{:S(2)}, u32[]{:S(2)}) collective-permute-start(bf16[256,2304]{1,0:T(8,128)(2,1)S(1)} %slice.315), channel_id=1, source_target_pairs={{0,24},{1,25},{2,26},{3,27},{8,0},{9,1},{10,2},{11,3},{16,8},{17,9... | collective-permute-start | bytes 3538952 | tf_op jit(solution)/shard_map/ppermute | solution.py:69
  219.8 16.7 %collective-permute-start.48 = (bf16[256,2304]{1,0:T(8,128)(2,1)S(1)}, bf16[256,2304]{1,0:T(8,128)(2,1)}, u32[]{:S(2)}, u32[]{:S(2)}) collective-permute-start(bf16[256,2304]{1,0:T(8,128)(2,1)S(1)} %slice.314), channel_id=1, source_target_pairs={{0,8},{1,9},{2,10},{3,11},{8,16},{9,17},{10,18},{11,19},{16,24},{1... | collective-permute-start | bytes 3538952 | tf_op jit(solution)/shard_map/ppermute | solution.py:69
  270.5 16.8 %collective-permute-start.59 = (bf16[256,2304]{1,0:T(8,128)(2,1)}, bf16[256,2304]{1,0:T(8,128)(2,1)S(1)}, u32[]{:S(2)}, u32[]{:S(2)}) collective-permute-start(bf16[256,2304]{1,0:T(8,128)(2,1)} %get-tuple-element.182), channel_id=1, source_target_pairs={{0,8},{1,9},{2,10},{3,11},{8,16},{9,17},{10,18},{11,19},{16,24},{1... | collective-permute-start | bytes 3538952 | tf_op jit(solution)/shard_map/ppermute | solution.py:69
  270.6 22.9 %collective-permute-start.50 = (bf16[256,1024]{1,0:T(8,128)(2,1)S(1)}, bf16[256,1024]{1,0:T(8,128)(2,1)S(1)}, u32[]{:S(2)}, u32[]{:S(2)}) collective-permute-start(bf16[256,1024]{1,0:T(8,128)(2,1)S(1)} %copy-done.31), channel_id=1, source_target_pairs={{0,32},{32,0},{1,33},{33,1},{2,34},{34,2},{3,35},{35,3},{4,36},{36... | collective-permute-start | bytes 1572872 | tf_op jit(solution)/shard_map/ppermute | solution.py:168
  271.1 22.7 %collective-permute-start.55 = (bf16[256,1024]{1,0:T(8,128)(2,1)}, bf16[256,1024]{1,0:T(8,128)(2,1)}, u32[]{:S(2)}, u32[]{:S(2)}) collective-permute-start(bf16[256,1024]{1,0:T(8,128)(2,1)} %get-tuple-element.174.refs_1_), channel_id=1, source_target_pairs={{0,32},{32,0},{1,33},{33,1},{2,34},{34,2},{3,35},{35,3},{4,36},{36... | collective-permute-start | bytes 1572872 | tf_op jit(solution)/shard_map/ppermute | solution.py:168
  272.8 16.1 %collective-permute-start.60 = (bf16[256,2304]{1,0:T(8,128)(2,1)}, bf16[256,2304]{1,0:T(8,128)(2,1)S(1)}, u32[]{:S(2)}, u32[]{:S(2)}) collective-permute-start(bf16[256,2304]{1,0:T(8,128)(2,1)} %get-tuple-element.183), channel_id=1, source_target_pairs={{0,24},{1,25},{2,26},{3,27},{8,0},{9,1},{10,2},{11,3},{16,8},{17,9... | collective-permute-start | bytes 3538952 | tf_op jit(solution)/shard_map/ppermute | solution.py:69
  290.4 28.9 %collective-permute-start.66 = (bf16[256,4608]{1,0:T(8,128)(2,1)S(1)}, bf16[256,4608]{1,0:T(8,128)(2,1)}, u32[]{:S(2)}, u32[]{:S(2)}) collective-permute-start(bf16[256,4608]{1,0:T(8,128)(2,1)S(1)} %pad_maximum_fusion.3), channel_id=1, source_target_pairs={{0,24},{1,25},{2,26},{3,27},{8,0},{9,1},{10,2},{11,3},{16,8},{17,9... | collective-permute-start | bytes 7077896 | tf_op jit(solution)/shard_map/ppermute | solution.py:69
  293.5 29.3 %collective-permute-start.65 = (bf16[256,4608]{1,0:T(8,128)(2,1)S(1)}, bf16[256,4608]{1,0:T(8,128)(2,1)}, u32[]{:S(2)}, u32[]{:S(2)}) collective-permute-start(bf16[256,4608]{1,0:T(8,128)(2,1)S(1)} %pad_maximum_fusion.2), channel_id=1, source_target_pairs={{0,8},{1,9},{2,10},{3,11},{8,16},{9,17},{10,18},{11,19},{16,24},{1... | collective-permute-start | bytes 7077896 | tf_op jit(solution)/shard_map/ppermute | solution.py:69
  312.8 14.9 %collective-permute-start.61 = (bf16[64,1536]{1,0:T(8,128)(2,1)}, bf16[64,1536]{1,0:T(8,128)(2,1)S(1)}, u32[]{:S(2)}, u32[]{:S(2)}) collective-permute-start(bf16[64,1536]{1,0:T(8,128)(2,1)} %get-tuple-element.186), channel_id=1, source_target_pairs={{0,4},{4,0},{64,68},{68,64},{1,5},{5,1},{65,69},{69,65},{2,6},{6,2... | collective-permute-start | bytes 589832 | tf_op jit(solution)/shard_map/ppermute | solution.py:178
  340.9 25.3 %collective-permute-start.71 = (bf16[64,4608]{1,0:T(8,128)(2,1)S(1)}, bf16[64,4608]{1,0:T(8,128)(2,1)S(1)}, u32[]{:S(2)}, u32[]{:S(2)}) collective-permute-start(bf16[64,4608]{1,0:T(8,128)(2,1)S(1)} %pad_maximum_fusion.9), channel_id=1, source_target_pairs={{0,3},{1,0},{2,1},{3,2},{8,11},{9,8},{10,9},{11,10},{16,19},{17,16... | collective-permute-start | bytes 1769480 | tf_op jit(solution)/shard_map/ppermute | solution.py:69
  341.0 25.3 %collective-permute-start.70 = (bf16[64,4608]{1,0:T(8,128)(2,1)S(1)}, bf16[64,4608]{1,0:T(8,128)(2,1)S(1)}, u32[]{:S(2)}, u32[]{:S(2)}) collective-permute-start(bf16[64,4608]{1,0:T(8,128)(2,1)S(1)} %pad_maximum_fusion.8), channel_id=1, source_target_pairs={{0,1},{1,2},{2,3},{3,0},{8,9},{9,10},{10,11},{11,8},{16,17},{17,18... | collective-permute-start | bytes 1769480 | tf_op jit(solution)/shard_map/ppermute | solution.py:69
  363.1 23.1 %collective-permute-start.75 = (bf16[256,3328]{1,0:T(8,128)(2,1)}, bf16[256,3328]{1,0:T(8,128)(2,1)}, u32[]{:S(2)}, u32[]{:S(2)}) collective-permute-start(bf16[256,3328]{1,0:T(8,128)(2,1)} %get-tuple-element.210), channel_id=1, source_target_pairs={{0,8},{1,9},{2,10},{3,11},{8,16},{9,17},{10,18},{11,19},{16,24},{1... | collective-permute-start | bytes 5111816 | tf_op jit(solution)/shard_map/ppermute | solution.py:69
  363.1 23.1 %collective-permute-start.76 = (bf16[256,3328]{1,0:T(8,128)(2,1)}, bf16[256,3328]{1,0:T(8,128)(2,1)}, u32[]{:S(2)}, u32[]{:S(2)}) collective-permute-start(bf16[256,3328]{1,0:T(8,128)(2,1)} %get-tuple-element.211), channel_id=1, source_target_pairs={{0,24},{1,25},{2,26},{3,27},{8,0},{9,1},{10,2},{11,3},{16,8},{17,9... | collective-permute-start | bytes 5111816 | tf_op jit(solution)/shard_map/ppermute | solution.py:69
  383.0 34.5 %collective-permute-start.103 = (bf16[32,3072]{1,0:T(8,128)(2,1)S(1)}, bf16[32,3072]{1,0:T(8,128)(2,1)S(1)}, u32[]{:S(2)}, u32[]{:S(2)}) collective-permute-start(bf16[32,3072]{1,0:T(8,128)(2,1)S(1)} %copy-done.47), channel_id=1, source_target_pairs={{0,4},{4,36},{32,0},{36,32},{1,5},{5,37},{33,1},{37,33},{2,6},{6,3... | collective-permute-start | bytes 589832 | tf_op jit(solution)/shard_map/ppermute | solution.py:164
  384.3 33.2 %collective-permute-start.102 = (bf16[32,6144]{1,0:T(8,128)(2,1)}, bf16[32,6144]{1,0:T(8,128)(2,1)S(1)}, u32[]{:S(2)}, u32[]{:S(2)}) collective-permute-start(bf16[32,6144]{1,0:T(8,128)(2,1)} %shard_map.164), channel_id=1, source_target_pairs={{0,0},{4,32},{32,4},{36,36},{1,1},{5,33},{33,5},{37,37},{2,2},{6,3... | collective-permute-start | bytes 1179656 | tf_op jit(solution)/shard_map/ppermute | solution.py:164
  400.8 50.7 %collective-permute-start.82 = (bf16[256,6656]{1,0:T(8,128)(2,1)S(1)}, bf16[256,6656]{1,0:T(8,128)(2,1)S(1)}, u32[]{:S(2)}, u32[]{:S(2)}) collective-permute-start(bf16[256,6656]{1,0:T(8,128)(2,1)S(1)} %pad_maximum_fusion.1), channel_id=1, source_target_pairs={{0,24},{1,25},{2,26},{3,27},{8,0},{9,1},{10,2},{11,3},{16,8},{17,9... | collective-permute-start | bytes 10223624 | tf_op jit(solution)/shard_map/ppermute | solution.py:69
  403.9 47.7 %collective-permute-start.81 = (bf16[256,6656]{1,0:T(8,128)(2,1)}, bf16[256,6656]{1,0:T(8,128)(2,1)}, u32[]{:S(2)}, u32[]{:S(2)}) collective-permute-start(bf16[256,6656]{1,0:T(8,128)(2,1)} %pad_maximum_fusion), channel_id=1, source_target_pairs={{0,8},{1,9},{2,10},{3,11},{8,16},{9,17},{10,18},{11,19},{16,24},{1... | collective-permute-start | bytes 10223624 | tf_op jit(solution)/shard_map/ppermute | solution.py:69
  416.6 33.6 %collective-permute-start.84 = (bf16[256,1024]{1,0:T(8,128)(2,1)}, bf16[256,1024]{1,0:T(8,128)(2,1)S(1)}, u32[]{:S(2)}, u32[]{:S(2)}) collective-permute-start(bf16[256,1024]{1,0:T(8,128)(2,1)} %get-tuple-element.227), channel_id=1, source_target_pairs={{0,8},{1,9},{2,10},{3,11},{8,16},{9,17},{10,18},{11,19},{16,24},{1... | collective-permute-start | bytes 1572872 | tf_op jit(solution)/shard_map/ppermute | solution.py:69
  426.1 32.3 %collective-permute-start.80 = (bf16[256,1024]{1,0:T(8,128)(2,1)S(1)}, bf16[256,1024]{1,0:T(8,128)(2,1)S(1)}, u32[]{:S(2)}, u32[]{:S(2)}) collective-permute-start(bf16[256,1024]{1,0:T(8,128)(2,1)S(1)} %copy-done.57), channel_id=1, source_target_pairs={{0,32},{32,0},{1,33},{33,1},{2,34},{34,2},{3,35},{35,3},{4,36},{36... | collective-permute-start | bytes 1572872 | tf_op jit(solution)/shard_map/ppermute | solution.py:168
  426.9 24.5 %collective-permute-start.86 = (bf16[256,1152]{1,0:T(8,128)(2,1)S(1)}, bf16[256,1152]{1,0:T(8,128)(2,1)S(1)}, u32[]{:S(2)}, u32[]{:S(2)}) collective-permute-start(bf16[256,1152]{1,0:T(8,128)(2,1)S(1)} %copy-done.56), channel_id=1, source_target_pairs={{0,24},{1,25},{2,26},{3,27},{8,0},{9,1},{10,2},{11,3},{16,8},{17,9... | collective-permute-start | bytes 1769480 | tf_op jit(solution)/shard_map/ppermute | solution.py:69
  457.0 16.9 %collective-permute-start.96 = (bf16[64,3328]{1,0:T(8,128)(2,1)}, bf16[64,3328]{1,0:T(8,128)(2,1)}, u32[]{:S(2)}, u32[]{:S(2)}) collective-permute-start(bf16[64,3328]{1,0:T(8,128)(2,1)} %get-tuple-element.255), channel_id=1, source_target_pairs={{0,3},{1,0},{2,1},{3,2},{8,11},{9,8},{10,9},{11,10},{16,19},{17,16... | collective-permute-start | bytes 1277960 | tf_op jit(solution)/shard_map/ppermute | solution.py:69
  457.0 16.9 %collective-permute-start.94 = (bf16[64,3328]{1,0:T(8,128)(2,1)}, bf16[64,3328]{1,0:T(8,128)(2,1)}, u32[]{:S(2)}, u32[]{:S(2)}) collective-permute-start(bf16[64,3328]{1,0:T(8,128)(2,1)} %get-tuple-element.254), channel_id=1, source_target_pairs={{0,1},{1,2},{2,3},{3,0},{8,9},{9,10},{10,11},{11,8},{16,17},{17,18... | collective-permute-start | bytes 1277960 | tf_op jit(solution)/shard_map/ppermute | solution.py:69
  469.7 20.1 %collective-permute-start.85 = (bf16[256,2176]{1,0:T(8,128)(2,1)S(1)}, bf16[256,2176]{1,0:T(8,128)(2,1)S(1)}, u32[]{:S(2)}, u32[]{:S(2)}) collective-permute-start(bf16[256,2176]{1,0:T(8,128)(2,1)S(1)} %copy-done.20), channel_id=1, source_target_pairs={{0,8},{1,9},{2,10},{3,11},{8,16},{9,17},{10,18},{11,19},{16,24},{1... | collective-permute-start | bytes 3342344 | tf_op jit(solution)/shard_map/ppermute | solution.py:69
  469.8 22.4 %collective-permute-start.87 = (bf16[256,2176]{1,0:T(8,128)(2,1)S(1)}, bf16[256,2176]{1,0:T(8,128)(2,1)S(1)}, u32[]{:S(2)}, u32[]{:S(2)}) collective-permute-start(bf16[256,2176]{1,0:T(8,128)(2,1)S(1)} %pad_maximum_fusion.5), channel_id=1, source_target_pairs={{0,24},{1,25},{2,26},{3,27},{8,0},{9,1},{10,2},{11,3},{16,8},{17,9... | collective-permute-start | bytes 3342344 | tf_op jit(solution)/shard_map/ppermute | solution.py:69
  475.8 22.2 %collective-permute-start.97 = (bf16[64,6656]{1,0:T(8,128)(2,1)S(1)}, bf16[64,6656]{1,0:T(8,128)(2,1)S(1)}, u32[]{:S(2)}, u32[]{:S(2)}) collective-permute-start(bf16[64,6656]{1,0:T(8,128)(2,1)S(1)} %pad_maximum_fusion.7), channel_id=1, source_target_pairs={{0,3},{1,0},{2,1},{3,2},{8,11},{9,8},{10,9},{11,10},{16,19},{17,16... | collective-permute-start | bytes 2555912 | tf_op jit(solution)/shard_map/ppermute | solution.py:69
  475.9 22.1 %collective-permute-start.95 = (bf16[64,6656]{1,0:T(8,128)(2,1)S(1)}, bf16[64,6656]{1,0:T(8,128)(2,1)S(1)}, u32[]{:S(2)}, u32[]{:S(2)}) collective-permute-start(bf16[64,6656]{1,0:T(8,128)(2,1)S(1)} %pad_maximum_fusion.6), channel_id=1, source_target_pairs={{0,1},{1,2},{2,3},{3,0},{8,9},{9,10},{10,11},{11,8},{16,17},{17,18... | collective-permute-start | bytes 2555912 | tf_op jit(solution)/shard_map/ppermute | solution.py:69
  497.8 25.2 %collective-permute-start.89 = (bf16[64,2176]{1,0:T(8,128)(2,1)S(1)}, bf16[64,2176]{1,0:T(8,128)(2,1)S(1)}, u32[]{:S(2)}, u32[]{:S(2)}) collective-permute-start(bf16[64,2176]{1,0:T(8,128)(2,1)S(1)} %pad_maximum_fusion.11), channel_id=1, source_target_pairs={{0,1},{1,2},{2,3},{3,0},{8,9},{9,10},{10,11},{11,8},{16,17},{17,18... | collective-permute-start | bytes 835592 | tf_op jit(solution)/shard_map/ppermute | solution.py:69
  503.5 15.0 %collective-permute-start.101 = (bf16[32,1536]{1,0:T(8,128)(2,1)}, bf16[32,1536]{1,0:T(8,128)(2,1)S(1)}, u32[]{:S(2)}, u32[]{:S(2)}) collective-permute-start(bf16[32,1536]{1,0:T(8,128)(2,1)} %shard_map.162), channel_id=1, source_target_pairs={{0,4},{4,36},{32,0},{36,32},{1,5},{5,37},{33,1},{37,33},{2,6},{6,3... | collective-permute-start | bytes 294920 | tf_op jit(solution)/shard_map/ppermute | solution.py:164
  516.1 15.0 %collective-permute-start.99 = (bf16[32,3072]{1,0:T(8,128)(2,1)S(1)}, bf16[32,3072]{1,0:T(8,128)(2,1)S(1)}, u32[]{:S(2)}, u32[]{:S(2)}) collective-permute-start(bf16[32,3072]{1,0:T(8,128)(2,1)S(1)} %copy-done.45), channel_id=1, source_target_pairs={{0,4},{4,36},{32,0},{36,32},{1,5},{5,37},{33,1},{37,33},{2,6},{6,3... | collective-permute-start | bytes 589832 | tf_op jit(solution)/shard_map/ppermute | solution.py:164
  (157 other events, 914.2 us)

commit v3 on v2

--- a/solution.py
+++ b/solution.py
@@ -101,7 +101,7 @@
         blocks = [(self.piece, whole, 0, 0), (self.left, whole, rows, 0)]
         blocks += [(self.right, whole, 2 * rows, 0)]
         blocks += [(done[0], part, 3 * rows, 0), (done[1], part, 3 * rows, half)]
-        self.piece = place_blocks(blocks, (4 * rows, width))
+        self.piece = place_blocks((blocks, (4 * rows, width)))[0]
         return done
 
     def three(self, *deps):
@@ -118,40 +118,62 @@
 class Scatter:
     def __init__(self, own, left, right, far_a, far_b):
         self.parts = own, left, right, far_a, far_b
-        self.parts_half = far_a.shape[1]
-
-    def far(self, axis_of_core, *deps):
-        own, left, right, far_a, far_b = self.parts
-        half = far_a.shape[1]
+        self.half = far_a.shape[1]
+
+    def far(self, axis_of_core, deps):
+        far_a, far_b = self.parts[3:]
         far_a = shift(after(far_a, *deps), axis_of_core, 1)
         far_b = shift(after(far_b, *deps), axis_of_core, -1)
+        self.got = far_a, far_b
+        return self.got
+
+    def far_sums(self, deps):
+        own, left, right = self.parts[:3]
+        far_a, far_b = after(self.got, *deps)
+        half = self.half
         right = jnp.concatenate([plus(right[:, :half], far_a).astype(BF), right[:, half:]], axis=1)
         left = jnp.concatenate([left[:, :half], plus(left[:, half:], far_b).astype(BF)], axis=1)
         self.parts = own, left, right
-        return far_a, far_b
-
-    def near(self, axis_of_core, *deps):
+        return left, right
+
+    def near(self, axis_of_core, deps):
         own, left, right = self.parts
         from_left = shift(after(right, *deps), axis_of_core, 1)
         from_right = shift(after(left, *deps), axis_of_core, -1)
-        self.block = (plus(own, from_left) + from_right.astype(F32)).astype(BF)
-        return (self.block,)
+        self.got = from_left, from_right
+        return self.got
+
+    def near_sums(self, deps):
+        from_left, from_right = after(self.got, *deps)
+        self.block = (plus(self.parts[0], from_left) + from_right.astype(F32)).astype(BF)
+        return self.block
 
     def one(self, *deps):
-        return self.far(SECOND, *deps)
+        return self.far(SECOND, deps)
+
+    def one_sums(self, *deps):
+        return self.far_sums(deps)
 
     def two(self, *deps):
-        done = self.near(SECOND, *deps)
-        own, left, right, far = [self.block[k * 64 : (k + 1) * 64] for k in range(4)]
-        half = self.parts_half
-        self.parts = own, left, right, far[:, :half], far[:, half:]
-        return done
+        return self.near(SECOND, deps)
+
+    def two_sums(self, *deps):
+        block = self.near_sums(deps)
+        own, left, right, far = [block[k * 64 : (k + 1) * 64] for k in range(4)]
+        self.parts = own, left, right, far[:, : self.half], far[:, self.half :]
+        return block
 
     def three(self, *deps):
-        return self.far(FIRST, *deps)
+        return self.far(FIRST, deps)
+
+    def three_sums(self, *deps):
+        return self.far_sums(deps)
 
     def four(self, *deps):
-        return self.near(FIRST, *deps)
+        return self.near(FIRST, deps)
+
+    def four_sums(self, *deps):
+        return self.near_sums(deps)
 
 
 def to_chip(value, place):
@@ -215,11 +237,16 @@
     out_ref[row_block(step), :] = (state * rsqrt_mean(state) * gain_ref[...]).astype(BF)
 
 
-def move_rows(a_s, mv_ref, mvt_ref, moved_s, moved_t_ref):
+def move_rows(a_s, mv_ref, moved_s):
     for j in range(D // TILE):
         cols = slice(j * TILE, (j + 1) * TILE)
         moved_s[:, cols] = dot(a_s[...], mv_ref[:, cols]).astype(BF)
-        moved_t_ref[cols, :] = dot_nt(mvt_ref[cols, :], a_s[...]).astype(BF)
+
+
+def turn_rows(a_ref, mvt_ref, turned_s):
+    for j in range(D // TILE):
+        cols = slice(j * TILE, (j + 1) * TILE)
+        turned_s[cols, :] = dot_nt(mvt_ref[cols, :], a_ref[...]).astype(BF)
 
 
 def dot_pieces(left_s, pieces, cols):
@@ -232,12 +259,12 @@
 
 def qkv_kernel(first, meta, ready, *refs):
     if first:
-        x_ref, gain_ref, mv_ref, mvt_ref, *refs = refs
+        x_ref, gain_ref, mv_ref, *refs = refs
     else:
-        x_ref, own_ref, other_ref, gain_ref, mv_ref, mvt_ref, *refs = refs
+        x_ref, own_ref, other_ref, gain_ref, mv_ref, *refs = refs
     pieces, refs = refs[:4], refs[4:]
-    h_ref, art_ref, *refs = refs
-    outs, (a_s, ar_s, qkv_s) = refs[:4], refs[4:]
+    h_ref, a_ref, *refs = refs
+    outs, (ar_s, qkv_s) = refs[:4], refs[4:]
 
     @pl.loop(0, TOKENS // 32)
     def _(step):
@@ -246,9 +273,9 @@
             state = state + own_ref[row_block(step), :].astype(F32)
             state = state + other_ref[row_block(step), :].astype(F32)
         h_ref[row_block(step), :] = state
-        norm_rows(step, state, gain_ref, a_s)
-
-    move_rows(a_s, mv_ref, mvt_ref, ar_s, art_ref)
+        norm_rows(step, state, gain_ref, a_ref)
+
+    move_rows(a_ref, mv_ref, ar_s)
     ready()
 
     @pl.loop(0, QKV // TILE)
@@ -379,35 +406,41 @@
 
 def out_kernel(meta, ready, *refs):
     blocks, pieces, refs = refs[:4], refs[4:8], refs[8:]
-    ort_ref, wo_ref, partial_ref, o_s, ot_s = refs
+    o_ref, partial_ref, wo_s = refs
     for k in range(POS):
-        o_s[chip_rows(meta, k), :] = blocks[k][...]
-    transpose_into(o_s, ot_s)
+        o_ref[chip_rows(meta, k), :] = blocks[k][...]
     ready()
-    unpack_rows(meta, pieces, wo_ref, 0)
-    for k in range(16):
-        ort_ref[k * 32 : (k + 1) * 32, :] = ot_s[pl.ds(pl.multiple_of(meta[k] * 32, 32), 32), :]
+    unpack_rows(meta, pieces, wo_s, 0)
     for j in range(D // TILE):
         cols = slice(j * TILE, (j + 1) * TILE)
-        partial_ref[:, cols] = dot(o_s[...], wo_ref[:, cols]).astype(BF)
+        partial_ref[:, cols] = dot(o_ref[...], wo_s[:, cols]).astype(BF)
+
+
+def unpack_down(meta, pieces, wd_s):
+    for k in range(16):
+        rows = pl.ds(pl.multiple_of(meta[k] * 64, 64), 64)
+        wd_s[rows, :] = pieces[k // 4][
+            (k % 4) * 64 : (k % 4 + 1) * 64, GATE_UP : GATE_UP + D
+        ]
+    unpack_rows(meta, [piece.at[:, pl.ds(GATE_UP + D, HALF)] for piece in pieces], wd_s, D)
 
 
 def ffn_kernel(counting, meta, ready, *refs):
-    h_ref, own_ref, other_ref, gain_ref, mv_ref, mvt_ref, *refs = refs
+    h_ref, own_ref, other_ref, gain_ref, mv_ref, *refs = refs
     pieces, refs = refs[:4], refs[4:]
-    m_ref, brt_ref, gate_ref, up_ref, actrt_ref, wd_ref, partial_ref, *refs = refs
+    m_ref, b_ref, gate_ref, up_ref, act_ref, partial_ref, *refs = refs
     if counting:
         total_ref, *refs = refs
-    b_s, br_s, act_s, actt_s = refs
+    br_s, wd_s = refs
 
     @pl.loop(0, TOKENS // 32)
     def _(step):
         state = h_ref[row_block(step), :] + own_ref[row_block(step), :].astype(F32)
         state = state + other_ref[row_block(step), :].astype(F32)
         m_ref[row_block(step), :] = state
-        norm_rows(step, state, gain_ref, b_s)
-
-    move_rows(b_s, mv_ref, mvt_ref, br_s, brt_ref)
+        norm_rows(step, state, gain_ref, b_ref)
+
+    move_rows(b_ref, mv_ref, br_s)
     ready()
 
     @pl.loop(0, UNITS // TILE)
@@ -417,31 +450,20 @@
         gate_ref[:, cols] = gate
         up = dot_pieces(br_s, pieces, lane_tile(step + UNITS // TILE))
         up_ref[:, cols] = up
-        act_s[:, cols] = (gate * jax.nn.sigmoid(gate) * up).astype(BF)
-
-    for k in range(16):
-        rows = pl.ds(pl.multiple_of(meta[k] * 64, 64), 64)
-        wd_ref[rows, :] = pieces[k // 4][
-            (k % 4) * 64 : (k % 4 + 1) * 64, GATE_UP : GATE_UP + D
-        ]
-    unpack_rows(meta, [piece.at[:, pl.ds(GATE_UP + D, HALF)] for piece in pieces], wd_ref, D)
+        act_ref[:, cols] = (gate * jax.nn.sigmoid(gate) * up).astype(BF)
+
+    unpack_down(meta, pieces, wd_s)
     if counting:
         total = jnp.zeros((1, LANES), F32)
         for k in range(16):
             rows = slice(D + k * 32, D + (k + 1) * 32)
-            total = total + wd_ref[rows, :LANES].astype(F32)[24:25]
+            total = total + wd_s[rows, :LANES].astype(F32)[24:25]
         total_ref[...] = total
-    transpose_into(act_s, actt_s)
-    for k in range(16):
-        rows = pl.ds(pl.multiple_of(meta[k] * 64, 64), 64)
-        actrt_ref[k * 64 : (k + 1) * 64, :] = actt_s[rows, :]
-        rows = pl.ds(pl.multiple_of(D + meta[k] * 32, 32), 32)
-        actrt_ref[D + k * 32 : D + (k + 1) * 32, :] = actt_s[rows, :]
 
     @pl.loop(0, D // TILE)
     def _(step):
         cols = lane_tile(step)
-        partial_ref[:, cols] = dot(act_s[...], wd_ref[:, cols]).astype(BF)
+        partial_ref[:, cols] = dot(act_ref[...], wd_s[:, cols]).astype(BF)
 
 
 def norm_backward(base_ref, own_ref, other_ref, state_ref, gain_ref, put):
@@ -488,19 +510,16 @@
         cot_ref, marks_ref, totals_ref, other_totals_ref, *refs = refs
     else:
         base_ref, own_ref, other_ref, state_ref, gain_ref, *refs = refs
-    actrt_ref, brt_ref, gate_ref, up_ref, wd_ref, mv_ref, *refs = refs
-    held = 4 if last else 8
-    pieces, refs = refs[:held], refs[held:]
-    g_ref, *refs = refs
+    gate_ref, up_ref, mv_ref, *refs = refs
+    pieces, refs = refs[:4], refs[4:]
+    g_ref, gf_ref, dgu_ref, partial_ref, *refs = refs
     if not last:
         dgain_ref, *refs = refs
-    partial_ref, *refs = refs
-    outs, (gf_s, dgu_s, dbr_s) = refs[:-3], refs[-3:]
-    pieces, above = pieces[:4], pieces[4:]
+    dbr_s, wd_s = refs
 
     def put(rows, value):
         g_ref[rows, :] = value
-        gf_s[rows, :] = value.astype(BF)
+        gf_ref[rows, :] = value.astype(BF)
 
     if last:
 
@@ -516,84 +535,103 @@
 
     else:
         dgain_ref[...] = norm_backward(base_ref, own_ref, other_ref, state_ref, gain_ref, put)
+    ready()
+    unpack_down(meta, pieces, wd_s)
 
     @pl.loop(0, UNITS // TILE)
     def _(step):
         cols = lane_tile(step)
-        grad_act = dot_nt(gf_s[...], wd_ref[cols, :])
+        grad_act = dot_nt(gf_ref[...], wd_s[cols, :])
         gate = gate_ref[:, cols]
         sigma = jax.nn.sigmoid(gate)
         grad_up = grad_act * gate * sigma
         grad_gate = grad_act * up_ref[:, cols] * sigma * (1.0 + gate * (1.0 - sigma))
-        dgu_s[:, cols] = grad_gate.astype(BF)
-        dgu_s[:, lane_tile(step + UNITS // TILE)] = grad_up.astype(BF)
-
+        dgu_ref[:, cols] = grad_gate.astype(BF)
+        dgu_ref[:, lane_tile(step + UNITS // TILE)] = grad_up.astype(BF)
+
+    for k in range(4):
+        value = dot_nt(dgu_ref[...], pieces[k][:, :GATE_UP])
+        dbr_s[:, k * TILE : (k + 1) * TILE] = value.astype(BF)
+    for j in range(D // TILE):
+        cols = slice(j * TILE, (j + 1) * TILE)
+        partial_ref[:, cols] = dot_nt(dbr_s[...], mv_ref[cols, :]).astype(BF)
+
+
+def ffn_gradient_kernel(last, meta, ready, *refs):
+    b_ref, act_ref, gf_ref, dgu_ref, mvt_ref, *refs = refs
+    above, refs = ([], refs) if last else (refs[:4], refs[4:])
+    outs, (brt_s, actt_s, actrt_s) = refs[:5], refs[5:]
+    turn_rows(b_ref, mvt_ref, brt_s)
+    transpose_into(act_ref, actt_s)
+    for k in range(16):
+        rows = pl.ds(pl.multiple_of(meta[k] * 64, 64), 64)
+        actrt_s[k * 64 : (k + 1) * 64, :] = actt_s[rows, :]
+        rows = pl.ds(pl.multiple_of(D + meta[k] * 32, 32), 32)
+        actrt_s[D + k * 32 : D + (k + 1) * 32, :] = actt_s[rows, :]
     everything = slice(0, TILE)
     for k in (3, 1, 2, 0):
         rows = slice(k * TILE, (k + 1) * TILE)
         for j in range(GATE_UP // TILE):
-            value = dot(brt_ref[rows, :], dgu_s[:, j * TILE : (j + 1) * TILE]).astype(BF)
+            value = dot(brt_s[rows, :], dgu_ref[:, j * TILE : (j + 1) * TILE]).astype(BF)
             put_piece(outs, k, everything, j * TILE, value)
         for j in range(D // TILE):
-            value = dot(actrt_ref[rows, :], gf_s[:, j * TILE : (j + 1) * TILE]).astype(BF)
+            value = dot(actrt_s[rows, :], gf_ref[:, j * TILE : (j + 1) * TILE]).astype(BF)
             put_piece(outs, k, everything, GATE_UP + j * TILE, value)
         tail = slice(D + k * 128, D + (k + 1) * 128)
         for j in range(D // TILE):
-            value = dot(actrt_ref[tail, :], gf_s[:, j * TILE : (j + 1) * TILE]).astype(BF)
+            value = dot(actrt_s[tail, :], gf_ref[:, j * TILE : (j + 1) * TILE]).astype(BF)
             put_packed(outs, k, GATE_UP + D, j, value)
     ready()
     for k, sums in enumerate(above):
         for j in range(ATTN // TILE):
             put_piece(outs, k, everything, FFN + j * TILE, sums[:, j * TILE : (j + 1) * TILE])
-    for k in range(4):
-        dbr_s[:, k * TILE : (k + 1) * TILE] = dot_nt(dgu_s[...], pieces[k][...]).astype(BF)
-    for j in range(D // TILE):
-        cols = slice(j * TILE, (j + 1) * TILE)
-        partial_ref[:, cols] = dot_nt(dbr_s[...], mv_ref[cols, :]).astype(BF)
 
 
 def out_backward_kernel(meta, ready, *refs):
-    base_ref, own_ref, other_ref, state_ref, gain_ref, ort_ref, wo_ref, *refs = refs
-    gm_ref, dgain_ref, dwo_ref, *refs = refs
-    outs, (ga_s, do_s) = refs[:4], refs[4:]
+    base_ref, own_ref, other_ref, state_ref, gain_ref, *refs = refs
+    pieces, refs = refs[:4], refs[4:]
+    gm_ref, dgain_ref, ga_ref, *refs = refs
+    outs, (do_s, wo_s) = refs[:4], refs[4:]
 
     def put(rows, value):
         gm_ref[rows, :] = value
-        ga_s[rows, :] = value.astype(BF)
+        ga_ref[rows, :] = value.astype(BF)
 
     dgain_ref[...] = norm_backward(base_ref, own_ref, other_ref, state_ref, gain_ref, put)
+    ready()
+    unpack_rows(meta, pieces, wo_s, 0)
     for j in range(HALF // TILE):
         cols = slice(j * TILE, (j + 1) * TILE)
-        do_s[:, cols] = dot_nt(ga_s[...], wo_ref[cols, :]).astype(BF)
+        do_s[:, cols] = dot_nt(ga_ref[...], wo_s[cols, :]).astype(BF)
     for k in range(POS):
         outs[k][...] = do_s[chip_rows(meta, k), :]
-    for k in range(4):
-        for j in range(D // TILE):
-            cols = slice(j * TILE, (j + 1) * TILE)
-            value = dot(ort_ref[k * 128 : (k + 1) * 128, :], ga_s[:, cols]).astype(BF)
-            for i in range(4):
-                row = k * TILE + i * 64 + (j // 2) * 32
-                part = slice((j % 2) * TILE, (j % 2 + 1) * TILE)
-                dwo_ref[row : row + 32, part] = value[i * 32 : (i + 1) * 32]
-
-
-def qkv_backward_kernel(first, meta, ready, *refs):
+
+
+def qkv_backward_kernel(meta, ready, *refs):
     blocks, refs = refs[:4], refs[4:]
-    art_ref, dwo_ref, mv_ref, *refs = refs
-    if first:
-        mvt_ref, state_ref, *gain_refs = refs[:5]
-        refs = refs[5:]
+    mv_ref, *refs = refs
     pieces, refs = refs[:4], refs[4:]
-    partial_ref, *refs = refs
-    outs, (dqkv_s, dar_s) = refs[:-2], refs[-2:]
+    partial_ref, dqkv_ref, dar_s = refs
     for k in range(POS):
-        dqkv_s[chip_rows(meta, k), :] = blocks[k][...]
+        dqkv_ref[chip_rows(meta, k), :] = blocks[k][...]
     ready()
     for k in range(4):
-        dar_s[:, k * TILE : (k + 1) * TILE] = dot_nt(dqkv_s[...], pieces[k][...]).astype(BF)
+        dar_s[:, k * TILE : (k + 1) * TILE] = dot_nt(dqkv_ref[...], pieces[k][...]).astype(BF)
     for j in range(D // TILE):
         cols = slice(j * TILE, (j + 1) * TILE)
         partial_ref[:, cols] = dot_nt(dar_s[...], mv_ref[cols, :]).astype(BF)
+
+
+def attn_gradient_kernel(first, meta, ready, *refs):
+    a_ref, dqkv_ref, o_ref, ga_ref, mvt_ref, *refs = refs
+    if first:
+        partial_ref, state_ref, *gain_refs = refs[:5]
+        refs = refs[5:]
+    outs, (art_s, ot_s, ort_s) = refs[:-3], refs[-3:]
+    turn_rows(a_ref, mvt_ref, art_s)
+    transpose_into(o_ref, ot_s)
+    for k in range(16):
+        ort_s[k * 32 : (k + 1) * 32, :] = ot_s[pl.ds(pl.multiple_of(meta[k] * 32, 32), 32), :]
     everything = slice(0, TILE)
     if first:
         def one_block(step, total):
@@ -610,9 +648,12 @@
     for k in (3, 1, 2, 0):
         rows = slice(k * TILE, (k + 1) * TILE)
         for j in range(QKV // TILE):
-            value = dot(art_ref[rows, :], dqkv_s[:, j * TILE : (j + 1) * TILE]).astype(BF)
+            value = dot(art_s[rows, :], dqkv_ref[:, j * TILE : (j + 1) * TILE]).astype(BF)
             put_piece(outs, k, everything, j * TILE, value)
-        put_piece(outs, k, everything, QKV, dwo_ref[rows, :])
+        for j in range(D // TILE):
+            cols = slice(j * TILE, (j + 1) * TILE)
+            value = dot(ort_s[k * 128 : (k + 1) * 128, :], ga_ref[:, cols]).astype(BF)
+            put_packed(outs, k, QKV, j, value)
 
 
 def last_kernel(meta, ready, *refs):
@@ -656,8 +697,7 @@
         one_ref[:, GATE_UP + k * D : GATE_UP + (k + 1) * D] = down_ref[k * 32 : (k + 1) * 32, :]
 
 
-def unpack_attn_kernel(meta, ready, *refs):
-    one_ref, two_ref, out_ref = refs
+def unpack_attn_kernel(meta, one_ref, two_ref, out_ref):
     low = meta[YL] == 0
     for k in range(QKV // LANES):
         cols = slice(k * LANES, (k + 1) * LANES)
@@ -667,9 +707,7 @@
     out_ref[:, 3 * D :] = one_ref[:, QKV : QKV + D].astype(F32)
 
 
-def unpack_ffn_kernel(meta, ready, *refs):
-    one_ref, two_ref, *picks = refs[:4]
-    out_ref, down_ref = refs[4:]
+def unpack_ffn_kernel(meta, one_ref, two_ref, picks, out_ref, down_ref):
     low = meta[YL] == 0
     halves = []
     for ref in (one_ref, two_ref):
@@ -755,31 +793,31 @@
     )(meta, *arrays)
 
 
-def place_blocks(blocks, shape):
-    count = len(blocks)
+def place_blocks(*targets):
+    moves = [(i, *block) for i, (blocks, _) in enumerate(targets) for block in blocks]
+    count = len(moves)
 
     def kernel(*refs):
-        out_ref, sems = refs[count], refs[count + 1]
+        out_refs, sems = refs[count:-1], refs[-1]
         copies = []
-        for i, (_, (rows, columns), row, column) in enumerate(blocks):
-            source = refs[i].at[pl.ds(rows[0], rows[1]), pl.ds(columns[0], columns[1])]
-            target = out_ref.at[pl.ds(row, rows[1]), pl.ds(column, columns[1])]
-            copies.append(pltpu.make_async_copy(source, target, sems.at[i]))
+        for k, (i, _, (rows, columns), row, column) in enumerate(moves):
+            source = refs[k].at[pl.ds(rows[0], rows[1]), pl.ds(columns[0], columns[1])]
+            target = out_refs[i].at[pl.ds(row, rows[1]), pl.ds(column, columns[1])]
+            copies.append(pltpu.make_async_copy(source, target, sems.at[k]))
             copies[-1].start()
         for copy in copies:
             copy.wait()
 
+    size = sum(math.prod(shape) for _, shape in targets)
     return pl.pallas_call(
         kernel,
-        out_shape=jax.ShapeDtypeStruct(shape, BF),
+        out_shape=[jax.ShapeDtypeStruct(shape, BF) for _, shape in targets],
         in_specs=[pl.BlockSpec(memory_space=pl.ANY)] * count,
-        out_specs=pl.BlockSpec(memory_space=pltpu.VMEM),
+        out_specs=[pl.BlockSpec(memory_space=pltpu.VMEM)] * len(targets),
         scratch_shapes=[pltpu.SemaphoreType.DMA((count,))],
         compiler_params=pltpu.CompilerParams(vmem_limit_bytes=VMEM_LIMIT),
-        cost_estimate=pl.CostEstimate(
-            flops=0, bytes_accessed=4 * math.prod(shape), transcendentals=0
-        ),
-    )(*[block[0] for block in blocks])
+        cost_estimate=pl.CostEstimate(flops=0, bytes_accessed=4 * size, transcendentals=0),
+    )(*[move[1] for move in moves])
 
 
 def body(frames_in, in_weights, down_weights, gains, cotangent, segment_ids, valid):
@@ -858,38 +896,52 @@
             (one, (rows, (tail + HALF, HALF)), 32, down),
         ]
 
-    def attn_to_owner(block, column, extra):
-        low, high = (0, 32), (32, 32)
-        one = [(block, (low, (column, ATTN)), 0, 0), (block, (high, (column + QKV, HALF)), 0, ATTN)]
-        two = [(block, (high, (column, QKV)), 0, 0)]
-        if extra:
-            columns = (column + ATTN, extra)
-            one.append((block, (low, columns), 0, ATTN + HALF))
-            two.append((block, (high, columns), 0, QKV))
-        one = to_owner(place_blocks(one, (32, ATTN + HALF + extra)), 0)
-        two = to_owner(place_blocks(two, (32, QKV + extra)), 1)
-        sums = plus(one[:, ATTN + HALF :], two[:, QKV:])[:, :4] if extra else None
-        return run(unpack_attn_kernel, meta, [one, two], [((32, 4 * D), F32)], [], 1.8)[0], sums
-
-    def ffn_to_owner(block):
+    def to_owners(block, has_ffn, attn_at, extra):
         low, high, down = (0, 32), (32, 32), GATE_UP + D
-        one = [
-            (block, (low, (0, down)), 0, 0),
-            (block, (high, (GATE_UP, D)), 0, down),
-            (block, (low, (down, HALF)), 0, down + D),
-            (block, (high, (down, HALF)), 0, down + D + HALF),
-        ]
-        one = to_owner(place_blocks(one, (32, GATE_UP + 3 * D)), 0)
-        two = to_owner(place_blocks([(block, (high, (0, GATE_UP)), 0, 0)], (32, GATE_UP)), 1)
-        units, down = run(
-            unpack_ffn_kernel,
-            meta,
-            [one, two, *picks],
-            [((32, 4 * PAIR), F32), ((96, D), F32)],
-            [],
-            4.5,
-        )
-        return units, down[:88]
+        one, two, outs, kernels = [], [], [], []
+        if has_ffn:
+            one = [
+                (block, (low, (0, down)), 0, 0),
+                (block, (high, (GATE_UP, D)), 0, down),
+                (block, (low, (down, HALF)), 0, down + D),
+                (block, (high, (down, HALF)), 0, down + D + HALF),
+            ]
+            two = [(block, (high, (0, GATE_UP)), 0, 0)]
+            outs += [((32, 4 * PAIR), F32), ((96, D), F32)]
+        wide, narrow = (GATE_UP + 3 * D, GATE_UP) if has_ffn else (0, 0)
+        first, second = wide, narrow
+        if attn_at is not None:
+            one += [(block, (low, (attn_at, ATTN)), 0, wide)]
+            one += [(block, (high, (attn_at + QKV, HALF)), 0, wide + ATTN)]
+            two += [(block, (high, (attn_at, QKV)), 0, narrow)]
+            wide, narrow = wide + ATTN + HALF, narrow + QKV
+            if extra:
+                columns = (attn_at + ATTN, extra)
+                one.append((block, (low, columns), 0, wide))
+                two.append((block, (high, columns), 0, narrow))
+                wide, narrow = wide + extra, narrow + extra
+            outs += [((32, 4 * D), F32)]
+        one, two = place_blocks((one, (32, wide)), (two, (32, narrow)))
+        one, two = to_owner(one, 0), to_owner(two, 1)
+        sums = plus(one[:, wide - extra :], two[:, narrow - extra :])[:, :4] if extra else None
+
+        def kernel(meta_ref, ready, one_ref, two_ref, *refs):
+            if has_ffn:
+                pick_refs, refs = refs[:2], refs[2:]
+                unpack_ffn_kernel(meta_ref, one_ref, two_ref, pick_refs, refs[0], refs[1])
+                refs = refs[2:]
+            if attn_at is not None:
+                cols = pl.ds(first, ATTN + HALF), pl.ds(second, QKV)
+                attn_refs = one_ref.at[:, cols[0]], two_ref.at[:, cols[1]]
+                unpack_attn_kernel(meta_ref, *attn_refs, refs[0])
+
+        operands = [one, two, *picks] if has_ffn else [one, two]
+        results = list(run(kernel, meta, operands, outs, [], 5.0 if has_ffn else 1.8))
+        if has_ffn:
+            results[1] = results[1][:88]
+        if attn_at is not None:
+            results.append(sums)
+        return results
 
     gain_rows = gains[:, 0].transpose(1, 2, 0).reshape(4, D)
 
@@ -903,7 +955,7 @@
     marked = jnp.concatenate([frames_in[:, 0], jnp.pad(marks, ((0, 0), (0, LANES - 2)))], axis=1)
 
     attn0 = pack_attn(in_weights[:, 0, 0, : 4 * D])
-    attn0 = Gather(place_blocks(attn_blocks(*attn0, 0), (64, ATTN)))
+    attn0 = Gather(place_blocks((attn_blocks(*attn0, 0), (64, ATTN)))[0])
     attn0.one()
     later = after(in_weights, attn0.piece)
     ffn0_parts = pack_ffn(later[:, 0, 0, 4 * D :], down_weights[:, 0, 0], None)
@@ -912,11 +964,11 @@
     attn0_three = attn0.three()
     blocks = ffn_blocks(*ffn0_parts)
     blocks += attn_blocks(*after(tuple(attn1_parts), blocks[0][0]), FFN)
-    middle0 = Gather(place_blocks(blocks, (64, FFN + ATTN)))
+    middle0 = Gather(place_blocks((blocks, (64, FFN + ATTN)))[0])
     later = after(in_weights, *attn1_parts)
     ffn1_parts = pack_ffn(later[:, 0, 1, 4 * D :], down_weights[:, 0, 1], counts)
     blocks = ffn_blocks(*after(tuple(ffn1_parts), blocks[-1][0]))
-    ffn1 = Gather(place_blocks(blocks, (64, FFN)))
+    ffn1 = Gather(place_blocks((blocks, (64, FFN)))[0])
     marked = frames_to_chip(after(marked, blocks[0][0]))
     state = marked[:, :D]
     marks = marked[:, D:]
@@ -941,7 +993,6 @@
 
     wide = ((TOKENS, D), F32)
     wide16 = ((TOKENS, D), BF)
-    turned = ((D, TOKENS), BF)
     row = ((1, D), F32)
     saved = []
     base = None
@@ -949,12 +1000,12 @@
         first = layer == 0
         attn, at = (attn0.blocks, 0) if first else (middle0.blocks, FFN)
         carried = [state] if first else list(base)
-        state, turned_a, *blocks = run(
+        state, normed, *blocks = run(
             lambda *refs, first=first: qkv_kernel(first, *refs),
             meta,
-            [*carried, gain_row(layer, 0), move, move_t] + windows(attn, at, at + QKV),
-            [wide, turned] + [((ROWS, QKV), BF)] * 4,
-            [(TOKENS, D), (TOKENS, D), (TOKENS, QKV)],
+            [*carried, gain_row(layer, 0), move] + windows(attn, at, at + QKV),
+            [wide, wide16] + [((ROWS, QKV), BF)] * 4,
+            [(TOKENS, D), (TOKENS, QKV)],
             7.7,
         )
         blocks = exchange_column(blocks)
@@ -971,30 +1022,30 @@
         if first:
             middle0.four()
         mixed = exchange_column(mixed)
-        turned_o, w_out, partial = run(
+        mixed16, partial = run(
             out_kernel,
             meta,
             mixed + windows(attn, at + QKV, at + ATTN),
-            [((HALF, TOKENS), BF), ((HALF, D), BF), wide16],
-            [(TOKENS, HALF), (HALF, TOKENS)],
+            [((TOKENS, HALF), BF), wide16],
+            [(HALF, D)],
             3.6,
         )
         ffn = (middle0 if first else ffn1).blocks
-        middle, turned_b, gate, up_part, turned_act, w_down, down_partial, *totals = run(
+        middle, branch, gate, up_part, activated, down_partial, *totals = run(
             lambda *refs, first=first: ffn_kernel(not first, *refs),
             meta,
-            [state, partial, other_core(partial), gain_row(layer, 1), move, move_t]
+            [state, partial, other_core(partial), gain_row(layer, 1), move]
             + windows(ffn, 0, FFN),
-            [wide, turned, ((TOKENS, UNITS), F32), ((TOKENS, UNITS), F32)]
-            + [((UNITS, TOKENS), BF), ((UNITS, D), BF), wide16]
+            [wide, wide16, ((TOKENS, UNITS), F32), ((TOKENS, UNITS), F32)]
+            + [((TOKENS, UNITS), BF), wide16]
             + ([] if first else [((1, LANES), F32)]),
-            [(TOKENS, D), (TOKENS, D), (TOKENS, UNITS), (UNITS, TOKENS)],
-            15.0,
+            [(TOKENS, D), (UNITS, D)],
+            11.0,
             (ffn1_joined,) if first else (),
         )
         saved.append(
-            (state, turned_a, blocks, turned_o, w_out, middle, turned_b, gate, up_part)
-            + (turned_act, w_down, attn, at, ffn)
+            (state, normed, blocks, mixed16, middle, branch, gate, up_part, activated)
+            + (attn, at, ffn)
         )
         base = (middle, down_partial, other_core(down_partial))
     totals = totals[0]
@@ -1014,92 +1065,121 @@
         return [((TILE, width), BF)] * 3 + [((TILE, half), BF), ((TILE, width - half), BF)]
 
     for layer in reversed(range(LAYERS)):
-        (state, turned_a, blocks, turned_o, w_out, middle, turned_b, gate, up_part) = saved[layer][:9]
-        turned_act, w_down, attn, at, ffn = saved[layer][9:]
+        state, normed, blocks, mixed16, middle, branch, gate, up_part, activated = saved[layer][:9]
+        attn, at, ffn = saved[layer][9:]
         last = layer == LAYERS - 1
         carried = [cot, marks, totals, other_totals] if last else list(base)
-        results = run(
+        grad, grad16, gate_up16, partial, *results = run(
             lambda *refs, last=last: ffn_backward_kernel(last, *refs),
             meta,
-            [*carried, turned_act, turned_b, gate, up_part, w_down, move]
-            + windows(ffn, 0, GATE_UP)
-            + ([] if last else windows(attn_above, 0, ATTN)),
-            [wide]
-            + ([] if last else [row])
-            + [wide16]
-            + gradient_blocks(FFN if last else FFN + ATTN),
-            [(TOKENS, D), (TOKENS, GATE_UP), (TOKENS, D)],
-            18.0,
+            [*carried, gate, up_part, move] + windows(ffn, 0, FFN),
+            [wide, wide16, ((TOKENS, GATE_UP), BF), wide16] + ([] if last else [row]),
+            [(TOKENS, D), (UNITS, D)],
+            9.0,
+            () if last else above_two,
+        )
+        if not last:
+            gain_list[layer + 1][0] = results[0]
+        other = other_core(partial)
+        base_grad = grad
+
+        def ffn_gradient(grad16):
+            return Scatter(
+                *run(
+                    lambda *refs, last=last: ffn_gradient_kernel(last, *refs),
+                    meta,
+                    [branch, activated, grad16, gate_up16, move_t]
+                    + ([] if last else windows(attn_above, 0, ATTN)),
+                    gradient_blocks(FFN if last else FFN + ATTN),
+                    [(D, TOKENS), (UNITS, TOKENS), (UNITS, TOKENS)],
+                    12.0,
+                )
+            )
+
+        if not last:
+            ffn_above.two_sums(partial)
+            above_three = ffn_above.three()
+            ffn_sum = ffn_gradient(grad16)
+            ffn_sum.one()
+        grad, gain_list[layer][1], attn16, *mixed = run(
+            out_backward_kernel,
+            meta,
+            [base_grad, partial, other, middle, gain_row(layer, 1)]
+            + windows(attn, at + QKV, at + ATTN),
+            [wide, row, wide16] + [((ROWS, HALF), BF)] * 4,
+            [(TOKENS, HALF), (HALF, D)],
+            4.5,
             () if last else above_three,
         )
-        grad, *results = results
-        if not last:
-            gain_list[layer + 1][0], *results = results
-        partial, *pieces = results
+        own = mixed[0]
+        mixed = exchange_column(mixed)
         if last:
-            ffn_above = Scatter(*pieces)
+            ffn_above = ffn_gradient(after(grad16, own))
             above_one = ffn_above.one()
-            above_two = ffn_above.two()
-            above_three = ffn_above.three()
-            above_four = ffn_above.four()
+            early = ()
         else:
-            ffn_sum = Scatter(*pieces)
-            ffn_one = ffn_sum.one()
-        other = other_core(partial)
-        grad, gain_list[layer][1], out_terms, *mixed = run(
-            out_backward_kernel,
-            meta,
-            [grad, partial, other, middle, gain_row(layer, 1), turned_o, w_out],
-            [wide, row, ((D, HALF), BF)] + [((ROWS, HALF), BF)] * 4,
-            [(TOKENS, D), (TOKENS, HALF)],
-            5.8,
-            () if last else above_four,
-        )
-        mixed = exchange_column(mixed)
-        if not last:
-            ffn_two = ffn_sum.two()
+            early = ffn_sum.one_sums(own)
+            ffn_sum.two()
         grads = run(
             attend_backward_kernel,
             meta,
             [*blocks, *mixed],
             [((ROWS, QKV), BF)] * 4,
             [(POS, ROWS, QKV), (POS, ROWS, HALF), (POS, ROWS, QKV)],
-            3.8,
-            above_one if last else ffn_one,
+            3.8 if last else 1.1,
+            early,
         )
         own = grads[0]
         grads = exchange_column(grads)
         if last:
+            ffn_above.one_sums(own)
+            above_two = ffn_above.two()
             grads[0] = after(own, output)
-        partial, *pieces = run(
-            lambda *refs, first=not last: qkv_backward_kernel(first, *refs),
+        else:
+            ffn_above.three_sums(own)
+        partial, qkv16 = run(
+            qkv_backward_kernel,
             meta,
-            [*grads, turned_a, out_terms, move]
-            + ([] if last else [move_t, state, gain_list[0][1], *gain_list[1]])
-            + windows(attn, at, at + QKV),
-            [wide16] + ([((D, ATTN), BF)] if last else gradient_blocks(ATTN_GAINS)),
-            [(TOKENS, QKV), (TOKENS, D)],
-            10.0,
+            [*grads, move] + windows(attn, at, at + QKV),
+            [wide16, ((TOKENS, QKV), BF)],
+            [(TOKENS, D)],
+            5.0 if last else 1.5,
+            above_one if last else (),
+        )
+        pieces = run(
+            lambda *refs, first=not last: attn_gradient_kernel(first, *refs),
+            meta,
+            [normed, qkv16, mixed16, attn16, move_t]
+            + ([] if last else [partial, state, gain_list[0][1], *gain_list[1]]),
+            [((D, ATTN), BF)] if last else gradient_blocks(ATTN_GAINS),
+            [(D, TOKENS), (HALF, TOKENS), (HALF, TOKENS)],
+            7.0 if last else 2.0,
         )
         if last:
             attn_above = pieces[0]
         else:
             attn_sum = Scatter(*pieces)
             attn_sum.one()
+            ffn_above.four(pieces[0])
         base = (grad, partial, other_core(partial), state, gain_row(layer, 0))
-    input_grad = run(last_kernel, meta, list(base), [wide16], [], 4.3, ffn_two)[0]
+    middle = ffn_sum.two_sums()
     ffn_sum.three()
-    attn_sum.two(ffn_two)
+    attn_sum.one_sums()
+    attn_sum.two(middle)
+    ffn_sum.three_sums()
     ffn_sum.four()
-    last_sums = attn_sum.three()
-    units_above, down_list[1] = ffn_to_owner(ffn_above.block)
+    middle = attn_sum.two_sums()
+    attn_sum.three()
+    input_grad = run(last_kernel, meta, list(base), [wide16], [], 4.3, (middle,))[0]
+    units_above, down_list[1] = to_owners(
+        after(ffn_above.four_sums(), pieces[0]), True, None, 0
+    )
+    last_sums = attn_sum.three_sums()
     attn_sum.four()
-    both = after(ffn_sum.block, last_sums)
-    attn_part, _ = attn_to_owner(both, FFN, 0)
-    in_parts = [None, [attn_part, units_above]]
-    units, down_list[0] = ffn_to_owner(both)
-    attn_part, gain_sums = attn_to_owner(attn_sum.block, 0, LANES)
-    in_parts[0] = [attn_part, units]
+    both = after(ffn_sum.four_sums(), last_sums)
+    units, down_list[0], attn_above, _ = to_owners(both, True, FFN, 0)
+    attn, gain_sums = to_owners(attn_sum.four_sums(), False, 0, LANES)
+    in_parts = [[attn, units], [attn_above, units_above]]
     in_list = [jnp.concatenate(parts, axis=1) for parts in in_parts]
     in_grads = jnp.stack(in_list, axis=1)[:, None]
     down_grads = jnp.stack(down_list, axis=1)[:, None]

time: 559 us -> 573 us (1.025)
  waiting for transfers between devices: 116 us -> 130 us
    ppermute x24, waiting for transfers between devices: 16.9 us -> 29.5 us  [exchange_column(): lax.ppermute(blocks[k], COLUMN, [(y, y ^ k) for y in range(POS)])]
    pallas_call x25 -> x28, Pallas kernels: 161 us -> 170 us  [run(): pl.pallas_call(whole, out_shape=[jax.ShapeDtypeStruct(shape, dtype) for s...]
    pallas_call x14 -> x9, Pallas kernels: 27.7 us -> 20.5 us  [place_blocks(): pl.pallas_call(kernel, out_shape=[jax.ShapeDtypeStruct(shape, BF) for _,...]
    ppermute x10 -> x8, starting transfers between devices: 29.1 us -> 25.6 us  [to_owner(): return lax.ppermute(value, ('c', 'yl'), pairs)]
    unnamed x205 -> x191, local copies, waits for them, and re-layouts: 29.9 us -> 29.9 us
  transfers between devices with their start and end apart: 104 -> 102, of which waited for: 29 -> 35; matrix products, arithmetic and copies ran while one was open for 9% -> 9% of each run, Pallas kernels for 25% -> 23%
where the time goes in v3:
time: 573 us; the launch traced here: 562 us
  Pallas kernels  190 us (33%)
  starting transfers between devices  154 us (27%)
  waiting for transfers between devices  130 us (23%)
  local copies, waits for them, and re-layouts  48.5 us (8%)
  other arithmetic  36.1 us (6%)
    pallas_call x28, Pallas kernels, run(): pl.pallas_call(whole, out_shape=[jax.ShapeDtypeStruct(shape, dtype) for s...  170 us
    ppermute x48, waiting for transfers between devices, shift(): return lax.ppermute(value, PLANE, ring_pairs(axis_of_core, step))  77.8 us
    ppermute x48, starting transfers between devices, shift(): return lax.ppermute(value, PLANE, ring_pairs(axis_of_core, step))  53.7 us
    ppermute x24, starting transfers between devices, exchange_column(): lax.ppermute(blocks[k], COLUMN, [(y, y ^ k) for y in range(POS)])  32.9 us
    unnamed x191, local copies, waits for them, and re-layouts  29.9 us
    ppermute x24, waiting for transfers between devices, exchange_column(): lax.ppermute(blocks[k], COLUMN, [(y, y ^ k) for y in range(POS)])  29.5 us
    ppermute x8, starting transfers between devices, to_owner(): return lax.ppermute(value, ('c', 'yl'), pairs)  25.6 us
    ppermute x13, starting transfers between devices, to_chip(): return lax.ppermute(value, ('c', 'yl'), pairs)  24.7 us
  transfers between devices with their start and end apart: 102, of which 35 were waited for; matrix products, arithmetic and copies ran while one was open for 9% of the time, Pallas kernels for 23%

profile of v3, /device:TPU:1, one launch (start us, length us, event | category | flops | bytes accessed | tf_op | source)
XLA Modules:
  0.0 561.8 jit_solution(15856582884642927952)
XLA Ops:
  16.9 3.8 collective-permute-start.9
  21.6 4.1 shard_map.130
  47.8 3.8 collective-permute-start.26
  51.6 4.1 shard_map.132
  58.9 6.6 %collective-permute-done.4.refs_0_.refs_1_.refs_3_.refs_4_ = bf16[32,6144]{1,0:T(8,128)(2,1)S(1)} collective-permute-done((bf16[32,6144]{1,0:T(8,128)(2,1)}, bf16[32,6144]{1,0:T(8,128)(2,1)S(1)}, u32[]{:S(2)}, u32[]{:S(2)}) %collective-permute-start.4) | collective-permute-done | bytes 393248 | tf_op jit(solution)/shard_map/ppermute | solution.py:181
  80.0 5.6 collective-permute-done.30.refs_1_
  87.8 7.0 %collective-permute-done.27.refs_3_ = bf16[64,3328]{1,0:T(8,128)(2,1)S(1)} collective-permute-done((bf16[64,3328]{1,0:T(8,128)(2,1)}, bf16[64,3328]{1,0:T(8,128)(2,1)S(1)}, u32[]{:S(2)}, u32[]{:S(2)}) %collective-permute-start.27) | collective-permute-done | bytes 426016 | tf_op jit(solution)/shard_map/ppermute | solution.py:69
  95.5 3.8 shard_map.138.refs_5_.refs_4_.refs_8_
  117.0 6.8 %shard_map.134 = (f32[256,1024]{1,0:T(8,128)}, bf16[256,1024]{1,0:T(8,128)(2,1)}, bf16[64,1536]{1,0:T(8,128)(2,1)}, bf16[64,1536]{1,0:T(8,128)(2,1)}, bf16[64,15...) custom-call(s32[18]{0:T(128)} %pad_add_fusion.meta_ref, bf16[256,1024]{1,0:T(8,128)(2,1)} %fusion.3.refs_0_, ...), custom_call_target="tpu_custom_call" | custom-call | flops 15399999488 | bytes 26180000 | tf_op jit(solution)/shard_map/pallas_call | solution.py:783
  127.8 12.0 %collective-permute-done.35.refs_7_.refs_6_.refs_10_ = bf16[256,6656]{1,0:T(8,128)(2,1)S(1)} collective-permute-done((bf16[256,6656]{1,0:T(8,128)(2,1)}, bf16[256,6656]{1,0:T(8,128)(2,1)S(1)}, u32[]{:S(2)}, u32[]{:S(2)}) %collective-permute-start.35) | collective-permute-done | bytes 3407904 | tf_op jit(solution)/shard_map/ppermute | solution.py:69
  153.9 3.9 collective-permute-done.20.refs_2_
  159.5 3.5 shard_map.136
  169.1 12.7 %shard_map.141 = (f32[256,1024]{1,0:T(8,128)}, bf16[256,1024]{1,0:T(8,128)(2,1)}, f32[256,1536]{1,0:T(8,128)}, f32[256,1536]{1,0:T(8,128)}, bf16[256,1536]{1,0:T(8,128)(2,1)}, /*index=5*/bf16[256,1024]{1,0:T(8,128)(2,1)}) custom-call(s32[18]{0:T(128)} %pad_add_fusion.meta_ref, f32[256,1024]{1,0:T(8,128)} %get-tuple-element.174.refs_0_.refs_6_.refs_3_, ...), custom_call_target="tpu_custom_call" | custom-call | flops 22000001024 | bytes 37400000 | tf_op jit(solution)/shard_map/pallas_call | solution.py:783
  187.3 7.1 %shard_map.142 = (f32[256,1024]{1,0:T(8,128)}, bf16[256,1024]{1,0:T(8,128)(2,1)}, bf16[64,1536]{1,0:T(8,128)(2,1)}, bf16[64,1536]{1,0:T(8,128)(2,1)}, bf16[64,15...) custom-call(s32[18]{0:T(128)} %pad_add_fusion.meta_ref, f32[256,1024]{1,0:T(8,128)} %get-tuple-element.187.refs_0_.refs_3_, ...), custom_call_target="tpu_custom_call" | custom-call | flops 15399999488 | bytes 26180000 | tf_op jit(solution)/shard_map/pallas_call | solution.py:783
  201.2 5.7 %collective-permute-done.40.refs_2_ = bf16[64,1536]{1,0:T(8,128)(2,1)S(1)} collective-permute-done((bf16[64,1536]{1,0:T(8,128)(2,1)}, bf16[64,1536]{1,0:T(8,128)(2,1)S(1)}, u32[]{:S(2)}, u32[]{:S(2)}) %collective-permute-start.40) | collective-permute-done | bytes 196640 | tf_op jit(solution)/shard_map/ppermute | solution.py:200
  221.1 3.5 shard_map.144
  227.0 3.6 collective-permute-start.52
  231.3 4.7 collective-permute-done.52
  237.3 12.7 %shard_map.145 = (f32[256,1024]{1,0:T(8,128)}, bf16[256,1024]{1,0:T(8,128)(2,1)}, f32[256,1536]{1,0:T(8,128)}, f32[256,1536]{1,0:T(8,128)}, bf16[256,1536]{1,0:T...) custom-call(s32[18]{0:T(128)} %pad_add_fusion.meta_ref, f32[256,1024]{1,0:T(8,128)} %get-tuple-element.189.refs_0_.refs_3_, ...), custom_call_target="tpu_custom_call" | custom-call | flops 22000001024 | bytes 37400000 | tf_op jit(solution)/shard_map/pallas_call | solution.py:783
  253.2 12.4 %shard_map.146 = (f32[256,1024]{1,0:T(8,128)}, bf16[256,1024]{1,0:T(8,128)(2,1)}, bf16[256,3072]{1,0:T(8,128)(2,1)}, bf16[256,1024]{1,0:T(8,128)(2,1)}) custom-call(s32[18]{0:T(128)} %pad_add_fusion.meta_ref, bf16[256,1024]{1,0:T(8,128)(2,1)} %pad_maximum_fusion.10.refs_0_, bf16[256,128]{1,0:T(8,128)(2,1)} %pad_maximum_fusion.13.refs_1_, ...), custom_call_target="tpu_custom_call" | custom-call | flops 17999998976 | bytes 30600000 | tf_op jit(solution)/shard_map/pallas_call | solution.py:783
  268.6 4.9 shard_map.147
  273.5 8.6 %shard_map.149 = (bf16[256,4608]{1,0:T(8,128)(2,1)}, bf16[256,4608]{1,0:T(8,128)(2,1)}, bf16[256,4608]{1,0:T(8,128)(2,1)}, bf16[256,2304]{1,0:T(8,128)(2,1)}, bf16[256,2304]{1,0:T(8,128)(2,1)}) custom-call(s32[18]{0:T(128)} %pad_add_fusion.meta_ref, bf16[256,1024]{1,0:T(8,128)(2,1)} %get-tuple-element.218.refs_0_, ...), custom_call_target="tpu_custom_call" | custom-call | flops 24000000000 | bytes 40800000 | tf_op jit(solution)/shard_map/pallas_call | solution.py:783
  291.5 3.8 shard_map.148
  303.5 3.7 collective-permute-done.60.refs_2_
  310.3 6.2 %shard_map.150 = (bf16[256,1024]{1,0:T(8,128)(2,1)}, bf16[256,1536]{1,0:T(8,128)(2,1)}) custom-call(s32[18]{0:T(128)} %pad_add_fusion.meta_ref, bf16[64,1536]{1,0:T(8,128)(2,1)} %get-tuple-element.214.refs_0_, bf16[64,1536]{1,0:T(8,128)(2,1)} %collective-permute-done.59.refs_1_, bf16[64,1536]{1,0:T(8,128)(2,1)} %collective-permute-done.60.refs_2_, ...), custom_call_target="tpu_custom_call" | custom-call | flops 10000000000 | bytes 17000000 | tf_op jit(solution)/shard_map/pallas_call | solution.py:783
  318.5 6.1 %shard_map.153.refs_5_.refs_6_.refs_7_.refs_8_ = bf16[1024,2048]{1,0:T(8,128)(2,1)} custom-call(s32[18]{0:T(128)} %pad_add_fusion.meta_ref, bf16[256,1024]{1,0:T(8,128)(2,1)} %get-tuple-element.246.refs_0_, bf16[256,1536]{1,0:T(8,128)(2,1)} %get-tuple-element.247.refs_1_, bf16[256,512]{1,0:T(8,128)(2,1)} %get-tuple-element.248.refs_2_, ...), custom_call_target="tpu_custom_call" | custom-call | flops 14000000000 | bytes 23800000 | tf_op jit(solution)/shard_map/pallas_call | solution.py:783
  324.6 5.3 collective-permute-done.66.refs_14_
  332.8 12.9 %shard_map.151 = (f32[256,1024]{1,0:T(8,128)}, bf16[256,1024]{1,0:T(8,128)(2,1)}, bf16[256,3072]{1,0:T(8,128)(2,1)}, bf16[256,1024]{1,0:T(8,128)(2,1)}, f32[1,1024]{1,0:T(1,128)}) custom-call(s32[18]{0:T(128)} %pad_add_fusion.meta_ref, f32[256,1024]{1,0:T(8,128)} %get-tuple-element.208.refs_0_, bf16[256,1024]{1,0:T(8,128)(2,1)} %get-tuple-element.225.refs_1_, ...), custom_call_target="tpu_custom_call" | custom-call | flops 17999998976 | bytes 30600000 | tf_op jit(solution)/shard_map/pallas_call | solution.py:783
  345.7 4.1 collective-permute-start.67
  349.9 12.6 %shard_map.154 = (bf16[256,6656]{1,0:T(8,128)(2,1)}, bf16[256,6656]{1,0:T(8,128)(2,1)}, bf16[256,6656]{1,0:T(8,128)(2,1)}, bf16[256,3328]{1,0:T(8,128)(2,1)}, bf16[256,3328]{1,0:T(8,128)(2,1)}) custom-call(s32[18]{0:T(128)} %pad_add_fusion.meta_ref, bf16[256,1024]{1,0:T(8,128)(2,1)} %get-tuple-element.242.refs_0_, ...), custom_call_target="tpu_custom_call" | custom-call | flops 24000000000 | bytes 40800000 | tf_op jit(solution)/shard_map/pallas_call | solution.py:783
  370.4 5.6 %collective-permute-done.69.refs_10_ = bf16[64,2304]{1,0:T(8,128)(2,1)S(1)} collective-permute-done((bf16[64,2304]{1,0:T(8,128)(2,1)S(1)}, bf16[64,2304]{1,0:T(8,128)(2,1)S(1)}, u32[]{:S(2)}, u32[]{:S(2)}) %collective-permute-start.69) | collective-permute-done | bytes 294944 | tf_op jit(solution)/shard_map/ppermute | solution.py:69
  379.2 4.9 shard_map.152
  398.9 3.7 shard_map.155
  408.2 3.6 collective-permute-done.76.refs_2_
  415.3 6.2 %shard_map.156 = (bf16[256,1024]{1,0:T(8,128)(2,1)}, bf16[256,1536]{1,0:T(8,128)(2,1)}) custom-call(s32[18]{0:T(128)} %pad_add_fusion.meta_ref, bf16[64,1536]{1,0:T(8,128)(2,1)} %get-tuple-element.256.refs_0_, bf16[64,1536]{1,0:T(8,128)(2,1)} %copy-done.73, bf16[64,1536]{1,0:T(8,128)(2,1)} %collective-permute-done.76.refs_2_, ...), custom_call_target="tpu_custom_call" | custom-call | flops 3000000000 | bytes 5100000 | tf_op jit(solution)/shard_map/pallas_call | solution.py:783
  421.5 7.4 %shard_map.157 = (bf16[256,2176]{1,0:T(8,128)(2,1)}, bf16[256,2176]{1,0:T(8,128)(2,1)}, bf16[256,2176]{1,0:T(8,128)(2,1)}, bf16[256,1024]{1,0:T(8,128)(2,1)}, bf16[256,1152]{1,0:T(8,128)(2,1)}) custom-call(s32[18]{0:T(128)} %pad_add_fusion.meta_ref, bf16[256,1024]{1,0:T(8,128)(2,1)} %get-tuple-element.261.refs_0_, ...), custom_call_target="tpu_custom_call" | custom-call | flops 4000000000 | bytes 6800000 | tf_op jit(solution)/shard_map/pallas_call | solution.py:783
  436.1 9.5 %collective-permute-done.98 = bf16[64,4608]{1,0:T(8,128)(2,1)S(1)} collective-permute-done((bf16[64,4608]{1,0:T(8,128)(2,1)S(1)}, bf16[64,4608]{1,0:T(8,128)(2,1)S(1)}, u32[]{:S(2)}, u32[]{:S(2)}) %collective-permute-start.98) | collective-permute-done | bytes 589856 | tf_op jit(solution)/shard_map/ppermute | solution.py:69
  451.2 8.8 %collective-permute-done.79 = bf16[256,1024]{1,0:T(8,128)(2,1)S(1)} collective-permute-done((bf16[256,1024]{1,0:T(8,128)(2,1)}, bf16[256,1024]{1,0:T(8,128)(2,1)S(1)}, u32[]{:S(2)}, u32[]{:S(2)}) %collective-permute-start.79) | collective-permute-done | bytes 524320 | tf_op jit(solution)/shard_map/ppermute | solution.py:69
  460.0 4.5 collective-permute-start.101
  471.5 4.2 add_convert_fusion
  478.9 4.9 shard_map.164
  488.7 12.0 %collective-permute-done.83 = bf16[256,2176]{1,0:T(8,128)(2,1)S(1)} collective-permute-done((bf16[256,2176]{1,0:T(8,128)(2,1)S(1)}, bf16[256,2176]{1,0:T(8,128)(2,1)S(1)}, u32[]{:S(2)}, u32[]{:S(2)}) %collective-permute-start.83) | collective-permute-done | bytes 1114144 | tf_op jit(solution)/shard_map/ppermute | solution.py:69
  509.4 4.2 shard_map.158
  514.7 6.8 %collective-permute-start.85 = (bf16[128,1024]{1,0:T(8,128)(2,1)S(1)}, bf16[128,1024]{1,0:T(8,128)(2,1)S(1)}, u32[]{:S(2)}, u32[]{:S(2)}) collective-permute-start(bf16[128,1024]{1,0:T(8,128)(2,1)S(1)} %slice_select_fusion), channel_id=1, source_target_pairs={{0,0},{4,32},{32,4},{36,36},{1,1},{5,33},{33,5},{37,37},{2,2},{6,3... | collective-permute-start | bytes 786440 | tf_op jit(solution)/shard_map/ppermute | solution.py:186
  525.0 4.1 collective-permute-start.91
  534.5 3.9 collective-permute-start.96
  541.0 5.8 %collective-permute-done.96.refs_0_ = bf16[32,8704]{1,0:T(8,128)(2,1)S(1)} collective-permute-done((bf16[32,8704]{1,0:T(8,128)(2,1)}, bf16[32,8704]{1,0:T(8,128)(2,1)S(1)}, u32[]{:S(2)}, u32[]{:S(2)}) %collective-permute-start.96) | collective-permute-done | bytes 557088 | tf_op jit(solution)/shard_map/ppermute | solution.py:186
  547.5 5.1 shard_map.162
  (478 shorter events, 258.2 us)
Async XLA Ops:
  25.7 18.6 %collective-permute-start.23 = (bf16[32,3072]{1,0:T(8,128)(2,1)}, bf16[32,3072]{1,0:T(8,128)(2,1)S(1)}, u32[]{:S(2)}, u32[]{:S(2)}) collective-permute-start(bf16[32,3072]{1,0:T(8,128)(2,1)} %get-tuple-element.161), channel_id=1, source_target_pairs={{0,32},{4,0},{32,36},{36,4},{1,33},{5,1},{33,37},{37,5},{2,34},{6,... | collective-permute-start | bytes 589832 | tf_op jit(solution)/shard_map/ppermute | solution.py:181
  41.8 29.5 %collective-permute-start.13 = (bf16[256,2048]{1,0:T(8,128)(2,1)}, bf16[256,2048]{1,0:T(8,128)(2,1)S(1)}, u32[]{:S(2)}, u32[]{:S(2)}) collective-permute-start(bf16[256,2048]{1,0:T(8,128)(2,1)} %shard_map.133.refs_3_.refs_4_.refs_5_), channel_id=1, source_target_pairs={{0,24},{1,25},{2,26},{3,27},{8,0},{9,1},{10,2},{11,3},{16,8},{17,9... | collective-permute-start | bytes 3145736 | tf_op jit(solution)/shard_map/ppermute | solution.py:69
  47.8 22.7 %collective-permute-start.26 = (bf16[64,6656]{1,0:T(8,128)(2,1)}, bf16[64,6656]{1,0:T(8,128)(2,1)S(1)}, u32[]{:S(2)}, u32[]{:S(2)}) collective-permute-start(bf16[64,6656]{1,0:T(8,128)(2,1)} %shard_map.137.refs_0_), channel_id=1, source_target_pairs={{0,3},{1,0},{2,1},{3,2},{8,11},{9,8},{10,9},{11,10},{16,19},{17,16... | collective-permute-start | bytes 2555912 | tf_op jit(solution)/shard_map/ppermute | solution.py:69
  55.7 20.5 %collective-permute-start.12 = (bf16[256,2048]{1,0:T(8,128)(2,1)S(1)}, bf16[256,2048]{1,0:T(8,128)(2,1)S(1)}, u32[]{:S(2)}, u32[]{:S(2)}) collective-permute-start(bf16[256,2048]{1,0:T(8,128)(2,1)S(1)} %copy-done.25), channel_id=1, source_target_pairs={{0,8},{1,9},{2,10},{3,11},{8,16},{9,17},{10,18},{11,19},{16,24},{1... | collective-permute-start | bytes 3145736 | tf_op jit(solution)/shard_map/ppermute | solution.py:69
  58.8 20.2 %collective-permute-start.25 = (bf16[64,6656]{1,0:T(8,128)(2,1)S(1)}, bf16[64,6656]{1,0:T(8,128)(2,1)S(1)}, u32[]{:S(2)}, u32[]{:S(2)}) collective-permute-start(bf16[64,6656]{1,0:T(8,128)(2,1)S(1)} %copy-done.8), channel_id=1, source_target_pairs={{0,1},{1,2},{2,3},{3,0},{8,9},{9,10},{10,11},{11,8},{16,17},{17,18... | collective-permute-start | bytes 2555912 | tf_op jit(solution)/shard_map/ppermute | solution.py:69
  70.5 15.1 %collective-permute-start.30 = (bf16[64,4608]{1,0:T(8,128)(2,1)}, bf16[64,4608]{1,0:T(8,128)(2,1)S(1)}, u32[]{:S(2)}, u32[]{:S(2)}) collective-permute-start(bf16[64,4608]{1,0:T(8,128)(2,1)} %shard_map.139.refs_0_), channel_id=1, source_target_pairs={{0,1},{1,2},{2,3},{3,0},{8,9},{9,10},{10,11},{11,8},{16,17},{17,18... | collective-permute-start | bytes 1769480 | tf_op jit(solution)/shard_map/ppermute | solution.py:69
  71.4 15.1 %collective-permute-start.28 = (bf16[64,3328]{1,0:T(8,128)(2,1)}, bf16[64,3328]{1,0:T(8,128)(2,1)}, u32[]{:S(2)}, u32[]{:S(2)}) collective-permute-start(bf16[64,3328]{1,0:T(8,128)(2,1)} %slice.307), channel_id=1, source_target_pairs={{0,3},{1,0},{2,1},{3,2},{8,11},{9,8},{10,9},{11,10},{16,19},{17,16... | collective-permute-start | bytes 1277960 | tf_op jit(solution)/shard_map/ppermute | solution.py:69
  76.2 23.1 %collective-permute-start.15 = (bf16[256,1024]{1,0:T(8,128)(2,1)S(1)}, bf16[256,1024]{1,0:T(8,128)(2,1)}, u32[]{:S(2)}, u32[]{:S(2)}) collective-permute-start(bf16[256,1024]{1,0:T(8,128)(2,1)S(1)} %slice.304), channel_id=1, source_target_pairs={{0,24},{1,25},{2,26},{3,27},{8,0},{9,1},{10,2},{11,3},{16,8},{17,9... | collective-permute-start | bytes 1572872 | tf_op jit(solution)/shard_map/ppermute | solution.py:69
  79.0 21.1 %collective-permute-start.14 = (bf16[256,1024]{1,0:T(8,128)(2,1)}, bf16[256,1024]{1,0:T(8,128)(2,1)}, u32[]{:S(2)}, u32[]{:S(2)}) collective-permute-start(bf16[256,1024]{1,0:T(8,128)(2,1)} %slice.303), channel_id=1, source_target_pairs={{0,8},{1,9},{2,10},{3,11},{8,16},{9,17},{10,18},{11,19},{16,24},{1... | collective-permute-start | bytes 1572872 | tf_op jit(solution)/shard_map/ppermute | solution.py:69
  79.9 14.9 %collective-permute-start.27 = (bf16[64,3328]{1,0:T(8,128)(2,1)}, bf16[64,3328]{1,0:T(8,128)(2,1)S(1)}, u32[]{:S(2)}, u32[]{:S(2)}) collective-permute-start(bf16[64,3328]{1,0:T(8,128)(2,1)} %slice.306), channel_id=1, source_target_pairs={{0,1},{1,2},{2,3},{3,0},{8,9},{9,10},{10,11},{11,8},{16,17},{17,18... | collective-permute-start | bytes 1277960 | tf_op jit(solution)/shard_map/ppermute | solution.py:69
  85.6 13.7 %collective-permute-start.33 = (bf16[64,2304]{1,0:T(8,128)(2,1)S(1)}, bf16[64,2304]{1,0:T(8,128)(2,1)S(1)}, u32[]{:S(2)}, u32[]{:S(2)}) collective-permute-start(bf16[64,2304]{1,0:T(8,128)(2,1)S(1)} %slice.309), channel_id=1, source_target_pairs={{0,3},{1,0},{2,1},{3,2},{8,11},{9,8},{10,9},{11,10},{16,19},{17,16... | collective-permute-start | bytes 884744 | tf_op jit(solution)/shard_map/ppermute | solution.py:69
  100.2 39.5 %collective-permute-start.35 = (bf16[256,6656]{1,0:T(8,128)(2,1)}, bf16[256,6656]{1,0:T(8,128)(2,1)S(1)}, u32[]{:S(2)}, u32[]{:S(2)}) collective-permute-start(bf16[256,6656]{1,0:T(8,128)(2,1)} %shard_map.138.refs_5_.refs_4_.refs_8_), channel_id=1, source_target_pairs={{0,24},{1,25},{2,26},{3,27},{8,0},{9,1},{10,2},{11,3},{16,8},{17,9... | collective-permute-start | bytes 10223624 | tf_op jit(solution)/shard_map/ppermute | solution.py:69
  101.5 42.5 %collective-permute-start.34 = (bf16[256,6656]{1,0:T(8,128)(2,1)}, bf16[256,6656]{1,0:T(8,128)(2,1)}, u32[]{:S(2)}, u32[]{:S(2)}) collective-permute-start(bf16[256,6656]{1,0:T(8,128)(2,1)} %shard_map.138.refs_5_.refs_4_.refs_8_), channel_id=1, source_target_pairs={{0,8},{1,9},{2,10},{3,11},{8,16},{9,17},{10,18},{11,19},{16,24},{1... | collective-permute-start | bytes 10223624 | tf_op jit(solution)/shard_map/ppermute | solution.py:69
  123.8 21.8 %collective-permute-start.16 = (bf16[64,1536]{1,0:T(8,128)(2,1)}, bf16[64,1536]{1,0:T(8,128)(2,1)}, u32[]{:S(2)}, u32[]{:S(2)}) collective-permute-start(bf16[64,1536]{1,0:T(8,128)(2,1)} %get-tuple-element.176), channel_id=1, source_target_pairs={{0,4},{4,0},{64,68},{68,64},{1,5},{5,1},{65,69},{69,65},{2,6},{6,2... | collective-permute-start | bytes 589832 | tf_op jit(solution)/shard_map/ppermute | solution.py:200
  123.9 21.7 %collective-permute-start.17 = (bf16[64,1536]{1,0:T(8,128)(2,1)}, bf16[64,1536]{1,0:T(8,128)(2,1)}, u32[]{:S(2)}, u32[]{:S(2)}) collective-permute-start(bf16[64,1536]{1,0:T(8,128)(2,1)} %get-tuple-element.177), channel_id=1, source_target_pairs={{0,64},{4,68},{64,0},{68,4},{1,65},{5,69},{65,1},{69,5},{2,66},{6,... | collective-permute-start | bytes 589832 | tf_op jit(solution)/shard_map/ppermute | solution.py:200
  126.9 18.7 %collective-permute-start.18 = (bf16[64,1536]{1,0:T(8,128)(2,1)}, bf16[64,1536]{1,0:T(8,128)(2,1)}, u32[]{:S(2)}, u32[]{:S(2)}) collective-permute-start(bf16[64,1536]{1,0:T(8,128)(2,1)} %get-tuple-element.178), channel_id=1, source_target_pairs={{0,68},{4,64},{64,4},{68,0},{1,69},{5,65},{65,5},{69,1},{2,70},{6,... | collective-permute-start | bytes 589832 | tf_op jit(solution)/shard_map/ppermute | solution.py:200
  141.5 25.9 %collective-permute-start.37 = (bf16[256,3328]{1,0:T(8,128)(2,1)S(1)}, bf16[256,3328]{1,0:T(8,128)(2,1)}, u32[]{:S(2)}, u32[]{:S(2)}) collective-permute-start(bf16[256,3328]{1,0:T(8,128)(2,1)S(1)} %slice.311), channel_id=1, source_target_pairs={{0,24},{1,25},{2,26},{3,27},{8,0},{9,1},{10,2},{11,3},{16,8},{17,9... | collective-permute-start | bytes 5111816 | tf_op jit(solution)/shard_map/ppermute | solution.py:69
  145.5 22.2 %collective-permute-start.36 = (bf16[256,3328]{1,0:T(8,128)(2,1)S(1)}, bf16[256,3328]{1,0:T(8,128)(2,1)S(1)}, u32[]{:S(2)}, u32[]{:S(2)}) collective-permute-start(bf16[256,3328]{1,0:T(8,128)(2,1)S(1)} %slice.310), channel_id=1, source_target_pairs={{0,8},{1,9},{2,10},{3,11},{8,16},{9,17},{10,18},{11,19},{16,24},{1... | collective-permute-start | bytes 5111816 | tf_op jit(solution)/shard_map/ppermute | solution.py:69
  184.8 32.0 %collective-permute-start.47 = (bf16[256,4608]{1,0:T(8,128)(2,1)S(1)}, bf16[256,4608]{1,0:T(8,128)(2,1)S(1)}, u32[]{:S(2)}, u32[]{:S(2)}) collective-permute-start(bf16[256,4608]{1,0:T(8,128)(2,1)S(1)} %copy-done.12), channel_id=1, source_target_pairs={{0,24},{1,25},{2,26},{3,27},{8,0},{9,1},{10,2},{11,3},{16,8},{17,9... | collective-permute-start | bytes 7077896 | tf_op jit(solution)/shard_map/ppermute | solution.py:69
  184.8 34.1 %collective-permute-start.46 = (bf16[256,4608]{1,0:T(8,128)(2,1)S(1)}, bf16[256,4608]{1,0:T(8,128)(2,1)}, u32[]{:S(2)}, u32[]{:S(2)}) collective-permute-start(bf16[256,4608]{1,0:T(8,128)(2,1)S(1)} %copy-done.12), channel_id=1, source_target_pairs={{0,8},{1,9},{2,10},{3,11},{8,16},{9,17},{10,18},{11,19},{16,24},{1... | collective-permute-start | bytes 7077896 | tf_op jit(solution)/shard_map/ppermute | solution.py:69
  216.9 19.1 %collective-permute-start.49 = (bf16[256,2304]{1,0:T(8,128)(2,1)S(1)}, bf16[256,2304]{1,0:T(8,128)(2,1)S(1)}, u32[]{:S(2)}, u32[]{:S(2)}) collective-permute-start(bf16[256,2304]{1,0:T(8,128)(2,1)S(1)} %slice.315), channel_id=1, source_target_pairs={{0,24},{1,25},{2,26},{3,27},{8,0},{9,1},{10,2},{11,3},{16,8},{17,9... | collective-permute-start | bytes 3538952 | tf_op jit(solution)/shard_map/ppermute | solution.py:69
  220.3 16.7 %collective-permute-start.48 = (bf16[256,2304]{1,0:T(8,128)(2,1)S(1)}, bf16[256,2304]{1,0:T(8,128)(2,1)}, u32[]{:S(2)}, u32[]{:S(2)}) collective-permute-start(bf16[256,2304]{1,0:T(8,128)(2,1)S(1)} %slice.314), channel_id=1, source_target_pairs={{0,8},{1,9},{2,10},{3,11},{8,16},{9,17},{10,18},{11,19},{16,24},{1... | collective-permute-start | bytes 3538952 | tf_op jit(solution)/shard_map/ppermute | solution.py:69
  266.0 17.7 %collective-permute-start.50 = (bf16[256,1024]{1,0:T(8,128)(2,1)S(1)}, bf16[256,1024]{1,0:T(8,128)(2,1)S(1)}, u32[]{:S(2)}, u32[]{:S(2)}) collective-permute-start(bf16[256,1024]{1,0:T(8,128)(2,1)S(1)} %copy-done.37), channel_id=1, source_target_pairs={{0,32},{32,0},{1,33},{33,1},{2,34},{34,2},{3,35},{35,3},{4,36},{36... | collective-permute-start | bytes 1572872 | tf_op jit(solution)/shard_map/ppermute | solution.py:190
  282.1 16.7 %collective-permute-start.63 = (bf16[256,2304]{1,0:T(8,128)(2,1)}, bf16[256,2304]{1,0:T(8,128)(2,1)S(1)}, u32[]{:S(2)}, u32[]{:S(2)}) collective-permute-start(bf16[256,2304]{1,0:T(8,128)(2,1)} %get-tuple-element.224), channel_id=1, source_target_pairs={{0,24},{1,25},{2,26},{3,27},{8,0},{9,1},{10,2},{11,3},{16,8},{17,9... | collective-permute-start | bytes 3538952 | tf_op jit(solution)/shard_map/ppermute | solution.py:69
  282.7 16.9 %collective-permute-start.62 = (bf16[256,2304]{1,0:T(8,128)(2,1)}, bf16[256,2304]{1,0:T(8,128)(2,1)}, u32[]{:S(2)}, u32[]{:S(2)}) collective-permute-start(bf16[256,2304]{1,0:T(8,128)(2,1)} %get-tuple-element.223), channel_id=1, source_target_pairs={{0,8},{1,9},{2,10},{3,11},{8,16},{9,17},{10,18},{11,19},{16,24},{1... | collective-permute-start | bytes 3538952 | tf_op jit(solution)/shard_map/ppermute | solution.py:69
  288.8 14.7 %collective-permute-start.51 = (bf16[128,1024]{1,0:T(8,128)(2,1)}, bf16[128,1024]{1,0:T(8,128)(2,1)}, u32[]{:S(2)}, u32[]{:S(2)}) collective-permute-start(bf16[128,1024]{1,0:T(8,128)(2,1)} %slice_select_fusion.1), channel_id=1, source_target_pairs={{0,0},{4,32},{32,4},{36,36},{1,1},{5,33},{33,5},{37,37},{2,2},{6,3... | collective-permute-start | bytes 786440 | tf_op jit(solution)/shard_map/ppermute | solution.py:186
  301.7 28.2 %collective-permute-start.66 = (bf16[256,4608]{1,0:T(8,128)(2,1)S(1)}, bf16[256,4608]{1,0:T(8,128)(2,1)S(1)}, u32[]{:S(2)}, u32[]{:S(2)}) collective-permute-start(bf16[256,4608]{1,0:T(8,128)(2,1)S(1)} %pad_maximum_fusion.3), channel_id=1, source_target_pairs={{0,24},{1,25},{2,26},{3,27},{8,0},{9,1},{10,2},{11,3},{16,8},{17,9... | collective-permute-start | bytes 7077896 | tf_op jit(solution)/shard_map/ppermute | solution.py:69
  303.5 29.3 %collective-permute-start.65 = (bf16[256,4608]{1,0:T(8,128)(2,1)S(1)}, bf16[256,4608]{1,0:T(8,128)(2,1)}, u32[]{:S(2)}, u32[]{:S(2)}) collective-permute-start(bf16[256,4608]{1,0:T(8,128)(2,1)S(1)} %pad_maximum_fusion.2), channel_id=1, source_target_pairs={{0,8},{1,9},{2,10},{3,11},{8,16},{9,17},{10,18},{11,19},{16,24},{1... | collective-permute-start | bytes 7077896 | tf_op jit(solution)/shard_map/ppermute | solution.py:69
  345.7 32.6 %collective-permute-start.67 = (bf16[256,1024]{1,0:T(8,128)(2,1)}, bf16[256,1024]{1,0:T(8,128)(2,1)S(1)}, u32[]{:S(2)}, u32[]{:S(2)}) collective-permute-start(bf16[256,1024]{1,0:T(8,128)(2,1)} %get-tuple-element.233.refs_1_), channel_id=1, source_target_pairs={{0,32},{32,0},{1,33},{33,1},{2,34},{34,2},{3,35},{35,3},{4,36},{36... | collective-permute-start | bytes 1572872 | tf_op jit(solution)/shard_map/ppermute | solution.py:190
  362.5 25.6 %collective-permute-start.74 = (bf16[256,3328]{1,0:T(8,128)(2,1)}, bf16[256,3328]{1,0:T(8,128)(2,1)}, u32[]{:S(2)}, u32[]{:S(2)}) collective-permute-start(bf16[256,3328]{1,0:T(8,128)(2,1)} %get-tuple-element.252), channel_id=1, source_target_pairs={{0,24},{1,25},{2,26},{3,27},{8,0},{9,1},{10,2},{11,3},{16,8},{17,9... | collective-permute-start | bytes 5111816 | tf_op jit(solution)/shard_map/ppermute | solution.py:69
  363.1 25.7 %collective-permute-start.73 = (bf16[256,3328]{1,0:T(8,128)(2,1)}, bf16[256,3328]{1,0:T(8,128)(2,1)}, u32[]{:S(2)}, u32[]{:S(2)}) collective-permute-start(bf16[256,3328]{1,0:T(8,128)(2,1)} %get-tuple-element.251), channel_id=1, source_target_pairs={{0,8},{1,9},{2,10},{3,11},{8,16},{9,17},{10,18},{11,19},{16,24},{1... | collective-permute-start | bytes 5111816 | tf_op jit(solution)/shard_map/ppermute | solution.py:69
  384.0 13.6 %collective-permute-start.70 = (bf16[64,512]{1,0:T(8,128)(2,1)}, bf16[64,512]{1,0:T(8,128)(2,1)S(1)}, u32[]{:S(2)}, u32[]{:S(2)}) collective-permute-start(bf16[64,512]{1,0:T(8,128)(2,1)} %get-tuple-element.239), channel_id=1, source_target_pairs={{0,4},{4,0},{64,68},{68,64},{1,5},{5,1},{65,69},{69,65},{2,6},{6,2... | collective-permute-start | bytes 196616 | tf_op jit(solution)/shard_map/ppermute | solution.py:200
  384.1 13.5 %collective-permute-start.71 = (bf16[64,512]{1,0:T(8,128)(2,1)}, bf16[64,512]{1,0:T(8,128)(2,1)S(1)}, u32[]{:S(2)}, u32[]{:S(2)}) collective-permute-start(bf16[64,512]{1,0:T(8,128)(2,1)} %get-tuple-element.240), channel_id=1, source_target_pairs={{0,64},{4,68},{64,0},{68,4},{1,65},{5,69},{65,1},{69,5},{2,66},{6,... | collective-permute-start | bytes 196616 | tf_op jit(solution)/shard_map/ppermute | solution.py:200
  406.5 63.9 %collective-permute-start.82 = (bf16[256,6656]{1,0:T(8,128)(2,1)}, bf16[256,6656]{1,0:T(8,128)(2,1)}, u32[]{:S(2)}, u32[]{:S(2)}) collective-permute-start(bf16[256,6656]{1,0:T(8,128)(2,1)} %pad_maximum_fusion.refs_8_), channel_id=1, source_target_pairs={{0,24},{1,25},{2,26},{3,27},{8,0},{9,1},{10,2},{11,3},{16,8},{17,9... | collective-permute-start | bytes 10223624 | tf_op jit(solution)/shard_map/ppermute | solution.py:69
  407.7 62.7 %collective-permute-start.81 = (bf16[256,6656]{1,0:T(8,128)(2,1)S(1)}, bf16[256,6656]{1,0:T(8,128)(2,1)}, u32[]{:S(2)}, u32[]{:S(2)}) collective-permute-start(bf16[256,6656]{1,0:T(8,128)(2,1)S(1)} %copy-done.7), channel_id=1, source_target_pairs={{0,8},{1,9},{2,10},{3,11},{8,16},{9,17},{10,18},{11,19},{16,24},{1... | collective-permute-start | bytes 10223624 | tf_op jit(solution)/shard_map/ppermute | solution.py:69
  428.9 16.7 %collective-permute-start.98 = (bf16[64,4608]{1,0:T(8,128)(2,1)S(1)}, bf16[64,4608]{1,0:T(8,128)(2,1)S(1)}, u32[]{:S(2)}, u32[]{:S(2)}) collective-permute-start(bf16[64,4608]{1,0:T(8,128)(2,1)S(1)} %pad_maximum_fusion.8), channel_id=1, source_target_pairs={{0,1},{1,2},{2,3},{3,0},{8,9},{9,10},{10,11},{11,8},{16,17},{17,18... | collective-permute-start | bytes 1769480 | tf_op jit(solution)/shard_map/ppermute | solution.py:69
  428.9 16.7 %collective-permute-start.99 = (bf16[64,4608]{1,0:T(8,128)(2,1)S(1)}, bf16[64,4608]{1,0:T(8,128)(2,1)S(1)}, u32[]{:S(2)}, u32[]{:S(2)}) collective-permute-start(bf16[64,4608]{1,0:T(8,128)(2,1)S(1)} %pad_maximum_fusion.9), channel_id=1, source_target_pairs={{0,3},{1,0},{2,1},{3,2},{8,11},{9,8},{10,9},{11,10},{16,19},{17,16... | collective-permute-start | bytes 1769480 | tf_op jit(solution)/shard_map/ppermute | solution.py:69
  431.5 77.9 %collective-permute-start.78 = (bf16[256,1024]{1,0:T(8,128)(2,1)}, bf16[256,1024]{1,0:T(8,128)(2,1)}, u32[]{:S(2)}, u32[]{:S(2)}) collective-permute-start(bf16[256,1024]{1,0:T(8,128)(2,1)} %get-tuple-element.260.refs_5_.refs_1_), channel_id=1, source_target_pairs={{0,32},{32,0},{1,33},{33,1},{2,34},{34,2},{3,35},{35,3},{4,36},{36... | collective-permute-start | bytes 1572872 | tf_op jit(solution)/shard_map/ppermute | solution.py:190
  445.6 14.5 %collective-permute-start.79 = (bf16[256,1024]{1,0:T(8,128)(2,1)}, bf16[256,1024]{1,0:T(8,128)(2,1)S(1)}, u32[]{:S(2)}, u32[]{:S(2)}) collective-permute-start(bf16[256,1024]{1,0:T(8,128)(2,1)} %get-tuple-element.270), channel_id=1, source_target_pairs={{0,8},{1,9},{2,10},{3,11},{8,16},{9,17},{10,18},{11,19},{16,24},{1... | collective-permute-start | bytes 1572872 | tf_op jit(solution)/shard_map/ppermute | solution.py:69
  445.6 19.0 %collective-permute-start.80 = (bf16[256,1152]{1,0:T(8,128)(2,1)}, bf16[256,1152]{1,0:T(8,128)(2,1)S(1)}, u32[]{:S(2)}, u32[]{:S(2)}) collective-permute-start(bf16[256,1152]{1,0:T(8,128)(2,1)} %get-tuple-element.271), channel_id=1, source_target_pairs={{0,24},{1,25},{2,26},{3,27},{8,0},{9,1},{10,2},{11,3},{16,8},{17,9... | collective-permute-start | bytes 1769480 | tf_op jit(solution)/shard_map/ppermute | solution.py:69
  460.0 18.2 %collective-permute-start.101 = (bf16[32,3072]{1,0:T(8,128)(2,1)}, bf16[32,3072]{1,0:T(8,128)(2,1)S(1)}, u32[]{:S(2)}, u32[]{:S(2)}) collective-permute-start(bf16[32,3072]{1,0:T(8,128)(2,1)} %get-tuple-element.305), channel_id=1, source_target_pairs={{0,4},{4,36},{32,0},{36,32},{1,5},{5,37},{33,1},{37,33},{2,6},{6,3... | collective-permute-start | bytes 589832 | tf_op jit(solution)/shard_map/ppermute | solution.py:186
  464.6 13.7 %collective-permute-start.100 = (bf16[32,6144]{1,0:T(8,128)(2,1)}, bf16[32,6144]{1,0:T(8,128)(2,1)}, u32[]{:S(2)}, u32[]{:S(2)}) collective-permute-start(bf16[32,6144]{1,0:T(8,128)(2,1)} %get-tuple-element.304), channel_id=1, source_target_pairs={{0,0},{4,32},{32,4},{36,36},{1,1},{5,33},{33,5},{37,37},{2,2},{6,3... | collective-permute-start | bytes 1179656 | tf_op jit(solution)/shard_map/ppermute | solution.py:186
  484.8 15.9 %collective-permute-start.83 = (bf16[256,2176]{1,0:T(8,128)(2,1)S(1)}, bf16[256,2176]{1,0:T(8,128)(2,1)S(1)}, u32[]{:S(2)}, u32[]{:S(2)}) collective-permute-start(bf16[256,2176]{1,0:T(8,128)(2,1)S(1)} %pad_maximum_fusion.4), channel_id=1, source_target_pairs={{0,8},{1,9},{2,10},{3,11},{8,16},{9,17},{10,18},{11,19},{16,24},{1... | collective-permute-start | bytes 3342344 | tf_op jit(solution)/shard_map/ppermute | solution.py:69
  484.9 15.8 %collective-permute-start.84 = (bf16[256,2176]{1,0:T(8,128)(2,1)S(1)}, bf16[256,2176]{1,0:T(8,128)(2,1)S(1)}, u32[]{:S(2)}, u32[]{:S(2)}) collective-permute-start(bf16[256,2176]{1,0:T(8,128)(2,1)S(1)} %copy-done.24), channel_id=1, source_target_pairs={{0,24},{1,25},{2,26},{3,27},{8,0},{9,1},{10,2},{11,3},{16,8},{17,9... | collective-permute-start | bytes 3342344 | tf_op jit(solution)/shard_map/ppermute | solution.py:69
  504.0 17.5 %collective-permute-start.94 = (bf16[64,6656]{1,0:T(8,128)(2,1)S(1)}, bf16[64,6656]{1,0:T(8,128)(2,1)S(1)}, u32[]{:S(2)}, u32[]{:S(2)}) collective-permute-start(bf16[64,6656]{1,0:T(8,128)(2,1)S(1)} %pad_maximum_fusion.6), channel_id=1, source_target_pairs={{0,1},{1,2},{2,3},{3,0},{8,9},{9,10},{10,11},{11,8},{16,17},{17,18... | collective-permute-start | bytes 2555912 | tf_op jit(solution)/shard_map/ppermute | solution.py:69
  504.1 17.4 %collective-permute-start.95 = (bf16[64,6656]{1,0:T(8,128)(2,1)}, bf16[64,6656]{1,0:T(8,128)(2,1)S(1)}, u32[]{:S(2)}, u32[]{:S(2)}) collective-permute-start(bf16[64,6656]{1,0:T(8,128)(2,1)} %pad_maximum_fusion.7), channel_id=1, source_target_pairs={{0,3},{1,0},{2,1},{3,2},{8,11},{9,8},{10,9},{11,10},{16,19},{17,16... | collective-permute-start | bytes 2555912 | tf_op jit(solution)/shard_map/ppermute | solution.py:69
  506.9 14.6 %collective-permute-start.89 = (bf16[64,2176]{1,0:T(8,128)(2,1)S(1)}, bf16[64,2176]{1,0:T(8,128)(2,1)S(1)}, u32[]{:S(2)}, u32[]{:S(2)}) collective-permute-start(bf16[64,2176]{1,0:T(8,128)(2,1)S(1)} %pad_maximum_fusion.12), channel_id=1, source_target_pairs={{0,3},{1,0},{2,1},{3,2},{8,11},{9,8},{10,9},{11,10},{16,19},{17,16... | collective-permute-start | bytes 835592 | tf_op jit(solution)/shard_map/ppermute | solution.py:69
  514.7 23.7 %collective-permute-start.85 = (bf16[128,1024]{1,0:T(8,128)(2,1)S(1)}, bf16[128,1024]{1,0:T(8,128)(2,1)S(1)}, u32[]{:S(2)}, u32[]{:S(2)}) collective-permute-start(bf16[128,1024]{1,0:T(8,128)(2,1)S(1)} %slice_select_fusion), channel_id=1, source_target_pairs={{0,0},{4,32},{32,4},{36,36},{1,1},{5,33},{33,5},{37,37},{2,2},{6,3... | collective-permute-start | bytes 786440 | tf_op jit(solution)/shard_map/ppermute | solution.py:186
  (147 other events, 882.8 us)

commit v4 on v2

--- a/solution.py
+++ b/solution.py
@@ -101,7 +101,7 @@
         blocks = [(self.piece, whole, 0, 0), (self.left, whole, rows, 0)]
         blocks += [(self.right, whole, 2 * rows, 0)]
         blocks += [(done[0], part, 3 * rows, 0), (done[1], part, 3 * rows, half)]
-        self.piece = place_blocks(blocks, (4 * rows, width))
+        self.piece = place_blocks((blocks, (4 * rows, width)))[0]
         return done
 
     def three(self, *deps):
@@ -113,45 +113,113 @@
 
 def plus(one, two):
     return one.astype(F32) + two.astype(F32)
+
+
+def add_halves(left, right, far_a, far_b):
+    rows, width = right.shape
+    half = far_a.shape[1]
+    rest = width - half
+
+    def kernel(left_ref, right_ref, a_ref, b_ref, left_out, right_out, held_a, held_b, a_s, b_s, sems):
+        first, last = pl.ds(0, half), pl.ds(half, rest)
+        loads = [
+            pltpu.make_async_copy(right_ref.at[:, first], held_a, sems.at[0]),
+            pltpu.make_async_copy(a_ref, a_s, sems.at[1]),
+            pltpu.make_async_copy(left_ref.at[:, last], held_b, sems.at[2]),
+            pltpu.make_async_copy(b_ref, b_s, sems.at[3]),
+        ]
+        for copy in loads:
+            copy.start()
+        stores = []
+        for place, (held, other, target) in enumerate(
+            ((held_a, a_s, right_out.at[:, first]), (held_b, b_s, left_out.at[:, last]))
+        ):
+            loads[2 * place].wait()
+            loads[2 * place + 1].wait()
+
+            @pl.loop(0, rows // 16)
+            def _(step):
+                part = pl.ds(pl.multiple_of(step * 16, 16), 16)
+                held[part, :] = (held[part, :].astype(F32) + other[part, :].astype(F32)).astype(BF)
+
+            stores.append(pltpu.make_async_copy(held, target, sems.at[4 + place]))
+            stores[-1].start()
+        for copy in stores:
+            copy.wait()
+
+    scratch = [(rows, half), (rows, rest), (rows, half), (rows, rest)]
+    return pl.pallas_call(
+        kernel,
+        out_shape=[jax.ShapeDtypeStruct(left.shape, BF), jax.ShapeDtypeStruct(right.shape, BF)],
+        in_specs=[pl.BlockSpec(memory_space=pl.ANY)] * 4,
+        out_specs=[pl.BlockSpec(memory_space=pl.ANY)] * 2,
+        scratch_shapes=[pltpu.VMEM(shape, BF) for shape in scratch]
+        + [pltpu.SemaphoreType.DMA((6,))],
+        input_output_aliases={0: 0, 1: 1},
+        compiler_params=pltpu.CompilerParams(vmem_limit_bytes=VMEM_LIMIT),
+        cost_estimate=pl.CostEstimate(
+            flops=0, bytes_accessed=6 * rows * width, transcendentals=0
+        ),
+    )(left, right, far_a, far_b)
 
 
 class Scatter:
     def __init__(self, own, left, right, far_a, far_b):
         self.parts = own, left, right, far_a, far_b
-        self.parts_half = far_a.shape[1]
-
-    def far(self, axis_of_core, *deps):
-        own, left, right, far_a, far_b = self.parts
-        half = far_a.shape[1]
+        self.half = far_a.shape[1]
+
+    def far(self, axis_of_core, deps):
+        far_a, far_b = self.parts[3:]
         far_a = shift(after(far_a, *deps), axis_of_core, 1)
         far_b = shift(after(far_b, *deps), axis_of_core, -1)
-        right = jnp.concatenate([plus(right[:, :half], far_a).astype(BF), right[:, half:]], axis=1)
-        left = jnp.concatenate([left[:, :half], plus(left[:, half:], far_b).astype(BF)], axis=1)
+        self.got = far_a, far_b
+        return self.got
+
+    def far_sums(self, deps):
+        own, left, right = self.parts[:3]
+        far_a, far_b = after(self.got, *deps)
+        left, right = add_halves(left, right, far_a, far_b)
         self.parts = own, left, right
-        return far_a, far_b
-
-    def near(self, axis_of_core, *deps):
+        return left, right
+
+    def near(self, axis_of_core, deps):
         own, left, right = self.parts
         from_left = shift(after(right, *deps), axis_of_core, 1)
         from_right = shift(after(left, *deps), axis_of_core, -1)
-        self.block = (plus(own, from_left) + from_right.astype(F32)).astype(BF)
-        return (self.block,)
+        self.got = from_left, from_right
+        return self.got
+
+    def near_sums(self, deps):
+        from_left, from_right = after(self.got, *deps)
+        self.block = (plus(self.parts[0], from_left) + from_right.astype(F32)).astype(BF)
+        return self.block
 
     def one(self, *deps):
-        return self.far(SECOND, *deps)
+        return self.far(SECOND, deps)
+
+    def one_sums(self, *deps):
+        return self.far_sums(deps)
 
     def two(self, *deps):
-        done = self.near(SECOND, *deps)
-        own, left, right, far = [self.block[k * 64 : (k + 1) * 64] for k in range(4)]
-        half = self.parts_half
-        self.parts = own, left, right, far[:, :half], far[:, half:]
-        return done
+        return self.near(SECOND, deps)
+
+    def two_sums(self, *deps):
+        block = self.near_sums(deps)
+        own, left, right, far = [block[k * 64 : (k + 1) * 64] for k in range(4)]
+        self.parts = own, left, right, far[:, : self.half], far[:, self.half :]
+        return block
 
     def three(self, *deps):
-        return self.far(FIRST, *deps)
+        return self.far(FIRST, deps)
+
+    def three_sums(self, *deps):
+        return self.far_sums(deps)
 
     def four(self, *deps):
-        return self.near(FIRST, *deps)
+        return self.near(FIRST, deps)
+
+    def four_sums(self, *deps):
+        return self.near_sums(deps)
 
 
 def to_chip(value, place):
@@ -656,8 +724,7 @@
         one_ref[:, GATE_UP + k * D : GATE_UP + (k + 1) * D] = down_ref[k * 32 : (k + 1) * 32, :]
 
 
-def unpack_attn_kernel(meta, ready, *refs):
-    one_ref, two_ref, out_ref = refs
+def unpack_attn_kernel(meta, one_ref, two_ref, out_ref):
     low = meta[YL] == 0
     for k in range(QKV // LANES):
         cols = slice(k * LANES, (k + 1) * LANES)
@@ -667,9 +734,7 @@
     out_ref[:, 3 * D :] = one_ref[:, QKV : QKV + D].astype(F32)
 
 
-def unpack_ffn_kernel(meta, ready, *refs):
-    one_ref, two_ref, *picks = refs[:4]
-    out_ref, down_ref = refs[4:]
+def unpack_ffn_kernel(meta, one_ref, two_ref, picks, out_ref, down_ref):
     low = meta[YL] == 0
     halves = []
     for ref in (one_ref, two_ref):
@@ -755,31 +820,31 @@
     )(meta, *arrays)
 
 
-def place_blocks(blocks, shape):
-    count = len(blocks)
+def place_blocks(*targets):
+    moves = [(i, *block) for i, (blocks, _) in enumerate(targets) for block in blocks]
+    count = len(moves)
 
     def kernel(*refs):
-        out_ref, sems = refs[count], refs[count + 1]
+        out_refs, sems = refs[count:-1], refs[-1]
         copies = []
-        for i, (_, (rows, columns), row, column) in enumerate(blocks):
-            source = refs[i].at[pl.ds(rows[0], rows[1]), pl.ds(columns[0], columns[1])]
-            target = out_ref.at[pl.ds(row, rows[1]), pl.ds(column, columns[1])]
-            copies.append(pltpu.make_async_copy(source, target, sems.at[i]))
+        for k, (i, _, (rows, columns), row, column) in enumerate(moves):
+            source = refs[k].at[pl.ds(rows[0], rows[1]), pl.ds(columns[0], columns[1])]
+            target = out_refs[i].at[pl.ds(row, rows[1]), pl.ds(column, columns[1])]
+            copies.append(pltpu.make_async_copy(source, target, sems.at[k]))
             copies[-1].start()
         for copy in copies:
             copy.wait()
 
+    size = sum(math.prod(shape) for _, shape in targets)
     return pl.pallas_call(
         kernel,
-        out_shape=jax.ShapeDtypeStruct(shape, BF),
+        out_shape=[jax.ShapeDtypeStruct(shape, BF) for _, shape in targets],
         in_specs=[pl.BlockSpec(memory_space=pl.ANY)] * count,
-        out_specs=pl.BlockSpec(memory_space=pltpu.VMEM),
+        out_specs=[pl.BlockSpec(memory_space=pltpu.VMEM)] * len(targets),
         scratch_shapes=[pltpu.SemaphoreType.DMA((count,))],
         compiler_params=pltpu.CompilerParams(vmem_limit_bytes=VMEM_LIMIT),
-        cost_estimate=pl.CostEstimate(
-            flops=0, bytes_accessed=4 * math.prod(shape), transcendentals=0
-        ),
-    )(*[block[0] for block in blocks])
+        cost_estimate=pl.CostEstimate(flops=0, bytes_accessed=4 * size, transcendentals=0),
+    )(*[move[1] for move in moves])
 
 
 def body(frames_in, in_weights, down_weights, gains, cotangent, segment_ids, valid):
@@ -858,38 +923,52 @@
             (one, (rows, (tail + HALF, HALF)), 32, down),
         ]
 
-    def attn_to_owner(block, column, extra):
-        low, high = (0, 32), (32, 32)
-        one = [(block, (low, (column, ATTN)), 0, 0), (block, (high, (column + QKV, HALF)), 0, ATTN)]
-        two = [(block, (high, (column, QKV)), 0, 0)]
-        if extra:
-            columns = (column + ATTN, extra)
-            one.append((block, (low, columns), 0, ATTN + HALF))
-            two.append((block, (high, columns), 0, QKV))
-        one = to_owner(place_blocks(one, (32, ATTN + HALF + extra)), 0)
-        two = to_owner(place_blocks(two, (32, QKV + extra)), 1)
-        sums = plus(one[:, ATTN + HALF :], two[:, QKV:])[:, :4] if extra else None
-        return run(unpack_attn_kernel, meta, [one, two], [((32, 4 * D), F32)], [], 1.8)[0], sums
-
-    def ffn_to_owner(block):
+    def to_owners(block, has_ffn, attn_at, extra):
         low, high, down = (0, 32), (32, 32), GATE_UP + D
-        one = [
-            (block, (low, (0, down)), 0, 0),
-            (block, (high, (GATE_UP, D)), 0, down),
-            (block, (low, (down, HALF)), 0, down + D),
-            (block, (high, (down, HALF)), 0, down + D + HALF),
-        ]
-        one = to_owner(place_blocks(one, (32, GATE_UP + 3 * D)), 0)
-        two = to_owner(place_blocks([(block, (high, (0, GATE_UP)), 0, 0)], (32, GATE_UP)), 1)
-        units, down = run(
-            unpack_ffn_kernel,
-            meta,
-            [one, two, *picks],
-            [((32, 4 * PAIR), F32), ((96, D), F32)],
-            [],
-            4.5,
-        )
-        return units, down[:88]
+        one, two, outs, kernels = [], [], [], []
+        if has_ffn:
+            one = [
+                (block, (low, (0, down)), 0, 0),
+                (block, (high, (GATE_UP, D)), 0, down),
+                (block, (low, (down, HALF)), 0, down + D),
+                (block, (high, (down, HALF)), 0, down + D + HALF),
+            ]
+            two = [(block, (high, (0, GATE_UP)), 0, 0)]
+            outs += [((32, 4 * PAIR), F32), ((96, D), F32)]
+        wide, narrow = (GATE_UP + 3 * D, GATE_UP) if has_ffn else (0, 0)
+        first, second = wide, narrow
+        if attn_at is not None:
+            one += [(block, (low, (attn_at, ATTN)), 0, wide)]
+            one += [(block, (high, (attn_at + QKV, HALF)), 0, wide + ATTN)]
+            two += [(block, (high, (attn_at, QKV)), 0, narrow)]
+            wide, narrow = wide + ATTN + HALF, narrow + QKV
+            if extra:
+                columns = (attn_at + ATTN, extra)
+                one.append((block, (low, columns), 0, wide))
+                two.append((block, (high, columns), 0, narrow))
+                wide, narrow = wide + extra, narrow + extra
+            outs += [((32, 4 * D), F32)]
+        one, two = place_blocks((one, (32, wide)), (two, (32, narrow)))
+        one, two = to_owner(one, 0), to_owner(two, 1)
+        sums = plus(one[:, wide - extra :], two[:, narrow - extra :])[:, :4] if extra else None
+
+        def kernel(meta_ref, ready, one_ref, two_ref, *refs):
+            if has_ffn:
+                pick_refs, refs = refs[:2], refs[2:]
+                unpack_ffn_kernel(meta_ref, one_ref, two_ref, pick_refs, refs[0], refs[1])
+                refs = refs[2:]
+            if attn_at is not None:
+                cols = pl.ds(first, ATTN + HALF), pl.ds(second, QKV)
+                attn_refs = one_ref.at[:, cols[0]], two_ref.at[:, cols[1]]
+                unpack_attn_kernel(meta_ref, *attn_refs, refs[0])
+
+        operands = [one, two, *picks] if has_ffn else [one, two]
+        results = list(run(kernel, meta, operands, outs, [], 5.0 if has_ffn else 1.8))
+        if has_ffn:
+            results[1] = results[1][:88]
+        if attn_at is not None:
+            results.append(sums)
+        return results
 
     gain_rows = gains[:, 0].transpose(1, 2, 0).reshape(4, D)
 
@@ -903,7 +982,7 @@
     marked = jnp.concatenate([frames_in[:, 0], jnp.pad(marks, ((0, 0), (0, LANES - 2)))], axis=1)
 
     attn0 = pack_attn(in_weights[:, 0, 0, : 4 * D])
-    attn0 = Gather(place_blocks(attn_blocks(*attn0, 0), (64, ATTN)))
+    attn0 = Gather(place_blocks((attn_blocks(*attn0, 0), (64, ATTN)))[0])
     attn0.one()
     later = after(in_weights, attn0.piece)
     ffn0_parts = pack_ffn(later[:, 0, 0, 4 * D :], down_weights[:, 0, 0], None)
@@ -912,11 +991,11 @@
     attn0_three = attn0.three()
     blocks = ffn_blocks(*ffn0_parts)
     blocks += attn_blocks(*after(tuple(attn1_parts), blocks[0][0]), FFN)
-    middle0 = Gather(place_blocks(blocks, (64, FFN + ATTN)))
+    middle0 = Gather(place_blocks((blocks, (64, FFN + ATTN)))[0])
     later = after(in_weights, *attn1_parts)
     ffn1_parts = pack_ffn(later[:, 0, 1, 4 * D :], down_weights[:, 0, 1], counts)
     blocks = ffn_blocks(*after(tuple(ffn1_parts), blocks[-1][0]))
-    ffn1 = Gather(place_blocks(blocks, (64, FFN)))
+    ffn1 = Gather(place_blocks((blocks, (64, FFN)))[0])
     marked = frames_to_chip(after(marked, blocks[0][0]))
     state = marked[:, :D]
     marks = marked[:, D:]
@@ -1030,7 +1109,7 @@
             + gradient_blocks(FFN if last else FFN + ATTN),
             [(TOKENS, D), (TOKENS, GATE_UP), (TOKENS, D)],
             18.0,
-            () if last else above_three,
+            () if last else (middle_above,),
         )
         grad, *results = results
         if not last:
@@ -1038,13 +1117,12 @@
         partial, *pieces = results
         if last:
             ffn_above = Scatter(*pieces)
-            above_one = ffn_above.one()
-            above_two = ffn_above.two()
-            above_three = ffn_above.three()
-            above_four = ffn_above.four()
+            ffn_above.one()
         else:
             ffn_sum = Scatter(*pieces)
-            ffn_one = ffn_sum.one()
+            ffn_sum.one()
+            ffn_above.three_sums(partial)
+            ffn_above.four()
         other = other_core(partial)
         grad, gain_list[layer][1], out_terms, *mixed = run(
             out_backward_kernel,
@@ -1053,19 +1131,18 @@
             [wide, row, ((D, HALF), BF)] + [((ROWS, HALF), BF)] * 4,
             [(TOKENS, D), (TOKENS, HALF)],
             5.8,
-            () if last else above_four,
         )
+        sums = (ffn_above if last else ffn_sum).one_sums(mixed[0])
         mixed = exchange_column(mixed)
-        if not last:
-            ffn_two = ffn_sum.two()
+        (ffn_above if last else ffn_sum).two()
         grads = run(
             attend_backward_kernel,
             meta,
             [*blocks, *mixed],
             [((ROWS, QKV), BF)] * 4,
             [(POS, ROWS, QKV), (POS, ROWS, HALF), (POS, ROWS, QKV)],
-            3.8,
-            above_one if last else ffn_one,
+            3.8 if last else 1.14,
+            sums,
         )
         own = grads[0]
         grads = exchange_column(grads)
@@ -1079,27 +1156,34 @@
             + windows(attn, at, at + QKV),
             [wide16] + ([((D, ATTN), BF)] if last else gradient_blocks(ATTN_GAINS)),
             [(TOKENS, QKV), (TOKENS, D)],
-            10.0,
+            10.0 if last else 3,
         )
         if last:
             attn_above = pieces[0]
+            middle_above = ffn_above.two_sums()
+            ffn_above.three()
         else:
             attn_sum = Scatter(*pieces)
             attn_sum.one()
         base = (grad, partial, other_core(partial), state, gain_row(layer, 0))
-    input_grad = run(last_kernel, meta, list(base), [wide16], [], 4.3, ffn_two)[0]
+    middle = ffn_sum.two_sums()
     ffn_sum.three()
-    attn_sum.two(ffn_two)
+    attn_sum.one_sums()
+    attn_sum.two(middle)
+    ffn_sum.three_sums()
     ffn_sum.four()
-    last_sums = attn_sum.three()
-    units_above, down_list[1] = ffn_to_owner(ffn_above.block)
+    middle = attn_sum.two_sums()
+    attn_sum.three()
+    input_grad = run(last_kernel, meta, list(base), [wide16], [], 4.3, (middle,))[0]
+    units_above, down_list[1] = to_owners(
+        after(ffn_above.four_sums(), partial), True, None, 0
+    )
+    last_sums = attn_sum.three_sums()
     attn_sum.four()
-    both = after(ffn_sum.block, last_sums)
-    attn_part, _ = attn_to_owner(both, FFN, 0)
-    in_parts = [None, [attn_part, units_above]]
-    units, down_list[0] = ffn_to_owner(both)
-    attn_part, gain_sums = attn_to_owner(attn_sum.block, 0, LANES)
-    in_parts[0] = [attn_part, units]
+    both = after(ffn_sum.four_sums(), last_sums)
+    units, down_list[0], attn_above, _ = to_owners(both, True, FFN, 0)
+    attn, gain_sums = to_owners(attn_sum.four_sums(), False, 0, LANES)
+    in_parts = [[attn, units], [attn_above, units_above]]
     in_list = [jnp.concatenate(parts, axis=1) for parts in in_parts]
     in_grads = jnp.stack(in_list, axis=1)[:, None]
     down_grads = jnp.stack(down_list, axis=1)[:, None]

time: 559 us -> 558 us (level)
  the two profiles are of different devices: /device:TPU:1 before, /device:TPU:62 now
where the time goes in v4:
time: 558 us; the launch traced here: 548 us
  Pallas kernels  197 us (35%)
  starting transfers between devices  146 us (26%)
  waiting for transfers between devices  125 us (22%)
  local copies, waits for them, and re-layouts  52.7 us (9%)
  other arithmetic  24.3 us (4%)
    pallas_call x24, Pallas kernels, run(): pl.pallas_call(whole, out_shape=[jax.ShapeDtypeStruct(shape, dtype) for s...  159 us
    ppermute x48, starting transfers between devices, shift(): return lax.ppermute(value, PLANE, ring_pairs(axis_of_core, step))  73.9 us
    ppermute x48, waiting for transfers between devices, shift(): return lax.ppermute(value, PLANE, ring_pairs(axis_of_core, step))  66.2 us
    ppermute x24, starting transfers between devices, exchange_column(): lax.ppermute(blocks[k], COLUMN, [(y, y ^ k) for y in range(POS)])  33.6 us
    unnamed x201, local copies, waits for them, and re-layouts  33.1 us
    ppermute x24, waiting for transfers between devices, exchange_column(): lax.ppermute(blocks[k], COLUMN, [(y, y ^ k) for y in range(POS)])  30.7 us
    ppermute x13, starting transfers between devices, to_chip(): return lax.ppermute(value, ('c', 'yl'), pairs)  22.8 us
    pallas_call x9, Pallas kernels, place_blocks(): pl.pallas_call(kernel, out_shape=[jax.ShapeDtypeStruct(shape, BF) for _,...  20.6 us
  transfers between devices with their start and end apart: 102, of which 39 were waited for; matrix products, arithmetic and copies ran while one was open for 7% of the time, Pallas kernels for 26%

profile of v4, /device:TPU:62, one launch (start us, length us, event | category | flops | bytes accessed | tf_op | source)
XLA Modules:
  0.0 548.0 jit_solution(17154863863687380366)
XLA Ops:
  19.6 4.1 shard_map.130
  45.1 4.1 shard_map.132
  49.7 3.8 collective-permute-start.4
  66.2 3.8 collective-permute-done.12.refs_5_.refs_13_
  70.0 3.5 collective-permute-start.15
  76.8 3.7 collective-permute-start.27
  87.6 3.8 shard_map.138.refs_6_.refs_4_.refs_7_.refs_11_
  99.1 3.4 collective-permute-start.5
  109.9 7.8 %shard_map.134 = (f32[256,1024]{1,0:T(8,128)}, bf16[1024,256]{1,0:T(8,128)(2,1)}, bf16[64,1536]{1,0:T(8,128)(2,1)}, bf16[64,1536]{1,0:T(8,128)(2,1)}, bf16[64,15...) custom-call(s32[18]{0:T(128)} %pad_add_fusion.meta_ref, bf16[256,1024]{1,0:T(8,128)(2,1)} %fusion.3.refs_0_, ...), custom_call_target="tpu_custom_call" | custom-call | flops 15399999488 | bytes 26180000 | tf_op jit(solution)/shard_map/pallas_call | solution.py:810
  122.4 10.9 %collective-permute-done.35.refs_8_.refs_6_.refs_9_.refs_13_ = bf16[256,6656]{1,0:T(8,128)(2,1)S(1)} collective-permute-done((bf16[256,6656]{1,0:T(8,128)(2,1)}, bf16[256,6656]{1,0:T(8,128)(2,1)S(1)}, u32[]{:S(2)}, u32[]{:S(2)}) %collective-permute-start.35) | collective-permute-done | bytes 3407904 | tf_op jit(solution)/shard_map/ppermute | solution.py:69
  151.7 3.5 shard_map.136
  159.8 14.9 %shard_map.141 = (f32[256,1024]{1,0:T(8,128)}, bf16[1024,256]{1,0:T(8,128)(2,1)}, f32[256,1536]{1,0:T(8,128)}, f32[256,1536]{1,0:T(8,128)}, bf16[1536,256]{1,0:T...) custom-call(s32[18]{0:T(128)} %pad_add_fusion.meta_ref, ...), custom_call_target="tpu_custom_call" | custom-call | flops 30000001024 | bytes 51000000 | tf_op jit(solution)/shard_map/pallas_call | solution.py:810
  179.2 8.2 %shard_map.142 = (f32[256,1024]{1,0:T(8,128)}, bf16[1024,256]{1,0:T(8,128)(2,1)}, bf16[64,1536]{1,0:T(8,128)(2,1)}, bf16[64,1536]{1,0:T(8,128)(2,1)}, bf16[64,15...) custom-call(s32[18]{0:T(128)} %pad_add_fusion.meta_ref, f32[256,1024]{1,0:T(8,128)} %get-tuple-element.195.refs_0_.refs_3_, ...), custom_call_target="tpu_custom_call" | custom-call | flops 15399999488 | bytes 26180000 | tf_op jit(solution)/shard_map/pallas_call | solution.py:810
  195.4 4.8 collective-permute-done.40.refs_2_
  206.5 3.6 collective-permute-start.43
  216.4 3.6 shard_map.144
  220.1 3.6 collective-permute-start.52
  224.4 4.3 collective-permute-done.52
  231.8 14.7 %shard_map.145 = (f32[256,1024]{1,0:T(8,128)}, bf16[1024,256]{1,0:T(8,128)(2,1)}, f32[256,1536]{1,0:T(8,128)}, f32[256,1536]{1,0:T(8,128)}, bf16[1536,256]{1,0:T...) custom-call(s32[18]{0:T(128)} %pad_add_fusion.meta_ref, ...), custom_call_target="tpu_custom_call" | custom-call | flops 30000001024 | bytes 51000000 | tf_op jit(solution)/shard_map/pallas_call | solution.py:810
  248.8 15.1 %shard_map.146 = (f32[256,1024]{1,0:T(8,128)}, bf16[256,1024]{1,0:T(8,128)(2,1)}, bf16[256,4608]{1,0:T(8,128)(2,1)}, bf16[256,4608]{1,0:T(8,128)(2,1)}, bf16[256...) custom-call(s32[18]{0:T(128)} %pad_add_fusion.meta_ref, ...), custom_call_target="tpu_custom_call" | custom-call | flops 35999997952 | bytes 61200000 | tf_op jit(solution)/shard_map/pallas_call | solution.py:810
  268.1 5.8 %shard_map.147 = (f32[256,1024]{1,0:T(8,128)}, f32[1,1024]{1,0:T(1,128)}, bf16[1024,512]{1,0:T(8,128)(2,1)}, bf16[64,512]{1,0:T(8,128)(2,1)}, bf16[64,512]{1,0:T...) custom-call(s32[18]{0:T(128)} %pad_add_fusion.meta_ref, f32[256,1024]{1,0:T(8,128)} %get-tuple-element.217.refs_0_, ...), custom_call_target="tpu_custom_call" | custom-call | flops 11600000000 | bytes 19720000 | tf_op jit(solution)/shard_map/pallas_call | solution.py:810
  284.3 3.8 shard_map.148
  292.8 3.8 shard_map.149
  297.9 3.4 collective-permute-start.63
  304.3 3.6 collective-permute-done.62.refs_2_
  311.4 8.7 %shard_map.150 = (bf16[256,1024]{1,0:T(8,128)(2,1)}, bf16[1024,2048]{1,0:T(8,128)(2,1)}) custom-call(s32[18]{0:T(128)} %pad_add_fusion.meta_ref, bf16[64,1536]{1,0:T(8,128)(2,1)} %get-tuple-element.235.refs_0_, bf16[64,1536]{1,0:T(8,128)(2,1)} %copy-done.77, bf16[64,1536]{1,0:T(8,128)(2,1)} %copy-done.78, bf16[64,1536]{1,0:T(8,128)(2,1)} %copy-done.80, ...), custom_call_target="tpu_custom_call" | custom-call | flops 20000000000 | bytes 34000000 | tf_op jit(solution)/shard_map/pallas_call | solution.py:810
  325.8 18.9 %shard_map.151 = (f32[256,1024]{1,0:T(8,128)}, f32[1,1024]{1,0:T(1,128)}, bf16[256,1024]{1,0:T(8,128)(2,1)}, bf16[256,6656]{1,0:T(8,128)(2,1)}, bf16[256,6656]{1...) custom-call(s32[18]{0:T(128)} %pad_add_fusion.meta_ref, ...), custom_call_target="tpu_custom_call" | custom-call | flops 35999997952 | bytes 61200000 | tf_op jit(solution)/shard_map/pallas_call | solution.py:810
  354.5 4.0 collective-permute-done.97.b_ref
  361.4 3.4 collective-permute-start.98
  365.6 5.8 %shard_map.152 = (f32[256,1024]{1,0:T(8,128)}, f32[1,1024]{1,0:T(1,128)}, bf16[1024,512]{1,0:T(8,128)(2,1)}, bf16[64,512]{1,0:T(8,128)(2,1)}, bf16[64,512]{1,0:T...) custom-call(s32[18]{0:T(128)} %pad_add_fusion.meta_ref, f32[256,1024]{1,0:T(8,128)} %get-tuple-element.251.refs_0_, ...), custom_call_target="tpu_custom_call" | custom-call | flops 11600000000 | bytes 19720000 | tf_op jit(solution)/shard_map/pallas_call | solution.py:810
  371.5 7.7 %collective-permute-done.99 = bf16[64,4608]{1,0:T(8,128)(2,1)S(1)} collective-permute-done((bf16[64,4608]{1,0:T(8,128)(2,1)}, bf16[64,4608]{1,0:T(8,128)(2,1)S(1)}, u32[]{:S(2)}, u32[]{:S(2)}) %collective-permute-start.99) | collective-permute-done | bytes 589856 | tf_op jit(solution)/shard_map/ppermute | solution.py:69
  381.0 4.7 shard_map.153
  390.7 3.7 shard_map.154
  407.7 11.3 %shard_map.155 = (bf16[256,1024]{1,0:T(8,128)(2,1)}, bf16[256,2176]{1,0:T(8,128)(2,1)}, bf16[256,2176]{1,0:T(8,128)(2,1)}, bf16[256,2176]{1,0:T(8,128)(2,1)}, bf...) custom-call(s32[18]{0:T(128)} %pad_add_fusion.meta_ref, bf16[64,1536]{1,0:T(8,128)(2,1)} %get-tuple-element.268.refs_0_, ...), custom_call_target="tpu_custom_call" | custom-call | flops 6000000000 | bytes 10200000 | tf_op jit(solution)/shard_map/pallas_call | solution.py:810
  424.8 6.1 %collective-permute-done.101.refs_1_ = bf16[32,3072]{1,0:T(8,128)(2,1)S(1)} collective-permute-done((bf16[32,3072]{1,0:T(8,128)(2,1)}, bf16[32,3072]{1,0:T(8,128)(2,1)S(1)}, u32[]{:S(2)}, u32[]{:S(2)}) %collective-permute-start.101) | collective-permute-done | bytes 196640 | tf_op jit(solution)/shard_map/ppermute | solution.py:232
  435.6 4.9 shard_map.166
  448.6 4.3 add_convert_fusion
  459.1 6.0 %collective-permute-done.90.a_ref = bf16[64,3328]{1,0:T(8,128)(2,1)} collective-permute-done((bf16[64,3328]{1,0:T(8,128)(2,1)S(1)}, bf16[64,3328]{1,0:T(8,128)(2,1)}, u32[]{:S(2)}, u32[]{:S(2)}) %collective-permute-start.90) | collective-permute-done | bytes 426016 | tf_op jit(solution)/shard_map/ppermute | solution.py:69
  465.1 3.9 collective-permute-done.91.b_ref
  474.6 6.2 %collective-permute-done.82 = bf16[256,2176]{1,0:T(8,128)(2,1)S(1)} collective-permute-done((bf16[256,2176]{1,0:T(8,128)(2,1)S(1)}, bf16[256,2176]{1,0:T(8,128)(2,1)S(1)}, u32[]{:S(2)}, u32[]{:S(2)}) %collective-permute-start.82) | collective-permute-done | bytes 1114144 | tf_op jit(solution)/shard_map/ppermute | solution.py:69
  483.5 5.9 %collective-permute-start.84 = (bf16[64,1024]{1,0:T(8,128)(2,1)S(1)}, bf16[64,1024]{1,0:T(8,128)(2,1)S(1)}, u32[]{:S(2)}, u32[]{:S(2)}) collective-permute-start(bf16[64,1024]{1,0:T(8,128)(2,1)S(1)} %slice.233), channel_id=1, source_target_pairs={{0,1},{1,2},{2,3},{3,0},{8,9},{9,10},{10,11},{11,8},{16,17},{17,18... | collective-permute-start | bytes 393224 | tf_op jit(solution)/shard_map/ppermute | solution.py:69
  492.0 3.8 collective-permute-done.85.b_ref
  501.7 4.2 shard_map.157
  512.5 3.6 collective-permute-start.88
  525.6 4.2 collective-permute-done.95.refs_1_
  529.7 4.2 collective-permute-done.94.refs_0_
  534.7 5.1 shard_map.163
  542.8 3.4 copy.55
  (465 shorter events, 265.6 us)
Async XLA Ops:
  15.4 12.9 %collective-permute-start.9 = (bf16[64,2048]{1,0:T(8,128)(2,1)}, bf16[64,2048]{1,0:T(8,128)(2,1)S(1)}, u32[]{:S(2)}, u32[]{:S(2)}) collective-permute-start(bf16[64,2048]{1,0:T(8,128)(2,1)} %shard_map.129.refs_0_), channel_id=1, source_target_pairs={{0,3},{1,0},{2,1},{3,2},{8,11},{9,8},{10,9},{11,10},{16,19},{17,16... | collective-permute-start | bytes 786440 | tf_op jit(solution)/shard_map/ppermute | solution.py:69
  23.7 17.0 %collective-permute-start.23 = (bf16[32,3072]{1,0:T(8,128)(2,1)}, bf16[32,3072]{1,0:T(8,128)(2,1)S(1)}, u32[]{:S(2)}, u32[]{:S(2)}) collective-permute-start(bf16[32,3072]{1,0:T(8,128)(2,1)} %get-tuple-element.169), channel_id=1, source_target_pairs={{0,32},{4,0},{32,36},{36,4},{1,33},{5,1},{33,37},{37,5},{2,34},{6,... | collective-permute-start | bytes 589832 | tf_op jit(solution)/shard_map/ppermute | solution.py:227
  39.8 26.3 %collective-permute-start.13 = (bf16[256,2048]{1,0:T(8,128)(2,1)}, bf16[256,2048]{1,0:T(8,128)(2,1)S(1)}, u32[]{:S(2)}, u32[]{:S(2)}) collective-permute-start(bf16[256,2048]{1,0:T(8,128)(2,1)} %shard_map.133.refs_4_.refs_12_), channel_id=1, source_target_pairs={{0,24},{1,25},{2,26},{3,27},{8,0},{9,1},{10,2},{11,3},{16,8},{17,9... | collective-permute-start | bytes 3145736 | tf_op jit(solution)/shard_map/ppermute | solution.py:69
  44.2 18.8 %collective-permute-start.26 = (bf16[64,6656]{1,0:T(8,128)(2,1)}, bf16[64,6656]{1,0:T(8,128)(2,1)S(1)}, u32[]{:S(2)}, u32[]{:S(2)}) collective-permute-start(bf16[64,6656]{1,0:T(8,128)(2,1)} %shard_map.137.refs_0_), channel_id=1, source_target_pairs={{0,3},{1,0},{2,1},{3,2},{8,11},{9,8},{10,9},{11,10},{16,19},{17,16... | collective-permute-start | bytes 2555912 | tf_op jit(solution)/shard_map/ppermute | solution.py:69
  49.2 20.8 %collective-permute-start.12 = (bf16[256,2048]{1,0:T(8,128)(2,1)S(1)}, bf16[256,2048]{1,0:T(8,128)(2,1)S(1)}, u32[]{:S(2)}, u32[]{:S(2)}) collective-permute-start(bf16[256,2048]{1,0:T(8,128)(2,1)S(1)} %copy-done.23), channel_id=1, source_target_pairs={{0,8},{1,9},{2,10},{3,11},{8,16},{9,17},{10,18},{11,19},{16,24},{1... | collective-permute-start | bytes 3145736 | tf_op jit(solution)/shard_map/ppermute | solution.py:69
  53.5 20.9 %collective-permute-start.25 = (bf16[64,6656]{1,0:T(8,128)(2,1)S(1)}, bf16[64,6656]{1,0:T(8,128)(2,1)S(1)}, u32[]{:S(2)}, u32[]{:S(2)}) collective-permute-start(bf16[64,6656]{1,0:T(8,128)(2,1)S(1)} %copy-done.5), channel_id=1, source_target_pairs={{0,1},{1,2},{2,3},{3,0},{8,9},{9,10},{10,11},{11,8},{16,17},{17,18... | collective-permute-start | bytes 2555912 | tf_op jit(solution)/shard_map/ppermute | solution.py:69
  62.0 14.7 %collective-permute-start.32 = (bf16[64,4608]{1,0:T(8,128)(2,1)}, bf16[64,4608]{1,0:T(8,128)(2,1)S(1)}, u32[]{:S(2)}, u32[]{:S(2)}) collective-permute-start(bf16[64,4608]{1,0:T(8,128)(2,1)} %shard_map.139.refs_0_), channel_id=1, source_target_pairs={{0,3},{1,0},{2,1},{3,2},{8,11},{9,8},{10,9},{11,10},{16,19},{17,16... | collective-permute-start | bytes 1769480 | tf_op jit(solution)/shard_map/ppermute | solution.py:69
  63.0 17.5 %collective-permute-start.30 = (bf16[64,4608]{1,0:T(8,128)(2,1)}, bf16[64,4608]{1,0:T(8,128)(2,1)S(1)}, u32[]{:S(2)}, u32[]{:S(2)}) collective-permute-start(bf16[64,4608]{1,0:T(8,128)(2,1)} %shard_map.139.refs_0_), channel_id=1, source_target_pairs={{0,1},{1,2},{2,3},{3,0},{8,9},{9,10},{10,11},{11,8},{16,17},{17,18... | collective-permute-start | bytes 1769480 | tf_op jit(solution)/shard_map/ppermute | solution.py:69
  66.1 17.5 %collective-permute-start.28 = (bf16[64,3328]{1,0:T(8,128)(2,1)}, bf16[64,3328]{1,0:T(8,128)(2,1)}, u32[]{:S(2)}, u32[]{:S(2)}) collective-permute-start(bf16[64,3328]{1,0:T(8,128)(2,1)} %slice.217), channel_id=1, source_target_pairs={{0,3},{1,0},{2,1},{3,2},{8,11},{9,8},{10,9},{11,10},{16,19},{17,16... | collective-permute-start | bytes 1277960 | tf_op jit(solution)/shard_map/ppermute | solution.py:69
  70.0 21.4 %collective-permute-start.15 = (bf16[256,1024]{1,0:T(8,128)(2,1)S(1)}, bf16[256,1024]{1,0:T(8,128)(2,1)}, u32[]{:S(2)}, u32[]{:S(2)}) collective-permute-start(bf16[256,1024]{1,0:T(8,128)(2,1)S(1)} %slice.214), channel_id=1, source_target_pairs={{0,24},{1,25},{2,26},{3,27},{8,0},{9,1},{10,2},{11,3},{16,8},{17,9... | collective-permute-start | bytes 1572872 | tf_op jit(solution)/shard_map/ppermute | solution.py:69
  74.4 17.7 %collective-permute-start.14 = (bf16[256,1024]{1,0:T(8,128)(2,1)}, bf16[256,1024]{1,0:T(8,128)(2,1)}, u32[]{:S(2)}, u32[]{:S(2)}) collective-permute-start(bf16[256,1024]{1,0:T(8,128)(2,1)} %slice.213), channel_id=1, source_target_pairs={{0,8},{1,9},{2,10},{3,11},{8,16},{9,17},{10,18},{11,19},{16,24},{1... | collective-permute-start | bytes 1572872 | tf_op jit(solution)/shard_map/ppermute | solution.py:69
  92.2 41.1 %collective-permute-start.35 = (bf16[256,6656]{1,0:T(8,128)(2,1)}, bf16[256,6656]{1,0:T(8,128)(2,1)S(1)}, u32[]{:S(2)}, u32[]{:S(2)}) collective-permute-start(bf16[256,6656]{1,0:T(8,128)(2,1)} %shard_map.138.refs_6_.refs_4_.refs_7_.refs_11_), channel_id=1, source_target_pairs={{0,24},{1,25},{2,26},{3,27},{8,0},{9,1},{10,2},{11,3},{16,8},{17,9... | collective-permute-start | bytes 10223624 | tf_op jit(solution)/shard_map/ppermute | solution.py:69
  95.5 40.5 %collective-permute-start.34 = (bf16[256,6656]{1,0:T(8,128)(2,1)}, bf16[256,6656]{1,0:T(8,128)(2,1)}, u32[]{:S(2)}, u32[]{:S(2)}) collective-permute-start(bf16[256,6656]{1,0:T(8,128)(2,1)} %shard_map.138.refs_6_.refs_4_.refs_7_.refs_11_), channel_id=1, source_target_pairs={{0,8},{1,9},{2,10},{3,11},{8,16},{9,17},{10,18},{11,19},{16,24},{1... | collective-permute-start | bytes 10223624 | tf_op jit(solution)/shard_map/ppermute | solution.py:69
  117.6 20.0 %collective-permute-start.16 = (bf16[64,1536]{1,0:T(8,128)(2,1)}, bf16[64,1536]{1,0:T(8,128)(2,1)S(1)}, u32[]{:S(2)}, u32[]{:S(2)}) collective-permute-start(bf16[64,1536]{1,0:T(8,128)(2,1)} %get-tuple-element.184), channel_id=1, source_target_pairs={{0,4},{4,0},{64,68},{68,64},{1,5},{5,1},{65,69},{69,65},{2,6},{6,2... | collective-permute-start | bytes 589832 | tf_op jit(solution)/shard_map/ppermute | solution.py:246
  117.7 19.9 %collective-permute-start.17 = (bf16[64,1536]{1,0:T(8,128)(2,1)}, bf16[64,1536]{1,0:T(8,128)(2,1)S(1)}, u32[]{:S(2)}, u32[]{:S(2)}) collective-permute-start(bf16[64,1536]{1,0:T(8,128)(2,1)} %get-tuple-element.185), channel_id=1, source_target_pairs={{0,64},{4,68},{64,0},{68,4},{1,65},{5,69},{65,1},{69,5},{2,66},{6,... | collective-permute-start | bytes 589832 | tf_op jit(solution)/shard_map/ppermute | solution.py:246
  119.1 18.6 %collective-permute-start.18 = (bf16[64,1536]{1,0:T(8,128)(2,1)}, bf16[64,1536]{1,0:T(8,128)(2,1)S(1)}, u32[]{:S(2)}, u32[]{:S(2)}) collective-permute-start(bf16[64,1536]{1,0:T(8,128)(2,1)} %get-tuple-element.186), channel_id=1, source_target_pairs={{0,68},{4,64},{64,4},{68,0},{1,69},{5,65},{65,5},{69,1},{2,70},{6,... | collective-permute-start | bytes 589832 | tf_op jit(solution)/shard_map/ppermute | solution.py:246
  133.5 25.0 %collective-permute-start.37 = (bf16[256,3328]{1,0:T(8,128)(2,1)S(1)}, bf16[256,3328]{1,0:T(8,128)(2,1)}, u32[]{:S(2)}, u32[]{:S(2)}) collective-permute-start(bf16[256,3328]{1,0:T(8,128)(2,1)S(1)} %slice.221), channel_id=1, source_target_pairs={{0,24},{1,25},{2,26},{3,27},{8,0},{9,1},{10,2},{11,3},{16,8},{17,9... | collective-permute-start | bytes 5111816 | tf_op jit(solution)/shard_map/ppermute | solution.py:69
  137.5 22.3 %collective-permute-start.36 = (bf16[256,3328]{1,0:T(8,128)(2,1)S(1)}, bf16[256,3328]{1,0:T(8,128)(2,1)}, u32[]{:S(2)}, u32[]{:S(2)}) collective-permute-start(bf16[256,3328]{1,0:T(8,128)(2,1)S(1)} %slice.220), channel_id=1, source_target_pairs={{0,8},{1,9},{2,10},{3,11},{8,16},{9,17},{10,18},{11,19},{16,24},{1... | collective-permute-start | bytes 5111816 | tf_op jit(solution)/shard_map/ppermute | solution.py:69
  175.1 36.1 %collective-permute-start.47 = (bf16[256,4608]{1,0:T(8,128)(2,1)S(1)}, bf16[256,4608]{1,0:T(8,128)(2,1)S(1)}, u32[]{:S(2)}, u32[]{:S(2)}) collective-permute-start(bf16[256,4608]{1,0:T(8,128)(2,1)S(1)} %copy-done.8), channel_id=1, source_target_pairs={{0,24},{1,25},{2,26},{3,27},{8,0},{9,1},{10,2},{11,3},{16,8},{17,9... | collective-permute-start | bytes 7077896 | tf_op jit(solution)/shard_map/ppermute | solution.py:69
  178.4 35.7 %collective-permute-start.46 = (bf16[256,4608]{1,0:T(8,128)(2,1)S(1)}, bf16[256,4608]{1,0:T(8,128)(2,1)}, u32[]{:S(2)}, u32[]{:S(2)}) collective-permute-start(bf16[256,4608]{1,0:T(8,128)(2,1)S(1)} %copy-done.8), channel_id=1, source_target_pairs={{0,8},{1,9},{2,10},{3,11},{8,16},{9,17},{10,18},{11,19},{16,24},{1... | collective-permute-start | bytes 7077896 | tf_op jit(solution)/shard_map/ppermute | solution.py:69
  211.2 17.6 %collective-permute-start.49 = (bf16[256,2304]{1,0:T(8,128)(2,1)S(1)}, bf16[256,2304]{1,0:T(8,128)(2,1)S(1)}, u32[]{:S(2)}, u32[]{:S(2)}) collective-permute-start(bf16[256,2304]{1,0:T(8,128)(2,1)S(1)} %slice.225), channel_id=1, source_target_pairs={{0,24},{1,25},{2,26},{3,27},{8,0},{9,1},{10,2},{11,3},{16,8},{17,9... | collective-permute-start | bytes 3538952 | tf_op jit(solution)/shard_map/ppermute | solution.py:69
  215.4 16.4 %collective-permute-start.48 = (bf16[256,2304]{1,0:T(8,128)(2,1)S(1)}, bf16[256,2304]{1,0:T(8,128)(2,1)}, u32[]{:S(2)}, u32[]{:S(2)}) collective-permute-start(bf16[256,2304]{1,0:T(8,128)(2,1)S(1)} %slice.224), channel_id=1, source_target_pairs={{0,8},{1,9},{2,10},{3,11},{8,16},{9,17},{10,18},{11,19},{16,24},{1... | collective-permute-start | bytes 3538952 | tf_op jit(solution)/shard_map/ppermute | solution.py:69
  247.4 19.7 %collective-permute-start.50 = (bf16[256,1024]{1,0:T(8,128)(2,1)}, bf16[256,1024]{1,0:T(8,128)(2,1)S(1)}, u32[]{:S(2)}, u32[]{:S(2)}) collective-permute-start(bf16[256,1024]{1,0:T(8,128)(2,1)} %get-tuple-element.209), channel_id=1, source_target_pairs={{0,32},{32,0},{1,33},{33,1},{2,34},{34,2},{3,35},{35,3},{4,36},{36... | collective-permute-start | bytes 1572872 | tf_op jit(solution)/shard_map/ppermute | solution.py:236
  264.1 17.3 %collective-permute-start.59 = (bf16[256,2304]{1,0:T(8,128)(2,1)}, bf16[256,2304]{1,0:T(8,128)(2,1)S(1)}, u32[]{:S(2)}, u32[]{:S(2)}) collective-permute-start(bf16[256,2304]{1,0:T(8,128)(2,1)} %get-tuple-element.228), channel_id=1, source_target_pairs={{0,8},{1,9},{2,10},{3,11},{8,16},{9,17},{10,18},{11,19},{16,24},{1... | collective-permute-start | bytes 3538952 | tf_op jit(solution)/shard_map/ppermute | solution.py:69
  264.1 19.2 %collective-permute-start.60 = (bf16[256,2304]{1,0:T(8,128)(2,1)}, bf16[256,2304]{1,0:T(8,128)(2,1)S(1)}, u32[]{:S(2)}, u32[]{:S(2)}) collective-permute-start(bf16[256,2304]{1,0:T(8,128)(2,1)} %get-tuple-element.229), channel_id=1, source_target_pairs={{0,24},{1,25},{2,26},{3,27},{8,0},{9,1},{10,2},{11,3},{16,8},{17,9... | collective-permute-start | bytes 3538952 | tf_op jit(solution)/shard_map/ppermute | solution.py:69
  273.9 14.9 %collective-permute-start.56 = (bf16[64,512]{1,0:T(8,128)(2,1)}, bf16[64,512]{1,0:T(8,128)(2,1)S(1)}, u32[]{:S(2)}, u32[]{:S(2)}) collective-permute-start(bf16[64,512]{1,0:T(8,128)(2,1)} %get-tuple-element.223), channel_id=1, source_target_pairs={{0,4},{4,0},{64,68},{68,64},{1,5},{5,1},{65,69},{69,65},{2,6},{6,2... | collective-permute-start | bytes 196616 | tf_op jit(solution)/shard_map/ppermute | solution.py:246
  273.9 17.6 %collective-permute-start.57 = (bf16[64,512]{1,0:T(8,128)(2,1)}, bf16[64,512]{1,0:T(8,128)(2,1)S(1)}, u32[]{:S(2)}, u32[]{:S(2)}) collective-permute-start(bf16[64,512]{1,0:T(8,128)(2,1)} %get-tuple-element.224), channel_id=1, source_target_pairs={{0,64},{4,68},{64,0},{68,4},{1,65},{5,69},{65,1},{69,5},{2,66},{6,... | collective-permute-start | bytes 196616 | tf_op jit(solution)/shard_map/ppermute | solution.py:246
  276.6 14.9 %collective-permute-start.58 = (bf16[64,512]{1,0:T(8,128)(2,1)}, bf16[64,512]{1,0:T(8,128)(2,1)S(1)}, u32[]{:S(2)}, u32[]{:S(2)}) collective-permute-start(bf16[64,512]{1,0:T(8,128)(2,1)} %get-tuple-element.225), channel_id=1, source_target_pairs={{0,68},{4,64},{64,4},{68,0},{1,69},{5,65},{65,5},{69,1},{2,70},{6,... | collective-permute-start | bytes 196616 | tf_op jit(solution)/shard_map/ppermute | solution.py:246
  281.4 16.6 %collective-permute-start.51 = (bf16[128,1024]{1,0:T(8,128)(2,1)S(1)}, bf16[128,1024]{1,0:T(8,128)(2,1)S(1)}, u32[]{:S(2)}, u32[]{:S(2)}) collective-permute-start(bf16[128,1024]{1,0:T(8,128)(2,1)S(1)} %slice_select_fusion.1), channel_id=1, source_target_pairs={{0,0},{4,32},{32,4},{36,36},{1,1},{5,33},{33,5},{37,37},{2,2},{6,3... | collective-permute-start | bytes 786440 | tf_op jit(solution)/shard_map/ppermute | solution.py:232
  288.1 32.1 %collective-permute-start.65 = (bf16[256,4608]{1,0:T(8,128)(2,1)}, bf16[256,4608]{1,0:T(8,128)(2,1)S(1)}, u32[]{:S(2)}, u32[]{:S(2)}) collective-permute-start(bf16[256,4608]{1,0:T(8,128)(2,1)} %get-tuple-element.233.refs_9_), channel_id=1, source_target_pairs={{0,8},{1,9},{2,10},{3,11},{8,16},{9,17},{10,18},{11,19},{16,24},{1... | collective-permute-start | bytes 7077896 | tf_op jit(solution)/shard_map/ppermute | solution.py:69
  288.9 31.4 %collective-permute-start.66 = (bf16[256,4608]{1,0:T(8,128)(2,1)}, bf16[256,4608]{1,0:T(8,128)(2,1)S(1)}, u32[]{:S(2)}, u32[]{:S(2)}) collective-permute-start(bf16[256,4608]{1,0:T(8,128)(2,1)} %get-tuple-element.232.refs_8_), channel_id=1, source_target_pairs={{0,24},{1,25},{2,26},{3,27},{8,0},{9,1},{10,2},{11,3},{16,8},{17,9... | collective-permute-start | bytes 7077896 | tf_op jit(solution)/shard_map/ppermute | solution.py:69
  297.9 12.8 %collective-permute-start.63 = (bf16[64,1536]{1,0:T(8,128)(2,1)}, bf16[64,1536]{1,0:T(8,128)(2,1)S(1)}, u32[]{:S(2)}, u32[]{:S(2)}) collective-permute-start(bf16[64,1536]{1,0:T(8,128)(2,1)} %get-tuple-element.238), channel_id=1, source_target_pairs={{0,68},{4,64},{64,4},{68,0},{1,69},{5,65},{65,5},{69,1},{2,70},{6,... | collective-permute-start | bytes 589832 | tf_op jit(solution)/shard_map/ppermute | solution.py:246
  344.6 20.2 %collective-permute-start.67 = (bf16[256,1024]{1,0:T(8,128)(2,1)}, bf16[256,1024]{1,0:T(8,128)(2,1)S(1)}, u32[]{:S(2)}, u32[]{:S(2)}) collective-permute-start(bf16[256,1024]{1,0:T(8,128)(2,1)} %get-tuple-element.252.refs_1_), channel_id=1, source_target_pairs={{0,32},{32,0},{1,33},{33,1},{2,34},{34,2},{3,35},{35,3},{4,36},{36... | collective-permute-start | bytes 1572872 | tf_op jit(solution)/shard_map/ppermute | solution.py:236
  348.2 31.0 %collective-permute-start.71 = (bf16[256,3328]{1,0:T(8,128)(2,1)}, bf16[256,3328]{1,0:T(8,128)(2,1)S(1)}, u32[]{:S(2)}, u32[]{:S(2)}) collective-permute-start(bf16[256,3328]{1,0:T(8,128)(2,1)} %get-tuple-element.262), channel_id=1, source_target_pairs={{0,8},{1,9},{2,10},{3,11},{8,16},{9,17},{10,18},{11,19},{16,24},{1... | collective-permute-start | bytes 5111816 | tf_op jit(solution)/shard_map/ppermute | solution.py:69
  348.2 31.0 %collective-permute-start.72 = (bf16[256,3328]{1,0:T(8,128)(2,1)}, bf16[256,3328]{1,0:T(8,128)(2,1)S(1)}, u32[]{:S(2)}, u32[]{:S(2)}) collective-permute-start(bf16[256,3328]{1,0:T(8,128)(2,1)} %get-tuple-element.263), channel_id=1, source_target_pairs={{0,24},{1,25},{2,26},{3,27},{8,0},{9,1},{10,2},{11,3},{16,8},{17,9... | collective-permute-start | bytes 5111816 | tf_op jit(solution)/shard_map/ppermute | solution.py:69
  361.4 17.8 %collective-permute-start.99 = (bf16[64,4608]{1,0:T(8,128)(2,1)}, bf16[64,4608]{1,0:T(8,128)(2,1)S(1)}, u32[]{:S(2)}, u32[]{:S(2)}) collective-permute-start(bf16[64,4608]{1,0:T(8,128)(2,1)} %get-tuple-element.316), channel_id=1, source_target_pairs={{0,3},{1,0},{2,1},{3,2},{8,11},{9,8},{10,9},{11,10},{16,19},{17,16... | collective-permute-start | bytes 1769480 | tf_op jit(solution)/shard_map/ppermute | solution.py:69
  361.4 17.7 %collective-permute-start.98 = (bf16[64,4608]{1,0:T(8,128)(2,1)}, bf16[64,4608]{1,0:T(8,128)(2,1)S(1)}, u32[]{:S(2)}, u32[]{:S(2)}) collective-permute-start(bf16[64,4608]{1,0:T(8,128)(2,1)} %get-tuple-element.315), channel_id=1, source_target_pairs={{0,1},{1,2},{2,3},{3,0},{8,9},{9,10},{10,11},{11,8},{16,17},{17,18... | collective-permute-start | bytes 1769480 | tf_op jit(solution)/shard_map/ppermute | solution.py:69
  371.4 18.0 %collective-permute-start.68 = (bf16[64,512]{1,0:T(8,128)(2,1)}, bf16[64,512]{1,0:T(8,128)(2,1)S(1)}, u32[]{:S(2)}, u32[]{:S(2)}) collective-permute-start(bf16[64,512]{1,0:T(8,128)(2,1)} %get-tuple-element.257), channel_id=1, source_target_pairs={{0,4},{4,0},{64,68},{68,64},{1,5},{5,1},{65,69},{69,65},{2,6},{6,2... | collective-permute-start | bytes 196616 | tf_op jit(solution)/shard_map/ppermute | solution.py:246
  385.7 61.1 %collective-permute-start.79 = (bf16[256,6656]{1,0:T(8,128)(2,1)}, bf16[256,6656]{1,0:T(8,128)(2,1)S(1)}, u32[]{:S(2)}, u32[]{:S(2)}) collective-permute-start(bf16[256,6656]{1,0:T(8,128)(2,1)} %get-tuple-element.267.refs_9_), channel_id=1, source_target_pairs={{0,8},{1,9},{2,10},{3,11},{8,16},{9,17},{10,18},{11,19},{16,24},{1... | collective-permute-start | bytes 10223624 | tf_op jit(solution)/shard_map/ppermute | solution.py:69
  387.5 59.4 %collective-permute-start.80 = (bf16[256,6656]{1,0:T(8,128)(2,1)}, bf16[256,6656]{1,0:T(8,128)(2,1)}, u32[]{:S(2)}, u32[]{:S(2)}) collective-permute-start(bf16[256,6656]{1,0:T(8,128)(2,1)} %get-tuple-element.266.refs_8_), channel_id=1, source_target_pairs={{0,24},{1,25},{2,26},{3,27},{8,0},{9,1},{10,2},{11,3},{16,8},{17,9... | collective-permute-start | bytes 10223624 | tf_op jit(solution)/shard_map/ppermute | solution.py:69
  423.0 78.7 %collective-permute-start.76 = (bf16[256,1024]{1,0:T(8,128)(2,1)}, bf16[256,1024]{1,0:T(8,128)(2,1)}, u32[]{:S(2)}, u32[]{:S(2)}) collective-permute-start(bf16[256,1024]{1,0:T(8,128)(2,1)} %get-tuple-element.277.refs_1_), channel_id=1, source_target_pairs={{0,32},{32,0},{1,33},{33,1},{2,34},{34,2},{3,35},{35,3},{4,36},{36... | collective-permute-start | bytes 1572872 | tf_op jit(solution)/shard_map/ppermute | solution.py:236
  454.7 14.3 %collective-permute-start.91 = (bf16[64,3328]{1,0:T(8,128)(2,1)S(1)}, bf16[64,3328]{1,0:T(8,128)(2,1)}, u32[]{:S(2)}, u32[]{:S(2)}) collective-permute-start(bf16[64,3328]{1,0:T(8,128)(2,1)S(1)} %get-tuple-element.340), channel_id=1, source_target_pairs={{0,3},{1,0},{2,1},{3,2},{8,11},{9,8},{10,9},{11,10},{16,19},{17,16... | collective-permute-start | bytes 1277960 | tf_op jit(solution)/shard_map/ppermute | solution.py:69
  455.4 19.2 %collective-permute-start.81 = (bf16[256,2176]{1,0:T(8,128)(2,1)}, bf16[256,2176]{1,0:T(8,128)(2,1)S(1)}, u32[]{:S(2)}, u32[]{:S(2)}) collective-permute-start(bf16[256,2176]{1,0:T(8,128)(2,1)} %get-tuple-element.289), channel_id=1, source_target_pairs={{0,8},{1,9},{2,10},{3,11},{8,16},{9,17},{10,18},{11,19},{16,24},{1... | collective-permute-start | bytes 3342344 | tf_op jit(solution)/shard_map/ppermute | solution.py:69
  456.9 23.9 %collective-permute-start.82 = (bf16[256,2176]{1,0:T(8,128)(2,1)S(1)}, bf16[256,2176]{1,0:T(8,128)(2,1)S(1)}, u32[]{:S(2)}, u32[]{:S(2)}) collective-permute-start(bf16[256,2176]{1,0:T(8,128)(2,1)S(1)} %copy-done.21), channel_id=1, source_target_pairs={{0,24},{1,25},{2,26},{3,27},{8,0},{9,1},{10,2},{11,3},{16,8},{17,9... | collective-permute-start | bytes 3342344 | tf_op jit(solution)/shard_map/ppermute | solution.py:69
  471.3 37.6 %collective-permute-start.93 = (bf16[64,6656]{1,0:T(8,128)(2,1)}, bf16[64,6656]{1,0:T(8,128)(2,1)}, u32[]{:S(2)}, u32[]{:S(2)}) collective-permute-start(bf16[64,6656]{1,0:T(8,128)(2,1)} %get-tuple-element.305), channel_id=1, source_target_pairs={{0,3},{1,0},{2,1},{3,2},{8,11},{9,8},{10,9},{11,10},{16,19},{17,16... | collective-permute-start | bytes 2555912 | tf_op jit(solution)/shard_map/ppermute | solution.py:69
  471.4 37.5 %collective-permute-start.92 = (bf16[64,6656]{1,0:T(8,128)(2,1)}, bf16[64,6656]{1,0:T(8,128)(2,1)}, u32[]{:S(2)}, u32[]{:S(2)}) collective-permute-start(bf16[64,6656]{1,0:T(8,128)(2,1)} %get-tuple-element.304), channel_id=1, source_target_pairs={{0,1},{1,2},{2,3},{3,0},{8,9},{9,10},{10,11},{11,8},{16,17},{17,18... | collective-permute-start | bytes 2555912 | tf_op jit(solution)/shard_map/ppermute | solution.py:69
  507.0 16.0 %collective-permute-start.83 = (bf16[128,1024]{1,0:T(8,128)(2,1)S(1)}, bf16[128,1024]{1,0:T(8,128)(2,1)S(1)}, u32[]{:S(2)}, u32[]{:S(2)}) collective-permute-start(bf16[128,1024]{1,0:T(8,128)(2,1)S(1)} %slice_select_fusion), channel_id=1, source_target_pairs={{0,0},{4,32},{32,4},{36,36},{1,1},{5,33},{33,5},{37,37},{2,2},{6,3... | collective-permute-start | bytes 786440 | tf_op jit(solution)/shard_map/ppermute | solution.py:232
  521.0 12.9 %collective-permute-start.94 = (bf16[32,8704]{1,0:T(8,128)(2,1)}, bf16[32,8704]{1,0:T(8,128)(2,1)S(1)}, u32[]{:S(2)}, u32[]{:S(2)}) collective-permute-start(bf16[32,8704]{1,0:T(8,128)(2,1)} %get-tuple-element.309), channel_id=1, source_target_pairs={{0,0},{4,32},{32,4},{36,36},{1,1},{5,33},{33,5},{37,37},{2,2},{6,3... | collective-permute-start | bytes 1671176 | tf_op jit(solution)/shard_map/ppermute | solution.py:232
  (152 other events, 878.1 us)

commit v5 on v4

--- a/solution.py
+++ b/solution.py
@@ -948,8 +948,8 @@
                 two.append((block, (high, columns), 0, narrow))
                 wide, narrow = wide + extra, narrow + extra
             outs += [((32, 4 * D), F32)]
-        one, two = place_blocks((one, (32, wide)), (two, (32, narrow)))
-        one, two = to_owner(one, 0), to_owner(two, 1)
+        cut = place_blocks((one, (32, wide)), (two, (32, narrow)))
+        one, two = to_owner(cut[0], 0), to_owner(cut[1], 1)
         sums = plus(one[:, wide - extra :], two[:, narrow - extra :])[:, :4] if extra else None
 
         def kernel(meta_ref, ready, one_ref, two_ref, *refs):
@@ -968,7 +968,7 @@
             results[1] = results[1][:88]
         if attn_at is not None:
             results.append(sums)
-        return results
+        return results, cut
 
     gain_rows = gains[:, 0].transpose(1, 2, 0).reshape(4, D)
 
@@ -1121,8 +1121,6 @@
         else:
             ffn_sum = Scatter(*pieces)
             ffn_sum.one()
-            ffn_above.three_sums(partial)
-            ffn_above.four()
         other = other_core(partial)
         grad, gain_list[layer][1], out_terms, *mixed = run(
             out_backward_kernel,
@@ -1132,8 +1130,8 @@
             [(TOKENS, D), (TOKENS, HALF)],
             5.8,
         )
-        sums = (ffn_above if last else ffn_sum).one_sums(mixed[0])
         mixed = exchange_column(mixed)
+        sums = (ffn_above if last else ffn_sum).one_sums(*mixed[1:])
         (ffn_above if last else ffn_sum).two()
         grads = run(
             attend_backward_kernel,
@@ -1146,6 +1144,8 @@
         )
         own = grads[0]
         grads = exchange_column(grads)
+        if not last:
+            ffn_above.three(*grads)
         if last:
             grads[0] = after(own, output)
         partial, *pieces = run(
@@ -1161,28 +1161,28 @@
         if last:
             attn_above = pieces[0]
             middle_above = ffn_above.two_sums()
-            ffn_above.three()
         else:
             attn_sum = Scatter(*pieces)
             attn_sum.one()
+            ffn_above.three_sums(partial)
+            ffn_above.four()
         base = (grad, partial, other_core(partial), state, gain_row(layer, 0))
-    middle = ffn_sum.two_sums()
+    ffn_sum.two_sums()
+    attn_sum.one_sums()
+    attn_sum.two(*ffn_sum.got)
     ffn_sum.three()
-    attn_sum.one_sums()
-    attn_sum.two(middle)
     ffn_sum.three_sums()
     ffn_sum.four()
-    middle = attn_sum.two_sums()
+    attn_sum.two_sums()
     attn_sum.three()
-    input_grad = run(last_kernel, meta, list(base), [wide16], [], 4.3, (middle,))[0]
-    units_above, down_list[1] = to_owners(
-        after(ffn_above.four_sums(), partial), True, None, 0
-    )
+    above = after(ffn_above.four_sums(), partial)
+    (units_above, down_list[1]), _ = to_owners(above, True, None, 0)
     last_sums = attn_sum.three_sums()
     attn_sum.four()
     both = after(ffn_sum.four_sums(), last_sums)
-    units, down_list[0], attn_above, _ = to_owners(both, True, FFN, 0)
-    attn, gain_sums = to_owners(attn_sum.four_sums(), False, 0, LANES)
+    (units, down_list[0], attn_above, _), cut = to_owners(both, True, FFN, 0)
+    input_grad = run(last_kernel, meta, list(base), [wide16], [], 4.3, cut)[0]
+    (attn, gain_sums), _ = to_owners(attn_sum.four_sums(), False, 0, LANES)
     in_parts = [[attn, units], [attn_above, units_above]]
     in_list = [jnp.concatenate(parts, axis=1) for parts in in_parts]
     in_grads = jnp.stack(in_list, axis=1)[:, None]

time: 558 us -> 556 us (level)
  the two profiles are of different devices: /device:TPU:62 before, /device:TPU:1 now
where the time goes in v5:
time: 556 us; the launch traced here: 546 us
  Pallas kernels  198 us (36%)
  starting transfers between devices  154 us (28%)
  waiting for transfers between devices  122 us (22%)
  local copies, waits for them, and re-layouts  46.2 us (8%)
  other arithmetic  23.3 us (4%)
    pallas_call x24, Pallas kernels, run(): pl.pallas_call(whole, out_shape=[jax.ShapeDtypeStruct(shape, dtype) for s...  160 us
    ppermute x48, waiting for transfers between devices, shift(): return lax.ppermute(value, PLANE, ring_pairs(axis_of_core, step))  67.7 us
    ppermute x48, starting transfers between devices, shift(): return lax.ppermute(value, PLANE, ring_pairs(axis_of_core, step))  58.7 us
    ppermute x24, starting transfers between devices, exchange_column(): lax.ppermute(blocks[k], COLUMN, [(y, y ^ k) for y in range(POS)])  32.7 us
    ppermute x24, waiting for transfers between devices, exchange_column(): lax.ppermute(blocks[k], COLUMN, [(y, y ^ k) for y in range(POS)])  32.3 us
    unnamed x203, local copies, waits for them, and re-layouts  28.9 us
    ppermute x13, starting transfers between devices, to_chip(): return lax.ppermute(value, ('c', 'yl'), pairs)  24.8 us
    ppermute x8, starting transfers between devices, to_owner(): return lax.ppermute(value, ('c', 'yl'), pairs)  22.6 us
  transfers between devices with their start and end apart: 102, of which 36 were waited for; matrix products, arithmetic and copies ran while one was open for 7% of the time, Pallas kernels for 24%

profile of v5, /device:TPU:1, one launch (start us, length us, event | category | flops | bytes accessed | tf_op | source)
XLA Modules:
  0.0 546.3 jit_solution(5112191743006918814)
XLA Ops:
  16.9 3.8 collective-permute-start.9
  21.6 4.1 shard_map.130
  47.9 3.8 collective-permute-start.26
  51.7 4.1 shard_map.132
  58.9 6.6 %collective-permute-done.4.refs_0_.refs_1_.refs_3_.refs_4_ = bf16[32,6144]{1,0:T(8,128)(2,1)S(1)} collective-permute-done((bf16[32,6144]{1,0:T(8,128)(2,1)}, bf16[32,6144]{1,0:T(8,128)(2,1)S(1)}, u32[]{:S(2)}, u32[]{:S(2)}) %collective-permute-start.4) | collective-permute-done | bytes 393248 | tf_op jit(solution)/shard_map/ppermute | solution.py:227
  80.0 5.7 %collective-permute-done.30.refs_1_ = bf16[64,4608]{1,0:T(8,128)(2,1)S(1)} collective-permute-done((bf16[64,4608]{1,0:T(8,128)(2,1)}, bf16[64,4608]{1,0:T(8,128)(2,1)S(1)}, u32[]{:S(2)}, u32[]{:S(2)}) %collective-permute-start.30) | collective-permute-done | bytes 589856 | tf_op jit(solution)/shard_map/ppermute | solution.py:69
  87.6 7.3 %collective-permute-done.27.refs_3_ = bf16[64,3328]{1,0:T(8,128)(2,1)} collective-permute-done((bf16[64,3328]{1,0:T(8,128)(2,1)}, bf16[64,3328]{1,0:T(8,128)(2,1)}, u32[]{:S(2)}, u32[]{:S(2)}) %collective-permute-start.27) | collective-permute-done | bytes 426016 | tf_op jit(solution)/shard_map/ppermute | solution.py:69
  94.8 3.8 shard_map.138.refs_6_.refs_4_.refs_7_.refs_11_
  102.3 3.4 collective-permute-start.6
  116.4 7.8 %shard_map.134 = (f32[256,1024]{1,0:T(8,128)}, bf16[1024,256]{1,0:T(8,128)(2,1)}, bf16[64,1536]{1,0:T(8,128)(2,1)}, bf16[64,1536]{1,0:T(8,128)(2,1)}, bf16[64,15...) custom-call(s32[18]{0:T(128)} %pad_add_fusion.meta_ref, bf16[256,1024]{1,0:T(8,128)(2,1)} %fusion.3.refs_0_, ...), custom_call_target="tpu_custom_call" | custom-call | flops 15399999488 | bytes 26180000 | tf_op jit(solution)/shard_map/pallas_call | solution.py:810
  128.1 10.9 %collective-permute-done.35.refs_8_.refs_6_.refs_9_.refs_13_ = bf16[256,6656]{1,0:T(8,128)(2,1)S(1)} collective-permute-done((bf16[256,6656]{1,0:T(8,128)(2,1)}, bf16[256,6656]{1,0:T(8,128)(2,1)S(1)}, u32[]{:S(2)}, u32[]{:S(2)}) %collective-permute-start.35) | collective-permute-done | bytes 3407904 | tf_op jit(solution)/shard_map/ppermute | solution.py:69
  152.5 3.9 collective-permute-done.20.refs_2_
  158.1 3.5 shard_map.136
  166.7 14.9 %shard_map.141 = (f32[256,1024]{1,0:T(8,128)}, bf16[1024,256]{1,0:T(8,128)(2,1)}, f32[256,1536]{1,0:T(8,128)}, f32[256,1536]{1,0:T(8,128)}, bf16[1536,256]{1,0:T...) custom-call(s32[18]{0:T(128)} %pad_add_fusion.meta_ref, ...), custom_call_target="tpu_custom_call" | custom-call | flops 30000001024 | bytes 51000000 | tf_op jit(solution)/shard_map/pallas_call | solution.py:810
  186.5 8.2 %shard_map.142 = (f32[256,1024]{1,0:T(8,128)}, bf16[1024,256]{1,0:T(8,128)(2,1)}, bf16[64,1536]{1,0:T(8,128)(2,1)}, bf16[64,1536]{1,0:T(8,128)(2,1)}, bf16[64,15...) custom-call(s32[18]{0:T(128)} %pad_add_fusion.meta_ref, f32[256,1024]{1,0:T(8,128)} %get-tuple-element.197.refs_0_.refs_3_, ...), custom_call_target="tpu_custom_call" | custom-call | flops 15399999488 | bytes 26180000 | tf_op jit(solution)/shard_map/pallas_call | solution.py:810
  201.1 5.7 %collective-permute-done.40.refs_2_ = bf16[64,1536]{1,0:T(8,128)(2,1)S(1)} collective-permute-done((bf16[64,1536]{1,0:T(8,128)(2,1)}, bf16[64,1536]{1,0:T(8,128)(2,1)S(1)}, u32[]{:S(2)}, u32[]{:S(2)}) %collective-permute-start.40) | collective-permute-done | bytes 196640 | tf_op jit(solution)/shard_map/ppermute | solution.py:246
  220.9 3.6 shard_map.144
  227.0 3.6 collective-permute-start.52
  231.3 4.7 collective-permute-done.52
  237.2 14.6 %shard_map.145 = (f32[256,1024]{1,0:T(8,128)}, bf16[1024,256]{1,0:T(8,128)(2,1)}, f32[256,1536]{1,0:T(8,128)}, f32[256,1536]{1,0:T(8,128)}, bf16[1536,256]{1,0:T...) custom-call(s32[18]{0:T(128)} %pad_add_fusion.meta_ref, ...), custom_call_target="tpu_custom_call" | custom-call | flops 30000001024 | bytes 51000000 | tf_op jit(solution)/shard_map/pallas_call | solution.py:810
  255.3 15.1 %shard_map.146 = (f32[256,1024]{1,0:T(8,128)}, bf16[256,1024]{1,0:T(8,128)(2,1)}, bf16[256,4608]{1,0:T(8,128)(2,1)}, bf16[256,4608]{1,0:T(8,128)(2,1)}, bf16[256...) custom-call(s32[18]{0:T(128)} %pad_add_fusion.meta_ref, ...), custom_call_target="tpu_custom_call" | custom-call | flops 35999997952 | bytes 61200000 | tf_op jit(solution)/shard_map/pallas_call | solution.py:810
  274.8 5.9 %shard_map.147 = (f32[256,1024]{1,0:T(8,128)}, f32[1,1024]{1,0:T(1,128)}, bf16[1024,512]{1,0:T(8,128)(2,1)}, bf16[64,512]{1,0:T(8,128)(2,1)}, bf16[64,512]{1,0:T...) custom-call(s32[18]{0:T(128)} %pad_add_fusion.meta_ref, f32[256,1024]{1,0:T(8,128)} %get-tuple-element.219.refs_0_, ...), custom_call_target="tpu_custom_call" | custom-call | flops 11600000000 | bytes 19720000 | tf_op jit(solution)/shard_map/pallas_call | solution.py:810
  289.7 3.8 shard_map.148
  296.3 3.8 shard_map.149
  305.1 3.9 collective-permute-done.62.refs_2_
  310.9 8.7 %shard_map.150 = (bf16[256,1024]{1,0:T(8,128)(2,1)}, bf16[1024,2048]{1,0:T(8,128)(2,1)}) custom-call(s32[18]{0:T(128)} %pad_add_fusion.meta_ref, bf16[64,1536]{1,0:T(8,128)(2,1)} %get-tuple-element.237.refs_0_, bf16[64,1536]{1,0:T(8,128)(2,1)} %copy-done.78, bf16[64,1536]{1,0:T(8,128)(2,1)} %copy-done.79, bf16[64,1536]{1,0:T(8,128)(2,1)} %copy-done.81, ...), custom_call_target="tpu_custom_call" | custom-call | flops 20000000000 | bytes 34000000 | tf_op jit(solution)/shard_map/pallas_call | solution.py:810
  319.7 4.7 collective-permute-start.64
  327.5 18.9 %shard_map.151 = (f32[256,1024]{1,0:T(8,128)}, f32[1,1024]{1,0:T(1,128)}, bf16[256,1024]{1,0:T(8,128)(2,1)}, bf16[256,6656]{1,0:T(8,128)(2,1)}, bf16[256,6656]{1...) custom-call(s32[18]{0:T(128)} %pad_add_fusion.meta_ref, ...), custom_call_target="tpu_custom_call" | custom-call | flops 35999997952 | bytes 61200000 | tf_op jit(solution)/shard_map/pallas_call | solution.py:810
  351.4 6.0 %shard_map.152 = (f32[256,1024]{1,0:T(8,128)}, f32[1,1024]{1,0:T(1,128)}, bf16[1024,512]{1,0:T(8,128)(2,1)}, bf16[64,512]{1,0:T(8,128)(2,1)}, bf16[64,512]{1,0:T...) custom-call(s32[18]{0:T(128)} %pad_add_fusion.meta_ref, f32[256,1024]{1,0:T(8,128)} %get-tuple-element.253.refs_0_, ...), custom_call_target="tpu_custom_call" | custom-call | flops 11600000000 | bytes 19720000 | tf_op jit(solution)/shard_map/pallas_call | solution.py:810
  364.7 5.5 %collective-permute-done.71.a_ref = bf16[256,3328]{1,0:T(8,128)(2,1)S(1)} collective-permute-done((bf16[256,3328]{1,0:T(8,128)(2,1)}, bf16[256,3328]{1,0:T(8,128)(2,1)S(1)}, u32[]{:S(2)}, u32[]{:S(2)}) %collective-permute-start.71) | collective-permute-done | bytes 1703968 | tf_op jit(solution)/shard_map/ppermute | solution.py:69
  372.1 4.7 shard_map.153
  376.9 3.9 shard_map.154
  387.4 4.1 collective-permute-done.74.refs_2_
  391.6 3.1 collective-permute-done.75.refs_3_
  397.7 11.3 %shard_map.155 = (bf16[256,1024]{1,0:T(8,128)(2,1)}, bf16[256,2176]{1,0:T(8,128)(2,1)}, bf16[256,2176]{1,0:T(8,128)(2,1)}, bf16[256,2176]{1,0:T(8,128)(2,1)}, bf...) custom-call(s32[18]{0:T(128)} %pad_add_fusion.meta_ref, bf16[64,1536]{1,0:T(8,128)(2,1)} %get-tuple-element.270.refs_0_, ...), custom_call_target="tpu_custom_call" | custom-call | flops 6000000000 | bytes 10200000 | tf_op jit(solution)/shard_map/pallas_call | solution.py:810
  413.4 14.3 %collective-permute-done.99 = bf16[64,4608]{1,0:T(8,128)(2,1)S(1)} collective-permute-done((bf16[64,4608]{1,0:T(8,128)(2,1)}, bf16[64,4608]{1,0:T(8,128)(2,1)S(1)}, u32[]{:S(2)}, u32[]{:S(2)}) %collective-permute-start.99) | collective-permute-done | bytes 589856 | tf_op jit(solution)/shard_map/ppermute | solution.py:69
  433.3 3.0 collective-permute-start.100
  436.4 4.1 collective-permute-done.83.a_ref
  448.1 4.9 shard_map.166
  453.0 5.3 add_convert_fusion
  472.3 7.4 %collective-permute-done.85 = bf16[256,2176]{1,0:T(8,128)(2,1)S(1)} collective-permute-done((bf16[256,2176]{1,0:T(8,128)(2,1)S(1)}, bf16[256,2176]{1,0:T(8,128)(2,1)S(1)}, u32[]{:S(2)}, u32[]{:S(2)}) %collective-permute-start.85) | collective-permute-done | bytes 1114144 | tf_op jit(solution)/shard_map/ppermute | solution.py:69
  486.3 3.5 collective-permute-done.87.a_ref
  500.2 4.2 shard_map.160
  505.6 8.4 %collective-permute-start.89 = (bf16[128,1024]{1,0:T(8,128)(2,1)S(1)}, bf16[128,1024]{1,0:T(8,128)(2,1)S(1)}, u32[]{:S(2)}, u32[]{:S(2)}) collective-permute-start(bf16[128,1024]{1,0:T(8,128)(2,1)S(1)} %slice_select_fusion), channel_id=1, source_target_pairs={{0,0},{4,32},{32,4},{36,36},{1,1},{5,33},{33,5},{37,37},{2,2},{6,3... | collective-permute-start | bytes 786440 | tf_op jit(solution)/shard_map/ppermute | solution.py:232
  518.8 3.6 collective-permute-start.94
  528.0 4.2 collective-permute-done.94.refs_0_
  533.0 5.1 shard_map.163
  541.0 3.4 copy.55
  (467 shorter events, 244.8 us)
Async XLA Ops:
  16.9 13.4 %collective-permute-start.9 = (bf16[64,2048]{1,0:T(8,128)(2,1)}, bf16[64,2048]{1,0:T(8,128)(2,1)S(1)}, u32[]{:S(2)}, u32[]{:S(2)}) collective-permute-start(bf16[64,2048]{1,0:T(8,128)(2,1)} %shard_map.129.refs_0_), channel_id=1, source_target_pairs={{0,3},{1,0},{2,1},{3,2},{8,11},{9,8},{10,9},{11,10},{16,19},{17,16... | collective-permute-start | bytes 786440 | tf_op jit(solution)/shard_map/ppermute | solution.py:69
  25.7 18.6 %collective-permute-start.23 = (bf16[32,3072]{1,0:T(8,128)(2,1)}, bf16[32,3072]{1,0:T(8,128)(2,1)S(1)}, u32[]{:S(2)}, u32[]{:S(2)}) collective-permute-start(bf16[32,3072]{1,0:T(8,128)(2,1)} %get-tuple-element.171), channel_id=1, source_target_pairs={{0,32},{4,0},{32,36},{36,4},{1,33},{5,1},{33,37},{37,5},{2,34},{6,... | collective-permute-start | bytes 589832 | tf_op jit(solution)/shard_map/ppermute | solution.py:227
  41.9 29.5 %collective-permute-start.13 = (bf16[256,2048]{1,0:T(8,128)(2,1)}, bf16[256,2048]{1,0:T(8,128)(2,1)S(1)}, u32[]{:S(2)}, u32[]{:S(2)}) collective-permute-start(bf16[256,2048]{1,0:T(8,128)(2,1)} %shard_map.133.refs_4_.refs_12_), channel_id=1, source_target_pairs={{0,24},{1,25},{2,26},{3,27},{8,0},{9,1},{10,2},{11,3},{16,8},{17,9... | collective-permute-start | bytes 3145736 | tf_op jit(solution)/shard_map/ppermute | solution.py:69
  47.9 22.7 %collective-permute-start.26 = (bf16[64,6656]{1,0:T(8,128)(2,1)}, bf16[64,6656]{1,0:T(8,128)(2,1)S(1)}, u32[]{:S(2)}, u32[]{:S(2)}) collective-permute-start(bf16[64,6656]{1,0:T(8,128)(2,1)} %shard_map.137.refs_0_), channel_id=1, source_target_pairs={{0,3},{1,0},{2,1},{3,2},{8,11},{9,8},{10,9},{11,10},{16,19},{17,16... | collective-permute-start | bytes 2555912 | tf_op jit(solution)/shard_map/ppermute | solution.py:69
  55.8 20.5 %collective-permute-start.12 = (bf16[256,2048]{1,0:T(8,128)(2,1)S(1)}, bf16[256,2048]{1,0:T(8,128)(2,1)S(1)}, u32[]{:S(2)}, u32[]{:S(2)}) collective-permute-start(bf16[256,2048]{1,0:T(8,128)(2,1)S(1)} %copy-done.20), channel_id=1, source_target_pairs={{0,8},{1,9},{2,10},{3,11},{8,16},{9,17},{10,18},{11,19},{16,24},{1... | collective-permute-start | bytes 3145736 | tf_op jit(solution)/shard_map/ppermute | solution.py:69
  58.9 20.2 %collective-permute-start.25 = (bf16[64,6656]{1,0:T(8,128)(2,1)S(1)}, bf16[64,6656]{1,0:T(8,128)(2,1)S(1)}, u32[]{:S(2)}, u32[]{:S(2)}) collective-permute-start(bf16[64,6656]{1,0:T(8,128)(2,1)S(1)} %copy-done.5), channel_id=1, source_target_pairs={{0,1},{1,2},{2,3},{3,0},{8,9},{9,10},{10,11},{11,8},{16,17},{17,18... | collective-permute-start | bytes 2555912 | tf_op jit(solution)/shard_map/ppermute | solution.py:69
  70.5 15.2 %collective-permute-start.30 = (bf16[64,4608]{1,0:T(8,128)(2,1)}, bf16[64,4608]{1,0:T(8,128)(2,1)S(1)}, u32[]{:S(2)}, u32[]{:S(2)}) collective-permute-start(bf16[64,4608]{1,0:T(8,128)(2,1)} %shard_map.139.refs_0_), channel_id=1, source_target_pairs={{0,1},{1,2},{2,3},{3,0},{8,9},{9,10},{10,11},{11,8},{16,17},{17,18... | collective-permute-start | bytes 1769480 | tf_op jit(solution)/shard_map/ppermute | solution.py:69
  71.4 15.1 %collective-permute-start.28 = (bf16[64,3328]{1,0:T(8,128)(2,1)}, bf16[64,3328]{1,0:T(8,128)(2,1)}, u32[]{:S(2)}, u32[]{:S(2)}) collective-permute-start(bf16[64,3328]{1,0:T(8,128)(2,1)} %slice.217), channel_id=1, source_target_pairs={{0,3},{1,0},{2,1},{3,2},{8,11},{9,8},{10,9},{11,10},{16,19},{17,16... | collective-permute-start | bytes 1277960 | tf_op jit(solution)/shard_map/ppermute | solution.py:69
  76.3 22.4 %collective-permute-start.15 = (bf16[256,1024]{1,0:T(8,128)(2,1)S(1)}, bf16[256,1024]{1,0:T(8,128)(2,1)}, u32[]{:S(2)}, u32[]{:S(2)}) collective-permute-start(bf16[256,1024]{1,0:T(8,128)(2,1)S(1)} %slice.214), channel_id=1, source_target_pairs={{0,24},{1,25},{2,26},{3,27},{8,0},{9,1},{10,2},{11,3},{16,8},{17,9... | collective-permute-start | bytes 1572872 | tf_op jit(solution)/shard_map/ppermute | solution.py:69
  79.0 20.4 %collective-permute-start.14 = (bf16[256,1024]{1,0:T(8,128)(2,1)}, bf16[256,1024]{1,0:T(8,128)(2,1)}, u32[]{:S(2)}, u32[]{:S(2)}) collective-permute-start(bf16[256,1024]{1,0:T(8,128)(2,1)} %slice.213), channel_id=1, source_target_pairs={{0,8},{1,9},{2,10},{3,11},{8,16},{9,17},{10,18},{11,19},{16,24},{1... | collective-permute-start | bytes 1572872 | tf_op jit(solution)/shard_map/ppermute | solution.py:69
  79.9 14.9 %collective-permute-start.27 = (bf16[64,3328]{1,0:T(8,128)(2,1)}, bf16[64,3328]{1,0:T(8,128)(2,1)}, u32[]{:S(2)}, u32[]{:S(2)}) collective-permute-start(bf16[64,3328]{1,0:T(8,128)(2,1)} %slice.216), channel_id=1, source_target_pairs={{0,1},{1,2},{2,3},{3,0},{8,9},{9,10},{10,11},{11,8},{16,17},{17,18... | collective-permute-start | bytes 1277960 | tf_op jit(solution)/shard_map/ppermute | solution.py:69
  99.5 39.5 %collective-permute-start.35 = (bf16[256,6656]{1,0:T(8,128)(2,1)}, bf16[256,6656]{1,0:T(8,128)(2,1)S(1)}, u32[]{:S(2)}, u32[]{:S(2)}) collective-permute-start(bf16[256,6656]{1,0:T(8,128)(2,1)} %shard_map.138.refs_6_.refs_4_.refs_7_.refs_11_), channel_id=1, source_target_pairs={{0,24},{1,25},{2,26},{3,27},{8,0},{9,1},{10,2},{11,3},{16,8},{17,9... | collective-permute-start | bytes 10223624 | tf_op jit(solution)/shard_map/ppermute | solution.py:69
  100.8 40.9 %collective-permute-start.34 = (bf16[256,6656]{1,0:T(8,128)(2,1)}, bf16[256,6656]{1,0:T(8,128)(2,1)}, u32[]{:S(2)}, u32[]{:S(2)}) collective-permute-start(bf16[256,6656]{1,0:T(8,128)(2,1)} %shard_map.138.refs_6_.refs_4_.refs_7_.refs_11_), channel_id=1, source_target_pairs={{0,8},{1,9},{2,10},{3,11},{8,16},{9,17},{10,18},{11,19},{16,24},{1... | collective-permute-start | bytes 10223624 | tf_op jit(solution)/shard_map/ppermute | solution.py:69
  124.2 19.2 %collective-permute-start.16 = (bf16[64,1536]{1,0:T(8,128)(2,1)}, bf16[64,1536]{1,0:T(8,128)(2,1)S(1)}, u32[]{:S(2)}, u32[]{:S(2)}) collective-permute-start(bf16[64,1536]{1,0:T(8,128)(2,1)} %get-tuple-element.186), channel_id=1, source_target_pairs={{0,4},{4,0},{64,68},{68,64},{1,5},{5,1},{65,69},{69,65},{2,6},{6,2... | collective-permute-start | bytes 589832 | tf_op jit(solution)/shard_map/ppermute | solution.py:246
  124.3 19.1 %collective-permute-start.17 = (bf16[64,1536]{1,0:T(8,128)(2,1)}, bf16[64,1536]{1,0:T(8,128)(2,1)S(1)}, u32[]{:S(2)}, u32[]{:S(2)}) collective-permute-start(bf16[64,1536]{1,0:T(8,128)(2,1)} %get-tuple-element.187), channel_id=1, source_target_pairs={{0,64},{4,68},{64,0},{68,4},{1,65},{5,69},{65,1},{69,5},{2,66},{6,... | collective-permute-start | bytes 589832 | tf_op jit(solution)/shard_map/ppermute | solution.py:246
  127.3 16.2 %collective-permute-start.18 = (bf16[64,1536]{1,0:T(8,128)(2,1)}, bf16[64,1536]{1,0:T(8,128)(2,1)S(1)}, u32[]{:S(2)}, u32[]{:S(2)}) collective-permute-start(bf16[64,1536]{1,0:T(8,128)(2,1)} %get-tuple-element.188), channel_id=1, source_target_pairs={{0,68},{4,64},{64,4},{68,0},{1,69},{5,65},{65,5},{69,1},{2,70},{6,... | collective-permute-start | bytes 589832 | tf_op jit(solution)/shard_map/ppermute | solution.py:246
  139.2 26.8 %collective-permute-start.37 = (bf16[256,3328]{1,0:T(8,128)(2,1)S(1)}, bf16[256,3328]{1,0:T(8,128)(2,1)}, u32[]{:S(2)}, u32[]{:S(2)}) collective-permute-start(bf16[256,3328]{1,0:T(8,128)(2,1)S(1)} %slice.221), channel_id=1, source_target_pairs={{0,24},{1,25},{2,26},{3,27},{8,0},{9,1},{10,2},{11,3},{16,8},{17,9... | collective-permute-start | bytes 5111816 | tf_op jit(solution)/shard_map/ppermute | solution.py:69
  143.3 22.7 %collective-permute-start.36 = (bf16[256,3328]{1,0:T(8,128)(2,1)S(1)}, bf16[256,3328]{1,0:T(8,128)(2,1)}, u32[]{:S(2)}, u32[]{:S(2)}) collective-permute-start(bf16[256,3328]{1,0:T(8,128)(2,1)S(1)} %slice.220), channel_id=1, source_target_pairs={{0,8},{1,9},{2,10},{3,11},{8,16},{9,17},{10,18},{11,19},{16,24},{1... | collective-permute-start | bytes 5111816 | tf_op jit(solution)/shard_map/ppermute | solution.py:69
  183.9 32.9 %collective-permute-start.47 = (bf16[256,4608]{1,0:T(8,128)(2,1)S(1)}, bf16[256,4608]{1,0:T(8,128)(2,1)S(1)}, u32[]{:S(2)}, u32[]{:S(2)}) collective-permute-start(bf16[256,4608]{1,0:T(8,128)(2,1)S(1)} %copy-done.6), channel_id=1, source_target_pairs={{0,24},{1,25},{2,26},{3,27},{8,0},{9,1},{10,2},{11,3},{16,8},{17,9... | collective-permute-start | bytes 7077896 | tf_op jit(solution)/shard_map/ppermute | solution.py:69
  183.9 34.8 %collective-permute-start.46 = (bf16[256,4608]{1,0:T(8,128)(2,1)S(1)}, bf16[256,4608]{1,0:T(8,128)(2,1)}, u32[]{:S(2)}, u32[]{:S(2)}) collective-permute-start(bf16[256,4608]{1,0:T(8,128)(2,1)S(1)} %copy-done.6), channel_id=1, source_target_pairs={{0,8},{1,9},{2,10},{3,11},{8,16},{9,17},{10,18},{11,19},{16,24},{1... | collective-permute-start | bytes 7077896 | tf_op jit(solution)/shard_map/ppermute | solution.py:69
  216.9 19.2 %collective-permute-start.49 = (bf16[256,2304]{1,0:T(8,128)(2,1)S(1)}, bf16[256,2304]{1,0:T(8,128)(2,1)S(1)}, u32[]{:S(2)}, u32[]{:S(2)}) collective-permute-start(bf16[256,2304]{1,0:T(8,128)(2,1)S(1)} %slice.225), channel_id=1, source_target_pairs={{0,24},{1,25},{2,26},{3,27},{8,0},{9,1},{10,2},{11,3},{16,8},{17,9... | collective-permute-start | bytes 3538952 | tf_op jit(solution)/shard_map/ppermute | solution.py:69
  220.1 16.7 %collective-permute-start.48 = (bf16[256,2304]{1,0:T(8,128)(2,1)S(1)}, bf16[256,2304]{1,0:T(8,128)(2,1)}, u32[]{:S(2)}, u32[]{:S(2)}) collective-permute-start(bf16[256,2304]{1,0:T(8,128)(2,1)S(1)} %slice.224), channel_id=1, source_target_pairs={{0,8},{1,9},{2,10},{3,11},{8,16},{9,17},{10,18},{11,19},{16,24},{1... | collective-permute-start | bytes 3538952 | tf_op jit(solution)/shard_map/ppermute | solution.py:69
  254.4 19.3 %collective-permute-start.50 = (bf16[256,1024]{1,0:T(8,128)(2,1)}, bf16[256,1024]{1,0:T(8,128)(2,1)S(1)}, u32[]{:S(2)}, u32[]{:S(2)}) collective-permute-start(bf16[256,1024]{1,0:T(8,128)(2,1)} %get-tuple-element.211), channel_id=1, source_target_pairs={{0,32},{32,0},{1,33},{33,1},{2,34},{34,2},{3,35},{35,3},{4,36},{36... | collective-permute-start | bytes 1572872 | tf_op jit(solution)/shard_map/ppermute | solution.py:236
  271.1 17.2 %collective-permute-start.59 = (bf16[256,2304]{1,0:T(8,128)(2,1)}, bf16[256,2304]{1,0:T(8,128)(2,1)S(1)}, u32[]{:S(2)}, u32[]{:S(2)}) collective-permute-start(bf16[256,2304]{1,0:T(8,128)(2,1)} %get-tuple-element.230), channel_id=1, source_target_pairs={{0,8},{1,9},{2,10},{3,11},{8,16},{9,17},{10,18},{11,19},{16,24},{1... | collective-permute-start | bytes 3538952 | tf_op jit(solution)/shard_map/ppermute | solution.py:69
  271.1 17.2 %collective-permute-start.60 = (bf16[256,2304]{1,0:T(8,128)(2,1)}, bf16[256,2304]{1,0:T(8,128)(2,1)S(1)}, u32[]{:S(2)}, u32[]{:S(2)}) collective-permute-start(bf16[256,2304]{1,0:T(8,128)(2,1)} %get-tuple-element.231), channel_id=1, source_target_pairs={{0,24},{1,25},{2,26},{3,27},{8,0},{9,1},{10,2},{11,3},{16,8},{17,9... | collective-permute-start | bytes 3538952 | tf_op jit(solution)/shard_map/ppermute | solution.py:69
  284.6 18.0 %collective-permute-start.51 = (bf16[128,1024]{1,0:T(8,128)(2,1)S(1)}, bf16[128,1024]{1,0:T(8,128)(2,1)S(1)}, u32[]{:S(2)}, u32[]{:S(2)}) collective-permute-start(bf16[128,1024]{1,0:T(8,128)(2,1)S(1)} %slice_select_fusion.1), channel_id=1, source_target_pairs={{0,0},{4,32},{32,4},{36,36},{1,1},{5,33},{33,5},{37,37},{2,2},{6,3... | collective-permute-start | bytes 786440 | tf_op jit(solution)/shard_map/ppermute | solution.py:232
  293.6 30.8 %collective-permute-start.65 = (bf16[256,4608]{1,0:T(8,128)(2,1)}, bf16[256,4608]{1,0:T(8,128)(2,1)S(1)}, u32[]{:S(2)}, u32[]{:S(2)}) collective-permute-start(bf16[256,4608]{1,0:T(8,128)(2,1)} %get-tuple-element.235.refs_9_), channel_id=1, source_target_pairs={{0,8},{1,9},{2,10},{3,11},{8,16},{9,17},{10,18},{11,19},{16,24},{1... | collective-permute-start | bytes 7077896 | tf_op jit(solution)/shard_map/ppermute | solution.py:69
  293.7 30.7 %collective-permute-start.66 = (bf16[256,4608]{1,0:T(8,128)(2,1)}, bf16[256,4608]{1,0:T(8,128)(2,1)S(1)}, u32[]{:S(2)}, u32[]{:S(2)}) collective-permute-start(bf16[256,4608]{1,0:T(8,128)(2,1)} %get-tuple-element.234.refs_8_), channel_id=1, source_target_pairs={{0,24},{1,25},{2,26},{3,27},{8,0},{9,1},{10,2},{11,3},{16,8},{17,9... | collective-permute-start | bytes 7077896 | tf_op jit(solution)/shard_map/ppermute | solution.py:69
  347.9 22.4 %collective-permute-start.71 = (bf16[256,3328]{1,0:T(8,128)(2,1)}, bf16[256,3328]{1,0:T(8,128)(2,1)S(1)}, u32[]{:S(2)}, u32[]{:S(2)}) collective-permute-start(bf16[256,3328]{1,0:T(8,128)(2,1)} %get-tuple-element.264), channel_id=1, source_target_pairs={{0,8},{1,9},{2,10},{3,11},{8,16},{9,17},{10,18},{11,19},{16,24},{1... | collective-permute-start | bytes 5111816 | tf_op jit(solution)/shard_map/ppermute | solution.py:69
  347.9 22.4 %collective-permute-start.72 = (bf16[256,3328]{1,0:T(8,128)(2,1)}, bf16[256,3328]{1,0:T(8,128)(2,1)S(1)}, u32[]{:S(2)}, u32[]{:S(2)}) collective-permute-start(bf16[256,3328]{1,0:T(8,128)(2,1)} %get-tuple-element.265), channel_id=1, source_target_pairs={{0,24},{1,25},{2,26},{3,27},{8,0},{9,1},{10,2},{11,3},{16,8},{17,9... | collective-permute-start | bytes 5111816 | tf_op jit(solution)/shard_map/ppermute | solution.py:69
  384.7 68.3 %collective-permute-start.77 = (bf16[256,6656]{1,0:T(8,128)(2,1)}, bf16[256,6656]{1,0:T(8,128)(2,1)}, u32[]{:S(2)}, u32[]{:S(2)}) collective-permute-start(bf16[256,6656]{1,0:T(8,128)(2,1)} %get-tuple-element.269.refs_9_), channel_id=1, source_target_pairs={{0,8},{1,9},{2,10},{3,11},{8,16},{9,17},{10,18},{11,19},{16,24},{1... | collective-permute-start | bytes 10223624 | tf_op jit(solution)/shard_map/ppermute | solution.py:69
  384.8 68.2 %collective-permute-start.78 = (bf16[256,6656]{1,0:T(8,128)(2,1)S(1)}, bf16[256,6656]{1,0:T(8,128)(2,1)}, u32[]{:S(2)}, u32[]{:S(2)}) collective-permute-start(bf16[256,6656]{1,0:T(8,128)(2,1)S(1)} %copy-done.4), channel_id=1, source_target_pairs={{0,24},{1,25},{2,26},{3,27},{8,0},{9,1},{10,2},{11,3},{16,8},{17,9... | collective-permute-start | bytes 10223624 | tf_op jit(solution)/shard_map/ppermute | solution.py:69
  394.7 14.3 %collective-permute-start.96 = (bf16[64,2304]{1,0:T(8,128)(2,1)S(1)}, bf16[64,2304]{1,0:T(8,128)(2,1)S(1)}, u32[]{:S(2)}, u32[]{:S(2)}) collective-permute-start(bf16[64,2304]{1,0:T(8,128)(2,1)S(1)} %get-tuple-element.315), channel_id=1, source_target_pairs={{0,1},{1,2},{2,3},{3,0},{8,9},{9,10},{10,11},{11,8},{16,17},{17,18... | collective-permute-start | bytes 884744 | tf_op jit(solution)/shard_map/ppermute | solution.py:69
  394.7 14.3 %collective-permute-start.97 = (bf16[64,2304]{1,0:T(8,128)(2,1)S(1)}, bf16[64,2304]{1,0:T(8,128)(2,1)S(1)}, u32[]{:S(2)}, u32[]{:S(2)}) collective-permute-start(bf16[64,2304]{1,0:T(8,128)(2,1)S(1)} %get-tuple-element.316), channel_id=1, source_target_pairs={{0,3},{1,0},{2,1},{3,2},{8,11},{9,8},{10,9},{11,10},{16,19},{17,16... | collective-permute-start | bytes 884744 | tf_op jit(solution)/shard_map/ppermute | solution.py:69
  411.9 15.8 %collective-permute-start.99 = (bf16[64,4608]{1,0:T(8,128)(2,1)}, bf16[64,4608]{1,0:T(8,128)(2,1)S(1)}, u32[]{:S(2)}, u32[]{:S(2)}) collective-permute-start(bf16[64,4608]{1,0:T(8,128)(2,1)} %get-tuple-element.320), channel_id=1, source_target_pairs={{0,3},{1,0},{2,1},{3,2},{8,11},{9,8},{10,9},{11,10},{16,19},{17,16... | collective-permute-start | bytes 1769480 | tf_op jit(solution)/shard_map/ppermute | solution.py:69
  413.4 16.9 %collective-permute-start.98 = (bf16[64,4608]{1,0:T(8,128)(2,1)}, bf16[64,4608]{1,0:T(8,128)(2,1)S(1)}, u32[]{:S(2)}, u32[]{:S(2)}) collective-permute-start(bf16[64,4608]{1,0:T(8,128)(2,1)} %get-tuple-element.319), channel_id=1, source_target_pairs={{0,1},{1,2},{2,3},{3,0},{8,9},{9,10},{10,11},{11,8},{16,17},{17,18... | collective-permute-start | bytes 1769480 | tf_op jit(solution)/shard_map/ppermute | solution.py:69
  413.4 27.1 %collective-permute-start.83 = (bf16[256,1024]{1,0:T(8,128)(2,1)}, bf16[256,1024]{1,0:T(8,128)(2,1)S(1)}, u32[]{:S(2)}, u32[]{:S(2)}) collective-permute-start(bf16[256,1024]{1,0:T(8,128)(2,1)} %get-tuple-element.292), channel_id=1, source_target_pairs={{0,8},{1,9},{2,10},{3,11},{8,16},{9,17},{10,18},{11,19},{16,24},{1... | collective-permute-start | bytes 1572872 | tf_op jit(solution)/shard_map/ppermute | solution.py:69
  427.7 15.4 %collective-permute-start.84 = (bf16[256,1152]{1,0:T(8,128)(2,1)}, bf16[256,1152]{1,0:T(8,128)(2,1)S(1)}, u32[]{:S(2)}, u32[]{:S(2)}) collective-permute-start(bf16[256,1152]{1,0:T(8,128)(2,1)} %get-tuple-element.293), channel_id=1, source_target_pairs={{0,24},{1,25},{2,26},{3,27},{8,0},{9,1},{10,2},{11,3},{16,8},{17,9... | collective-permute-start | bytes 1769480 | tf_op jit(solution)/shard_map/ppermute | solution.py:69
  433.3 13.3 %collective-permute-start.100 = (bf16[32,6144]{1,0:T(8,128)(2,1)}, bf16[32,6144]{1,0:T(8,128)(2,1)S(1)}, u32[]{:S(2)}, u32[]{:S(2)}) collective-permute-start(bf16[32,6144]{1,0:T(8,128)(2,1)} %get-tuple-element.324), channel_id=1, source_target_pairs={{0,0},{4,32},{32,4},{36,36},{1,1},{5,33},{33,5},{37,37},{2,2},{6,3... | collective-permute-start | bytes 1179656 | tf_op jit(solution)/shard_map/ppermute | solution.py:232
  443.1 57.0 %collective-permute-start.76 = (bf16[256,1024]{1,0:T(8,128)(2,1)}, bf16[256,1024]{1,0:T(8,128)(2,1)}, u32[]{:S(2)}, u32[]{:S(2)}) collective-permute-start(bf16[256,1024]{1,0:T(8,128)(2,1)} %get-tuple-element.279.refs_1_), channel_id=1, source_target_pairs={{0,32},{32,0},{1,33},{33,1},{2,34},{34,2},{3,35},{35,3},{4,36},{36... | collective-permute-start | bytes 1572872 | tf_op jit(solution)/shard_map/ppermute | solution.py:236
  461.4 18.3 %collective-permute-start.85 = (bf16[256,2176]{1,0:T(8,128)(2,1)S(1)}, bf16[256,2176]{1,0:T(8,128)(2,1)S(1)}, u32[]{:S(2)}, u32[]{:S(2)}) collective-permute-start(bf16[256,2176]{1,0:T(8,128)(2,1)S(1)} %copy-done.19), channel_id=1, source_target_pairs={{0,8},{1,9},{2,10},{3,11},{8,16},{9,17},{10,18},{11,19},{16,24},{1... | collective-permute-start | bytes 3342344 | tf_op jit(solution)/shard_map/ppermute | solution.py:69
  461.4 19.5 %collective-permute-start.86 = (bf16[256,2176]{1,0:T(8,128)(2,1)S(1)}, bf16[256,2176]{1,0:T(8,128)(2,1)}, u32[]{:S(2)}, u32[]{:S(2)}) collective-permute-start(bf16[256,2176]{1,0:T(8,128)(2,1)S(1)} %copy-done.18), channel_id=1, source_target_pairs={{0,24},{1,25},{2,26},{3,27},{8,0},{9,1},{10,2},{11,3},{16,8},{17,9... | collective-permute-start | bytes 3342344 | tf_op jit(solution)/shard_map/ppermute | solution.py:69
  470.6 24.8 %collective-permute-start.82 = (bf16[64,6656]{1,0:T(8,128)(2,1)}, bf16[64,6656]{1,0:T(8,128)(2,1)}, u32[]{:S(2)}, u32[]{:S(2)}) collective-permute-start(bf16[64,6656]{1,0:T(8,128)(2,1)} %get-tuple-element.286), channel_id=1, source_target_pairs={{0,3},{1,0},{2,1},{3,2},{8,11},{9,8},{10,9},{11,10},{16,19},{17,16... | collective-permute-start | bytes 2555912 | tf_op jit(solution)/shard_map/ppermute | solution.py:69
  472.3 23.0 %collective-permute-start.81 = (bf16[64,6656]{1,0:T(8,128)(2,1)}, bf16[64,6656]{1,0:T(8,128)(2,1)}, u32[]{:S(2)}, u32[]{:S(2)}) collective-permute-start(bf16[64,6656]{1,0:T(8,128)(2,1)} %get-tuple-element.285), channel_id=1, source_target_pairs={{0,1},{1,2},{2,3},{3,0},{8,9},{9,10},{10,11},{11,8},{16,17},{17,18... | collective-permute-start | bytes 2555912 | tf_op jit(solution)/shard_map/ppermute | solution.py:69
  492.6 21.5 %collective-permute-start.90 = (bf16[64,2176]{1,0:T(8,128)(2,1)}, bf16[64,2176]{1,0:T(8,128)(2,1)S(1)}, u32[]{:S(2)}, u32[]{:S(2)}) collective-permute-start(bf16[64,2176]{1,0:T(8,128)(2,1)} %get-tuple-element.305), channel_id=1, source_target_pairs={{0,1},{1,2},{2,3},{3,0},{8,9},{9,10},{10,11},{11,8},{16,17},{17,18... | collective-permute-start | bytes 835592 | tf_op jit(solution)/shard_map/ppermute | solution.py:69
  493.7 20.4 %collective-permute-start.91 = (bf16[64,2176]{1,0:T(8,128)(2,1)}, bf16[64,2176]{1,0:T(8,128)(2,1)S(1)}, u32[]{:S(2)}, u32[]{:S(2)}) collective-permute-start(bf16[64,2176]{1,0:T(8,128)(2,1)} %get-tuple-element.304), channel_id=1, source_target_pairs={{0,3},{1,0},{2,1},{3,2},{8,11},{9,8},{10,9},{11,10},{16,19},{17,16... | collective-permute-start | bytes 835592 | tf_op jit(solution)/shard_map/ppermute | solution.py:69
  505.6 16.9 %collective-permute-start.89 = (bf16[128,1024]{1,0:T(8,128)(2,1)S(1)}, bf16[128,1024]{1,0:T(8,128)(2,1)S(1)}, u32[]{:S(2)}, u32[]{:S(2)}) collective-permute-start(bf16[128,1024]{1,0:T(8,128)(2,1)S(1)} %slice_select_fusion), channel_id=1, source_target_pairs={{0,0},{4,32},{32,4},{36,36},{1,1},{5,33},{33,5},{37,37},{2,2},{6,3... | collective-permute-start | bytes 786440 | tf_op jit(solution)/shard_map/ppermute | solution.py:232
  518.8 13.4 %collective-permute-start.94 = (bf16[32,8704]{1,0:T(8,128)(2,1)S(1)}, bf16[32,8704]{1,0:T(8,128)(2,1)S(1)}, u32[]{:S(2)}, u32[]{:S(2)}) collective-permute-start(bf16[32,8704]{1,0:T(8,128)(2,1)S(1)} %copy-done.57), channel_id=1, source_target_pairs={{0,0},{4,32},{32,4},{36,36},{1,1},{5,33},{33,5},{37,37},{2,2},{6,3... | collective-permute-start | bytes 1671176 | tf_op jit(solution)/shard_map/ppermute | solution.py:232
  (153 other events, 939.6 us)

commit v6 on v5

--- a/solution.py
+++ b/solution.py
@@ -1170,12 +1170,12 @@
     ffn_sum.two_sums()
     attn_sum.one_sums()
     attn_sum.two(*ffn_sum.got)
-    ffn_sum.three()
+    sums = ffn_sum.three()
     ffn_sum.three_sums()
     ffn_sum.four()
     attn_sum.two_sums()
     attn_sum.three()
-    above = after(ffn_above.four_sums(), partial)
+    above = after(ffn_above.four_sums(), *sums)
     (units_above, down_list[1]), _ = to_owners(above, True, None, 0)
     last_sums = attn_sum.three_sums()
     attn_sum.four()

time: 556 us -> 545 us (0.980)
  waiting for transfers between devices: 122 us -> 102 us
  starting transfers between devices: 154 us -> 162 us
    ppermute x48, waiting for transfers between devices: 67.7 us -> 45 us  [shift(): return lax.ppermute(value, PLANE, ring_pairs(axis_of_core, step))]
    ppermute x9, starting transfers between devices: 15 us -> 25.3 us  [other_core(): return lax.ppermute(value, 'c', [(0, 1), (1, 0)])]
    unnamed x203 -> x199, local copies, waits for them, and re-layouts: 28.9 us -> 29.7 us
  transfers between devices with their start and end apart: 102 -> 102, of which waited for: 36 -> 36; matrix products, arithmetic and copies ran while one was open for 7% -> 7% of each run, Pallas kernels for 24% -> 25%
where the time goes in v6:
time: 545 us; the launch traced here: 536 us
  Pallas kernels  198 us (36%)
  starting transfers between devices  162 us (30%)
  waiting for transfers between devices  102 us (19%)
  local copies, waits for them, and re-layouts  47 us (9%)
  other arithmetic  24.7 us (5%)
    pallas_call x24, Pallas kernels, run(): pl.pallas_call(whole, out_shape=[jax.ShapeDtypeStruct(shape, dtype) for s...  160 us
    ppermute x48, starting transfers between devices, shift(): return lax.ppermute(value, PLANE, ring_pairs(axis_of_core, step))  62 us
    ppermute x48, waiting for transfers between devices, shift(): return lax.ppermute(value, PLANE, ring_pairs(axis_of_core, step))  45 us
    ppermute x24, waiting for transfers between devices, exchange_column(): lax.ppermute(blocks[k], COLUMN, [(y, y ^ k) for y in range(POS)])  32.9 us
    ppermute x24, starting transfers between devices, exchange_column(): lax.ppermute(blocks[k], COLUMN, [(y, y ^ k) for y in range(POS)])  32.5 us
    unnamed x199, local copies, waits for them, and re-layouts  29.7 us
    ppermute x9, starting transfers between devices, other_core(): return lax.ppermute(value, 'c', [(0, 1), (1, 0)])  25.3 us
    ppermute x13, starting transfers between devices, to_chip(): return lax.ppermute(value, ('c', 'yl'), pairs)  24.8 us
  transfers between devices with their start and end apart: 102, of which 36 were waited for; matrix products, arithmetic and copies ran while one was open for 7% of the time, Pallas kernels for 25%

profile of v6, /device:TPU:1, one launch (start us, length us, event | category | flops | bytes accessed | tf_op | source)
XLA Modules:
  0.0 535.7 jit_solution(8582801365598810575)
XLA Ops:
  16.8 3.8 collective-permute-start.9
  21.5 4.1 shard_map.130
  47.8 3.8 collective-permute-start.26
  51.6 4.1 shard_map.132
  58.8 6.6 %collective-permute-done.4.refs_0_.refs_1_.refs_3_.refs_4_ = bf16[32,6144]{1,0:T(8,128)(2,1)S(1)} collective-permute-done((bf16[32,6144]{1,0:T(8,128)(2,1)}, bf16[32,6144]{1,0:T(8,128)(2,1)S(1)}, u32[]{:S(2)}, u32[]{:S(2)}) %collective-permute-start.4) | collective-permute-done | bytes 393248 | tf_op jit(solution)/shard_map/ppermute | solution.py:227
  79.9 5.7 %collective-permute-done.30.refs_1_ = bf16[64,4608]{1,0:T(8,128)(2,1)S(1)} collective-permute-done((bf16[64,4608]{1,0:T(8,128)(2,1)}, bf16[64,4608]{1,0:T(8,128)(2,1)S(1)}, u32[]{:S(2)}, u32[]{:S(2)}) %collective-permute-start.30) | collective-permute-done | bytes 589856 | tf_op jit(solution)/shard_map/ppermute | solution.py:69
  87.5 7.3 %collective-permute-done.27.refs_3_ = bf16[64,3328]{1,0:T(8,128)(2,1)} collective-permute-done((bf16[64,3328]{1,0:T(8,128)(2,1)}, bf16[64,3328]{1,0:T(8,128)(2,1)}, u32[]{:S(2)}, u32[]{:S(2)}) %collective-permute-start.27) | collective-permute-done | bytes 426016 | tf_op jit(solution)/shard_map/ppermute | solution.py:69
  94.7 3.8 shard_map.138.refs_6_.refs_4_.refs_7_.refs_11_
  102.2 3.4 collective-permute-start.6
  105.6 3.0 collective-permute-start.5
  116.3 7.8 %shard_map.134 = (f32[256,1024]{1,0:T(8,128)}, bf16[1024,256]{1,0:T(8,128)(2,1)}, bf16[64,1536]{1,0:T(8,128)(2,1)}, bf16[64,1536]{1,0:T(8,128)(2,1)}, bf16[64,15...) custom-call(s32[18]{0:T(128)} %pad_add_fusion.meta_ref, bf16[256,1024]{1,0:T(8,128)(2,1)} %fusion.3.refs_0_, ...), custom_call_target="tpu_custom_call" | custom-call | flops 15399999488 | bytes 26180000 | tf_op jit(solution)/shard_map/pallas_call | solution.py:810
  124.2 3.0 collective-permute-start.17
  128.0 10.9 %collective-permute-done.35.refs_8_.refs_6_.refs_9_.refs_13_ = bf16[256,6656]{1,0:T(8,128)(2,1)S(1)} collective-permute-done((bf16[256,6656]{1,0:T(8,128)(2,1)}, bf16[256,6656]{1,0:T(8,128)(2,1)S(1)}, u32[]{:S(2)}, u32[]{:S(2)}) %collective-permute-start.35) | collective-permute-done | bytes 3407904 | tf_op jit(solution)/shard_map/ppermute | solution.py:69
  152.4 3.9 collective-permute-done.20.refs_2_
  158.0 3.5 shard_map.136
  162.8 3.0 shard_map.140.refs_11_.refs_6_.refs_10_
  166.7 14.9 %shard_map.141 = (f32[256,1024]{1,0:T(8,128)}, bf16[1024,256]{1,0:T(8,128)(2,1)}, f32[256,1536]{1,0:T(8,128)}, f32[256,1536]{1,0:T(8,128)}, bf16[1536,256]{1,0:T...) custom-call(s32[18]{0:T(128)} %pad_add_fusion.meta_ref, ...), custom_call_target="tpu_custom_call" | custom-call | flops 30000001024 | bytes 51000000 | tf_op jit(solution)/shard_map/pallas_call | solution.py:810
  186.4 8.2 %shard_map.142 = (f32[256,1024]{1,0:T(8,128)}, bf16[1024,256]{1,0:T(8,128)(2,1)}, bf16[64,1536]{1,0:T(8,128)(2,1)}, bf16[64,1536]{1,0:T(8,128)(2,1)}, bf16[64,15...) custom-call(s32[18]{0:T(128)} %pad_add_fusion.meta_ref, f32[256,1024]{1,0:T(8,128)} %get-tuple-element.197.refs_0_.refs_3_, ...), custom_call_target="tpu_custom_call" | custom-call | flops 15399999488 | bytes 26180000 | tf_op jit(solution)/shard_map/pallas_call | solution.py:810
  201.0 5.7 %collective-permute-done.40.refs_2_ = bf16[64,1536]{1,0:T(8,128)(2,1)S(1)} collective-permute-done((bf16[64,1536]{1,0:T(8,128)(2,1)}, bf16[64,1536]{1,0:T(8,128)(2,1)S(1)}, u32[]{:S(2)}, u32[]{:S(2)}) %collective-permute-start.40) | collective-permute-done | bytes 196640 | tf_op jit(solution)/shard_map/ppermute | solution.py:246
  220.7 3.6 shard_map.144
  226.9 3.6 collective-permute-start.52
  231.2 4.7 collective-permute-done.52
  237.1 14.7 %shard_map.145 = (f32[256,1024]{1,0:T(8,128)}, bf16[1024,256]{1,0:T(8,128)(2,1)}, f32[256,1536]{1,0:T(8,128)}, f32[256,1536]{1,0:T(8,128)}, bf16[1536,256]{1,0:T...) custom-call(s32[18]{0:T(128)} %pad_add_fusion.meta_ref, ...), custom_call_target="tpu_custom_call" | custom-call | flops 30000001024 | bytes 51000000 | tf_op jit(solution)/shard_map/pallas_call | solution.py:810
  255.2 15.1 %shard_map.146 = (f32[256,1024]{1,0:T(8,128)}, bf16[256,1024]{1,0:T(8,128)(2,1)}, bf16[256,4608]{1,0:T(8,128)(2,1)}, bf16[256,4608]{1,0:T(8,128)(2,1)}, bf16[256...) custom-call(s32[18]{0:T(128)} %pad_add_fusion.meta_ref, ...), custom_call_target="tpu_custom_call" | custom-call | flops 35999997952 | bytes 61200000 | tf_op jit(solution)/shard_map/pallas_call | solution.py:810
  274.6 5.8 %shard_map.147 = (f32[256,1024]{1,0:T(8,128)}, f32[1,1024]{1,0:T(1,128)}, bf16[1024,512]{1,0:T(8,128)(2,1)}, bf16[64,512]{1,0:T(8,128)(2,1)}, bf16[64,512]{1,0:T...) custom-call(s32[18]{0:T(128)} %pad_add_fusion.meta_ref, f32[256,1024]{1,0:T(8,128)} %get-tuple-element.219.refs_0_, ...), custom_call_target="tpu_custom_call" | custom-call | flops 11600000000 | bytes 19720000 | tf_op jit(solution)/shard_map/pallas_call | solution.py:810
  289.6 3.8 shard_map.148
  296.1 3.8 shard_map.149
  304.9 3.9 collective-permute-done.62.refs_2_
  310.7 8.7 %shard_map.150 = (bf16[256,1024]{1,0:T(8,128)(2,1)}, bf16[1024,2048]{1,0:T(8,128)(2,1)}) custom-call(s32[18]{0:T(128)} %pad_add_fusion.meta_ref, bf16[64,1536]{1,0:T(8,128)(2,1)} %get-tuple-element.237.refs_0_, bf16[64,1536]{1,0:T(8,128)(2,1)} %copy-done.77, bf16[64,1536]{1,0:T(8,128)(2,1)} %copy-done.78, bf16[64,1536]{1,0:T(8,128)(2,1)} %copy-done.79, ...), custom_call_target="tpu_custom_call" | custom-call | flops 20000000000 | bytes 34000000 | tf_op jit(solution)/shard_map/pallas_call | solution.py:810
  319.5 4.7 collective-permute-start.64
  327.3 18.8 %shard_map.151 = (f32[256,1024]{1,0:T(8,128)}, f32[1,1024]{1,0:T(1,128)}, bf16[256,1024]{1,0:T(8,128)(2,1)}, bf16[256,6656]{1,0:T(8,128)(2,1)}, bf16[256,6656]{1...) custom-call(s32[18]{0:T(128)} %pad_add_fusion.meta_ref, ...), custom_call_target="tpu_custom_call" | custom-call | flops 35999997952 | bytes 61200000 | tf_op jit(solution)/shard_map/pallas_call | solution.py:810
  353.5 5.8 %shard_map.152 = (f32[256,1024]{1,0:T(8,128)}, f32[1,1024]{1,0:T(1,128)}, bf16[1024,512]{1,0:T(8,128)(2,1)}, bf16[64,512]{1,0:T(8,128)(2,1)}, bf16[64,512]{1,0:T...) custom-call(s32[18]{0:T(128)} %pad_add_fusion.meta_ref, f32[256,1024]{1,0:T(8,128)} %get-tuple-element.253.refs_0_, ...), custom_call_target="tpu_custom_call" | custom-call | flops 11600000000 | bytes 19720000 | tf_op jit(solution)/shard_map/pallas_call | solution.py:810
  370.4 4.7 shard_map.153
  378.1 3.9 shard_map.154
  387.1 4.0 collective-permute-done.74.refs_2_
  393.1 11.3 %shard_map.155 = (bf16[256,1024]{1,0:T(8,128)(2,1)}, bf16[256,2176]{1,0:T(8,128)(2,1)}, bf16[256,2176]{1,0:T(8,128)(2,1)}, bf16[256,2176]{1,0:T(8,128)(2,1)}, bf...) custom-call(s32[18]{0:T(128)} %pad_add_fusion.meta_ref, bf16[64,1536]{1,0:T(8,128)(2,1)} %get-tuple-element.270.refs_0_, ...), custom_call_target="tpu_custom_call" | custom-call | flops 6000000000 | bytes 10200000 | tf_op jit(solution)/shard_map/pallas_call | solution.py:810
  408.2 6.5 %collective-permute-done.96.a_ref = bf16[64,2304]{1,0:T(8,128)(2,1)S(1)} collective-permute-done((bf16[64,2304]{1,0:T(8,128)(2,1)S(1)}, bf16[64,2304]{1,0:T(8,128)(2,1)S(1)}, u32[]{:S(2)}, u32[]{:S(2)}) %collective-permute-start.96) | collective-permute-done | bytes 294944 | tf_op jit(solution)/shard_map/ppermute | solution.py:69
  420.4 4.2 collective-permute-done.83.a_ref
  424.9 9.8 %collective-permute-start.76 = (bf16[256,1024]{1,0:T(8,128)(2,1)}, bf16[256,1024]{1,0:T(8,128)(2,1)}, u32[]{:S(2)}, u32[]{:S(2)}) collective-permute-start(bf16[256,1024]{1,0:T(8,128)(2,1)} %get-tuple-element.279.refs_1_), channel_id=1, source_target_pairs={{0,32},{32,0},{1,33},{33,1},{2,34},{34,2},{3,35},{35,3},{4,36},{36... | collective-permute-start | bytes 1572872 | tf_op jit(solution)/shard_map/ppermute | solution.py:236
  439.5 5.2 add_convert_fusion
  464.4 4.0 collective-permute-start.82
  470.2 4.9 shard_map.166
  494.1 4.2 shard_map.160
  499.5 4.0 collective-permute-start.89
  508.3 3.6 collective-permute-start.94
  517.4 4.2 collective-permute-done.94.refs_0_
  522.5 5.1 shard_map.163
  530.5 3.4 copy.55
  (463 shorter events, 246.5 us)
Async XLA Ops:
  16.8 13.4 %collective-permute-start.9 = (bf16[64,2048]{1,0:T(8,128)(2,1)}, bf16[64,2048]{1,0:T(8,128)(2,1)S(1)}, u32[]{:S(2)}, u32[]{:S(2)}) collective-permute-start(bf16[64,2048]{1,0:T(8,128)(2,1)} %shard_map.129.refs_0_), channel_id=1, source_target_pairs={{0,3},{1,0},{2,1},{3,2},{8,11},{9,8},{10,9},{11,10},{16,19},{17,16... | collective-permute-start | bytes 786440 | tf_op jit(solution)/shard_map/ppermute | solution.py:69
  25.6 18.6 %collective-permute-start.23 = (bf16[32,3072]{1,0:T(8,128)(2,1)}, bf16[32,3072]{1,0:T(8,128)(2,1)S(1)}, u32[]{:S(2)}, u32[]{:S(2)}) collective-permute-start(bf16[32,3072]{1,0:T(8,128)(2,1)} %get-tuple-element.171), channel_id=1, source_target_pairs={{0,32},{4,0},{32,36},{36,4},{1,33},{5,1},{33,37},{37,5},{2,34},{6,... | collective-permute-start | bytes 589832 | tf_op jit(solution)/shard_map/ppermute | solution.py:227
  41.8 29.5 %collective-permute-start.13 = (bf16[256,2048]{1,0:T(8,128)(2,1)}, bf16[256,2048]{1,0:T(8,128)(2,1)S(1)}, u32[]{:S(2)}, u32[]{:S(2)}) collective-permute-start(bf16[256,2048]{1,0:T(8,128)(2,1)} %shard_map.133.refs_4_.refs_12_), channel_id=1, source_target_pairs={{0,24},{1,25},{2,26},{3,27},{8,0},{9,1},{10,2},{11,3},{16,8},{17,9... | collective-permute-start | bytes 3145736 | tf_op jit(solution)/shard_map/ppermute | solution.py:69
  47.8 22.7 %collective-permute-start.26 = (bf16[64,6656]{1,0:T(8,128)(2,1)}, bf16[64,6656]{1,0:T(8,128)(2,1)S(1)}, u32[]{:S(2)}, u32[]{:S(2)}) collective-permute-start(bf16[64,6656]{1,0:T(8,128)(2,1)} %shard_map.137.refs_0_), channel_id=1, source_target_pairs={{0,3},{1,0},{2,1},{3,2},{8,11},{9,8},{10,9},{11,10},{16,19},{17,16... | collective-permute-start | bytes 2555912 | tf_op jit(solution)/shard_map/ppermute | solution.py:69
  55.7 20.5 %collective-permute-start.12 = (bf16[256,2048]{1,0:T(8,128)(2,1)S(1)}, bf16[256,2048]{1,0:T(8,128)(2,1)S(1)}, u32[]{:S(2)}, u32[]{:S(2)}) collective-permute-start(bf16[256,2048]{1,0:T(8,128)(2,1)S(1)} %copy-done.21), channel_id=1, source_target_pairs={{0,8},{1,9},{2,10},{3,11},{8,16},{9,17},{10,18},{11,19},{16,24},{1... | collective-permute-start | bytes 3145736 | tf_op jit(solution)/shard_map/ppermute | solution.py:69
  58.7 20.2 %collective-permute-start.25 = (bf16[64,6656]{1,0:T(8,128)(2,1)S(1)}, bf16[64,6656]{1,0:T(8,128)(2,1)S(1)}, u32[]{:S(2)}, u32[]{:S(2)}) collective-permute-start(bf16[64,6656]{1,0:T(8,128)(2,1)S(1)} %copy-done.4), channel_id=1, source_target_pairs={{0,1},{1,2},{2,3},{3,0},{8,9},{9,10},{10,11},{11,8},{16,17},{17,18... | collective-permute-start | bytes 2555912 | tf_op jit(solution)/shard_map/ppermute | solution.py:69
  70.4 15.2 %collective-permute-start.30 = (bf16[64,4608]{1,0:T(8,128)(2,1)}, bf16[64,4608]{1,0:T(8,128)(2,1)S(1)}, u32[]{:S(2)}, u32[]{:S(2)}) collective-permute-start(bf16[64,4608]{1,0:T(8,128)(2,1)} %shard_map.139.refs_0_), channel_id=1, source_target_pairs={{0,1},{1,2},{2,3},{3,0},{8,9},{9,10},{10,11},{11,8},{16,17},{17,18... | collective-permute-start | bytes 1769480 | tf_op jit(solution)/shard_map/ppermute | solution.py:69
  71.3 15.0 %collective-permute-start.28 = (bf16[64,3328]{1,0:T(8,128)(2,1)}, bf16[64,3328]{1,0:T(8,128)(2,1)}, u32[]{:S(2)}, u32[]{:S(2)}) collective-permute-start(bf16[64,3328]{1,0:T(8,128)(2,1)} %slice.217), channel_id=1, source_target_pairs={{0,3},{1,0},{2,1},{3,2},{8,11},{9,8},{10,9},{11,10},{16,19},{17,16... | collective-permute-start | bytes 1277960 | tf_op jit(solution)/shard_map/ppermute | solution.py:69
  76.2 22.4 %collective-permute-start.15 = (bf16[256,1024]{1,0:T(8,128)(2,1)S(1)}, bf16[256,1024]{1,0:T(8,128)(2,1)}, u32[]{:S(2)}, u32[]{:S(2)}) collective-permute-start(bf16[256,1024]{1,0:T(8,128)(2,1)S(1)} %slice.214), channel_id=1, source_target_pairs={{0,24},{1,25},{2,26},{3,27},{8,0},{9,1},{10,2},{11,3},{16,8},{17,9... | collective-permute-start | bytes 1572872 | tf_op jit(solution)/shard_map/ppermute | solution.py:69
  78.9 20.3 %collective-permute-start.14 = (bf16[256,1024]{1,0:T(8,128)(2,1)}, bf16[256,1024]{1,0:T(8,128)(2,1)}, u32[]{:S(2)}, u32[]{:S(2)}) collective-permute-start(bf16[256,1024]{1,0:T(8,128)(2,1)} %slice.213), channel_id=1, source_target_pairs={{0,8},{1,9},{2,10},{3,11},{8,16},{9,17},{10,18},{11,19},{16,24},{1... | collective-permute-start | bytes 1572872 | tf_op jit(solution)/shard_map/ppermute | solution.py:69
  79.8 14.9 %collective-permute-start.27 = (bf16[64,3328]{1,0:T(8,128)(2,1)}, bf16[64,3328]{1,0:T(8,128)(2,1)}, u32[]{:S(2)}, u32[]{:S(2)}) collective-permute-start(bf16[64,3328]{1,0:T(8,128)(2,1)} %slice.216), channel_id=1, source_target_pairs={{0,1},{1,2},{2,3},{3,0},{8,9},{9,10},{10,11},{11,8},{16,17},{17,18... | collective-permute-start | bytes 1277960 | tf_op jit(solution)/shard_map/ppermute | solution.py:69
  85.6 13.0 %collective-permute-start.33 = (bf16[64,2304]{1,0:T(8,128)(2,1)S(1)}, bf16[64,2304]{1,0:T(8,128)(2,1)S(1)}, u32[]{:S(2)}, u32[]{:S(2)}) collective-permute-start(bf16[64,2304]{1,0:T(8,128)(2,1)S(1)} %slice.219), channel_id=1, source_target_pairs={{0,3},{1,0},{2,1},{3,2},{8,11},{9,8},{10,9},{11,10},{16,19},{17,16... | collective-permute-start | bytes 884744 | tf_op jit(solution)/shard_map/ppermute | solution.py:69
  86.4 12.2 %collective-permute-start.31 = (bf16[64,2304]{1,0:T(8,128)(2,1)S(1)}, bf16[64,2304]{1,0:T(8,128)(2,1)S(1)}, u32[]{:S(2)}, u32[]{:S(2)}) collective-permute-start(bf16[64,2304]{1,0:T(8,128)(2,1)S(1)} %slice.218), channel_id=1, source_target_pairs={{0,1},{1,2},{2,3},{3,0},{8,9},{9,10},{10,11},{11,8},{16,17},{17,18... | collective-permute-start | bytes 884744 | tf_op jit(solution)/shard_map/ppermute | solution.py:69
  99.4 39.5 %collective-permute-start.35 = (bf16[256,6656]{1,0:T(8,128)(2,1)}, bf16[256,6656]{1,0:T(8,128)(2,1)S(1)}, u32[]{:S(2)}, u32[]{:S(2)}) collective-permute-start(bf16[256,6656]{1,0:T(8,128)(2,1)} %shard_map.138.refs_6_.refs_4_.refs_7_.refs_11_), channel_id=1, source_target_pairs={{0,24},{1,25},{2,26},{3,27},{8,0},{9,1},{10,2},{11,3},{16,8},{17,9... | collective-permute-start | bytes 10223624 | tf_op jit(solution)/shard_map/ppermute | solution.py:69
  100.7 40.9 %collective-permute-start.34 = (bf16[256,6656]{1,0:T(8,128)(2,1)}, bf16[256,6656]{1,0:T(8,128)(2,1)}, u32[]{:S(2)}, u32[]{:S(2)}) collective-permute-start(bf16[256,6656]{1,0:T(8,128)(2,1)} %shard_map.138.refs_6_.refs_4_.refs_7_.refs_11_), channel_id=1, source_target_pairs={{0,8},{1,9},{2,10},{3,11},{8,16},{9,17},{10,18},{11,19},{16,24},{1... | collective-permute-start | bytes 10223624 | tf_op jit(solution)/shard_map/ppermute | solution.py:69
  102.2 13.2 %collective-permute-start.6 = (bf16[128,1152]{1,0:T(8,128)(2,1)S(1)}, bf16[128,1152]{1,0:T(8,128)(2,1)S(1)}, u32[]{:S(2)}, u32[]{:S(2)}) collective-permute-start(bf16[128,1152]{1,0:T(8,128)(2,1)S(1)} %fusion.5), channel_id=1, source_target_pairs={{0,32},{4,0},{32,36},{36,4},{1,33},{5,1},{33,37},{37,5},{2,34},{6,... | collective-permute-start | bytes 884744 | tf_op jit(solution)/shard_map/ppermute | solution.py:227
  124.1 19.2 %collective-permute-start.16 = (bf16[64,1536]{1,0:T(8,128)(2,1)}, bf16[64,1536]{1,0:T(8,128)(2,1)S(1)}, u32[]{:S(2)}, u32[]{:S(2)}) collective-permute-start(bf16[64,1536]{1,0:T(8,128)(2,1)} %get-tuple-element.186), channel_id=1, source_target_pairs={{0,4},{4,0},{64,68},{68,64},{1,5},{5,1},{65,69},{69,65},{2,6},{6,2... | collective-permute-start | bytes 589832 | tf_op jit(solution)/shard_map/ppermute | solution.py:246
  124.2 19.1 %collective-permute-start.17 = (bf16[64,1536]{1,0:T(8,128)(2,1)}, bf16[64,1536]{1,0:T(8,128)(2,1)S(1)}, u32[]{:S(2)}, u32[]{:S(2)}) collective-permute-start(bf16[64,1536]{1,0:T(8,128)(2,1)} %get-tuple-element.187), channel_id=1, source_target_pairs={{0,64},{4,68},{64,0},{68,4},{1,65},{5,69},{65,1},{69,5},{2,66},{6,... | collective-permute-start | bytes 589832 | tf_op jit(solution)/shard_map/ppermute | solution.py:246
  127.2 16.1 %collective-permute-start.18 = (bf16[64,1536]{1,0:T(8,128)(2,1)}, bf16[64,1536]{1,0:T(8,128)(2,1)S(1)}, u32[]{:S(2)}, u32[]{:S(2)}) collective-permute-start(bf16[64,1536]{1,0:T(8,128)(2,1)} %get-tuple-element.188), channel_id=1, source_target_pairs={{0,68},{4,64},{64,4},{68,0},{1,69},{5,65},{65,5},{69,1},{2,70},{6,... | collective-permute-start | bytes 589832 | tf_op jit(solution)/shard_map/ppermute | solution.py:246
  139.0 26.8 %collective-permute-start.37 = (bf16[256,3328]{1,0:T(8,128)(2,1)S(1)}, bf16[256,3328]{1,0:T(8,128)(2,1)}, u32[]{:S(2)}, u32[]{:S(2)}) collective-permute-start(bf16[256,3328]{1,0:T(8,128)(2,1)S(1)} %slice.221), channel_id=1, source_target_pairs={{0,24},{1,25},{2,26},{3,27},{8,0},{9,1},{10,2},{11,3},{16,8},{17,9... | collective-permute-start | bytes 5111816 | tf_op jit(solution)/shard_map/ppermute | solution.py:69
  143.2 22.7 %collective-permute-start.36 = (bf16[256,3328]{1,0:T(8,128)(2,1)S(1)}, bf16[256,3328]{1,0:T(8,128)(2,1)}, u32[]{:S(2)}, u32[]{:S(2)}) collective-permute-start(bf16[256,3328]{1,0:T(8,128)(2,1)S(1)} %slice.220), channel_id=1, source_target_pairs={{0,8},{1,9},{2,10},{3,11},{8,16},{9,17},{10,18},{11,19},{16,24},{1... | collective-permute-start | bytes 5111816 | tf_op jit(solution)/shard_map/ppermute | solution.py:69
  183.8 32.8 %collective-permute-start.47 = (bf16[256,4608]{1,0:T(8,128)(2,1)S(1)}, bf16[256,4608]{1,0:T(8,128)(2,1)S(1)}, u32[]{:S(2)}, u32[]{:S(2)}) collective-permute-start(bf16[256,4608]{1,0:T(8,128)(2,1)S(1)} %copy-done.6), channel_id=1, source_target_pairs={{0,24},{1,25},{2,26},{3,27},{8,0},{9,1},{10,2},{11,3},{16,8},{17,9... | collective-permute-start | bytes 7077896 | tf_op jit(solution)/shard_map/ppermute | solution.py:69
  183.8 34.8 %collective-permute-start.46 = (bf16[256,4608]{1,0:T(8,128)(2,1)S(1)}, bf16[256,4608]{1,0:T(8,128)(2,1)}, u32[]{:S(2)}, u32[]{:S(2)}) collective-permute-start(bf16[256,4608]{1,0:T(8,128)(2,1)S(1)} %copy-done.6), channel_id=1, source_target_pairs={{0,8},{1,9},{2,10},{3,11},{8,16},{9,17},{10,18},{11,19},{16,24},{1... | collective-permute-start | bytes 7077896 | tf_op jit(solution)/shard_map/ppermute | solution.py:69
  194.6 12.1 %collective-permute-start.40 = (bf16[64,1536]{1,0:T(8,128)(2,1)}, bf16[64,1536]{1,0:T(8,128)(2,1)S(1)}, u32[]{:S(2)}, u32[]{:S(2)}) collective-permute-start(bf16[64,1536]{1,0:T(8,128)(2,1)} %get-tuple-element.202), channel_id=1, source_target_pairs={{0,64},{4,68},{64,0},{68,4},{1,65},{5,69},{65,1},{69,5},{2,66},{6,... | collective-permute-start | bytes 589832 | tf_op jit(solution)/shard_map/ppermute | solution.py:246
  216.8 19.2 %collective-permute-start.49 = (bf16[256,2304]{1,0:T(8,128)(2,1)S(1)}, bf16[256,2304]{1,0:T(8,128)(2,1)S(1)}, u32[]{:S(2)}, u32[]{:S(2)}) collective-permute-start(bf16[256,2304]{1,0:T(8,128)(2,1)S(1)} %slice.225), channel_id=1, source_target_pairs={{0,24},{1,25},{2,26},{3,27},{8,0},{9,1},{10,2},{11,3},{16,8},{17,9... | collective-permute-start | bytes 3538952 | tf_op jit(solution)/shard_map/ppermute | solution.py:69
  220.0 16.7 %collective-permute-start.48 = (bf16[256,2304]{1,0:T(8,128)(2,1)S(1)}, bf16[256,2304]{1,0:T(8,128)(2,1)}, u32[]{:S(2)}, u32[]{:S(2)}) collective-permute-start(bf16[256,2304]{1,0:T(8,128)(2,1)S(1)} %slice.224), channel_id=1, source_target_pairs={{0,8},{1,9},{2,10},{3,11},{8,16},{9,17},{10,18},{11,19},{16,24},{1... | collective-permute-start | bytes 3538952 | tf_op jit(solution)/shard_map/ppermute | solution.py:69
  254.3 19.3 %collective-permute-start.50 = (bf16[256,1024]{1,0:T(8,128)(2,1)}, bf16[256,1024]{1,0:T(8,128)(2,1)S(1)}, u32[]{:S(2)}, u32[]{:S(2)}) collective-permute-start(bf16[256,1024]{1,0:T(8,128)(2,1)} %get-tuple-element.211), channel_id=1, source_target_pairs={{0,32},{32,0},{1,33},{33,1},{2,34},{34,2},{3,35},{35,3},{4,36},{36... | collective-permute-start | bytes 1572872 | tf_op jit(solution)/shard_map/ppermute | solution.py:236
  270.9 17.3 %collective-permute-start.59 = (bf16[256,2304]{1,0:T(8,128)(2,1)}, bf16[256,2304]{1,0:T(8,128)(2,1)S(1)}, u32[]{:S(2)}, u32[]{:S(2)}) collective-permute-start(bf16[256,2304]{1,0:T(8,128)(2,1)} %get-tuple-element.230), channel_id=1, source_target_pairs={{0,8},{1,9},{2,10},{3,11},{8,16},{9,17},{10,18},{11,19},{16,24},{1... | collective-permute-start | bytes 3538952 | tf_op jit(solution)/shard_map/ppermute | solution.py:69
  270.9 17.3 %collective-permute-start.60 = (bf16[256,2304]{1,0:T(8,128)(2,1)}, bf16[256,2304]{1,0:T(8,128)(2,1)S(1)}, u32[]{:S(2)}, u32[]{:S(2)}) collective-permute-start(bf16[256,2304]{1,0:T(8,128)(2,1)} %get-tuple-element.231), channel_id=1, source_target_pairs={{0,24},{1,25},{2,26},{3,27},{8,0},{9,1},{10,2},{11,3},{16,8},{17,9... | collective-permute-start | bytes 3538952 | tf_op jit(solution)/shard_map/ppermute | solution.py:69
  284.4 17.9 %collective-permute-start.51 = (bf16[128,1024]{1,0:T(8,128)(2,1)S(1)}, bf16[128,1024]{1,0:T(8,128)(2,1)S(1)}, u32[]{:S(2)}, u32[]{:S(2)}) collective-permute-start(bf16[128,1024]{1,0:T(8,128)(2,1)S(1)} %slice_select_fusion.1), channel_id=1, source_target_pairs={{0,0},{4,32},{32,4},{36,36},{1,1},{5,33},{33,5},{37,37},{2,2},{6,3... | collective-permute-start | bytes 786440 | tf_op jit(solution)/shard_map/ppermute | solution.py:232
  293.4 30.8 %collective-permute-start.65 = (bf16[256,4608]{1,0:T(8,128)(2,1)}, bf16[256,4608]{1,0:T(8,128)(2,1)S(1)}, u32[]{:S(2)}, u32[]{:S(2)}) collective-permute-start(bf16[256,4608]{1,0:T(8,128)(2,1)} %get-tuple-element.235.refs_9_), channel_id=1, source_target_pairs={{0,8},{1,9},{2,10},{3,11},{8,16},{9,17},{10,18},{11,19},{16,24},{1... | collective-permute-start | bytes 7077896 | tf_op jit(solution)/shard_map/ppermute | solution.py:69
  293.5 30.7 %collective-permute-start.66 = (bf16[256,4608]{1,0:T(8,128)(2,1)}, bf16[256,4608]{1,0:T(8,128)(2,1)S(1)}, u32[]{:S(2)}, u32[]{:S(2)}) collective-permute-start(bf16[256,4608]{1,0:T(8,128)(2,1)} %get-tuple-element.234.refs_8_), channel_id=1, source_target_pairs={{0,24},{1,25},{2,26},{3,27},{8,0},{9,1},{10,2},{11,3},{16,8},{17,9... | collective-permute-start | bytes 7077896 | tf_op jit(solution)/shard_map/ppermute | solution.py:69
  346.1 22.5 %collective-permute-start.71 = (bf16[256,3328]{1,0:T(8,128)(2,1)}, bf16[256,3328]{1,0:T(8,128)(2,1)S(1)}, u32[]{:S(2)}, u32[]{:S(2)}) collective-permute-start(bf16[256,3328]{1,0:T(8,128)(2,1)} %get-tuple-element.264), channel_id=1, source_target_pairs={{0,8},{1,9},{2,10},{3,11},{8,16},{9,17},{10,18},{11,19},{16,24},{1... | collective-permute-start | bytes 5111816 | tf_op jit(solution)/shard_map/ppermute | solution.py:69
  346.2 22.4 %collective-permute-start.72 = (bf16[256,3328]{1,0:T(8,128)(2,1)}, bf16[256,3328]{1,0:T(8,128)(2,1)S(1)}, u32[]{:S(2)}, u32[]{:S(2)}) collective-permute-start(bf16[256,3328]{1,0:T(8,128)(2,1)} %get-tuple-element.265), channel_id=1, source_target_pairs={{0,24},{1,25},{2,26},{3,27},{8,0},{9,1},{10,2},{11,3},{16,8},{17,9... | collective-permute-start | bytes 5111816 | tf_op jit(solution)/shard_map/ppermute | solution.py:69
  375.1 62.3 %collective-permute-start.77 = (bf16[256,6656]{1,0:T(8,128)(2,1)}, bf16[256,6656]{1,0:T(8,128)(2,1)S(1)}, u32[]{:S(2)}, u32[]{:S(2)}) collective-permute-start(bf16[256,6656]{1,0:T(8,128)(2,1)} %get-tuple-element.269.refs_9_), channel_id=1, source_target_pairs={{0,8},{1,9},{2,10},{3,11},{8,16},{9,17},{10,18},{11,19},{16,24},{1... | collective-permute-start | bytes 10223624 | tf_op jit(solution)/shard_map/ppermute | solution.py:69
  375.2 62.2 %collective-permute-start.78 = (bf16[256,6656]{1,0:T(8,128)(2,1)}, bf16[256,6656]{1,0:T(8,128)(2,1)}, u32[]{:S(2)}, u32[]{:S(2)}) collective-permute-start(bf16[256,6656]{1,0:T(8,128)(2,1)} %get-tuple-element.268.refs_8_), channel_id=1, source_target_pairs={{0,24},{1,25},{2,26},{3,27},{8,0},{9,1},{10,2},{11,3},{16,8},{17,9... | collective-permute-start | bytes 10223624 | tf_op jit(solution)/shard_map/ppermute | solution.py:69
  407.1 17.5 %collective-permute-start.83 = (bf16[256,1024]{1,0:T(8,128)(2,1)}, bf16[256,1024]{1,0:T(8,128)(2,1)S(1)}, u32[]{:S(2)}, u32[]{:S(2)}) collective-permute-start(bf16[256,1024]{1,0:T(8,128)(2,1)} %get-tuple-element.292), channel_id=1, source_target_pairs={{0,8},{1,9},{2,10},{3,11},{8,16},{9,17},{10,18},{11,19},{16,24},{1... | collective-permute-start | bytes 1572872 | tf_op jit(solution)/shard_map/ppermute | solution.py:69
  418.2 19.2 %collective-permute-start.99 = (bf16[64,4608]{1,0:T(8,128)(2,1)}, bf16[64,4608]{1,0:T(8,128)(2,1)S(1)}, u32[]{:S(2)}, u32[]{:S(2)}) collective-permute-start(bf16[64,4608]{1,0:T(8,128)(2,1)} %get-tuple-element.320), channel_id=1, source_target_pairs={{0,3},{1,0},{2,1},{3,2},{8,11},{9,8},{10,9},{11,10},{16,19},{17,16... | collective-permute-start | bytes 1769480 | tf_op jit(solution)/shard_map/ppermute | solution.py:69
  424.6 12.8 %collective-permute-start.98 = (bf16[64,4608]{1,0:T(8,128)(2,1)}, bf16[64,4608]{1,0:T(8,128)(2,1)S(1)}, u32[]{:S(2)}, u32[]{:S(2)}) collective-permute-start(bf16[64,4608]{1,0:T(8,128)(2,1)} %get-tuple-element.319), channel_id=1, source_target_pairs={{0,1},{1,2},{2,3},{3,0},{8,9},{9,10},{10,11},{11,8},{16,17},{17,18... | collective-permute-start | bytes 1769480 | tf_op jit(solution)/shard_map/ppermute | solution.py:69
  424.9 69.2 %collective-permute-start.76 = (bf16[256,1024]{1,0:T(8,128)(2,1)}, bf16[256,1024]{1,0:T(8,128)(2,1)}, u32[]{:S(2)}, u32[]{:S(2)}) collective-permute-start(bf16[256,1024]{1,0:T(8,128)(2,1)} %get-tuple-element.279.refs_1_), channel_id=1, source_target_pairs={{0,32},{32,0},{1,33},{33,1},{2,34},{34,2},{3,35},{35,3},{4,36},{36... | collective-permute-start | bytes 1572872 | tf_op jit(solution)/shard_map/ppermute | solution.py:236
  450.5 24.6 %collective-permute-start.85 = (bf16[256,2176]{1,0:T(8,128)(2,1)S(1)}, bf16[256,2176]{1,0:T(8,128)(2,1)S(1)}, u32[]{:S(2)}, u32[]{:S(2)}) collective-permute-start(bf16[256,2176]{1,0:T(8,128)(2,1)S(1)} %copy-done.19), channel_id=1, source_target_pairs={{0,8},{1,9},{2,10},{3,11},{8,16},{9,17},{10,18},{11,19},{16,24},{1... | collective-permute-start | bytes 3342344 | tf_op jit(solution)/shard_map/ppermute | solution.py:69
  450.5 24.6 %collective-permute-start.86 = (bf16[256,2176]{1,0:T(8,128)(2,1)S(1)}, bf16[256,2176]{1,0:T(8,128)(2,1)}, u32[]{:S(2)}, u32[]{:S(2)}) collective-permute-start(bf16[256,2176]{1,0:T(8,128)(2,1)S(1)} %copy-done.18), channel_id=1, source_target_pairs={{0,24},{1,25},{2,26},{3,27},{8,0},{9,1},{10,2},{11,3},{16,8},{17,9... | collective-permute-start | bytes 3342344 | tf_op jit(solution)/shard_map/ppermute | solution.py:69
  464.4 24.9 %collective-permute-start.82 = (bf16[64,6656]{1,0:T(8,128)(2,1)}, bf16[64,6656]{1,0:T(8,128)(2,1)}, u32[]{:S(2)}, u32[]{:S(2)}) collective-permute-start(bf16[64,6656]{1,0:T(8,128)(2,1)} %get-tuple-element.286), channel_id=1, source_target_pairs={{0,3},{1,0},{2,1},{3,2},{8,11},{9,8},{10,9},{11,10},{16,19},{17,16... | collective-permute-start | bytes 2555912 | tf_op jit(solution)/shard_map/ppermute | solution.py:69
  468.5 20.8 %collective-permute-start.81 = (bf16[64,6656]{1,0:T(8,128)(2,1)}, bf16[64,6656]{1,0:T(8,128)(2,1)}, u32[]{:S(2)}, u32[]{:S(2)}) collective-permute-start(bf16[64,6656]{1,0:T(8,128)(2,1)} %get-tuple-element.285), channel_id=1, source_target_pairs={{0,1},{1,2},{2,3},{3,0},{8,9},{9,10},{10,11},{11,8},{16,17},{17,18... | collective-permute-start | bytes 2555912 | tf_op jit(solution)/shard_map/ppermute | solution.py:69
  486.6 17.0 %collective-permute-start.90 = (bf16[64,2176]{1,0:T(8,128)(2,1)}, bf16[64,2176]{1,0:T(8,128)(2,1)S(1)}, u32[]{:S(2)}, u32[]{:S(2)}) collective-permute-start(bf16[64,2176]{1,0:T(8,128)(2,1)} %get-tuple-element.305), channel_id=1, source_target_pairs={{0,1},{1,2},{2,3},{3,0},{8,9},{9,10},{10,11},{11,8},{16,17},{17,18... | collective-permute-start | bytes 835592 | tf_op jit(solution)/shard_map/ppermute | solution.py:69
  487.7 15.8 %collective-permute-start.91 = (bf16[64,2176]{1,0:T(8,128)(2,1)}, bf16[64,2176]{1,0:T(8,128)(2,1)S(1)}, u32[]{:S(2)}, u32[]{:S(2)}) collective-permute-start(bf16[64,2176]{1,0:T(8,128)(2,1)} %get-tuple-element.304), channel_id=1, source_target_pairs={{0,3},{1,0},{2,1},{3,2},{8,11},{9,8},{10,9},{11,10},{16,19},{17,16... | collective-permute-start | bytes 835592 | tf_op jit(solution)/shard_map/ppermute | solution.py:69
  499.5 12.4 %collective-permute-start.89 = (bf16[128,1024]{1,0:T(8,128)(2,1)S(1)}, bf16[128,1024]{1,0:T(8,128)(2,1)S(1)}, u32[]{:S(2)}, u32[]{:S(2)}) collective-permute-start(bf16[128,1024]{1,0:T(8,128)(2,1)S(1)} %slice_select_fusion), channel_id=1, source_target_pairs={{0,0},{4,32},{32,4},{36,36},{1,1},{5,33},{33,5},{37,37},{2,2},{6,3... | collective-permute-start | bytes 786440 | tf_op jit(solution)/shard_map/ppermute | solution.py:232
  508.3 13.4 %collective-permute-start.94 = (bf16[32,8704]{1,0:T(8,128)(2,1)S(1)}, bf16[32,8704]{1,0:T(8,128)(2,1)S(1)}, u32[]{:S(2)}, u32[]{:S(2)}) collective-permute-start(bf16[32,8704]{1,0:T(8,128)(2,1)S(1)} %copy-done.57), channel_id=1, source_target_pairs={{0,0},{4,32},{32,4},{36,36},{1,1},{5,33},{33,5},{37,37},{2,2},{6,3... | collective-permute-start | bytes 1671176 | tf_op jit(solution)/shard_map/ppermute | solution.py:232
  (151 other events, 875.6 us)
